TPU v7x, 512 devices: a whole 4x4x16 slice. The times are simulated.
512 devices in a mesh: wide: 32 (over x, z_lo), narrow: 16 (over z_hi, y, core).
Axes of the slice: x: 4, y: 4, z: 16 (z_hi: 2, z_lo: 8; z = z_hi * 8 + z_lo), core: 2. Of those that a mesh axis runs over, the one named last changes fastest.
Arguments:
- query_in: bfloat16 [32768, 4096], P(('wide', 'narrow')), may hold values from -100 to 100
- key_in: bfloat16 [32768, 4096], P(('wide', 'narrow')), may hold values from -20 to 20
- value_in: bfloat16 [32768, 4096], P(('wide', 'narrow')), may hold values from -3 to 3
- grad_out: bfloat16 [32768, 4096], P(('wide', 'narrow')), may hold values from -6 to 6
- row_start: int32 [32], replicated, may hold values from 0 to 1023
- col_start: int32 [8], replicated, may hold values from 0 to 31
Outputs:
- grad_query: bfloat16 [32768, 4096], P(('wide', 'narrow'))
- grad_key: bfloat16 [32768, 4096], P(('wide', 'narrow'))
- grad_value: bfloat16 [32768, 4096], P(('wide', 'narrow'))
All inputs are finite; a program needn't handle non-finite values.
Results may differ from a plain program's by a relative error of at most 0.01055.
Values may be sent and summed in bfloat16 or wider, within the bound.
No kernel may reach another device: no remote copies, remote signals or barrier semaphores. Data moves between devices by JAX's collectives and lax.ppermute only.
A program may use at most 128 MiB of HBM per device.

v0:
```python
import math

import jax
import jax.numpy as jnp
from jax import lax
from jax.sharding import PartitionSpec as P

HEAD = 128
CB = 128


masked_low = -1e30


def merge_stats(maxima_a, totals_a, weighted_a, maxima_b, totals_b, weighted_b):
    maxima = jnp.maximum(maxima_a, maxima_b)
    factor_a = jnp.exp(maxima_a - maxima)
    factor_b = jnp.exp(maxima_b - maxima)
    totals = totals_a * factor_a + totals_b * factor_b
    return (maxima + jnp.log(totals), (weighted_a * factor_a + weighted_b * factor_b) / totals)


def body(query_in, key_in, value_in, grad_out, row_start, col_start):
    score_scale = 1.0 / math.sqrt(HEAD)
    q_all, k_all, v_all, g_all = (
        lax.all_to_all(query_in, "narrow", split_axis=1, concat_axis=0, tiled=True),
        lax.all_to_all(key_in, "narrow", split_axis=1, concat_axis=0, tiled=True),
        lax.all_to_all(value_in, "narrow", split_axis=1, concat_axis=0, tiled=True),
        lax.all_to_all(grad_out, "narrow", split_axis=1, concat_axis=0, tiled=True),
    )
    length = q_all.shape[0]
    heads_here = q_all.shape[1] // HEAD
    lane_count = lax.axis_size("wide")
    lane_index = lax.axis_index("wide")
    width_col = length // lane_count
    positions = jnp.arange(length, dtype=jnp.int32)
    start_row = jnp.sum(
        jnp.where(jnp.arange(lane_count, dtype=jnp.int32) == lane_index, row_start, 0)
    )
    row_mask = (positions[None, :] <= positions[:, None]) & (
        (positions[None, :] >= start_row) | (positions[None, :] == positions[:, None])
    )
    row_scores, row_dprob, maxima_list, totals_list, weighted_list = ([], [], [], [], [])
    for head_index in range(heads_here):
        feat_cols = slice(head_index * HEAD, (head_index + 1) * HEAD)
        scores = (
            jnp.einsum(
                "td,ud->tu",
                q_all[:, feat_cols],
                k_all[:, feat_cols],
                preferred_element_type=jnp.float32,
            )
            * score_scale
        )
        dprob = jnp.einsum(
            "td,ud->tu",
            g_all[:, feat_cols],
            v_all[:, feat_cols],
            preferred_element_type=jnp.float32,
        )
        maxima = jnp.max(jnp.where(row_mask, scores, masked_low), 1)
        expo_vals = jnp.where(row_mask, jnp.exp(scores - maxima[:, None]), 0.0)
        row_scores.append(scores)
        row_dprob.append(dprob)
        maxima_list.append(maxima)
        totals_list.append(jnp.sum(expo_vals, 1))
        weighted_list.append(jnp.sum(expo_vals * dprob, 1))
    maxima_rows = jnp.stack(maxima_list, axis=1)
    totals_rows = jnp.stack(totals_list, axis=1)
    weighted_rows = jnp.stack(weighted_list, axis=1)
    q_col, k_col, v_col, g_col = (
        lax.all_to_all(q_all, "wide", split_axis=0, concat_axis=0, tiled=True),
        lax.all_to_all(k_all, "wide", split_axis=0, concat_axis=0, tiled=True),
        lax.all_to_all(v_all, "wide", split_axis=0, concat_axis=0, tiled=True),
        lax.all_to_all(g_all, "wide", split_axis=0, concat_axis=0, tiled=True),
    )
    q_four = q_col.reshape(lane_count, width_col, heads_here, HEAD)
    k_four = k_col.reshape(lane_count, width_col, heads_here, HEAD)
    v_four = v_col.reshape(lane_count, width_col, heads_here, HEAD)
    g_four = g_col.reshape(lane_count, width_col, heads_here, HEAD)
    col_scores = (
        jnp.einsum("rxhd,sxhd->xhrs", q_four, k_four, preferred_element_type=jnp.float32)
        * score_scale
    )
    col_dprob = jnp.einsum("rxhd,sxhd->xhrs", g_four, v_four, preferred_element_type=jnp.float32)
    col_number = lane_index * width_col + jnp.arange(width_col, dtype=jnp.int32)
    block_ids = col_number // CB
    block_count = col_start.shape[0]
    col_first = jnp.sum(
        jnp.where(
            block_ids[:, None] == jnp.arange(block_count, dtype=jnp.int32)[None, :],
            col_start[None, :],
            0,
        ),
        1,
    )
    row_ids = jnp.arange(lane_count, dtype=jnp.int32)
    col_mask = (
        (row_ids[None, None, :] < row_ids[None, :, None])
        & (row_ids[None, None, :] >= col_first[:, None, None])
    )[:, None]
    maxima_col = jnp.max(jnp.where(col_mask, col_scores, masked_low), -1)
    expo_col = jnp.where(col_mask, jnp.exp(col_scores - maxima_col[..., None]), 0.0)
    totals_col = jnp.sum(expo_col, -1)
    weighted_col = jnp.sum(expo_col * col_dprob, -1)

    def tokens_major(array):
        return array.transpose(2, 0, 1).reshape(lane_count * width_col, heads_here)

    def heads_major(array):
        return array.reshape(lane_count, width_col, heads_here).transpose(1, 2, 0)[..., None]

    max_back, tot_back, wgt_back = (
        lax.all_to_all(tokens_major(maxima_col), "wide", split_axis=0, concat_axis=0, tiled=True),
        lax.all_to_all(tokens_major(totals_col), "wide", split_axis=0, concat_axis=0, tiled=True),
        lax.all_to_all(tokens_major(weighted_col), "wide", split_axis=0, concat_axis=0, tiled=True),
    )
    lse_rows, delta_rows = merge_stats(
        maxima_rows, totals_rows, weighted_rows, max_back, tot_back, wgt_back
    )
    lse_cols, delta_cols = (
        lax.all_to_all(lse_rows, "wide", split_axis=0, concat_axis=0, tiled=True),
        lax.all_to_all(delta_rows, "wide", split_axis=0, concat_axis=0, tiled=True),
    )
    col_probs = jnp.where(col_mask, jnp.exp(col_scores - heads_major(lse_cols)), 0.0)
    col_dscore = (col_probs * (col_dprob - heads_major(delta_cols))).astype(jnp.bfloat16)
    col_weights = col_probs.astype(jnp.bfloat16)
    grad_q_col = (
        jnp.einsum("xhrs,sxhd->rxhd", col_dscore, k_four, preferred_element_type=jnp.float32)
        * score_scale
    ).reshape(length, heads_here * HEAD)
    grad_k_col = (
        jnp.einsum("xhrs,rxhd->sxhd", col_dscore, q_four, preferred_element_type=jnp.float32)
        * score_scale
    ).reshape(length, heads_here * HEAD)
    grad_v_col = jnp.einsum(
        "xhrs,rxhd->sxhd", col_weights, g_four, preferred_element_type=jnp.float32
    ).reshape(length, heads_here * HEAD)
    q_back, k_back, v_back = (
        lax.all_to_all(grad_q_col, "wide", split_axis=0, concat_axis=0, tiled=True),
        lax.all_to_all(grad_k_col, "wide", split_axis=0, concat_axis=0, tiled=True),
        lax.all_to_all(grad_v_col, "wide", split_axis=0, concat_axis=0, tiled=True),
    )
    q_parts, k_parts, v_parts = ([], [], [])
    for head_index in range(heads_here):
        feat_cols = slice(head_index * HEAD, (head_index + 1) * HEAD)
        weights = jnp.where(
            row_mask, jnp.exp(row_scores[head_index] - lse_rows[:, head_index][:, None]), 0.0
        )
        dscore = (weights * (row_dprob[head_index] - delta_rows[:, head_index][:, None])).astype(
            jnp.bfloat16
        )
        q_parts.append(
            jnp.dot(dscore, k_all[:, feat_cols], preferred_element_type=jnp.float32) * score_scale
        )
        k_parts.append(
            jnp.einsum("tu,td->ud", dscore, q_all[:, feat_cols], preferred_element_type=jnp.float32)
            * score_scale
        )
        v_parts.append(
            jnp.einsum(
                "tu,td->ud",
                weights.astype(jnp.bfloat16),
                g_all[:, feat_cols],
                preferred_element_type=jnp.float32,
            )
        )
    grad_q = (jnp.concatenate(q_parts, axis=1) + q_back).astype(jnp.bfloat16)
    grad_k = (jnp.concatenate(k_parts, axis=1) + k_back).astype(jnp.bfloat16)
    grad_v = (jnp.concatenate(v_parts, axis=1) + v_back).astype(jnp.bfloat16)
    return (
        lax.all_to_all(grad_q, "narrow", split_axis=0, concat_axis=1, tiled=True),
        lax.all_to_all(grad_k, "narrow", split_axis=0, concat_axis=1, tiled=True),
        lax.all_to_all(grad_v, "narrow", split_axis=0, concat_axis=1, tiled=True),
    )


def solution(mesh):
    placed = (
        P(("wide", "narrow"), None),
        P(("wide", "narrow"), None),
        P(("wide", "narrow"), None),
        P(("wide", "narrow"), None),
        P(),
        P(),
    )
    return jax.shard_map(
        body,
        mesh=mesh,
        in_specs=placed,
        out_specs=(
            P(("wide", "narrow"), None),
            P(("wide", "narrow"), None),
            P(("wide", "narrow"), None),
        ),
        check_vma=False,
    )
```

profile of v0, /device:TPU:1, one launch (start us, length us, event | category | flops | bytes accessed | tf_op | source)
XLA Modules:
  0.0 642.6 jit_solution(4040949927191045162)
XLA Ops:
  2.6 19.2 %all-to-all-start = ((bf16[64,16,256]{2,0,1:T(8,128)(2,1)}), bf16[64,16,256]{2,0,1:T(8,128)(2,1)S(1)}, u32[]{:S(2)}, u32[]{:S(2)}) async-start(bf16[64,16,256]{2,0,1:T(8,128)(2,1)} %bitcast.89), calls=%async_computation | async-start | bytes 1048576 | tf_op jit(solution)/shard_map/all_to_all | solution.py:26
  23.7 17.4 %all-to-all-done = bf16[64,16,256]{2,0,1:T(8,128)(2,1)S(1)} async-done(((bf16[64,16,256]{2,0,1:T(8,128)(2,1)}), bf16[64,16,256]{2,0,1:T(8,128)(2,1)S(1)}, u32[]{:S(2)}, u32[]{:S(2)}) %all-to-all-start) | async-done | bytes 524320 | tf_op jit(solution)/shard_map/all_to_all | solution.py:26
  46.4 17.7 %all-to-all-done.1 = bf16[64,16,256]{2,0,1:T(8,128)(2,1)S(1)} async-done(((bf16[64,16,256]{2,0,1:T(8,128)(2,1)}), bf16[64,16,256]{2,0,1:T(8,128)(2,1)S(1)}, u32[]{:S(2)}, u32[]{:S(2)}) %all-to-all-start.1) | async-done | bytes 524320 | tf_op jit(solution)/shard_map/all_to_all | solution.py:27
  64.1 8.5 %all-to-all-start.6 = ((bf16[64,16,256]{2,0,1:T(8,128)(2,1)}), bf16[64,16,256]{2,0,1:T(8,128)(2,1)}, u32[]{:S(2)}, u32[]{:S(2)}) async-start(bf16[64,16,256]{2,0,1:T(8,128)(2,1)} %bitcast.87), calls=%async_computation.6 | async-start | bytes 1048576 | tf_op jit(solution)/shard_map/all_to_all | solution.py:29
  72.7 18.6 %all-to-all-done.6 = bf16[64,16,256]{2,0,1:T(8,128)(2,1)} async-done(((bf16[64,16,256]{2,0,1:T(8,128)(2,1)}), bf16[64,16,256]{2,0,1:T(8,128)(2,1)}, u32[]{:S(2)}, u32[]{:S(2)}) %all-to-all-start.6) | async-done | bytes 524320 | tf_op jit(solution)/shard_map/all_to_all | solution.py:29
  91.3 29.9 %all_to_all.235 = bf16[64,16,256]{2,0,1:T(8,128)(2,1)} all-to-all(bf16[64,16,256]{2,0,1:T(8,128)(2,1)S(1)} %bitcast.108), channel_id=1, replica_groups=mesh['wide'=32,'narrow'=16] {'narrow'}, dimensions={1} | all-to-all | bytes 1048576 | tf_op jit(solution)/shard_map/all_to_all | solution.py:28
  121.1 57.4 %all_to_all.236 = bf16[32,32,256]{2,1,0:T(8,128)(2,1)S(1)} all-to-all(bf16[32,32,256]{2,1,0:T(8,128)(2,1)S(1)} %bitcast.98), channel_id=1, replica_groups=mesh['wide'=32,'narrow'=16] {'wide'}, dimensions={0} | all-to-all | bytes 1048576 | tf_op jit(solution)/shard_map/all_to_all | solution.py:72
  178.5 34.5 %all_to_all.237 = bf16[32,32,256]{2,1,0:T(8,128)(2,1)S(1)} all-to-all(bf16[32,32,256]{2,1,0:T(8,128)(2,1)S(1)} %bitcast.93), channel_id=1, replica_groups=mesh['wide'=32,'narrow'=16] {'wide'}, dimensions={0} | all-to-all | bytes 1048576 | tf_op jit(solution)/shard_map/all_to_all | solution.py:73
  213.1 5.4 all-to-all-start.8
  219.3 28.5 %all-to-all-done.8 = bf16[32,32,256]{2,1,0:T(8,128)(2,1)S(1)} async-done(((bf16[32,32,256]{2,1,0:T(8,128)(2,1)}), bf16[32,32,256]{2,1,0:T(8,128)(2,1)S(1)}, u32[]{:S(2)}, u32[]{:S(2)}) %all-to-all-start.8) | async-done | bytes 524320 | tf_op jit(solution)/shard_map/all_to_all | solution.py:75
  247.8 5.6 all-to-all-start.9
  266.8 15.9 %all-to-all-done.9 = bf16[32,32,256]{2,1,0:T(8,128)(2,1)} async-done(((bf16[32,32,256]{2,1,0:T(8,128)(2,1)}), bf16[32,32,256]{2,1,0:T(8,128)(2,1)}, u32[]{:S(2)}, u32[]{:S(2)}) %all-to-all-start.9) | async-done | bytes 524320 | tf_op jit(solution)/shard_map/all_to_all | solution.py:74
  286.5 5.4 all-to-all-start.10
  291.9 5.3 fusion.3
  298.0 5.3 all-to-all-done.10
  303.4 6.6 %all-to-all-start.5 = ((f32[32,32,2]{1,2,0:T(2,128)}), f32[32,32,2]{1,2,0:T(2,128)S(1)}, u32[]{:S(2)}, u32[]{:S(2)}) async-start(f32[32,32,2]{1,2,0:T(2,128)} %copy.93), calls=%async_computation.5 | async-start | bytes 65536 | tf_op jit(solution)/shard_map/all_to_all | solution.py:115
  310.7 10.6 %all-to-all-done.5 = f32[32,32,2]{1,2,0:T(2,128)S(1)} async-done(((f32[32,32,2]{1,2,0:T(2,128)}), f32[32,32,2]{1,2,0:T(2,128)S(1)}, u32[]{:S(2)}, u32[]{:S(2)}) %all-to-all-start.5) | async-done | bytes 8224 | tf_op jit(solution)/shard_map/all_to_all | solution.py:115
  325.5 11.1 %all-to-all-done.4 = f32[32,32,2]{1,2,0:T(2,128)S(1)} async-done(((f32[32,32,2]{1,2,0:T(2,128)}), f32[32,32,2]{1,2,0:T(2,128)S(1)}, u32[]{:S(2)}, u32[]{:S(2)}) %all-to-all-start.4) | async-done | bytes 8224 | tf_op jit(solution)/shard_map/all_to_all | solution.py:114
  341.9 10.8 %all-to-all-done.11 = f32[32,32,2]{1,2,0:T(2,128)S(1)} async-done(((f32[32,32,2]{1,2,0:T(2,128)}), f32[32,32,2]{1,2,0:T(2,128)S(1)}, u32[]{:S(2)}, u32[]{:S(2)}) %all-to-all-start.11) | async-done | bytes 8224 | tf_op jit(solution)/shard_map/all_to_all | solution.py:122
  359.9 8.1 %all-to-all-done.12 = f32[32,32,2]{1,2,0:T(2,128)S(1)} async-done(((f32[32,32,2]{1,2,0:T(2,128)}), f32[32,32,2]{1,2,0:T(2,128)S(1)}, u32[]{:S(2)}, u32[]{:S(2)}) %all-to-all-start.12) | async-done | bytes 8224 | tf_op jit(solution)/shard_map/all_to_all | solution.py:123
  378.5 43.1 %all-to-all-done.17 = f32[32,32,256]{2,1,0:T(8,128)} async-done(((f32[32,32,256]{2,1,0:T(8,128)}), f32[32,32,256]{2,1,0:T(8,128)}, u32[]{:S(2)}, u32[]{:S(2)}) %all-to-all-start.17) | async-done | bytes 1048608 | tf_op jit(solution)/shard_map/all_to_all | solution.py:142
  421.7 7.1 %all-to-all-start.15 = ((f32[32,32,256]{2,1,0:T(8,128)}), f32[32,32,256]{2,1,0:T(8,128)S(1)}, u32[]{:S(2)}, u32[]{:S(2)}) async-start(f32[32,32,256]{2,1,0:T(8,128)} %all_to_all.204), calls=%async_computation.15 | async-start | bytes 2097152 | tf_op jit(solution)/shard_map/all_to_all | solution.py:141
  431.9 47.2 %all-to-all-done.15 = f32[32,32,256]{2,1,0:T(8,128)S(1)} async-done(((f32[32,32,256]{2,1,0:T(8,128)}), f32[32,32,256]{2,1,0:T(8,128)S(1)}, u32[]{:S(2)}, u32[]{:S(2)}) %all-to-all-start.15) | async-done | bytes 1048608 | tf_op jit(solution)/shard_map/all_to_all | solution.py:141
  480.1 5.8 all-to-all-start.13
  494.3 42.0 %all-to-all-done.13 = f32[32,32,256]{2,1,0:T(8,128)S(1)} async-done(((f32[32,32,256]{2,1,0:T(8,128)}), f32[32,32,256]{2,1,0:T(8,128)S(1)}, u32[]{:S(2)}, u32[]{:S(2)}) %all-to-all-start.13) | async-done | bytes 1048608 | tf_op jit(solution)/shard_map/all_to_all | solution.py:140
  536.3 7.0 %all-to-all-start.18 = ((bf16[16,64,256]{2,1,0:T(8,128)(2,1)}), bf16[16,64,256]{2,1,0:T(8,128)(2,1)}, u32[]{:S(2)}, u32[]{:S(2)}) async-start(bf16[16,64,256]{2,1,0:T(8,128)(2,1)} %fusion.16), calls=%async_computation.18 | async-start | bytes 1048576 | tf_op jit(solution)/shard_map/all_to_all | solution.py:174
  543.3 7.8 %multiply_convert_fusion.1 = (bf16[1024,1024]{0,1:T(8,128)(2,1)S(1)}, bf16[1024,1024]{0,1:T(8,128)(2,1)S(1)}) fusion(f32[1024,1024]{0,1:T(8,128)} %get-tuple-element.25, f32[1024,1024]{0,1:T(8,128)} %copy-done.7, f32[1024]{0:T(1024)S(1)} %bitcast.130, f32[1024]{0:T(1024)S(1)} %bitcast.126, pred[1024]{0:T(1024)(128)(4,1)S(1)} %iota_compare_fusion.5, ...), kind=kLoop, calls=%fused_computation.2 | loop fusion | flops 16777216 | bytes 20988928 | tf_op jit(solution)/shard_map/convert_element_type | solution.py:150
  554.8 14.5 %all-to-all-done.18 = bf16[16,64,256]{2,1,0:T(8,128)(2,1)} async-done(((bf16[16,64,256]{2,1,0:T(8,128)(2,1)}), bf16[16,64,256]{2,1,0:T(8,128)(2,1)}, u32[]{:S(2)}, u32[]{:S(2)}) %all-to-all-start.18) | async-done | bytes 524320 | tf_op jit(solution)/shard_map/all_to_all | solution.py:174
  569.3 4.9 all-to-all-start.16
  578.4 14.9 %all-to-all-done.16 = bf16[16,64,256]{2,1,0:T(8,128)(2,1)} async-done(((bf16[16,64,256]{2,1,0:T(8,128)(2,1)}), bf16[16,64,256]{2,1,0:T(8,128)(2,1)}, u32[]{:S(2)}, u32[]{:S(2)}) %all-to-all-start.16) | async-done | bytes 524320 | tf_op jit(solution)/shard_map/all_to_all | solution.py:173
  593.2 19.0 %all-to-all-start.14 = ((bf16[16,64,256]{2,1,0:T(8,128)(2,1)}), bf16[16,64,256]{2,1,0:T(8,128)(2,1)S(1)}, u32[]{:S(2)}, u32[]{:S(2)}) async-start(bf16[16,64,256]{2,1,0:T(8,128)(2,1)} %fusion.14), calls=%async_computation.14 | async-start | bytes 1048576 | tf_op jit(solution)/shard_map/all_to_all | solution.py:172
  616.0 25.8 %all-to-all-done.14 = bf16[16,64,256]{2,1,0:T(8,128)(2,1)S(1)} async-done(((bf16[16,64,256]{2,1,0:T(8,128)(2,1)}), bf16[16,64,256]{2,1,0:T(8,128)(2,1)S(1)}, u32[]{:S(2)}, u32[]{:S(2)}) %all-to-all-start.14) | async-done | bytes 524320 | tf_op jit(solution)/shard_map/all_to_all | solution.py:172
  (94 shorter events, 80.5 us)
Async XLA Ops:
  0.6 44.9 %copy-start.9 = (bf16[64,4096]{1,0:T(8,128)(2,1)S(1)}, bf16[64,4096]{1,0:T(8,128)(2,1)}, u32[]{:S(2)}) copy-start(bf16[64,4096]{1,0:T(8,128)(2,1)} %param.9) | copy-start | bytes 1572868
  0.6 72.0 %copy-start.10 = (bf16[64,4096]{1,0:T(8,128)(2,1)S(1)}, bf16[64,4096]{1,0:T(8,128)(2,1)}, u32[]{:S(2)}) copy-start(bf16[64,4096]{1,0:T(8,128)(2,1)} %param.8) | copy-start | bytes 1572868
  2.6 38.6 %all-to-all-start = ((bf16[64,16,256]{2,0,1:T(8,128)(2,1)}), bf16[64,16,256]{2,0,1:T(8,128)(2,1)S(1)}, u32[]{:S(2)}, u32[]{:S(2)}) async-start(bf16[64,16,256]{2,0,1:T(8,128)(2,1)} %bitcast.89), calls=%async_computation | async-start | bytes 1048576 | tf_op jit(solution)/shard_map/all_to_all | solution.py:26
  41.2 177.4 %copy-start.11 = (s32[32]{0:T(128)S(1)}, s32[32]{0:T(128)}, u32[]{:S(2)}) copy-start(s32[32]{0:T(128)} %param.10) | copy-start | bytes 388
  41.2 178.0 %copy-start.12 = (s32[8]{0:T(128)S(1)}, s32[8]{0:T(128)}, u32[]{:S(2)}) copy-start(s32[8]{0:T(128)} %param.11) | copy-start | bytes 100
  41.2 22.9 %all-to-all-start.1 = ((bf16[64,16,256]{2,0,1:T(8,128)(2,1)}), bf16[64,16,256]{2,0,1:T(8,128)(2,1)S(1)}, u32[]{:S(2)}, u32[]{:S(2)}) async-start(bf16[64,16,256]{2,0,1:T(8,128)(2,1)} %bitcast.88), calls=%async_computation.1 | async-start | bytes 1048576 | tf_op jit(solution)/shard_map/all_to_all | solution.py:27
  64.1 27.1 %all-to-all-start.6 = ((bf16[64,16,256]{2,0,1:T(8,128)(2,1)}), bf16[64,16,256]{2,0,1:T(8,128)(2,1)}, u32[]{:S(2)}, u32[]{:S(2)}) async-start(bf16[64,16,256]{2,0,1:T(8,128)(2,1)} %bitcast.87), calls=%async_computation.6 | async-start | bytes 1048576 | tf_op jit(solution)/shard_map/all_to_all | solution.py:29
  213.1 34.8 %all-to-all-start.8 = ((bf16[32,32,256]{2,1,0:T(8,128)(2,1)}), bf16[32,32,256]{2,1,0:T(8,128)(2,1)S(1)}, u32[]{:S(2)}, u32[]{:S(2)}) async-start(bf16[32,32,256]{2,1,0:T(8,128)(2,1)} %bitcast.23), calls=%async_computation.8 | async-start | bytes 1048576 | tf_op jit(solution)/shard_map/all_to_all | solution.py:75
  247.8 34.9 %all-to-all-start.9 = ((bf16[32,32,256]{2,1,0:T(8,128)(2,1)}), bf16[32,32,256]{2,1,0:T(8,128)(2,1)}, u32[]{:S(2)}, u32[]{:S(2)}) async-start(bf16[32,32,256]{2,1,0:T(8,128)(2,1)} %bitcast.24), calls=%async_computation.9 | async-start | bytes 1048576 | tf_op jit(solution)/shard_map/all_to_all | solution.py:74
  255.0 2.0 copy-start.1
  255.8 2.5 copy-start.7
  286.5 16.9 %all-to-all-start.10 = ((f32[32,32,2]{1,2,0:T(2,128)}), f32[32,32,2]{1,2,0:T(2,128)S(1)}, u32[]{:S(2)}, u32[]{:S(2)}) async-start(f32[32,32,2]{1,2,0:T(2,128)} %copy.99), calls=%async_computation.10 | async-start | bytes 65536 | tf_op jit(solution)/shard_map/all_to_all | solution.py:116
  303.4 18.0 %all-to-all-start.5 = ((f32[32,32,2]{1,2,0:T(2,128)}), f32[32,32,2]{1,2,0:T(2,128)S(1)}, u32[]{:S(2)}, u32[]{:S(2)}) async-start(f32[32,32,2]{1,2,0:T(2,128)} %copy.93), calls=%async_computation.5 | async-start | bytes 65536 | tf_op jit(solution)/shard_map/all_to_all | solution.py:115
  321.4 15.2 %all-to-all-start.4 = ((f32[32,32,2]{1,2,0:T(2,128)}), f32[32,32,2]{1,2,0:T(2,128)S(1)}, u32[]{:S(2)}, u32[]{:S(2)}) async-start(f32[32,32,2]{1,2,0:T(2,128)} %copy.91), calls=%async_computation.4 | async-start | bytes 65536 | tf_op jit(solution)/shard_map/all_to_all | solution.py:114
  337.3 15.4 %all-to-all-start.11 = ((f32[32,32,2]{1,2,0:T(2,128)}), f32[32,32,2]{1,2,0:T(2,128)S(1)}, u32[]{:S(2)}, u32[]{:S(2)}) async-start(f32[32,32,2]{1,2,0:T(2,128)} %copy.104), calls=%async_computation.11 | async-start | bytes 65536 | tf_op jit(solution)/shard_map/all_to_all | solution.py:122
  352.7 15.3 %all-to-all-start.12 = ((f32[32,32,2]{1,2,0:T(2,128)}), f32[32,32,2]{1,2,0:T(2,128)S(1)}, u32[]{:S(2)}, u32[]{:S(2)}) async-start(f32[32,32,2]{1,2,0:T(2,128)} %copy.107), calls=%async_computation.12 | async-start | bytes 65536 | tf_op jit(solution)/shard_map/all_to_all | solution.py:123
  368.0 53.7 %all-to-all-start.17 = ((f32[32,32,256]{2,1,0:T(8,128)}), f32[32,32,256]{2,1,0:T(8,128)}, u32[]{:S(2)}, u32[]{:S(2)}) async-start(f32[32,32,256]{2,1,0:T(8,128)} %all_to_all.210), calls=%async_computation.17 | async-start | bytes 2097152 | tf_op jit(solution)/shard_map/all_to_all | solution.py:142
  374.3 54.5 %copy-start.8 = (bf16[32,32,2,128]{3,2,1,0:T(2,128)(2,1)S(1)}, bf16[32,32,2,128]{3,2,1,0:T(2,128)(2,1)}, u32[]{:S(2)}) copy-start(bf16[32,32,2,128]{3,2,1,0:T(2,128)(2,1)} %reshape.184) | copy-start | bytes 1572868
  421.7 57.5 %all-to-all-start.15 = ((f32[32,32,256]{2,1,0:T(8,128)}), f32[32,32,256]{2,1,0:T(8,128)S(1)}, u32[]{:S(2)}, u32[]{:S(2)}) async-start(f32[32,32,256]{2,1,0:T(8,128)} %all_to_all.204), calls=%async_computation.15 | async-start | bytes 2097152 | tf_op jit(solution)/shard_map/all_to_all | solution.py:141
  479.2 1.0 copy-start.5
  480.1 56.2 %all-to-all-start.13 = ((f32[32,32,256]{2,1,0:T(8,128)}), f32[32,32,256]{2,1,0:T(8,128)S(1)}, u32[]{:S(2)}, u32[]{:S(2)}) async-start(f32[32,32,256]{2,1,0:T(8,128)} %all_to_all.198), calls=%async_computation.13 | async-start | bytes 2097152 | tf_op jit(solution)/shard_map/all_to_all | solution.py:140
  486.3 4.1 copy-start.2
  536.3 7.0 %copy-start.3 = (f32[32,32,256]{2,1,0:T(8,128)}, f32[32,32,256]{2,1,0:T(8,128)S(1)}, u32[]{:S(2)}) copy-start(f32[32,32,256]{2,1,0:T(8,128)S(1)} %all-to-all-done.13) | copy-start | bytes 3145732
  536.3 33.0 %all-to-all-start.18 = ((bf16[16,64,256]{2,1,0:T(8,128)(2,1)}), bf16[16,64,256]{2,1,0:T(8,128)(2,1)}, u32[]{:S(2)}, u32[]{:S(2)}) async-start(bf16[16,64,256]{2,1,0:T(8,128)(2,1)} %fusion.16), calls=%async_computation.18 | async-start | bytes 1048576 | tf_op jit(solution)/shard_map/all_to_all | solution.py:174
  551.2 1.3 copy-start
  551.2 2.8 copy-start.6
  569.3 23.9 %all-to-all-start.16 = ((bf16[16,64,256]{2,1,0:T(8,128)(2,1)}), bf16[16,64,256]{2,1,0:T(8,128)(2,1)}, u32[]{:S(2)}, u32[]{:S(2)}) async-start(bf16[16,64,256]{2,1,0:T(8,128)(2,1)} %fusion.15), calls=%async_computation.16 | async-start | bytes 1048576 | tf_op jit(solution)/shard_map/all_to_all | solution.py:173
  574.2 3.2 copy-start.4
  593.2 48.5 %all-to-all-start.14 = ((bf16[16,64,256]{2,1,0:T(8,128)(2,1)}), bf16[16,64,256]{2,1,0:T(8,128)(2,1)S(1)}, u32[]{:S(2)}, u32[]{:S(2)}) async-start(bf16[16,64,256]{2,1,0:T(8,128)(2,1)} %fusion.14), calls=%async_computation.14 | async-start | bytes 1048576 | tf_op jit(solution)/shard_map/all_to_all | solution.py:172
where the time goes:
time: 645 us; the launch traced here: 643 us
  waiting for transfers between devices  332 us (51%)
  blocking collectives  122 us (19%)
  starting transfers between devices  115 us (18%)
  local copies, waits for them, and re-layouts  29.3 us (5%)
  matrix products  28.4 us (4%)
  other arithmetic  15.2 us (2%)
    all_to_all x1, blocking collectives, body(): lax.all_to_all(q_all, 'wide', split_axis=0, concat_axis=0, tiled=True)  57.4 us
    all_to_all x1, waiting for transfers between devices, body(): lax.all_to_all(grad_k_col, 'wide', split_axis=0, concat_axis=0, tiled=True)  47.2 us
    all_to_all x1, waiting for transfers between devices, body(): lax.all_to_all(grad_v_col, 'wide', split_axis=0, concat_axis=0, tiled=True)  43.1 us
    all_to_all x1, waiting for transfers between devices, body(): lax.all_to_all(grad_q_col, 'wide', split_axis=0, concat_axis=0, tiled=True)  42 us
    all_to_all x1, blocking collectives, body(): lax.all_to_all(k_all, 'wide', split_axis=0, concat_axis=0, tiled=True)  34.5 us
    all_to_all x1, blocking collectives, body(): lax.all_to_all(value_in, 'narrow', split_axis=1, concat_axis=0, tiled=True)  29.9 us
    all_to_all x1, waiting for transfers between devices, body(): lax.all_to_all(g_all, 'wide', split_axis=0, concat_axis=0, tiled=True)  28.5 us
    all_to_all x1, waiting for transfers between devices, body(): lax.all_to_all(grad_q, 'narrow', split_axis=0, concat_axis=1, tiled=True)  25.8 us
  transfers between devices with their start and end apart: 16, of which 16 were waited for; matrix products, arithmetic and copies ran while one was open for 9% of the time, Pallas kernels for 0%

commit v1 on v0

v1 whole, which is shorter than its diff:
```python
import math

import jax
import jax.numpy as jnp
from jax import lax
from jax.experimental import pallas as pl
from jax.experimental.pallas import tpu as pltpu
from jax.sharding import PartitionSpec as P

HEAD = 128
CB = 128
HALVES = 2

masked_low = -1e30
f32 = jnp.float32
bf16 = jnp.bfloat16
QI, GI, KI, VI = 2, 3, 0, 1


def dot_nt(a, b):
    return lax.dot_general(a, b, (((1,), (1,)), ((), ())), preferred_element_type=f32)


def dot_nn(a, b):
    return lax.dot_general(a, b, (((1,), (0,)), ((), ())), preferred_element_type=f32)


def dot_tn(a, b):
    return lax.dot_general(a, b, (((0,), (0,)), ((), ())), preferred_element_type=f32)


def params(n_axes=1):
    return pltpu.CompilerParams(
        dimension_semantics=("arbitrary",) * n_axes, vmem_limit_bytes=48 * 1024 * 1024
    )


def cost(units):
    return pl.CostEstimate(
        flops=units * 10 * 512 * 512 * 128, bytes_accessed=4 << 20, transcendentals=units * 512 * 512
    )


def pack_body(k_ref, v_ref, q_ref, g_ref, out_ref):
    _, subs, _, cols, _ = out_ref.shape
    for a, ref in enumerate((k_ref, v_ref, q_ref, g_ref)):
        for s in range(subs):
            out_ref[0, s, a] = ref[s * cols : (s + 1) * cols, :]


def pack(k, v, q, g, groups, subs, cols):
    tokens, feats = k.shape
    wide_feats = feats // groups
    return pl.pallas_call(
        pack_body,
        grid=(groups,),
        in_specs=[pl.BlockSpec((tokens, wide_feats), lambda j: (0, j))] * 4,
        out_specs=pl.BlockSpec((1, subs, 4, cols, wide_feats), lambda j: (j, 0, 0, 0, 0)),
        out_shape=jax.ShapeDtypeStruct((groups, subs, 4, cols, wide_feats), bf16),
        compiler_params=params(),
        name="pack",
    )(k, v, q, g)


def unpack_body(in_ref, q_ref, k_ref, v_ref):
    _, subs, _, cols, _ = in_ref.shape
    for a, ref in enumerate((q_ref, k_ref, v_ref)):
        for s in range(subs):
            ref[s * cols : (s + 1) * cols, :] = in_ref[0, s, a]


def unpack(arr, tokens, feats):
    groups, subs, _, cols, wide_feats = arr.shape
    out = jax.ShapeDtypeStruct((tokens, feats), bf16)
    return pl.pallas_call(
        unpack_body,
        grid=(groups,),
        in_specs=[pl.BlockSpec((1, subs, 3, cols, wide_feats), lambda j: (j, 0, 0, 0, 0))],
        out_specs=[pl.BlockSpec((tokens, wide_feats), lambda j: (0, j))] * 3,
        out_shape=[out] * 3,
        compiler_params=params(),
        name="unpack",
    )(arr)


def flat(ref, index):
    block = ref[:, index]
    return block.reshape(block.shape[0] * block.shape[1], block.shape[2])


def row_masks(scal_ref, n):
    first = scal_ref[1] - scal_ref[0] * n
    u = lax.broadcasted_iota(jnp.int32, (n, n), 0)
    t = lax.broadcasted_iota(jnp.int32, (n, n), 1)
    return (u == t) | ((u < t) & (u >= first))


def off_mask(scal_ref, n):
    u = lax.broadcasted_iota(jnp.int32, (n, n), 0)
    return u >= scal_ref[1]


def col_mask(scal_ref, n, cols):
    u = lax.broadcasted_iota(jnp.int32, (n, n), 0)
    t = lax.broadcasted_iota(jnp.int32, (n, n), 1)
    same = (u & (cols - 1)) == (t & (cols - 1))
    return same & (u < t) & (u >= scal_ref[2] * cols)


def partial_stats(k, v, q, g, mask, scale):
    s = jnp.where(mask, dot_nt(k, q) * scale, masked_low)
    m = jnp.max(s, axis=0, keepdims=True)
    e = jnp.where(mask, jnp.exp(s - m), 0.0)
    total = jnp.sum(e, axis=0, keepdims=True)
    weighted = jnp.sum(e * dot_nt(v, g), axis=0, keepdims=True)
    some = total > 0.0
    total = jnp.where(some, total, 1.0)
    return jnp.where(some, m + jnp.log(total), masked_low), weighted / total


def merge(lse_a, delta_a, lse_b, delta_b):
    top = jnp.maximum(lse_a, lse_b)
    a = jnp.exp(lse_a - top)
    b = jnp.exp(lse_b - top)
    total = a + b
    return top + jnp.log(total), (a * delta_a + b * delta_b) / total


def row_stats_body(scale, scal_ref, t_ref, far_ref, out_ref):
    k, v, q, g = (flat(t_ref, i) for i in range(4))
    n = k.shape[0]
    lse, delta = partial_stats(k, v, q, g, row_masks(scal_ref, n), scale)
    out_ref[0, 0:1] = lse
    out_ref[0, 1:2] = delta

    @pl.when(scal_ref[0] == 1)
    def _():
        lse_f, delta_f = partial_stats(
            flat(far_ref, 0), flat(far_ref, 1), q, g, off_mask(scal_ref, n), scale
        )
        lse_m, delta_m = merge(lse, delta, lse_f, delta_f)
        out_ref[0, 0:1] = lse_m
        out_ref[0, 1:2] = delta_m


def col_stats_body(scale, scal_ref, t_ref, out_ref):
    k, v, q, g = (flat(t_ref, i) for i in range(4))
    n = k.shape[0]
    lse, delta = partial_stats(k, v, q, g, col_mask(scal_ref, n, t_ref.shape[2]), scale)
    out_ref[0, 0:1] = lse
    out_ref[0, 1:2] = delta


def smem():
    return pl.BlockSpec(memory_space=pltpu.SMEM)


def head_block(arr):
    a, b, c, _ = arr.shape
    return pl.BlockSpec((a, b, c, HEAD), lambda h: (0, 0, 0, h))


def stats_call(body, scale, scal, arrays, name, units):
    heads = arrays[0].shape[3] // HEAD
    n = arrays[0].shape[0] * arrays[0].shape[2]
    return pl.pallas_call(
        lambda *refs: body(scale, *refs),
        grid=(heads,),
        in_specs=[smem()] + [head_block(a) for a in arrays],
        out_specs=pl.BlockSpec((1, 2, n), lambda h: (h, 0, 0)),
        out_shape=jax.ShapeDtypeStruct((heads, 2, n), f32),
        compiler_params=params(),
        cost_estimate=cost(units),
        name=name,
    )(scal, *arrays)


def block_grads(k, v, q, g, mask, lse, delta, scale):
    p = jnp.where(mask, jnp.exp(dot_nt(k, q) * scale - lse), 0.0)
    ds = (p * (dot_nt(v, g) - delta)).astype(bf16)
    dv = dot_nn(p.astype(bf16), g)
    dk = dot_nn(ds, q) * scale
    dq = dot_tn(ds, k) * scale
    return dq, dk, dv


def row_grads_body(scale, scal_ref, t_ref, far_ref, stat_ref, out_ref, back_ref):
    k, v, q, g = (flat(t_ref, i) for i in range(4))
    n = k.shape[0]
    lse, delta = stat_ref[0, 0:1], stat_ref[0, 1:2]
    dq, dk, dv = block_grads(k, v, q, g, row_masks(scal_ref, n), lse, delta, scale)
    out_ref[0] = dq
    out_ref[1] = dk
    out_ref[2] = dv

    @pl.when(scal_ref[0] == 1)
    def _():
        dq_f, dk_f, dv_f = block_grads(
            flat(far_ref, 0), flat(far_ref, 1), q, g, off_mask(scal_ref, n), lse, delta, scale
        )
        out_ref[0] += dq_f
        back_ref[0] = dk_f.astype(bf16)
        back_ref[1] = dv_f.astype(bf16)


def col_grads_body(scale, scal_ref, t_ref, stat_ref, out_ref):
    k, v, q, g = (flat(t_ref, i) for i in range(4))
    n = k.shape[0]
    lse, delta = stat_ref[0, 0:1], stat_ref[0, 1:2]
    grads = block_grads(k, v, q, g, col_mask(scal_ref, n, t_ref.shape[2]), lse, delta, scale)
    for a, d in enumerate(grads):
        out_ref[:, a] = d.astype(bf16).reshape(out_ref.shape[0], out_ref.shape[2], HEAD)


def row_grads(scale, scal, t, far, stats):
    rows, _, cols, feats = t.shape
    n = rows * cols
    return pl.pallas_call(
        lambda *refs: row_grads_body(scale, *refs),
        grid=(feats // HEAD,),
        in_specs=[smem(), head_block(t), head_block(far), pl.BlockSpec((1, 2, n), lambda h: (h, 0, 0))],
        out_specs=[
            pl.BlockSpec((3, n, HEAD), lambda h: (0, 0, h)),
            pl.BlockSpec((2, n, HEAD), lambda h: (0, 0, h)),
        ],
        out_shape=[
            jax.ShapeDtypeStruct((3, n, feats), f32),
            jax.ShapeDtypeStruct((2, n, feats), bf16),
        ],
        compiler_params=params(),
        cost_estimate=cost(16),
        name="row_grads",
    )(scal, t, far, stats)


def col_grads(scale, scal, t, stats):
    rows, _, cols, feats = t.shape
    n = rows * cols
    return pl.pallas_call(
        lambda *refs: col_grads_body(scale, *refs),
        grid=(feats // HEAD,),
        in_specs=[smem(), head_block(t), pl.BlockSpec((1, 2, n), lambda h: (h, 0, 0))],
        out_specs=pl.BlockSpec((rows, 3, cols, HEAD), lambda h: (0, 0, 0, h)),
        out_shape=jax.ShapeDtypeStruct((rows, 3, cols, feats), bf16),
        compiler_params=params(),
        cost_estimate=cost(8),
        name="col_grads",
    )(scal, t, stats)


def join_body(row_ref, col_ref, far_ref, out_ref):
    for a in range(3):
        total = row_ref[a] + col_ref[:, a].astype(f32).reshape(row_ref.shape[1:])
        if a > 0:
            total = total + far_ref[a - 1].astype(f32)
        out_ref[:, a] = total.astype(bf16).reshape(out_ref.shape[0], *out_ref.shape[2:])


def join(row, col, far):
    rows, _, cols, feats = col.shape
    steps = 4
    part = rows // steps
    n = part * cols
    return pl.pallas_call(
        join_body,
        grid=(steps,),
        in_specs=[
            pl.BlockSpec((3, n, feats), lambda i: (0, i, 0)),
            pl.BlockSpec((part, 3, cols, feats), lambda i: (i, 0, 0, 0)),
            pl.BlockSpec((2, n, feats), lambda i: (0, i, 0)),
        ],
        out_specs=pl.BlockSpec((part, 3, cols, feats), lambda i: (i, 0, 0, 0)),
        out_shape=jax.ShapeDtypeStruct(col.shape, bf16),
        compiler_params=params(),
        name="join",
    )(row, col, far)


def body(query_in, key_in, value_in, grad_out, row_start, col_start):
    scale = 1.0 / math.sqrt(HEAD)
    tokens, feats = query_in.shape
    lanes = lax.axis_size("wide")
    narrow = lax.axis_size("narrow")
    groups = narrow // HALVES
    half_cols = tokens * groups
    cols = half_cols // lanes
    subs = tokens // cols
    near = [[half * groups + j for j in range(groups)] for half in range(HALVES)]

    def exchange_near(arr):
        return lax.all_to_all(
            arr, "narrow", split_axis=0, concat_axis=0, axis_index_groups=near, tiled=True
        )

    def exchange_wide(arr):
        return lax.all_to_all(arr, "wide", split_axis=0, concat_axis=0, tiled=True)

    wide_index = lax.axis_index("wide")
    half = lax.axis_index("narrow") // groups
    first_col = lax.dynamic_index_in_dim(row_start, wide_index, keepdims=False)
    block_id = (half * half_cols + wide_index * cols) // CB
    first_row = lax.dynamic_index_in_dim(col_start, block_id, keepdims=False)
    scal = jnp.stack([half, first_col, first_row]).astype(jnp.int32)

    packed = pack(key_in, value_in, query_in, grad_out, groups, subs, cols)
    near_feats = feats // groups
    t = exchange_near(packed).reshape(lanes, 4, cols, near_feats)
    far = lax.ppermute(t[:, :2], "narrow", [(j, j + groups) for j in range(groups)])
    by_col = exchange_wide(t)
    heads = near_feats // HEAD
    row_part = stats_call(row_stats_body, scale, scal, (t, far), "row_stats", 6)
    col_part = stats_call(col_stats_body, scale, scal, (by_col,), "col_stats", 4)

    both = jnp.stack([row_part, col_part]).reshape(4 * heads, lanes, cols)
    sent = both.transpose(1, 0, 2).reshape(lanes, (4 * heads * cols) // HEAD, HEAD)
    got = exchange_wide(sent).reshape(lanes, 4 * heads, cols).transpose(1, 0, 2)
    got = got.reshape(2, heads, 2, lanes * cols)
    row_lse, row_delta = merge(row_part[:, 0], row_part[:, 1], got[1, :, 0], got[1, :, 1])
    col_lse, col_delta = merge(col_part[:, 0], col_part[:, 1], got[0, :, 0], got[0, :, 1])
    row_full = jnp.stack([row_lse, row_delta], axis=1)
    col_full = jnp.stack([col_lse, col_delta], axis=1)

    from_col = exchange_wide(col_grads(scale, scal, by_col, col_full))
    row_terms, far_terms = row_grads(scale, scal, t, far, row_full)
    far_back = lax.ppermute(far_terms, "narrow", [(j + groups, j) for j in range(groups)])
    joined = join(row_terms, from_col, far_back)
    out = exchange_near(joined.reshape(groups, subs, 3, cols, near_feats))
    return unpack(out, tokens, feats)


def solution(mesh):
    placed = P(("wide", "narrow"), None)
    return jax.shard_map(
        body,
        mesh=mesh,
        in_specs=(placed,) * 4 + (P(), P()),
        out_specs=(placed,) * 3,
        check_vma=False,
    )
```

time: 645 us -> 420 us (0.65)
  the two profiles are of different devices: /device:TPU:1 before, /device:TPU:100 now
where the time goes in v1:
time: 420 us; the launch traced here: 419 us
  waiting for transfers between devices  274 us (65%)
  blocking collectives  73.3 us (17%)
  starting transfers between devices  32.5 us (8%)
  Pallas kernels  24.3 us (6%)
  local copies, waits for them, and re-layouts  12.7 us (3%)
    ppermute x1, waiting for transfers between devices, body(): lax.ppermute(t[:, :2], 'narrow', [(j, j + groups) for j in range(groups)])  138 us
    ppermute x1, waiting for transfers between devices, body(): lax.ppermute(far_terms, 'narrow', [(j + groups, j) for j in range(groups)])  136 us
    all_to_all x2, blocking collectives, exchange_near(): lax.all_to_all(arr, 'narrow', split_axis=0, concat_axis=0, axis_index_gro...  56.1 us
    all_to_all x2, starting transfers between devices, exchange_wide(): return lax.all_to_all(arr, 'wide', split_axis=0, concat_axis=0, tiled=True)  23 us
    all_to_all x1, blocking collectives, exchange_wide(): return lax.all_to_all(arr, 'wide', split_axis=0, concat_axis=0, tiled=True)  17.2 us
  transfers between devices with their start and end apart: 4, of which 2 were waited for; matrix products, arithmetic and copies ran while one was open for 1% of the time, Pallas kernels for 2%

profile of v1, /device:TPU:100, one launch (start us, length us, event | category | flops | bytes accessed | tf_op | source)
XLA Modules:
  0.0 419.2 jit_solution(16382030252308919105)
XLA Ops:
  0.6 1.0 copy-done.1
  1.7 1.0 copy-done.2
  2.7 1.0 copy-done.3
  3.8 1.0 copy-done.4
  4.8 0.5 pack.1
  5.3 31.9 %all_to_all.25 = bf16[8,4,4,16,512]{4,3,2,1,0:T(8,128)(2,1)} all-to-all(bf16[8,4,4,16,512]{4,3,2,1,0:T(8,128)(2,1)S(1)} %pack.1), channel_id=1, replica_groups={{0,1,2,3,4,5,6,7},{8,9,10,11,12,13,14,15},{16,17,18,19,20,21,22,23},{24..., dimensions={0} | all-to-all | bytes 4194304 | tf_op jit(solution)/shard_map/all_to_all | solution.py:291
  37.2 14.3 %all-to-all-start.1 = ((bf16[32,4,16,512]{3,2,1,0:T(8,128)(2,1)}), bf16[32,4,16,512]{3,2,1,0:T(8,128)(2,1)S(1)}, u32[]{:S(2)}, u32[]{:S(2)}) async-start(bf16[32,4,16,512]{3,2,1,0:T(8,128)(2,1)} %bitcast.1.refs_1_), calls=%async_computation.1 | async-start | bytes 4194304 | tf_op jit(solution)/shard_map/all_to_all | solution.py:296
  51.5 2.4 slice.36
  53.9 8.3 %collective-permute-start = (bf16[32,2,16,512]{3,2,1,0:T(8,128)(2,1)}, bf16[32,2,16,512]{3,2,1,0:T(8,128)(2,1)S(1)}, u32[]{:S(2)}, u32[]{:S(2)}) collective-permute-start(bf16[32,2,16,512]{3,2,1,0:T(8,128)(2,1)} %slice.36), channel_id=1, source_target_pairs={{0,8},{1,9},{2,10},{3,11},{4,12},{5,13},{6,14},{7,15},{16,24},{17,... | collective-permute-start | bytes 3145736 | tf_op jit(solution)/shard_map/ppermute | solution.py:308
  62.2 0.6 dynamic_slice.9
  62.8 0.6 dynamic_slice.8
  63.4 1.4 pad_add_fusion.refs_0_
  64.7 138.2 %collective-permute-done.refs_2_ = bf16[32,2,16,512]{3,2,1,0:T(8,128)(2,1)S(1)} collective-permute-done((bf16[32,2,16,512]{3,2,1,0:T(8,128)(2,1)}, bf16[32,2,16,512]{3,2,1,0:T(8,128)(2,1)S(1)}, u32[]{:S(2)}, u32[]{:S(2)}) %collective-permute-start) | collective-permute-done | bytes 1048608 | tf_op jit(solution)/shard_map/ppermute | solution.py:308
  203.0 4.0 row_stats.1
  207.0 3.3 col_stats.1
  210.3 0.1 reshape.31
  210.4 0.8 copy.15
  211.2 1.0 copy.16
  212.2 17.2 %all_to_all.26 = f32[32,2,128]{2,1,0:T(2,128)S(1)} all-to-all(f32[32,2,128]{2,1,0:T(2,128)S(1)} %copy.16), channel_id=1, replica_groups=mesh['wide'=32,'narrow'=16] {'wide'}, dimensions={0} | all-to-all | bytes 65536 | tf_op jit(solution)/shard_map/all_to_all | solution.py:296
  229.4 0.8 copy.17
  230.1 1.0 copy.18
  231.2 0.2 reshape.34
  231.3 0.1 log_add_fusion
  231.5 4.7 %col_grads.1 = bf16[32,3,16,512]{3,2,1,0:T(8,128)(2,1)S(1)} custom-call(s32[3]{0:T(128)S(1)} %pad_add_fusion.refs_0_, bf16[32,4,16,512]{3,2,1,0:T(8,128)(2,1)S(1)} %all-to-all-done.1.refs_1_, f32[4,2,512]{2,1,0:T(2,128)S(1)} %pad_maximum_fusion.2.refs_2_), custom_call_target="tpu_custom_call" | custom-call | flops 2684354560 | bytes 4194304 | tf_op jit(solution)/shard_map/col_grads/pallas_call | solution.py:239
  236.2 1.2 copy-done
  237.4 8.7 %all-to-all-start.3 = ((bf16[32,3,16,512]{3,2,1,0:T(8,128)(2,1)}), bf16[32,3,16,512]{3,2,1,0:T(8,128)(2,1)S(1)}, u32[]{:S(2)}, u32[]{:S(2)}) async-start(bf16[32,3,16,512]{3,2,1,0:T(8,128)(2,1)} %copy-done), calls=%async_computation.3 | async-start | bytes 3145728 | tf_op jit(solution)/shard_map/all_to_all | solution.py:296
  246.1 6.2 %row_grads.1 = (f32[3,512,512]{2,1,0:T(8,128)}, bf16[2,512,512]{2,1,0:T(8,128)(2,1)S(1)}) custom-call(s32[3]{0:T(128)S(1)} %pad_add_fusion.refs_0_, bf16[32,4,16,512]{3,2,1,0:T(8,128)(2,1)} %bitcast.1.refs_1_, bf16[32,2,16,512]{3,2,1,0:T(8,128)(2,1)S(1)} %collective-permute-done.refs_2_, f32[4,2,512]{2,1,0:T(2,128)S(1)} %pad_maximum_fusion.1.refs_3_), custom_call_target="tpu_custom_call" | custom-call | flops 5368709120 | bytes 4194304 | tf_op jit(solution)/shard_map/row_grads/pallas_call | solution.py:218
  252.3 1.3 collective-permute-start.1
  253.6 135.7 %collective-permute-done.1.far_ref = bf16[2,512,512]{2,1,0:T(8,128)(2,1)S(1)} collective-permute-done((bf16[2,512,512]{2,1,0:T(8,128)(2,1)S(1)}, bf16[2,512,512]{2,1,0:T(8,128)(2,1)S(1)}, u32[]{:S(2)}, u32[]{:S(2)}) %collective-permute-start.1) | collective-permute-done | bytes 1048608 | tf_op jit(solution)/shard_map/ppermute | solution.py:325
  389.3 2.8 join.1
  392.1 24.2 %all_to_all.27.in_ref = bf16[8,4,3,16,512]{4,3,2,1,0:T(8,128)(2,1)S(1)} all-to-all(bf16[8,4,3,16,512]{4,3,2,1,0:T(8,128)(2,1)S(1)} %bitcast.54), channel_id=1, replica_groups={{0,1,2,3,4,5,6,7},{8,9,10,11,12,13,14,15},{16,17,18,19,20,21,22,23},{24..., dimensions={0} | all-to-all | bytes 3145728 | tf_op jit(solution)/shard_map/all_to_all | solution.py:291
  416.4 2.8 unpack.1
  (14 shorter events, 0.1 us)
Async XLA Ops:
  0.6 1.0 copy-start.1
  1.7 1.0 copy-start.2
  2.7 1.0 copy-start.3
  3.8 1.0 copy-start.4
  37.2 169.8 %all-to-all-start.1 = ((bf16[32,4,16,512]{3,2,1,0:T(8,128)(2,1)}), bf16[32,4,16,512]{3,2,1,0:T(8,128)(2,1)S(1)}, u32[]{:S(2)}, u32[]{:S(2)}) async-start(bf16[32,4,16,512]{3,2,1,0:T(8,128)(2,1)} %bitcast.1.refs_1_), calls=%async_computation.1 | async-start | bytes 4194304 | tf_op jit(solution)/shard_map/all_to_all | solution.py:296
  51.5 10.7 %copy-start.5 = (s32[8]{0:T(128)S(1)}, s32[8]{0:T(128)}, u32[]{:S(2)}) copy-start(s32[8]{0:T(128)} %param.11) | copy-start | bytes 100
  51.5 11.3 %copy-start.6 = (s32[32]{0:T(128)S(1)}, s32[32]{0:T(128)}, u32[]{:S(2)}) copy-start(s32[32]{0:T(128)} %param.10) | copy-start | bytes 388
  53.9 149.1 %collective-permute-start = (bf16[32,2,16,512]{3,2,1,0:T(8,128)(2,1)}, bf16[32,2,16,512]{3,2,1,0:T(8,128)(2,1)S(1)}, u32[]{:S(2)}, u32[]{:S(2)}) collective-permute-start(bf16[32,2,16,512]{3,2,1,0:T(8,128)(2,1)} %slice.36), channel_id=1, source_target_pairs={{0,8},{1,9},{2,10},{3,11},{4,12},{5,13},{6,14},{7,15},{16,24},{17,... | collective-permute-start | bytes 3145736 | tf_op jit(solution)/shard_map/ppermute | solution.py:308
  236.2 1.2 copy-start
  237.4 151.9 %all-to-all-start.3 = ((bf16[32,3,16,512]{3,2,1,0:T(8,128)(2,1)}), bf16[32,3,16,512]{3,2,1,0:T(8,128)(2,1)S(1)}, u32[]{:S(2)}, u32[]{:S(2)}) async-start(bf16[32,3,16,512]{3,2,1,0:T(8,128)(2,1)} %copy-done), calls=%async_computation.3 | async-start | bytes 3145728 | tf_op jit(solution)/shard_map/all_to_all | solution.py:296
  252.3 137.0 %collective-permute-start.1 = (bf16[2,512,512]{2,1,0:T(8,128)(2,1)S(1)}, bf16[2,512,512]{2,1,0:T(8,128)(2,1)S(1)}, u32[]{:S(2)}, u32[]{:S(2)}) collective-permute-start(bf16[2,512,512]{2,1,0:T(8,128)(2,1)S(1)} %get-tuple-element.6), channel_id=1, source_target_pairs={{8,0},{9,1},{10,2},{11,3},{12,4},{13,5},{14,6},{15,7},{24,16},{25,... | collective-permute-start | bytes 3145736 | tf_op jit(solution)/shard_map/ppermute | solution.py:325

commit v2 on v1

--- a/solution.py
+++ b/solution.py
@@ -41,11 +41,13 @@
     )
 
 
-def pack_body(k_ref, v_ref, q_ref, g_ref, out_ref):
+def pack_body(k_ref, v_ref, q_ref, g_ref, out_ref, qg_ref):
     _, subs, _, cols, _ = out_ref.shape
     for a, ref in enumerate((k_ref, v_ref, q_ref, g_ref)):
         for s in range(subs):
             out_ref[0, s, a] = ref[s * cols : (s + 1) * cols, :]
+            if a >= QI:
+                qg_ref[0, s, a - QI] = ref[s * cols : (s + 1) * cols, :]
 
 
 def pack(k, v, q, g, groups, subs, cols):
@@ -55,8 +57,12 @@
         pack_body,
         grid=(groups,),
         in_specs=[pl.BlockSpec((tokens, wide_feats), lambda j: (0, j))] * 4,
-        out_specs=pl.BlockSpec((1, subs, 4, cols, wide_feats), lambda j: (j, 0, 0, 0, 0)),
-        out_shape=jax.ShapeDtypeStruct((groups, subs, 4, cols, wide_feats), bf16),
+        out_specs=[
+            pl.BlockSpec((1, subs, n, cols, wide_feats), lambda j: (j, 0, 0, 0, 0)) for n in (4, 2)
+        ],
+        out_shape=[
+            jax.ShapeDtypeStruct((groups, subs, n, cols, wide_feats), bf16) for n in (4, 2)
+        ],
         compiler_params=params(),
         name="pack",
     )(k, v, q, g)
@@ -126,21 +132,35 @@
     return top + jnp.log(total), (a * delta_a + b * delta_b) / total
 
 
-def row_stats_body(scale, scal_ref, t_ref, far_ref, out_ref):
+def row_stats_body(scale, scal_ref, t_ref, out_ref):
     k, v, q, g = (flat(t_ref, i) for i in range(4))
-    n = k.shape[0]
-    lse, delta = partial_stats(k, v, q, g, row_masks(scal_ref, n), scale)
+    lse, delta = partial_stats(k, v, q, g, row_masks(scal_ref, k.shape[0]), scale)
     out_ref[0, 0:1] = lse
     out_ref[0, 1:2] = delta
 
-    @pl.when(scal_ref[0] == 1)
+
+def gather_far(scal_ref, piece_refs, q_buf, g_buf):
+    for i, ref in enumerate(piece_refs):
+        place = scal_ref[3] ^ i
+        q_buf[place] = flat(ref, 0)
+        g_buf[place] = flat(ref, 1)
+    return (b[...].reshape(b.shape[0] * b.shape[1], HEAD) for b in (q_buf, g_buf))
+
+
+def off_stats_body(scale, scal_ref, t_ref, *refs):
+    *piece_refs, out_ref, q_buf, g_buf = refs
+
+    @pl.when(scal_ref[0] == 0)
     def _():
-        lse_f, delta_f = partial_stats(
-            flat(far_ref, 0), flat(far_ref, 1), q, g, off_mask(scal_ref, n), scale
-        )
-        lse_m, delta_m = merge(lse, delta, lse_f, delta_f)
-        out_ref[0, 0:1] = lse_m
-        out_ref[0, 1:2] = delta_m
+        q, g = gather_far(scal_ref, piece_refs, q_buf, g_buf)
+        k, v = flat(t_ref, KI), flat(t_ref, VI)
+        lse, delta = partial_stats(k, v, q, g, off_mask(scal_ref, k.shape[0]), scale)
+        out_ref[0, 0:1] = lse
+        out_ref[0, 1:2] = delta
+
+    @pl.when(scal_ref[0] != 0)
+    def _():
+        out_ref[...] = jnp.zeros_like(out_ref)
 
 
 def col_stats_body(scale, scal_ref, t_ref, out_ref):
@@ -160,7 +180,13 @@
     return pl.BlockSpec((a, b, c, HEAD), lambda h: (0, 0, 0, h))
 
 
-def stats_call(body, scale, scal, arrays, name, units):
+def far_scratch(pieces):
+    _, _, cols, _ = pieces[0].shape
+    tokens = pieces[0].shape[0] * cols
+    return [pltpu.VMEM((len(pieces), tokens, HEAD), bf16)] * 2
+
+
+def stats_call(body, scale, scal, arrays, name, units, scratch=()):
     heads = arrays[0].shape[3] // HEAD
     n = arrays[0].shape[0] * arrays[0].shape[2]
     return pl.pallas_call(
@@ -169,6 +195,7 @@
         in_specs=[smem()] + [head_block(a) for a in arrays],
         out_specs=pl.BlockSpec((1, 2, n), lambda h: (h, 0, 0)),
         out_shape=jax.ShapeDtypeStruct((heads, 2, n), f32),
+        scratch_shapes=list(scratch),
         compiler_params=params(),
         cost_estimate=cost(units),
         name=name,
@@ -184,23 +211,26 @@
     return dq, dk, dv
 
 
-def row_grads_body(scale, scal_ref, t_ref, far_ref, stat_ref, out_ref, back_ref):
+def row_grads_body(scale, scal_ref, t_ref, stat_ref, far_stat_ref, *refs):
+    *piece_refs, out_ref, back_ref, q_buf, g_buf = refs
     k, v, q, g = (flat(t_ref, i) for i in range(4))
     n = k.shape[0]
-    lse, delta = stat_ref[0, 0:1], stat_ref[0, 1:2]
-    dq, dk, dv = block_grads(k, v, q, g, row_masks(scal_ref, n), lse, delta, scale)
+    dq, dk, dv = block_grads(
+        k, v, q, g, row_masks(scal_ref, n), stat_ref[0, 0:1], stat_ref[0, 1:2], scale
+    )
     out_ref[0] = dq
     out_ref[1] = dk
     out_ref[2] = dv
 
-    @pl.when(scal_ref[0] == 1)
+    @pl.when(scal_ref[0] == 0)
     def _():
+        q_f, g_f = gather_far(scal_ref, piece_refs, q_buf, g_buf)
         dq_f, dk_f, dv_f = block_grads(
-            flat(far_ref, 0), flat(far_ref, 1), q, g, off_mask(scal_ref, n), lse, delta, scale
+            k, v, q_f, g_f, off_mask(scal_ref, n), far_stat_ref[0, 0:1], far_stat_ref[0, 1:2], scale
         )
-        out_ref[0] += dq_f
-        back_ref[0] = dk_f.astype(bf16)
-        back_ref[1] = dv_f.astype(bf16)
+        out_ref[1] += dk_f
+        out_ref[2] += dv_f
+        back_ref[...] = dq_f.astype(bf16)
 
 
 def col_grads_body(scale, scal_ref, t_ref, stat_ref, out_ref):
@@ -212,25 +242,27 @@
         out_ref[:, a] = d.astype(bf16).reshape(out_ref.shape[0], out_ref.shape[2], HEAD)
 
 
-def row_grads(scale, scal, t, far, stats):
+def row_grads(scale, scal, t, stats, far_stats, pieces):
     rows, _, cols, feats = t.shape
     n = rows * cols
+    stat_spec = pl.BlockSpec((1, 2, n), lambda h: (h, 0, 0))
     return pl.pallas_call(
         lambda *refs: row_grads_body(scale, *refs),
         grid=(feats // HEAD,),
-        in_specs=[smem(), head_block(t), head_block(far), pl.BlockSpec((1, 2, n), lambda h: (h, 0, 0))],
+        in_specs=[smem(), head_block(t), stat_spec, stat_spec] + [head_block(p) for p in pieces],
         out_specs=[
             pl.BlockSpec((3, n, HEAD), lambda h: (0, 0, h)),
-            pl.BlockSpec((2, n, HEAD), lambda h: (0, 0, h)),
+            pl.BlockSpec((n, HEAD), lambda h: (0, h)),
         ],
         out_shape=[
             jax.ShapeDtypeStruct((3, n, feats), f32),
-            jax.ShapeDtypeStruct((2, n, feats), bf16),
-        ],
+            jax.ShapeDtypeStruct((n, feats), bf16),
+        ],
+        scratch_shapes=far_scratch(pieces),
         compiler_params=params(),
         cost_estimate=cost(16),
         name="row_grads",
-    )(scal, t, far, stats)
+    )(scal, t, stats, far_stats, *pieces)
 
 
 def col_grads(scale, scal, t, stats):
@@ -251,8 +283,8 @@
 def join_body(row_ref, col_ref, far_ref, out_ref):
     for a in range(3):
         total = row_ref[a] + col_ref[:, a].astype(f32).reshape(row_ref.shape[1:])
-        if a > 0:
-            total = total + far_ref[a - 1].astype(f32)
+        if a == 0:
+            total = total + far_ref[...].astype(f32)
         out_ref[:, a] = total.astype(bf16).reshape(out_ref.shape[0], *out_ref.shape[2:])
 
 
@@ -267,7 +299,7 @@
         in_specs=[
             pl.BlockSpec((3, n, feats), lambda i: (0, i, 0)),
             pl.BlockSpec((part, 3, cols, feats), lambda i: (i, 0, 0, 0)),
-            pl.BlockSpec((2, n, feats), lambda i: (0, i, 0)),
+            pl.BlockSpec((n, feats), lambda i: (i, 0)),
         ],
         out_specs=pl.BlockSpec((part, 3, cols, feats), lambda i: (i, 0, 0, 0)),
         out_shape=jax.ShapeDtypeStruct(col.shape, bf16),
@@ -295,20 +327,40 @@
     def exchange_wide(arr):
         return lax.all_to_all(arr, "wide", split_axis=0, concat_axis=0, tiled=True)
 
+    def shift(arr, source, target):
+        pairs = [(source * groups + j, target * groups + j) for j in range(groups)]
+        return lax.ppermute(arr, "narrow", pairs)
+
+    def swap(arr, step):
+        pairs = [(i, i ^ step) for i in range(narrow)]
+        return lax.ppermute(arr, "narrow", pairs)
+
     wide_index = lax.axis_index("wide")
-    half = lax.axis_index("narrow") // groups
+    narrow_index = lax.axis_index("narrow")
+    half = narrow_index // groups
+    near_index = narrow_index % groups
     first_col = lax.dynamic_index_in_dim(row_start, wide_index, keepdims=False)
     block_id = (half * half_cols + wide_index * cols) // CB
     first_row = lax.dynamic_index_in_dim(col_start, block_id, keepdims=False)
-    scal = jnp.stack([half, first_col, first_row]).astype(jnp.int32)
-
-    packed = pack(key_in, value_in, query_in, grad_out, groups, subs, cols)
+    scal = jnp.stack([half, first_col, first_row, near_index]).astype(jnp.int32)
+
+    packed, packed_qg = pack(key_in, value_in, query_in, grad_out, groups, subs, cols)
     near_feats = feats // groups
+    far = shift(packed_qg, 1, 0)
     t = exchange_near(packed).reshape(lanes, 4, cols, near_feats)
-    far = lax.ppermute(t[:, :2], "narrow", [(j, j + groups) for j in range(groups)])
     by_col = exchange_wide(t)
+    pieces = []
+    for step in range(groups):
+        piece = lax.dynamic_index_in_dim(far, near_index ^ step, keepdims=False)
+        pieces.append(swap(piece, step) if step else piece)
     heads = near_feats // HEAD
-    row_part = stats_call(row_stats_body, scale, scal, (t, far), "row_stats", 6)
+    diag_part = stats_call(row_stats_body, scale, scal, (t,), "row_stats", 4)
+    off_part = stats_call(
+        off_stats_body, scale, scal, (t, *pieces), "off_stats", 4, far_scratch(pieces)
+    )
+    off_part = shift(off_part, 0, 1)
+    lse, delta = merge(diag_part[:, 0], diag_part[:, 1], off_part[:, 0], off_part[:, 1])
+    row_part = jnp.where(half == 1, jnp.stack([lse, delta], axis=1), diag_part)
     col_part = stats_call(col_stats_body, scale, scal, (by_col,), "col_stats", 4)
 
     both = jnp.stack([row_part, col_part]).reshape(4 * heads, lanes, cols)
@@ -321,8 +373,9 @@
     col_full = jnp.stack([col_lse, col_delta], axis=1)
 
     from_col = exchange_wide(col_grads(scale, scal, by_col, col_full))
-    row_terms, far_terms = row_grads(scale, scal, t, far, row_full)
-    far_back = lax.ppermute(far_terms, "narrow", [(j + groups, j) for j in range(groups)])
+    far_full = shift(row_full, 1, 0)
+    row_terms, far_terms = row_grads(scale, scal, t, row_full, far_full, pieces)
+    far_back = shift(far_terms, 0, 1)
     joined = join(row_terms, from_col, far_back)
     out = exchange_near(joined.reshape(groups, subs, 3, cols, near_feats))
     return unpack(out, tokens, feats)

time: 420 us -> 425 us (1.012)
  the two profiles are of different devices: /device:TPU:100 before, /device:TPU:390 now
where the time goes in v2:
time: 425 us; the launch traced here: 424 us
  waiting for transfers between devices  259 us (61%)
  starting transfers between devices  67 us (16%)
  blocking collectives  56.1 us (13%)
  Pallas kernels  26.6 us (6%)
  local copies, waits for them, and re-layouts  13.1 us (3%)
    ppermute x4, waiting for transfers between devices, shift(): return lax.ppermute(arr, 'narrow', pairs)  252 us
    all_to_all x2, blocking collectives, exchange_near(): lax.all_to_all(arr, 'narrow', split_axis=0, concat_axis=0, axis_index_gro...  56.1 us
    all_to_all x3, starting transfers between devices, exchange_wide(): return lax.all_to_all(arr, 'wide', split_axis=0, concat_axis=0, tiled=True)  31.5 us
    ppermute x7, starting transfers between devices, swap(): return lax.ppermute(arr, 'narrow', pairs)  21.4 us
    ppermute x4, starting transfers between devices, shift(): return lax.ppermute(arr, 'narrow', pairs)  14.1 us
    pallas_call x3, Pallas kernels, stats_call(): pl.pallas_call(lambda *refs: body(scale, *refs), grid=(heads,), in_specs=...  9.58 us
  transfers between devices with their start and end apart: 14, of which 6 were waited for; matrix products, arithmetic and copies ran while one was open for 1% of the time, Pallas kernels for 3%

profile of v2, /device:TPU:390, one launch (start us, length us, event | category | flops | bytes accessed | tf_op | source)
XLA Modules:
  0.0 424.1 jit_solution(7595456320331603866)
XLA Ops:
  5.4 31.9 %all_to_all.25 = bf16[8,4,4,16,512]{4,3,2,1,0:T(8,128)(2,1)} all-to-all(bf16[8,4,4,16,512]{4,3,2,1,0:T(8,128)(2,1)S(1)} %get-tuple-element.7), channel_id=1, replica_groups={{0,1,2,3,4,5,6,7},{8,9,10,11,12,13,14,15},{16,17,18,19,20,21,22,23},{24..., dimensions={0} | all-to-all | bytes 4194304 | tf_op jit(solution)/shard_map/all_to_all | solution.py:323
  37.2 11.2 %all-to-all-start.1 = ((bf16[32,4,16,512]{3,2,1,0:T(8,128)(2,1)}), bf16[32,4,16,512]{3,2,1,0:T(8,128)(2,1)S(1)}, u32[]{:S(2)}, u32[]{:S(2)}) async-start(bf16[32,4,16,512]{3,2,1,0:T(8,128)(2,1)} %bitcast.2.refs_1_), calls=%async_computation.1 | async-start | bytes 4194304 | tf_op jit(solution)/shard_map/all_to_all | solution.py:328
  48.5 7.4 %collective-permute-start = (bf16[8,4,2,16,512]{4,3,2,1,0:T(8,128)(2,1)S(1)}, bf16[8,4,2,16,512]{4,3,2,1,0:T(8,128)(2,1)}, u32[]{:S(2)}, u32[]{:S(2)}) collective-permute-start(bf16[8,4,2,16,512]{4,3,2,1,0:T(8,128)(2,1)S(1)} %get-tuple-element.8), channel_id=1, source_target_pairs={{8,0},{9,1},{10,2},{11,3},{12,4},{13,5},{14,6},{15,7},{24,16},{25,... | collective-permute-start | bytes 3145736 | tf_op jit(solution)/shard_map/ppermute | solution.py:332
  55.8 144.1 %collective-permute-done = bf16[8,4,2,16,512]{4,3,2,1,0:T(8,128)(2,1)} collective-permute-done((bf16[8,4,2,16,512]{4,3,2,1,0:T(8,128)(2,1)S(1)}, bf16[8,4,2,16,512]{4,3,2,1,0:T(8,128)(2,1)}, u32[]{:S(2)}, u32[]{:S(2)}) %collective-permute-start) | collective-permute-done | bytes 1048608 | tf_op jit(solution)/shard_map/ppermute | solution.py:332
  199.9 2.1 dynamic-slice_bitcast_fusion
  201.9 2.6 collective-permute-start.7
  204.6 4.0 collective-permute-start.6
  208.6 1.9 collective-permute-start.5
  210.5 5.2 %collective-permute-start.4 = (bf16[4,2,16,512]{3,2,1,0:T(8,128)(2,1)}, bf16[4,2,16,512]{3,2,1,0:T(8,128)(2,1)S(1)}, u32[]{:S(2)}, u32[]{:S(2)}) collective-permute-start(bf16[4,2,16,512]{3,2,1,0:T(8,128)(2,1)} %get-tuple-element.14), channel_id=1, source_target_pairs={{0,4},{1,5},{2,6},{3,7},{4,0},{5,1},{6,2},{7,3},{8,12},{9,13},{10,... | collective-permute-start | bytes 393224 | tf_op jit(solution)/shard_map/ppermute | solution.py:336
  215.8 1.9 collective-permute-start.3
  217.7 3.5 collective-permute-start.2
  221.3 2.1 collective-permute-start.1
  224.7 1.3 pad_add_fusion.refs_0_
  226.5 2.4 off_stats.1
  228.9 1.3 collective-permute-start.8
  230.2 3.9 row_stats.1
  234.1 10.9 %collective-permute-done.8 = f32[4,2,512]{2,1,0:T(2,128)S(1)} collective-permute-done((f32[4,2,512]{2,1,0:T(2,128)S(1)}, f32[4,2,512]{2,1,0:T(2,128)S(1)}, u32[]{:S(2)}, u32[]{:S(2)}) %collective-permute-start.8) | collective-permute-done | bytes 16416 | tf_op jit(solution)/shard_map/ppermute | solution.py:332
  245.1 3.3 col_stats.1
  249.3 1.6 copy.16
  250.9 9.8 %all-to-all-start.2 = ((f32[32,2,128]{2,1,0:T(2,128)}), f32[32,2,128]{2,1,0:T(2,128)S(1)}, u32[]{:S(2)}, u32[]{:S(2)}) async-start(f32[32,2,128]{2,1,0:T(2,128)} %copy.16), calls=%async_computation.2 | async-start | bytes 65536 | tf_op jit(solution)/shard_map/all_to_all | solution.py:328
  260.8 6.0 %all-to-all-done.2 = f32[32,2,128]{2,1,0:T(2,128)S(1)} async-done(((f32[32,2,128]{2,1,0:T(2,128)}), f32[32,2,128]{2,1,0:T(2,128)S(1)}, u32[]{:S(2)}, u32[]{:S(2)}) %all-to-all-start.2) | async-done | bytes 32800 | tf_op jit(solution)/shard_map/all_to_all | solution.py:328
  268.8 4.7 %col_grads.1 = bf16[32,3,16,512]{3,2,1,0:T(8,128)(2,1)S(1)} custom-call(s32[4]{0:T(128)S(1)} %pad_add_fusion.refs_0_, bf16[32,4,16,512]{3,2,1,0:T(8,128)(2,1)S(1)} %all-to-all-done.1.refs_1_, f32[4,2,512]{2,1,0:T(2,128)S(1)} %pad_maximum_fusion.2.refs_2_), custom_call_target="tpu_custom_call" | custom-call | flops 2684354560 | bytes 4194304 | tf_op jit(solution)/shard_map/col_grads/pallas_call | solution.py:271
  273.6 1.2 copy-done
  274.7 10.5 %all-to-all-start.3 = ((bf16[32,3,16,512]{3,2,1,0:T(8,128)(2,1)}), bf16[32,3,16,512]{3,2,1,0:T(8,128)(2,1)S(1)}, u32[]{:S(2)}, u32[]{:S(2)}) async-start(bf16[32,3,16,512]{3,2,1,0:T(8,128)(2,1)} %copy-done), calls=%async_computation.3 | async-start | bytes 3145728 | tf_op jit(solution)/shard_map/all_to_all | solution.py:328
  285.3 4.1 collective-permute-start.9
  289.4 59.3 %collective-permute-done.9.refs_3_ = f32[4,2,512]{2,1,0:T(2,128)S(1)} collective-permute-done((f32[4,2,512]{2,1,0:T(2,128)S(1)}, f32[4,2,512]{2,1,0:T(2,128)S(1)}, u32[]{:S(2)}, u32[]{:S(2)}) %collective-permute-start.9) | collective-permute-done | bytes 16416 | tf_op jit(solution)/shard_map/ppermute | solution.py:332
  348.8 6.2 %row_grads.1 = (f32[3,512,512]{2,1,0:T(8,128)}, bf16[512,512]{1,0:T(8,128)(2,1)S(1)}) custom-call(s32[4]{0:T(128)S(1)} %pad_add_fusion.refs_0_, bf16[32,4,16,512]{3,2,1,0:T(8,128)(2,1)} %bitcast.2.refs_1_, f32[4,2,512]{2,1,0:T(2,128)S(1)} %pad_maximum_fusion.1.refs_2_, f32[4,2,512]{2,1,0:T(2,128)S(1)} %collective-permute-done.9.refs_3_, ...), custom_call_target="tpu_custom_call" | custom-call | flops 5368709120 | bytes 4194304 | tf_op jit(solution)/shard_map/row_grads/pallas_call | solution.py:249
  355.0 1.3 collective-permute-start.10
  356.3 38.0 %collective-permute-done.10.far_ref = bf16[512,512]{1,0:T(8,128)(2,1)S(1)} collective-permute-done((bf16[512,512]{1,0:T(8,128)(2,1)S(1)}, bf16[512,512]{1,0:T(8,128)(2,1)S(1)}, u32[]{:S(2)}, u32[]{:S(2)}) %collective-permute-start.10) | collective-permute-done | bytes 524320 | tf_op jit(solution)/shard_map/ppermute | solution.py:332
  394.3 2.8 join.1
  397.0 24.2 %all_to_all.26.in_ref = bf16[8,4,3,16,512]{4,3,2,1,0:T(8,128)(2,1)S(1)} all-to-all(bf16[8,4,3,16,512]{4,3,2,1,0:T(8,128)(2,1)S(1)} %bitcast.72), channel_id=1, replica_groups={{0,1,2,3,4,5,6,7},{8,9,10,11,12,13,14,15},{16,17,18,19,20,21,22,23},{24..., dimensions={0} | all-to-all | bytes 3145728 | tf_op jit(solution)/shard_map/all_to_all | solution.py:323
  421.3 2.8 unpack.1
  (37 shorter events, 9.6 us)
Async XLA Ops:
  0.6 1.0 copy-start.1
  1.7 1.0 copy-start.2
  2.7 1.0 copy-start.3
  3.8 1.0 copy-start.4
  37.2 207.8 %all-to-all-start.1 = ((bf16[32,4,16,512]{3,2,1,0:T(8,128)(2,1)}), bf16[32,4,16,512]{3,2,1,0:T(8,128)(2,1)S(1)}, u32[]{:S(2)}, u32[]{:S(2)}) async-start(bf16[32,4,16,512]{3,2,1,0:T(8,128)(2,1)} %bitcast.2.refs_1_), calls=%async_computation.1 | async-start | bytes 4194304 | tf_op jit(solution)/shard_map/all_to_all | solution.py:328
  48.4 175.0 %copy-start.5 = (s32[8]{0:T(128)S(1)}, s32[8]{0:T(128)}, u32[]{:S(2)}) copy-start(s32[8]{0:T(128)} %param.11) | copy-start | bytes 100
  48.4 175.6 %copy-start.6 = (s32[32]{0:T(128)S(1)}, s32[32]{0:T(128)}, u32[]{:S(2)}) copy-start(s32[32]{0:T(128)} %param.10) | copy-start | bytes 388
  48.5 151.4 %collective-permute-start = (bf16[8,4,2,16,512]{4,3,2,1,0:T(8,128)(2,1)S(1)}, bf16[8,4,2,16,512]{4,3,2,1,0:T(8,128)(2,1)}, u32[]{:S(2)}, u32[]{:S(2)}) collective-permute-start(bf16[8,4,2,16,512]{4,3,2,1,0:T(8,128)(2,1)S(1)} %get-tuple-element.8), channel_id=1, source_target_pairs={{8,0},{9,1},{10,2},{11,3},{12,4},{13,5},{14,6},{15,7},{24,16},{25,... | collective-permute-start | bytes 3145736 | tf_op jit(solution)/shard_map/ppermute | solution.py:332
  201.9 15.8 %collective-permute-start.7 = (bf16[4,2,16,512]{3,2,1,0:T(8,128)(2,1)S(1)}, bf16[4,2,16,512]{3,2,1,0:T(8,128)(2,1)S(1)}, u32[]{:S(2)}, u32[]{:S(2)}) collective-permute-start(bf16[4,2,16,512]{3,2,1,0:T(8,128)(2,1)S(1)} %get-tuple-element.11), channel_id=1, source_target_pairs={{0,7},{1,6},{2,5},{3,4},{4,3},{5,2},{6,1},{7,0},{8,15},{9,14},{10,... | collective-permute-start | bytes 393224 | tf_op jit(solution)/shard_map/ppermute | solution.py:336
  204.6 16.7 %collective-permute-start.6 = (bf16[4,2,16,512]{3,2,1,0:T(8,128)(2,1)S(1)}, bf16[4,2,16,512]{3,2,1,0:T(8,128)(2,1)S(1)}, u32[]{:S(2)}, u32[]{:S(2)}) collective-permute-start(bf16[4,2,16,512]{3,2,1,0:T(8,128)(2,1)S(1)} %get-tuple-element.12), channel_id=1, source_target_pairs={{0,6},{1,7},{2,4},{3,5},{4,2},{5,3},{6,0},{7,1},{8,14},{9,15},{10,... | collective-permute-start | bytes 393224 | tf_op jit(solution)/shard_map/ppermute | solution.py:336
  208.6 17.4 %collective-permute-start.5 = (bf16[4,2,16,512]{3,2,1,0:T(8,128)(2,1)}, bf16[4,2,16,512]{3,2,1,0:T(8,128)(2,1)S(1)}, u32[]{:S(2)}, u32[]{:S(2)}) collective-permute-start(bf16[4,2,16,512]{3,2,1,0:T(8,128)(2,1)} %get-tuple-element.13), channel_id=1, source_target_pairs={{0,5},{1,4},{2,7},{3,6},{4,1},{5,0},{6,3},{7,2},{8,13},{9,12},{10,... | collective-permute-start | bytes 393224 | tf_op jit(solution)/shard_map/ppermute | solution.py:336
  210.5 15.5 %collective-permute-start.4 = (bf16[4,2,16,512]{3,2,1,0:T(8,128)(2,1)}, bf16[4,2,16,512]{3,2,1,0:T(8,128)(2,1)S(1)}, u32[]{:S(2)}, u32[]{:S(2)}) collective-permute-start(bf16[4,2,16,512]{3,2,1,0:T(8,128)(2,1)} %get-tuple-element.14), channel_id=1, source_target_pairs={{0,4},{1,5},{2,6},{3,7},{4,0},{5,1},{6,2},{7,3},{8,12},{9,13},{10,... | collective-permute-start | bytes 393224 | tf_op jit(solution)/shard_map/ppermute | solution.py:336
  215.8 10.2 %collective-permute-start.3 = (bf16[4,2,16,512]{3,2,1,0:T(8,128)(2,1)}, bf16[4,2,16,512]{3,2,1,0:T(8,128)(2,1)S(1)}, u32[]{:S(2)}, u32[]{:S(2)}) collective-permute-start(bf16[4,2,16,512]{3,2,1,0:T(8,128)(2,1)} %get-tuple-element.15), channel_id=1, source_target_pairs={{0,3},{1,2},{2,1},{3,0},{4,7},{5,6},{6,5},{7,4},{8,11},{9,10},{10,... | collective-permute-start | bytes 393224 | tf_op jit(solution)/shard_map/ppermute | solution.py:336
  217.7 8.8 %collective-permute-start.2 = (bf16[4,2,16,512]{3,2,1,0:T(8,128)(2,1)S(1)}, bf16[4,2,16,512]{3,2,1,0:T(8,128)(2,1)S(1)}, u32[]{:S(2)}, u32[]{:S(2)}) collective-permute-start(bf16[4,2,16,512]{3,2,1,0:T(8,128)(2,1)S(1)} %get-tuple-element.16), channel_id=1, source_target_pairs={{0,2},{1,3},{2,0},{3,1},{4,6},{5,7},{6,4},{7,5},{8,10},{9,11},{10,... | collective-permute-start | bytes 393224 | tf_op jit(solution)/shard_map/ppermute | solution.py:336
  221.3 5.2 %collective-permute-start.1 = (bf16[4,2,16,512]{3,2,1,0:T(8,128)(2,1)S(1)}, bf16[4,2,16,512]{3,2,1,0:T(8,128)(2,1)S(1)}, u32[]{:S(2)}, u32[]{:S(2)}) collective-permute-start(bf16[4,2,16,512]{3,2,1,0:T(8,128)(2,1)S(1)} %get-tuple-element.17), channel_id=1, source_target_pairs={{0,1},{1,0},{2,3},{3,2},{4,5},{5,4},{6,7},{7,6},{8,9},{9,8},{10,11... | collective-permute-start | bytes 393224 | tf_op jit(solution)/shard_map/ppermute | solution.py:336
  228.9 16.1 %collective-permute-start.8 = (f32[4,2,512]{2,1,0:T(2,128)S(1)}, f32[4,2,512]{2,1,0:T(2,128)S(1)}, u32[]{:S(2)}, u32[]{:S(2)}) collective-permute-start(f32[4,2,512]{2,1,0:T(2,128)S(1)} %off_stats.1), channel_id=1, source_target_pairs={{0,8},{1,9},{2,10},{3,11},{4,12},{5,13},{6,14},{7,15},{16,24},{17,... | collective-permute-start | bytes 49160 | tf_op jit(solution)/shard_map/ppermute | solution.py:332
  250.9 15.8 %all-to-all-start.2 = ((f32[32,2,128]{2,1,0:T(2,128)}), f32[32,2,128]{2,1,0:T(2,128)S(1)}, u32[]{:S(2)}, u32[]{:S(2)}) async-start(f32[32,2,128]{2,1,0:T(2,128)} %copy.16), calls=%async_computation.2 | async-start | bytes 65536 | tf_op jit(solution)/shard_map/all_to_all | solution.py:328
  273.6 1.2 copy-start
  274.7 119.5 %all-to-all-start.3 = ((bf16[32,3,16,512]{3,2,1,0:T(8,128)(2,1)}), bf16[32,3,16,512]{3,2,1,0:T(8,128)(2,1)S(1)}, u32[]{:S(2)}, u32[]{:S(2)}) async-start(bf16[32,3,16,512]{3,2,1,0:T(8,128)(2,1)} %copy-done), calls=%async_computation.3 | async-start | bytes 3145728 | tf_op jit(solution)/shard_map/all_to_all | solution.py:328
  285.3 63.5 %collective-permute-start.9 = (f32[4,2,512]{2,1,0:T(2,128)S(1)}, f32[4,2,512]{2,1,0:T(2,128)S(1)}, u32[]{:S(2)}, u32[]{:S(2)}) collective-permute-start(f32[4,2,512]{2,1,0:T(2,128)S(1)} %pad_maximum_fusion.1.refs_2_), channel_id=1, source_target_pairs={{8,0},{9,1},{10,2},{11,3},{12,4},{13,5},{14,6},{15,7},{24,16},{25,... | collective-permute-start | bytes 49160 | tf_op jit(solution)/shard_map/ppermute | solution.py:332
  355.0 39.3 %collective-permute-start.10 = (bf16[512,512]{1,0:T(8,128)(2,1)S(1)}, bf16[512,512]{1,0:T(8,128)(2,1)S(1)}, u32[]{:S(2)}, u32[]{:S(2)}) collective-permute-start(bf16[512,512]{1,0:T(8,128)(2,1)S(1)} %get-tuple-element.10), channel_id=1, source_target_pairs={{0,8},{1,9},{2,10},{3,11},{4,12},{5,13},{6,14},{7,15},{16,24},{17,... | collective-permute-start | bytes 1572872 | tf_op jit(solution)/shard_map/ppermute | solution.py:332

commit v3 on v1

--- a/solution.py
+++ b/solution.py
@@ -41,46 +41,82 @@
     )
 
 
-def pack_body(k_ref, v_ref, q_ref, g_ref, out_ref):
+def pack_body(scal_ref, k_ref, v_ref, q_ref, g_ref, out_ref, far_ref):
     _, subs, _, cols, _ = out_ref.shape
+    far_feats = far_ref.shape[-1]
     for a, ref in enumerate((k_ref, v_ref, q_ref, g_ref)):
         for s in range(subs):
             out_ref[0, s, a] = ref[s * cols : (s + 1) * cols, :]
 
-
-def pack(k, v, q, g, groups, subs, cols):
+    def fill(pair, feats):
+        for a, ref in enumerate(pair):
+            for s in range(subs):
+                far_ref[0, s, a] = ref[s * cols : (s + 1) * cols, feats]
+
+    @pl.when(scal_ref[0] == 0)
+    def _():
+        fill((k_ref, v_ref), slice(far_feats, 2 * far_feats))
+
+    @pl.when(scal_ref[0] != 0)
+    def _():
+        fill((q_ref, g_ref), slice(0, far_feats))
+
+
+def pack(scal, k, v, q, g, groups, subs, cols):
     tokens, feats = k.shape
-    wide_feats = feats // groups
+    near_feats = feats // groups
+    shapes = [(subs, 4, cols, near_feats), (subs, 2, cols, near_feats // HALVES)]
     return pl.pallas_call(
         pack_body,
         grid=(groups,),
-        in_specs=[pl.BlockSpec((tokens, wide_feats), lambda j: (0, j))] * 4,
-        out_specs=pl.BlockSpec((1, subs, 4, cols, wide_feats), lambda j: (j, 0, 0, 0, 0)),
-        out_shape=jax.ShapeDtypeStruct((groups, subs, 4, cols, wide_feats), bf16),
+        in_specs=[smem()] + [pl.BlockSpec((tokens, near_feats), lambda j: (0, j))] * 4,
+        out_specs=[pl.BlockSpec((1, *shape), lambda j: (j, 0, 0, 0, 0)) for shape in shapes],
+        out_shape=[jax.ShapeDtypeStruct((groups, *shape), bf16) for shape in shapes],
         compiler_params=params(),
         name="pack",
-    )(k, v, q, g)
-
-
-def unpack_body(in_ref, q_ref, k_ref, v_ref):
+    )(scal, k, v, q, g)
+
+
+def unpack_body(scal_ref, in_ref, far_ref, q_ref, k_ref, v_ref):
     _, subs, _, cols, _ = in_ref.shape
+    far_feats = far_ref.shape[-1]
     for a, ref in enumerate((q_ref, k_ref, v_ref)):
         for s in range(subs):
             ref[s * cols : (s + 1) * cols, :] = in_ref[0, s, a]
 
-
-def unpack(arr, tokens, feats):
-    groups, subs, _, cols, wide_feats = arr.shape
+    def add(ref, terms, feats):
+        ref[:, feats] = (ref[:, feats].astype(f32) + terms.astype(f32)).astype(bf16)
+
+    @pl.when(scal_ref[0] == 0)
+    def _():
+        upper = slice(far_feats, 2 * far_feats)
+        add(k_ref, far_ref[0, 0], upper)
+        add(v_ref, far_ref[0, 1], upper)
+
+    @pl.when(scal_ref[0] != 0)
+    def _():
+        add(q_ref, far_ref[0, 0], slice(0, far_feats))
+
+
+def unpack(scal, arr, far, tokens, feats):
+    groups, subs, _, cols, near_feats = arr.shape
     out = jax.ShapeDtypeStruct((tokens, feats), bf16)
+    far_spec = pl.BlockSpec((1, *far.shape[1:]), lambda j, scal_ref: (j ^ scal_ref[3], 0, 0, 0))
     return pl.pallas_call(
         unpack_body,
-        grid=(groups,),
-        in_specs=[pl.BlockSpec((1, subs, 3, cols, wide_feats), lambda j: (j, 0, 0, 0, 0))],
-        out_specs=[pl.BlockSpec((tokens, wide_feats), lambda j: (0, j))] * 3,
+        grid_spec=pltpu.PrefetchScalarGridSpec(
+            num_scalar_prefetch=1,
+            grid=(groups,),
+            in_specs=[
+                pl.BlockSpec((1, subs, 3, cols, near_feats), lambda j, scal_ref: (j, 0, 0, 0, 0)),
+                far_spec,
+            ],
+            out_specs=[pl.BlockSpec((tokens, near_feats), lambda j, scal_ref: (0, j))] * 3,
+        ),
         out_shape=[out] * 3,
         compiler_params=params(),
         name="unpack",
-    )(arr)
+    )(scal, arr, far)
 
 
 def flat(ref, index):
@@ -126,21 +162,36 @@
     return top + jnp.log(total), (a * delta_a + b * delta_b) / total
 
 
-def row_stats_body(scale, scal_ref, t_ref, far_ref, out_ref):
+def row_stats_body(scale, scal_ref, t_ref, out_ref):
     k, v, q, g = (flat(t_ref, i) for i in range(4))
-    n = k.shape[0]
-    lse, delta = partial_stats(k, v, q, g, row_masks(scal_ref, n), scale)
+    lse, delta = partial_stats(k, v, q, g, row_masks(scal_ref, k.shape[0]), scale)
     out_ref[0, 0:1] = lse
     out_ref[0, 1:2] = delta
 
-    @pl.when(scal_ref[0] == 1)
-    def _():
-        lse_f, delta_f = partial_stats(
-            flat(far_ref, 0), flat(far_ref, 1), q, g, off_mask(scal_ref, n), scale
-        )
-        lse_m, delta_m = merge(lse, delta, lse_f, delta_f)
-        out_ref[0, 0:1] = lse_m
-        out_ref[0, 1:2] = delta_m
+
+def gather_far(scal_ref, piece_refs, buf):
+    for i, ref in enumerate(piece_refs):
+        for a in range(2):
+            buf[a, scal_ref[3] ^ i] = flat(ref, a)
+    return (buf[a].reshape(buf.shape[1] * buf.shape[2], HEAD) for a in range(2))
+
+
+def off_stats_body(scale, scal_ref, t_ref, *refs):
+    *piece_refs, out_ref, buf = refs
+    far_a, far_b = gather_far(scal_ref, piece_refs, buf)
+
+    def run(k, v, q, g):
+        lse, delta = partial_stats(k, v, q, g, off_mask(scal_ref, k.shape[0]), scale)
+        out_ref[0, 0:1] = lse
+        out_ref[0, 1:2] = delta
+
+    @pl.when(scal_ref[0] == 0)
+    def _():
+        run(flat(t_ref, KI), flat(t_ref, VI), far_a, far_b)
+
+    @pl.when(scal_ref[0] != 0)
+    def _():
+        run(far_a, far_b, flat(t_ref, QI), flat(t_ref, GI))
 
 
 def col_stats_body(scale, scal_ref, t_ref, out_ref):
@@ -158,6 +209,84 @@
 def head_block(arr):
     a, b, c, _ = arr.shape
     return pl.BlockSpec((a, b, c, HEAD), lambda h: (0, 0, 0, h))
+
+
+def off_block(arr, heads):
+    a, b, c, _ = arr.shape
+    return pl.BlockSpec((a, b, c, HEAD), lambda h, scal_ref: (0, 0, 0, h + scal_ref[0] * heads))
+
+
+def off_call(body, scale, scal, t, extra, pieces, out_specs, out_shape, units, name):
+    heads = pieces[0].shape[3] // HEAD
+    tokens = pieces[0].shape[0] * pieces[0].shape[2]
+    rows, _, cols, _ = t.shape
+    stat_spec = pl.BlockSpec((1, 2, rows * cols), lambda h, scal_ref: (h, 0, 0))
+    piece_specs = [
+        pl.BlockSpec((*p.shape[:3], HEAD), lambda h, scal_ref: (0, 0, 0, h)) for p in pieces
+    ]
+    return pl.pallas_call(
+        lambda *refs: body(scale, *refs),
+        grid_spec=pltpu.PrefetchScalarGridSpec(
+            num_scalar_prefetch=1,
+            grid=(heads,),
+            in_specs=[off_block(t, heads)] + [stat_spec] * len(extra) + piece_specs,
+            out_specs=out_specs,
+            scratch_shapes=[pltpu.VMEM((2, len(pieces), tokens, HEAD), bf16)],
+        ),
+        out_shape=out_shape,
+        compiler_params=params(),
+        cost_estimate=cost(units),
+        name=name,
+    )(scal, t, *extra, *pieces)
+
+
+def off_stats(scale, scal, t, pieces):
+    heads = pieces[0].shape[3] // HEAD
+    n = t.shape[0] * t.shape[2]
+    return off_call(
+        off_stats_body, scale, scal, t, (), pieces,
+        pl.BlockSpec((1, 2, n), lambda h, scal_ref: (h, 0, 0)),
+        jax.ShapeDtypeStruct((heads, 2, n), f32), 2, "off_stats",
+    )
+
+
+def off_grads_body(scale, scal_ref, t_ref, stat_ref, *refs):
+    *piece_refs, near_ref, far_ref, buf = refs
+    far_a, far_b = gather_far(scal_ref, piece_refs, buf)
+    lse, delta = stat_ref[0, 0:1], stat_ref[0, 1:2]
+
+    def run(k, v, q, g):
+        return block_grads(k, v, q, g, off_mask(scal_ref, k.shape[0]), lse, delta, scale)
+
+    @pl.when(scal_ref[0] == 0)
+    def _():
+        dq, dk, dv = run(flat(t_ref, KI), flat(t_ref, VI), far_a, far_b)
+        near_ref[0] = dk
+        near_ref[1] = dv
+        far_ref[:, 0] = dq.astype(bf16).reshape(far_ref.shape[0], far_ref.shape[2], HEAD)
+
+    @pl.when(scal_ref[0] != 0)
+    def _():
+        dq, dk, dv = run(far_a, far_b, flat(t_ref, QI), flat(t_ref, GI))
+        near_ref[0] = dq
+        for a, d in enumerate((dk, dv)):
+            far_ref[:, a] = d.astype(bf16).reshape(far_ref.shape[0], far_ref.shape[2], HEAD)
+
+
+def off_grads(scale, scal, t, stats, pieces):
+    n = t.shape[0] * t.shape[2]
+    feats = pieces[0].shape[3]
+    far_shape = (len(pieces), 2, n // len(pieces), feats)
+    return off_call(
+        off_grads_body, scale, scal, t, (stats,), pieces,
+        [
+            pl.BlockSpec((2, n, HEAD), lambda h, scal_ref: (0, 0, h)),
+            pl.BlockSpec((*far_shape[:3], HEAD), lambda h, scal_ref: (0, 0, 0, h)),
+        ],
+        [jax.ShapeDtypeStruct((2, n, feats), f32), jax.ShapeDtypeStruct(far_shape, bf16)],
+        5,
+        "off_grads",
+    )
 
 
 def stats_call(body, scale, scal, arrays, name, units):
@@ -184,23 +313,12 @@
     return dq, dk, dv
 
 
-def row_grads_body(scale, scal_ref, t_ref, far_ref, stat_ref, out_ref, back_ref):
+def row_grads_body(scale, scal_ref, t_ref, stat_ref, out_ref):
     k, v, q, g = (flat(t_ref, i) for i in range(4))
-    n = k.shape[0]
-    lse, delta = stat_ref[0, 0:1], stat_ref[0, 1:2]
-    dq, dk, dv = block_grads(k, v, q, g, row_masks(scal_ref, n), lse, delta, scale)
-    out_ref[0] = dq
-    out_ref[1] = dk
-    out_ref[2] = dv
-
-    @pl.when(scal_ref[0] == 1)
-    def _():
-        dq_f, dk_f, dv_f = block_grads(
-            flat(far_ref, 0), flat(far_ref, 1), q, g, off_mask(scal_ref, n), lse, delta, scale
-        )
-        out_ref[0] += dq_f
-        back_ref[0] = dk_f.astype(bf16)
-        back_ref[1] = dv_f.astype(bf16)
+    mask = row_masks(scal_ref, k.shape[0])
+    grads = block_grads(k, v, q, g, mask, stat_ref[0, 0:1], stat_ref[0, 1:2], scale)
+    for a, d in enumerate(grads):
+        out_ref[a] = d
 
 
 def col_grads_body(scale, scal_ref, t_ref, stat_ref, out_ref):
@@ -212,25 +330,19 @@
         out_ref[:, a] = d.astype(bf16).reshape(out_ref.shape[0], out_ref.shape[2], HEAD)
 
 
-def row_grads(scale, scal, t, far, stats):
+def row_grads(scale, scal, t, stats):
     rows, _, cols, feats = t.shape
     n = rows * cols
     return pl.pallas_call(
         lambda *refs: row_grads_body(scale, *refs),
         grid=(feats // HEAD,),
-        in_specs=[smem(), head_block(t), head_block(far), pl.BlockSpec((1, 2, n), lambda h: (h, 0, 0))],
-        out_specs=[
-            pl.BlockSpec((3, n, HEAD), lambda h: (0, 0, h)),
-            pl.BlockSpec((2, n, HEAD), lambda h: (0, 0, h)),
-        ],
-        out_shape=[
-            jax.ShapeDtypeStruct((3, n, feats), f32),
-            jax.ShapeDtypeStruct((2, n, feats), bf16),
-        ],
-        compiler_params=params(),
-        cost_estimate=cost(16),
+        in_specs=[smem(), head_block(t), pl.BlockSpec((1, 2, n), lambda h: (h, 0, 0))],
+        out_specs=pl.BlockSpec((3, n, HEAD), lambda h: (0, 0, h)),
+        out_shape=jax.ShapeDtypeStruct((3, n, feats), f32),
+        compiler_params=params(),
+        cost_estimate=cost(8),
         name="row_grads",
-    )(scal, t, far, stats)
+    )(scal, t, stats)
 
 
 def col_grads(scale, scal, t, stats):
@@ -248,15 +360,25 @@
     )(scal, t, stats)
 
 
-def join_body(row_ref, col_ref, far_ref, out_ref):
+def join_body(scal_ref, row_ref, off_ref, col_ref, out_ref, total_ref):
+    half_feats = off_ref.shape[2]
     for a in range(3):
-        total = row_ref[a] + col_ref[:, a].astype(f32).reshape(row_ref.shape[1:])
-        if a > 0:
-            total = total + far_ref[a - 1].astype(f32)
-        out_ref[:, a] = total.astype(bf16).reshape(out_ref.shape[0], *out_ref.shape[2:])
-
-
-def join(row, col, far):
+        total_ref[a] = row_ref[a] + col_ref[:, a].astype(f32).reshape(row_ref.shape[1:])
+
+    @pl.when(scal_ref[0] == 0)
+    def _():
+        for a in range(2):
+            total_ref[a + 1, :, :half_feats] += off_ref[a]
+
+    @pl.when(scal_ref[0] != 0)
+    def _():
+        total_ref[0, :, half_feats:] += off_ref[0]
+
+    for a in range(3):
+        out_ref[:, a] = total_ref[a].astype(bf16).reshape(out_ref.shape[0], *out_ref.shape[2:])
+
+
+def join(scal, row, off, col):
     rows, _, cols, feats = col.shape
     steps = 4
     part = rows // steps
@@ -265,15 +387,17 @@
         join_body,
         grid=(steps,),
         in_specs=[
+            smem(),
             pl.BlockSpec((3, n, feats), lambda i: (0, i, 0)),
+            pl.BlockSpec((2, n, off.shape[2]), lambda i: (0, i, 0)),
             pl.BlockSpec((part, 3, cols, feats), lambda i: (i, 0, 0, 0)),
-            pl.BlockSpec((2, n, feats), lambda i: (0, i, 0)),
         ],
         out_specs=pl.BlockSpec((part, 3, cols, feats), lambda i: (i, 0, 0, 0)),
         out_shape=jax.ShapeDtypeStruct(col.shape, bf16),
+        scratch_shapes=[pltpu.VMEM((3, n, feats), f32)],
         compiler_params=params(),
         name="join",
-    )(row, col, far)
+    )(scal, row, off, col)
 
 
 def body(query_in, key_in, value_in, grad_out, row_start, col_start):
@@ -295,20 +419,44 @@
     def exchange_wide(arr):
         return lax.all_to_all(arr, "wide", split_axis=0, concat_axis=0, tiled=True)
 
+    def shift(arr, source, target):
+        pairs = [(source * groups + j, target * groups + j) for j in range(groups)]
+        return lax.ppermute(arr, "narrow", pairs)
+
+    def swap(arr, step):
+        pairs = [(i, i ^ step) for i in range(narrow)]
+        return lax.ppermute(arr, "narrow", pairs)
+
+    def spread(arr):
+        pieces = []
+        for step in range(groups):
+            piece = lax.dynamic_index_in_dim(arr, near_index ^ step, keepdims=False)
+            pieces.append(swap(piece, step) if step else piece)
+        return pieces
+
     wide_index = lax.axis_index("wide")
-    half = lax.axis_index("narrow") // groups
+    narrow_index = lax.axis_index("narrow")
+    half = narrow_index // groups
+    near_index = narrow_index % groups
     first_col = lax.dynamic_index_in_dim(row_start, wide_index, keepdims=False)
     block_id = (half * half_cols + wide_index * cols) // CB
     first_row = lax.dynamic_index_in_dim(col_start, block_id, keepdims=False)
-    scal = jnp.stack([half, first_col, first_row]).astype(jnp.int32)
-
-    packed = pack(key_in, value_in, query_in, grad_out, groups, subs, cols)
+    scal = jnp.stack([half, first_col, first_row, near_index]).astype(jnp.int32)
+
+    packed, packed_far = pack(scal, key_in, value_in, query_in, grad_out, groups, subs, cols)
     near_feats = feats // groups
+    heads = near_feats // HEAD
+    near_heads = heads // HALVES
+    far = swap(packed_far, groups)
     t = exchange_near(packed).reshape(lanes, 4, cols, near_feats)
-    far = lax.ppermute(t[:, :2], "narrow", [(j, j + groups) for j in range(groups)])
+    t, far = lax.optimization_barrier((t, far))
     by_col = exchange_wide(t)
-    heads = near_feats // HEAD
-    row_part = stats_call(row_stats_body, scale, scal, (t, far), "row_stats", 6)
+    pieces = spread(far)
+    diag_part = stats_call(row_stats_body, scale, scal, (t,), "row_stats", 4)
+    own_off = off_stats(scale, scal, t, pieces)
+    off_part = jnp.concatenate([shift(own_off, 0, 1), own_off])
+    lse, delta = merge(diag_part[:, 0], diag_part[:, 1], off_part[:, 0], off_part[:, 1])
+    row_part = jnp.where(half == 1, jnp.stack([lse, delta], axis=1), diag_part)
     col_part = stats_call(col_stats_body, scale, scal, (by_col,), "col_stats", 4)
 
     both = jnp.stack([row_part, col_part]).reshape(4 * heads, lanes, cols)
@@ -320,12 +468,19 @@
     row_full = jnp.stack([row_lse, row_delta], axis=1)
     col_full = jnp.stack([col_lse, col_delta], axis=1)
 
-    from_col = exchange_wide(col_grads(scale, scal, by_col, col_full))
-    row_terms, far_terms = row_grads(scale, scal, t, far, row_full)
-    far_back = lax.ppermute(far_terms, "narrow", [(j + groups, j) for j in range(groups)])
-    joined = join(row_terms, from_col, far_back)
+    far_full = shift(row_full[:near_heads], 1, 0)
+    col_terms = col_grads(scale, scal, by_col, col_full)
+    col_terms, far_full = lax.optimization_barrier((col_terms, far_full))
+    from_col = exchange_wide(col_terms)
+    row_terms = row_grads(scale, scal, t, row_full)
+    off_full = jnp.where(half == 1, row_full[near_heads:], far_full)
+    off_terms, far_terms = off_grads(scale, scal, t, off_full, pieces)
+    far_terms = jnp.stack(spread(far_terms))
+    from_col, far_terms = lax.optimization_barrier((from_col, far_terms))
+    back = swap(far_terms, groups)
+    joined = join(scal, row_terms, off_terms, from_col)
     out = exchange_near(joined.reshape(groups, subs, 3, cols, near_feats))
-    return unpack(out, tokens, feats)
+    return unpack(scal, out, back, tokens, feats)
 
 
 def solution(mesh):

time: 420 us -> 370 us (0.88)
  the two profiles are of different devices: /device:TPU:100 before, /device:TPU:1 now
where the time goes in v3:
time: 370 us; the launch traced here: 369 us
  waiting for transfers between devices  179 us (48%)
  starting transfers between devices  135 us (36%)
  Pallas kernels  34.9 us (9%)
  local copies, waits for them, and re-layouts  15.9 us (4%)
    all_to_all x3, waiting for transfers between devices, exchange_wide(): return lax.all_to_all(arr, 'wide', split_axis=0, concat_axis=0, tiled=True)  89.6 us
    ppermute x16, waiting for transfers between devices, swap(): return lax.ppermute(arr, 'narrow', pairs)  84 us
    ppermute x16, starting transfers between devices, swap(): return lax.ppermute(arr, 'narrow', pairs)  63.5 us
    all_to_all x3, starting transfers between devices, exchange_wide(): return lax.all_to_all(arr, 'wide', split_axis=0, concat_axis=0, tiled=True)  43.4 us
    all_to_all x2, starting transfers between devices, exchange_near(): lax.all_to_all(arr, 'narrow', split_axis=0, concat_axis=0, axis_index_gro...  17.8 us
    ppermute x2, starting transfers between devices, shift(): return lax.ppermute(arr, 'narrow', pairs)  10.8 us
    unnamed x18, local copies, waits for them, and re-layouts  10.7 us
  transfers between devices with their start and end apart: 23, of which 10 were waited for; matrix products, arithmetic and copies ran while one was open for 1% of the time, Pallas kernels for 6%

profile of v3, /device:TPU:1, one launch (start us, length us, event | category | flops | bytes accessed | tf_op | source)
XLA Modules:
  0.0 368.6 jit_solution(6129282271267992265)
XLA Ops:
  8.7 3.7 pack.1
  12.4 11.1 %all-to-all-start = ((bf16[8,4,4,16,512]{4,3,2,1,0:T(8,128)(2,1)}), bf16[8,4,4,16,512]{4,3,2,1,0:T(8,128)(2,1)}, u32[]{:S(2)}, u32[]{:S(2)}) async-start(bf16[8,4,4,16,512]{4,3,2,1,0:T(8,128)(2,1)} %get-tuple-element.13), calls=%async_computation | async-start | bytes 4194304 | tf_op jit(solution)/shard_map/all_to_all | solution.py:415
  23.5 10.3 %collective-permute-start = (bf16[8,4,2,16,256]{4,3,2,1,0:T(8,128)(2,1)S(1)}, bf16[8,4,2,16,256]{4,3,2,1,0:T(8,128)(2,1)S(1)}, u32[]{:S(2)}, u32[]{:S(2)}) collective-permute-start(bf16[8,4,2,16,256]{4,3,2,1,0:T(8,128)(2,1)S(1)} %get-tuple-element.14), channel_id=1, source_target_pairs={{0,8},{1,9},{2,10},{3,11},{4,12},{5,13},{6,14},{7,15},{8,0},{9,1},... | collective-permute-start | bytes 1572872 | tf_op jit(solution)/shard_map/ppermute | solution.py:428
  33.8 25.9 %collective-permute-done = bf16[8,4,2,16,256]{4,3,2,1,0:T(8,128)(2,1)S(1)} collective-permute-done((bf16[8,4,2,16,256]{4,3,2,1,0:T(8,128)(2,1)S(1)}, bf16[8,4,2,16,256]{4,3,2,1,0:T(8,128)(2,1)S(1)}, u32[]{:S(2)}, u32[]{:S(2)}) %collective-permute-start) | collective-permute-done | bytes 524320 | tf_op jit(solution)/shard_map/ppermute | solution.py:428
  59.6 29.8 %all-to-all-start.1 = ((bf16[32,4,16,512]{3,2,1,0:T(8,128)(2,1)}), bf16[32,4,16,512]{3,2,1,0:T(8,128)(2,1)S(1)}, u32[]{:S(2)}, u32[]{:S(2)}) async-start(bf16[32,4,16,512]{3,2,1,0:T(8,128)(2,1)} %bitcast.2.refs_1_), calls=%async_computation.1 | async-start | bytes 4194304 | tf_op jit(solution)/shard_map/all_to_all | solution.py:420
  89.5 5.4 %collective-permute-start.7 = (bf16[4,2,16,256]{3,2,1,0:T(8,128)(2,1)S(1)}, bf16[4,2,16,256]{3,2,1,0:T(8,128)(2,1)S(1)}, u32[]{:S(2)}, u32[]{:S(2)}) collective-permute-start(bf16[4,2,16,256]{3,2,1,0:T(8,128)(2,1)S(1)} %get-tuple-element.31), channel_id=1, source_target_pairs={{0,7},{1,6},{2,5},{3,4},{4,3},{5,2},{6,1},{7,0},{8,15},{9,14},{10,... | collective-permute-start | bytes 196616 | tf_op jit(solution)/shard_map/ppermute | solution.py:428
  96.9 3.3 collective-permute-start.5
  100.2 3.7 %collective-permute-start.4 = (bf16[4,2,16,256]{3,2,1,0:T(8,128)(2,1)S(1)}, bf16[4,2,16,256]{3,2,1,0:T(8,128)(2,1)S(1)}, u32[]{:S(2)}, u32[]{:S(2)}) collective-permute-start(bf16[4,2,16,256]{3,2,1,0:T(8,128)(2,1)S(1)} %get-tuple-element.34), channel_id=1, source_target_pairs={{0,4},{1,5},{2,6},{3,7},{4,0},{5,1},{6,2},{7,3},{8,12},{9,13},{10,... | collective-permute-start | bytes 196616 | tf_op jit(solution)/shard_map/ppermute | solution.py:428
  106.4 3.2 collective-permute-start.2
  112.7 3.0 off_stats.1
  115.7 9.5 %collective-permute-start.8 = (f32[2,2,512]{2,1,0:T(2,128)S(1)}, f32[2,2,512]{2,1,0:T(2,128)S(1)}, u32[]{:S(2)}, u32[]{:S(2)}) collective-permute-start(f32[2,2,512]{2,1,0:T(2,128)S(1)} %off_stats.1), channel_id=1, source_target_pairs={{0,8},{1,9},{2,10},{3,11},{4,12},{5,13},{6,14},{7,15},{16,24},{17,... | collective-permute-start | bytes 24584 | tf_op jit(solution)/shard_map/ppermute | solution.py:424
  125.2 3.9 %row_stats.1 = f32[4,2,512]{2,1,0:T(2,128)S(1)} custom-call(s32[4]{0:T(128)S(1)} %pad_add_fusion.scal_ref.refs_0_, bf16[32,4,16,512]{3,2,1,0:T(8,128)(2,1)} %bitcast.2.refs_1_), custom_call_target="tpu_custom_call" | custom-call | flops 1342177280 | bytes 4194304 | tf_op jit(solution)/shard_map/row_stats/pallas_call | solution.py:295
  129.2 52.9 %all-to-all-done.1.refs_1_ = bf16[32,4,16,512]{3,2,1,0:T(8,128)(2,1)S(1)} async-done(((bf16[32,4,16,512]{3,2,1,0:T(8,128)(2,1)}), bf16[32,4,16,512]{3,2,1,0:T(8,128)(2,1)S(1)}, u32[]{:S(2)}, u32[]{:S(2)}) %all-to-all-start.1) | async-done | bytes 2097184 | tf_op jit(solution)/shard_map/all_to_all | solution.py:420
  182.2 3.3 col_stats.1
  186.4 9.6 %all-to-all-start.2 = ((f32[32,2,128]{2,1,0:T(2,128)}), f32[32,2,128]{2,1,0:T(2,128)S(1)}, u32[]{:S(2)}, u32[]{:S(2)}) async-start(f32[32,2,128]{2,1,0:T(2,128)} %copy.16), calls=%async_computation.2 | async-start | bytes 65536 | tf_op jit(solution)/shard_map/all_to_all | solution.py:420
  196.1 11.4 %all-to-all-done.2 = f32[32,2,128]{2,1,0:T(2,128)S(1)} async-done(((f32[32,2,128]{2,1,0:T(2,128)}), f32[32,2,128]{2,1,0:T(2,128)S(1)}, u32[]{:S(2)}, u32[]{:S(2)}) %all-to-all-start.2) | async-done | bytes 32800 | tf_op jit(solution)/shard_map/all_to_all | solution.py:420
  209.4 4.7 %col_grads.1 = bf16[32,3,16,512]{3,2,1,0:T(8,128)(2,1)S(1)} custom-call(s32[4]{0:T(128)S(1)} %pad_add_fusion.scal_ref.refs_0_, bf16[32,4,16,512]{3,2,1,0:T(8,128)(2,1)S(1)} %all-to-all-done.1.refs_1_, f32[4,2,512]{2,1,0:T(2,128)S(1)} %pad_maximum_fusion.2.refs_2_), custom_call_target="tpu_custom_call" | custom-call | flops 2684354560 | bytes 4194304 | tf_op jit(solution)/shard_map/col_grads/pallas_call | solution.py:351
  215.2 5.9 %collective-permute-done.9 = f32[2,2,512]{2,1,0:T(2,128)S(1)} collective-permute-done((f32[2,2,512]{2,1,0:T(2,128)S(1)}, f32[2,2,512]{2,1,0:T(2,128)S(1)}, u32[]{:S(2)}, u32[]{:S(2)}) %collective-permute-start.9) | collective-permute-done | bytes 8224 | tf_op jit(solution)/shard_map/ppermute | solution.py:424
  221.2 4.0 %all-to-all-start.3 = ((bf16[32,3,16,512]{3,2,1,0:T(8,128)(2,1)}), bf16[32,3,16,512]{3,2,1,0:T(8,128)(2,1)S(1)}, u32[]{:S(2)}, u32[]{:S(2)}) async-start(bf16[32,3,16,512]{3,2,1,0:T(8,128)(2,1)} %copy-done.1), calls=%async_computation.3 | async-start | bytes 3145728 | tf_op jit(solution)/shard_map/all_to_all | solution.py:420
  225.2 3.7 %off_grads.1 = (f32[2,512,256]{2,1,0:T(8,128)S(1)}, bf16[8,2,64,256]{3,2,1,0:T(8,128)(2,1)S(1)}) custom-call(s32[4]{0:T(128)S(1)} %pad_add_fusion.scal_ref.refs_0_, bf16[32,4,16,512]{3,2,1,0:T(8,128)(2,1)} %bitcast.2.refs_1_, f32[2,2,512]{2,1,0:T(2,128)S(1)} %fusion.2.refs_2_, bf16[4,2,16,256]{3,2,1,0:T(8,128)(2,1)S(1)} %get-tuple-element.38.refs_2_.refs_3_, ...), custom_call_target="tpu_custom_call" | custom-call | flops 1677721600 | bytes 4194304 | tf_op jit(solution)/shard_map/off_grads/pallas_call | solution.py:227
  229.6 5.4 %collective-permute-start.10 = (bf16[2,64,256]{2,1,0:T(8,128)(2,1)S(1)}, bf16[2,64,256]{2,1,0:T(8,128)(2,1)S(1)}, u32[]{:S(2)}, u32[]{:S(2)}) collective-permute-start(bf16[2,64,256]{2,1,0:T(8,128)(2,1)S(1)} %get-tuple-element.29), channel_id=1, source_target_pairs={{0,1},{1,0},{2,3},{3,2},{4,5},{5,4},{6,7},{7,6},{8,9},{9,8},{10,11... | collective-permute-start | bytes 196616 | tf_op jit(solution)/shard_map/ppermute | solution.py:428
  235.0 5.1 %row_grads.1.row_ref = f32[3,512,512]{2,1,0:T(8,128)S(1)} custom-call(s32[4]{0:T(128)S(1)} %pad_add_fusion.scal_ref.refs_0_, bf16[32,4,16,512]{3,2,1,0:T(8,128)(2,1)} %bitcast.2.refs_1_, f32[4,2,512]{2,1,0:T(2,128)S(1)} %pad_maximum_fusion.1.refs_2_), custom_call_target="tpu_custom_call" | custom-call | flops 2684354560 | bytes 4194304 | tf_op jit(solution)/shard_map/row_grads/pallas_call | solution.py:336
  241.7 4.4 %collective-permute-start.16 = (bf16[2,64,256]{2,1,0:T(8,128)(2,1)S(1)}, bf16[2,64,256]{2,1,0:T(8,128)(2,1)S(1)}, u32[]{:S(2)}, u32[]{:S(2)}) collective-permute-start(bf16[2,64,256]{2,1,0:T(8,128)(2,1)S(1)} %get-tuple-element.23), channel_id=1, source_target_pairs={{0,7},{1,6},{2,5},{3,4},{4,3},{5,2},{6,1},{7,0},{8,15},{9,14},{10,... | collective-permute-start | bytes 196616 | tf_op jit(solution)/shard_map/ppermute | solution.py:428
  248.1 4.2 %collective-permute-start.14 = (bf16[2,64,256]{2,1,0:T(8,128)(2,1)S(1)}, bf16[2,64,256]{2,1,0:T(8,128)(2,1)S(1)}, u32[]{:S(2)}, u32[]{:S(2)}) collective-permute-start(bf16[2,64,256]{2,1,0:T(8,128)(2,1)S(1)} %get-tuple-element.25), channel_id=1, source_target_pairs={{0,5},{1,4},{2,7},{3,6},{4,1},{5,0},{6,3},{7,2},{8,13},{9,12},{10,... | collective-permute-start | bytes 196616 | tf_op jit(solution)/shard_map/ppermute | solution.py:428
  252.3 3.2 collective-permute-start.13
  261.1 2.9 collective-permute-start.12
  270.8 25.2 %all-to-all-done.3.col_ref = bf16[32,3,16,512]{3,2,1,0:T(8,128)(2,1)S(1)} async-done(((bf16[32,3,16,512]{3,2,1,0:T(8,128)(2,1)}), bf16[32,3,16,512]{3,2,1,0:T(8,128)(2,1)S(1)}, u32[]{:S(2)}, u32[]{:S(2)}) %all-to-all-start.3) | async-done | bytes 1572896 | tf_op jit(solution)/shard_map/all_to_all | solution.py:420
  296.0 4.1 %join.1 = bf16[32,3,16,512]{3,2,1,0:T(8,128)(2,1)} custom-call(s32[4]{0:T(128)S(1)} %pad_add_fusion.scal_ref.refs_0_, f32[3,512,512]{2,1,0:T(8,128)} %copy-done, f32[2,512,256]{2,1,0:T(8,128)S(1)} %get-tuple-element.18.off_ref, bf16[32,3,16,512]{3,2,1,0:T(8,128)(2,1)S(1)} %all-to-all-done.3.col_ref), custom_call_target="tpu_custom_call" | custom-call | tf_op jit(solution)/shard_map/join/pallas_call | solution.py:386
  300.1 6.7 %all-to-all-start.4 = ((bf16[8,4,3,16,512]{4,3,2,1,0:T(8,128)(2,1)}), bf16[8,4,3,16,512]{4,3,2,1,0:T(8,128)(2,1)S(1)}, u32[]{:S(2)}, u32[]{:S(2)}) async-start(bf16[8,4,3,16,512]{4,3,2,1,0:T(8,128)(2,1)} %bitcast.35), calls=%async_computation.4 | async-start | bytes 3145728 | tf_op jit(solution)/shard_map/all_to_all | solution.py:415
  306.8 6.7 %collective-permute-start.17 = (bf16[8,2,64,256]{3,2,1,0:T(8,128)(2,1)}, bf16[8,2,64,256]{3,2,1,0:T(8,128)(2,1)S(1)}, u32[]{:S(2)}, u32[]{:S(2)}) collective-permute-start(bf16[8,2,64,256]{3,2,1,0:T(8,128)(2,1)} %bitcast_dynamic-update-slice_fusion), channel_id=1, source_target_pairs={{0,8},{1,9},{2,10},{3,11},{4,12},{5,13},{6,14},{7,15},{8,0},{9,1},... | collective-permute-start | bytes 1572872 | tf_op jit(solution)/shard_map/ppermute | solution.py:428
  313.6 51.5 %collective-permute-done.17.far_ref = bf16[8,2,64,256]{3,2,1,0:T(8,128)(2,1)S(1)} collective-permute-done((bf16[8,2,64,256]{3,2,1,0:T(8,128)(2,1)}, bf16[8,2,64,256]{3,2,1,0:T(8,128)(2,1)S(1)}, u32[]{:S(2)}, u32[]{:S(2)}) %collective-permute-start.17) | collective-permute-done | bytes 524320 | tf_op jit(solution)/shard_map/ppermute | solution.py:428
  365.1 3.5 unpack.1
  (62 shorter events, 36.2 us)
Async XLA Ops:
  4.5 1.0 copy-start.2
  5.6 1.0 copy-start.3
  6.6 1.0 copy-start.4
  7.6 1.0 copy-start.5
  12.4 47.2 %all-to-all-start = ((bf16[8,4,4,16,512]{4,3,2,1,0:T(8,128)(2,1)}), bf16[8,4,4,16,512]{4,3,2,1,0:T(8,128)(2,1)}, u32[]{:S(2)}, u32[]{:S(2)}) async-start(bf16[8,4,4,16,512]{4,3,2,1,0:T(8,128)(2,1)} %get-tuple-element.13), calls=%async_computation | async-start | bytes 4194304 | tf_op jit(solution)/shard_map/all_to_all | solution.py:415
  23.5 36.1 %collective-permute-start = (bf16[8,4,2,16,256]{4,3,2,1,0:T(8,128)(2,1)S(1)}, bf16[8,4,2,16,256]{4,3,2,1,0:T(8,128)(2,1)S(1)}, u32[]{:S(2)}, u32[]{:S(2)}) collective-permute-start(bf16[8,4,2,16,256]{4,3,2,1,0:T(8,128)(2,1)S(1)} %get-tuple-element.14), channel_id=1, source_target_pairs={{0,8},{1,9},{2,10},{3,11},{4,12},{5,13},{6,14},{7,15},{8,0},{9,1},... | collective-permute-start | bytes 1572872 | tf_op jit(solution)/shard_map/ppermute | solution.py:428
  59.6 122.5 %all-to-all-start.1 = ((bf16[32,4,16,512]{3,2,1,0:T(8,128)(2,1)}), bf16[32,4,16,512]{3,2,1,0:T(8,128)(2,1)S(1)}, u32[]{:S(2)}, u32[]{:S(2)}) async-start(bf16[32,4,16,512]{3,2,1,0:T(8,128)(2,1)} %bitcast.2.refs_1_), calls=%async_computation.1 | async-start | bytes 4194304 | tf_op jit(solution)/shard_map/all_to_all | solution.py:420
  89.5 16.8 %collective-permute-start.7 = (bf16[4,2,16,256]{3,2,1,0:T(8,128)(2,1)S(1)}, bf16[4,2,16,256]{3,2,1,0:T(8,128)(2,1)S(1)}, u32[]{:S(2)}, u32[]{:S(2)}) collective-permute-start(bf16[4,2,16,256]{3,2,1,0:T(8,128)(2,1)S(1)} %get-tuple-element.31), channel_id=1, source_target_pairs={{0,7},{1,6},{2,5},{3,4},{4,3},{5,2},{6,1},{7,0},{8,15},{9,14},{10,... | collective-permute-start | bytes 196616 | tf_op jit(solution)/shard_map/ppermute | solution.py:428
  94.9 14.7 %collective-permute-start.6 = (bf16[4,2,16,256]{3,2,1,0:T(8,128)(2,1)S(1)}, bf16[4,2,16,256]{3,2,1,0:T(8,128)(2,1)S(1)}, u32[]{:S(2)}, u32[]{:S(2)}) collective-permute-start(bf16[4,2,16,256]{3,2,1,0:T(8,128)(2,1)S(1)} %get-tuple-element.32), channel_id=1, source_target_pairs={{0,6},{1,7},{2,4},{3,5},{4,2},{5,3},{6,0},{7,1},{8,14},{9,15},{10,... | collective-permute-start | bytes 196616 | tf_op jit(solution)/shard_map/ppermute | solution.py:428
  96.9 14.9 %collective-permute-start.5 = (bf16[4,2,16,256]{3,2,1,0:T(8,128)(2,1)S(1)}, bf16[4,2,16,256]{3,2,1,0:T(8,128)(2,1)S(1)}, u32[]{:S(2)}, u32[]{:S(2)}) collective-permute-start(bf16[4,2,16,256]{3,2,1,0:T(8,128)(2,1)S(1)} %get-tuple-element.33), channel_id=1, source_target_pairs={{0,5},{1,4},{2,7},{3,6},{4,1},{5,0},{6,3},{7,2},{8,13},{9,12},{10,... | collective-permute-start | bytes 196616 | tf_op jit(solution)/shard_map/ppermute | solution.py:428
  100.2 11.7 %collective-permute-start.4 = (bf16[4,2,16,256]{3,2,1,0:T(8,128)(2,1)S(1)}, bf16[4,2,16,256]{3,2,1,0:T(8,128)(2,1)S(1)}, u32[]{:S(2)}, u32[]{:S(2)}) collective-permute-start(bf16[4,2,16,256]{3,2,1,0:T(8,128)(2,1)S(1)} %get-tuple-element.34), channel_id=1, source_target_pairs={{0,4},{1,5},{2,6},{3,7},{4,0},{5,1},{6,2},{7,3},{8,12},{9,13},{10,... | collective-permute-start | bytes 196616 | tf_op jit(solution)/shard_map/ppermute | solution.py:428
  103.9 7.9 %collective-permute-start.3 = (bf16[4,2,16,256]{3,2,1,0:T(8,128)(2,1)S(1)}, bf16[4,2,16,256]{3,2,1,0:T(8,128)(2,1)S(1)}, u32[]{:S(2)}, u32[]{:S(2)}) collective-permute-start(bf16[4,2,16,256]{3,2,1,0:T(8,128)(2,1)S(1)} %get-tuple-element.35), channel_id=1, source_target_pairs={{0,3},{1,2},{2,1},{3,0},{4,7},{5,6},{6,5},{7,4},{8,11},{9,10},{10,... | collective-permute-start | bytes 196616 | tf_op jit(solution)/shard_map/ppermute | solution.py:428
  106.4 5.7 %collective-permute-start.2 = (bf16[4,2,16,256]{3,2,1,0:T(8,128)(2,1)S(1)}, bf16[4,2,16,256]{3,2,1,0:T(8,128)(2,1)S(1)}, u32[]{:S(2)}, u32[]{:S(2)}) collective-permute-start(bf16[4,2,16,256]{3,2,1,0:T(8,128)(2,1)S(1)} %get-tuple-element.36), channel_id=1, source_target_pairs={{0,2},{1,3},{2,0},{3,1},{4,6},{5,7},{6,4},{7,5},{8,10},{9,11},{10,... | collective-permute-start | bytes 196616 | tf_op jit(solution)/shard_map/ppermute | solution.py:428
  109.6 3.1 collective-permute-start.1
  115.7 13.4 %collective-permute-start.8 = (f32[2,2,512]{2,1,0:T(2,128)S(1)}, f32[2,2,512]{2,1,0:T(2,128)S(1)}, u32[]{:S(2)}, u32[]{:S(2)}) collective-permute-start(f32[2,2,512]{2,1,0:T(2,128)S(1)} %off_stats.1), channel_id=1, source_target_pairs={{0,8},{1,9},{2,10},{3,11},{4,12},{5,13},{6,14},{7,15},{16,24},{17,... | collective-permute-start | bytes 24584 | tf_op jit(solution)/shard_map/ppermute | solution.py:424
  186.4 21.1 %all-to-all-start.2 = ((f32[32,2,128]{2,1,0:T(2,128)}), f32[32,2,128]{2,1,0:T(2,128)S(1)}, u32[]{:S(2)}, u32[]{:S(2)}) async-start(f32[32,2,128]{2,1,0:T(2,128)} %copy.16), calls=%async_computation.2 | async-start | bytes 65536 | tf_op jit(solution)/shard_map/all_to_all | solution.py:420
  208.1 13.1 %collective-permute-start.9 = (f32[2,2,512]{2,1,0:T(2,128)S(1)}, f32[2,2,512]{2,1,0:T(2,128)S(1)}, u32[]{:S(2)}, u32[]{:S(2)}) collective-permute-start(f32[2,2,512]{2,1,0:T(2,128)S(1)} %fusion.3), channel_id=1, source_target_pairs={{8,0},{9,1},{10,2},{11,3},{12,4},{13,5},{14,6},{15,7},{24,16},{25,... | collective-permute-start | bytes 24584 | tf_op jit(solution)/shard_map/ppermute | solution.py:424
  214.1 1.1 copy-start.1
  221.2 74.9 %all-to-all-start.3 = ((bf16[32,3,16,512]{3,2,1,0:T(8,128)(2,1)}), bf16[32,3,16,512]{3,2,1,0:T(8,128)(2,1)S(1)}, u32[]{:S(2)}, u32[]{:S(2)}) async-start(bf16[32,3,16,512]{3,2,1,0:T(8,128)(2,1)} %copy-done.1), calls=%async_computation.3 | async-start | bytes 3145728 | tf_op jit(solution)/shard_map/all_to_all | solution.py:420
  229.6 26.0 %collective-permute-start.10 = (bf16[2,64,256]{2,1,0:T(8,128)(2,1)S(1)}, bf16[2,64,256]{2,1,0:T(8,128)(2,1)S(1)}, u32[]{:S(2)}, u32[]{:S(2)}) collective-permute-start(bf16[2,64,256]{2,1,0:T(8,128)(2,1)S(1)} %get-tuple-element.29), channel_id=1, source_target_pairs={{0,1},{1,0},{2,3},{3,2},{4,5},{5,4},{6,7},{7,6},{8,9},{9,8},{10,11... | collective-permute-start | bytes 196616 | tf_op jit(solution)/shard_map/ppermute | solution.py:428
  240.0 1.6 copy-start
  241.7 28.5 %collective-permute-start.16 = (bf16[2,64,256]{2,1,0:T(8,128)(2,1)S(1)}, bf16[2,64,256]{2,1,0:T(8,128)(2,1)S(1)}, u32[]{:S(2)}, u32[]{:S(2)}) collective-permute-start(bf16[2,64,256]{2,1,0:T(8,128)(2,1)S(1)} %get-tuple-element.23), channel_id=1, source_target_pairs={{0,7},{1,6},{2,5},{3,4},{4,3},{5,2},{6,1},{7,0},{8,15},{9,14},{10,... | collective-permute-start | bytes 196616 | tf_op jit(solution)/shard_map/ppermute | solution.py:428
  246.0 23.5 %collective-permute-start.15 = (bf16[2,64,256]{2,1,0:T(8,128)(2,1)S(1)}, bf16[2,64,256]{2,1,0:T(8,128)(2,1)S(1)}, u32[]{:S(2)}, u32[]{:S(2)}) collective-permute-start(bf16[2,64,256]{2,1,0:T(8,128)(2,1)S(1)} %get-tuple-element.24), channel_id=1, source_target_pairs={{0,6},{1,7},{2,4},{3,5},{4,2},{5,3},{6,0},{7,1},{8,14},{9,15},{10,... | collective-permute-start | bytes 196616 | tf_op jit(solution)/shard_map/ppermute | solution.py:428
  248.1 20.8 %collective-permute-start.14 = (bf16[2,64,256]{2,1,0:T(8,128)(2,1)S(1)}, bf16[2,64,256]{2,1,0:T(8,128)(2,1)S(1)}, u32[]{:S(2)}, u32[]{:S(2)}) collective-permute-start(bf16[2,64,256]{2,1,0:T(8,128)(2,1)S(1)} %get-tuple-element.25), channel_id=1, source_target_pairs={{0,5},{1,4},{2,7},{3,6},{4,1},{5,0},{6,3},{7,2},{8,13},{9,12},{10,... | collective-permute-start | bytes 196616 | tf_op jit(solution)/shard_map/ppermute | solution.py:428
  252.3 15.9 %collective-permute-start.13 = (bf16[2,64,256]{2,1,0:T(8,128)(2,1)S(1)}, bf16[2,64,256]{2,1,0:T(8,128)(2,1)S(1)}, u32[]{:S(2)}, u32[]{:S(2)}) collective-permute-start(bf16[2,64,256]{2,1,0:T(8,128)(2,1)S(1)} %get-tuple-element.26), channel_id=1, source_target_pairs={{0,4},{1,5},{2,6},{3,7},{4,0},{5,1},{6,2},{7,3},{8,12},{9,13},{10,... | collective-permute-start | bytes 196616 | tf_op jit(solution)/shard_map/ppermute | solution.py:428
  255.5 5.6 %collective-permute-start.11 = (bf16[2,64,256]{2,1,0:T(8,128)(2,1)S(1)}, bf16[2,64,256]{2,1,0:T(8,128)(2,1)S(1)}, u32[]{:S(2)}, u32[]{:S(2)}) collective-permute-start(bf16[2,64,256]{2,1,0:T(8,128)(2,1)S(1)} %get-tuple-element.28), channel_id=1, source_target_pairs={{0,2},{1,3},{2,0},{3,1},{4,6},{5,7},{6,4},{7,5},{8,10},{9,11},{10,... | collective-permute-start | bytes 196616 | tf_op jit(solution)/shard_map/ppermute | solution.py:428
  261.1 6.4 %collective-permute-start.12 = (bf16[2,64,256]{2,1,0:T(8,128)(2,1)S(1)}, bf16[2,64,256]{2,1,0:T(8,128)(2,1)S(1)}, u32[]{:S(2)}, u32[]{:S(2)}) collective-permute-start(bf16[2,64,256]{2,1,0:T(8,128)(2,1)S(1)} %get-tuple-element.27), channel_id=1, source_target_pairs={{0,3},{1,2},{2,1},{3,0},{4,7},{5,6},{6,5},{7,4},{8,11},{9,10},{10,... | collective-permute-start | bytes 196616 | tf_op jit(solution)/shard_map/ppermute | solution.py:428
  300.1 65.0 %all-to-all-start.4 = ((bf16[8,4,3,16,512]{4,3,2,1,0:T(8,128)(2,1)}), bf16[8,4,3,16,512]{4,3,2,1,0:T(8,128)(2,1)S(1)}, u32[]{:S(2)}, u32[]{:S(2)}) async-start(bf16[8,4,3,16,512]{4,3,2,1,0:T(8,128)(2,1)} %bitcast.35), calls=%async_computation.4 | async-start | bytes 3145728 | tf_op jit(solution)/shard_map/all_to_all | solution.py:415
  306.8 58.3 %collective-permute-start.17 = (bf16[8,2,64,256]{3,2,1,0:T(8,128)(2,1)}, bf16[8,2,64,256]{3,2,1,0:T(8,128)(2,1)S(1)}, u32[]{:S(2)}, u32[]{:S(2)}) collective-permute-start(bf16[8,2,64,256]{3,2,1,0:T(8,128)(2,1)} %bitcast_dynamic-update-slice_fusion), channel_id=1, source_target_pairs={{0,8},{1,9},{2,10},{3,11},{4,12},{5,13},{6,14},{7,15},{8,0},{9,1},... | collective-permute-start | bytes 1572872 | tf_op jit(solution)/shard_map/ppermute | solution.py:428

commit v4 on v3

--- a/solution.py
+++ b/solution.py
@@ -10,6 +10,7 @@
 HEAD = 128
 CB = 128
 HALVES = 2
+VMEM_BYTES = 16 * 1024 * 1024
 
 masked_low = -1e30
 f32 = jnp.float32
@@ -31,7 +32,7 @@
 
 def params(n_axes=1):
     return pltpu.CompilerParams(
-        dimension_semantics=("arbitrary",) * n_axes, vmem_limit_bytes=48 * 1024 * 1024
+        dimension_semantics=("arbitrary",) * n_axes, vmem_limit_bytes=VMEM_BYTES
     )
 
 
@@ -41,40 +42,95 @@
     )
 
 
-def pack_body(scal_ref, k_ref, v_ref, q_ref, g_ref, out_ref, far_ref):
-    _, subs, _, cols, _ = out_ref.shape
-    far_feats = far_ref.shape[-1]
-    for a, ref in enumerate((k_ref, v_ref, q_ref, g_ref)):
-        for s in range(subs):
-            out_ref[0, s, a] = ref[s * cols : (s + 1) * cols, :]
-
-    def fill(pair, feats):
-        for a, ref in enumerate(pair):
-            for s in range(subs):
-                far_ref[0, s, a] = ref[s * cols : (s + 1) * cols, feats]
-
-    @pl.when(scal_ref[0] == 0)
-    def _():
-        fill((k_ref, v_ref), slice(far_feats, 2 * far_feats))
-
-    @pl.when(scal_ref[0] != 0)
-    def _():
-        fill((q_ref, g_ref), slice(0, far_feats))
-
-
-def pack(scal, k, v, q, g, groups, subs, cols):
-    tokens, feats = k.shape
-    near_feats = feats // groups
-    shapes = [(subs, 4, cols, near_feats), (subs, 2, cols, near_feats // HALVES)]
+def pack_body(k_ref, v_ref, q_ref, g_ref, far_a_ref, far_b_ref, out_ref, near_sem, far_sem):
+    groups, feats, far_feats = out_ref.shape[0], out_ref.shape[-1], far_a_ref.shape[-1]
+    lower = lax.axis_index("narrow") < groups
+
+    def far_copies(pair, first):
+        for ref, far_ref in zip(pair, (far_a_ref, far_b_ref)):
+            for j in range(groups):
+                src = ref.at[:, :, pl.ds(j * feats + first, far_feats)]
+                yield pltpu.make_async_copy(src, far_ref.at[j], far_sem)
+
+    def near_copies():
+        for j in range(groups):
+            for a, ref in enumerate((k_ref, v_ref, q_ref, g_ref)):
+                src = ref.at[:, :, pl.ds(j * feats, feats)]
+                yield pltpu.make_async_copy(src, out_ref.at[j, :, a], near_sem)
+
+    @pl.when(lower)
+    def _():
+        for copy in far_copies((k_ref, v_ref), far_feats):
+            copy.start()
+
+    @pl.when(jnp.logical_not(lower))
+    def _():
+        for copy in far_copies((q_ref, g_ref), 0):
+            copy.start()
+
+    for copy in near_copies():
+        copy.start()
+    for copy in far_copies((k_ref, v_ref), 0):
+        copy.wait()
+    for copy in near_copies():
+        copy.wait()
+
+
+def pack(k, v, q, g, groups, subs, cols):
+    near_feats = k.shape[1] // groups
+    far = (subs, cols, near_feats // HALVES)
+    shapes = [far, far, (subs, 4, cols, near_feats)]
+    split = [a.reshape(subs, cols, a.shape[1]) for a in (k, v, q, g)]
     return pl.pallas_call(
         pack_body,
-        grid=(groups,),
-        in_specs=[smem()] + [pl.BlockSpec((tokens, near_feats), lambda j: (0, j))] * 4,
-        out_specs=[pl.BlockSpec((1, *shape), lambda j: (j, 0, 0, 0, 0)) for shape in shapes],
+        in_specs=[pl.BlockSpec(memory_space=pltpu.HBM)] * 4,
+        out_specs=[pl.BlockSpec(memory_space=pltpu.VMEM)] * 3,
         out_shape=[jax.ShapeDtypeStruct((groups, *shape), bf16) for shape in shapes],
-        compiler_params=params(),
+        scratch_shapes=[pltpu.SemaphoreType.DMA, pltpu.SemaphoreType.DMA],
+        compiler_params=pltpu.CompilerParams(vmem_limit_bytes=VMEM_BYTES),
         name="pack",
-    )(scal, k, v, q, g)
+    )(*split)
+
+
+LONG = pl.CostEstimate(flops=200_000_000_000, bytes_accessed=400 << 20, transcendentals=0)
+
+
+def hold_body(in_ref, out_ref):
+    out_ref[...] = in_ref[...]
+
+
+def hold(arr):
+    return pl.pallas_call(
+        hold_body,
+        in_specs=[pl.BlockSpec(memory_space=pltpu.VMEM)],
+        out_specs=pl.BlockSpec(memory_space=pltpu.VMEM),
+        out_shape=jax.ShapeDtypeStruct(arr.shape, arr.dtype),
+        compiler_params=pltpu.CompilerParams(vmem_limit_bytes=VMEM_BYTES),
+        cost_estimate=LONG,
+        name="hold",
+    )(arr)
+
+
+def split_body(a_ref, b_ref, *out_refs):
+    groups = len(out_refs)
+    near = lax.rem(lax.axis_index("narrow"), groups)
+    for step, ref in enumerate(out_refs):
+        for i, far_ref in enumerate((a_ref, b_ref)):
+            ref[:, i] = far_ref[near ^ step]
+
+
+def split(far_a, far_b):
+    groups, subs, cols, feats = far_a.shape
+    whole = pl.BlockSpec(memory_space=pltpu.VMEM)
+    return pl.pallas_call(
+        split_body,
+        in_specs=[whole] * 2,
+        out_specs=[whole] * groups,
+        out_shape=[jax.ShapeDtypeStruct((subs, 2, cols, feats), bf16)] * groups,
+        compiler_params=pltpu.CompilerParams(vmem_limit_bytes=VMEM_BYTES),
+        cost_estimate=LONG,
+        name="split",
+    )(far_a, far_b)
 
 
 def unpack_body(scal_ref, in_ref, far_ref, q_ref, k_ref, v_ref):
@@ -313,12 +369,26 @@
     return dq, dk, dv
 
 
-def row_grads_body(scale, scal_ref, t_ref, stat_ref, out_ref):
+def row_grads_body(scale, scal_ref, t_ref, stat_ref, off_ref, out_ref, sum_ref):
     k, v, q, g = (flat(t_ref, i) for i in range(4))
     mask = row_masks(scal_ref, k.shape[0])
     grads = block_grads(k, v, q, g, mask, stat_ref[0, 0:1], stat_ref[0, 1:2], scale)
+    upper = scal_ref[0] != 0
+    has_off = (pl.program_id(0) >= pl.num_programs(0) // HALVES) == upper
     for a, d in enumerate(grads):
-        out_ref[a] = d
+        sum_ref[a] = d
+
+    @pl.when(has_off & upper)
+    def _():
+        sum_ref[0] += off_ref[0]
+
+    @pl.when(has_off & jnp.logical_not(upper))
+    def _():
+        sum_ref[1] += off_ref[0]
+        sum_ref[2] += off_ref[1]
+
+    for a in range(3):
+        out_ref[:, a] = sum_ref[a].astype(bf16).reshape(out_ref.shape[0], out_ref.shape[2], HEAD)
 
 
 def col_grads_body(scale, scal_ref, t_ref, stat_ref, out_ref):
@@ -330,19 +400,26 @@
         out_ref[:, a] = d.astype(bf16).reshape(out_ref.shape[0], out_ref.shape[2], HEAD)
 
 
-def row_grads(scale, scal, t, stats):
+def row_grads(scale, scal, t, stats, off):
     rows, _, cols, feats = t.shape
     n = rows * cols
+    near_heads = off.shape[2] // HEAD
     return pl.pallas_call(
         lambda *refs: row_grads_body(scale, *refs),
         grid=(feats // HEAD,),
-        in_specs=[smem(), head_block(t), pl.BlockSpec((1, 2, n), lambda h: (h, 0, 0))],
-        out_specs=pl.BlockSpec((3, n, HEAD), lambda h: (0, 0, h)),
-        out_shape=jax.ShapeDtypeStruct((3, n, feats), f32),
+        in_specs=[
+            smem(),
+            head_block(t),
+            pl.BlockSpec((1, 2, n), lambda h: (h, 0, 0)),
+            pl.BlockSpec((2, n, HEAD), lambda h: (0, 0, h % near_heads)),
+        ],
+        out_specs=pl.BlockSpec((rows, 3, cols, HEAD), lambda h: (0, 0, 0, h)),
+        out_shape=jax.ShapeDtypeStruct((rows, 3, cols, feats), bf16),
+        scratch_shapes=[pltpu.VMEM((3, n, HEAD), f32)],
         compiler_params=params(),
         cost_estimate=cost(8),
         name="row_grads",
-    )(scal, t, stats)
+    )(scal, t, stats, off)
 
 
 def col_grads(scale, scal, t, stats):
@@ -360,44 +437,23 @@
     )(scal, t, stats)
 
 
-def join_body(scal_ref, row_ref, off_ref, col_ref, out_ref, total_ref):
-    half_feats = off_ref.shape[2]
-    for a in range(3):
-        total_ref[a] = row_ref[a] + col_ref[:, a].astype(f32).reshape(row_ref.shape[1:])
-
-    @pl.when(scal_ref[0] == 0)
-    def _():
-        for a in range(2):
-            total_ref[a + 1, :, :half_feats] += off_ref[a]
-
-    @pl.when(scal_ref[0] != 0)
-    def _():
-        total_ref[0, :, half_feats:] += off_ref[0]
-
-    for a in range(3):
-        out_ref[:, a] = total_ref[a].astype(bf16).reshape(out_ref.shape[0], *out_ref.shape[2:])
-
-
-def join(scal, row, off, col):
-    rows, _, cols, feats = col.shape
+def join_body(row_ref, col_ref, out_ref):
+    out_ref[...] = (row_ref[...].astype(f32) + col_ref[...].astype(f32)).astype(bf16)
+
+
+def join(row, col):
+    rows, arrays, cols, feats = col.shape
     steps = 4
-    part = rows // steps
-    n = part * cols
+    spec = pl.BlockSpec((rows // steps, arrays, cols, feats), lambda i: (i, 0, 0, 0))
     return pl.pallas_call(
         join_body,
         grid=(steps,),
-        in_specs=[
-            smem(),
-            pl.BlockSpec((3, n, feats), lambda i: (0, i, 0)),
-            pl.BlockSpec((2, n, off.shape[2]), lambda i: (0, i, 0)),
-            pl.BlockSpec((part, 3, cols, feats), lambda i: (i, 0, 0, 0)),
-        ],
-        out_specs=pl.BlockSpec((part, 3, cols, feats), lambda i: (i, 0, 0, 0)),
+        in_specs=[spec, spec],
+        out_specs=spec,
         out_shape=jax.ShapeDtypeStruct(col.shape, bf16),
-        scratch_shapes=[pltpu.VMEM((3, n, feats), f32)],
         compiler_params=params(),
         name="join",
-    )(scal, row, off, col)
+    )(row, col)
 
 
 def body(query_in, key_in, value_in, grad_out, row_start, col_start):
@@ -427,12 +483,8 @@
         pairs = [(i, i ^ step) for i in range(narrow)]
         return lax.ppermute(arr, "narrow", pairs)
 
-    def spread(arr):
-        pieces = []
-        for step in range(groups):
-            piece = lax.dynamic_index_in_dim(arr, near_index ^ step, keepdims=False)
-            pieces.append(swap(piece, step) if step else piece)
-        return pieces
+    def spread(pieces):
+        return [swap(piece, step) if step else piece for step, piece in enumerate(pieces)]
 
     wide_index = lax.axis_index("wide")
     narrow_index = lax.axis_index("narrow")
@@ -443,15 +495,16 @@
     first_row = lax.dynamic_index_in_dim(col_start, block_id, keepdims=False)
     scal = jnp.stack([half, first_col, first_row, near_index]).astype(jnp.int32)
 
-    packed, packed_far = pack(scal, key_in, value_in, query_in, grad_out, groups, subs, cols)
+    far_a, far_b, packed = pack(key_in, value_in, query_in, grad_out, groups, subs, cols)
     near_feats = feats // groups
     heads = near_feats // HEAD
     near_heads = heads // HALVES
-    far = swap(packed_far, groups)
+    far_a = hold(swap(far_a, groups))
+    far_b = swap(far_b, groups)
     t = exchange_near(packed).reshape(lanes, 4, cols, near_feats)
-    t, far = lax.optimization_barrier((t, far))
+    t, far_a = lax.optimization_barrier((t, far_a))
     by_col = exchange_wide(t)
-    pieces = spread(far)
+    pieces = spread(split(far_a, far_b))
     diag_part = stats_call(row_stats_body, scale, scal, (t,), "row_stats", 4)
     own_off = off_stats(scale, scal, t, pieces)
     off_part = jnp.concatenate([shift(own_off, 0, 1), own_off])
@@ -468,17 +521,19 @@
     row_full = jnp.stack([row_lse, row_delta], axis=1)
     col_full = jnp.stack([col_lse, col_delta], axis=1)
 
-    far_full = shift(row_full[:near_heads], 1, 0)
-    col_terms = col_grads(scale, scal, by_col, col_full)
-    col_terms, far_full = lax.optimization_barrier((col_terms, far_full))
-    from_col = exchange_wide(col_terms)
-    row_terms = row_grads(scale, scal, t, row_full)
+    far_full = hold(shift(row_full[:near_heads], 1, 0))
+    from_col = exchange_wide(col_grads(scale, scal, by_col, col_full))
     off_full = jnp.where(half == 1, row_full[near_heads:], far_full)
     off_terms, far_terms = off_grads(scale, scal, t, off_full, pieces)
-    far_terms = jnp.stack(spread(far_terms))
-    from_col, far_terms = lax.optimization_barrier((from_col, far_terms))
-    back = swap(far_terms, groups)
-    joined = join(scal, row_terms, off_terms, from_col)
+    row_terms = row_grads(scale, scal, t, row_full, off_terms)
+    by_step = [
+        lax.dynamic_index_in_dim(far_terms, near_index ^ step, keepdims=False)
+        for step in range(groups)
+    ]
+    far_terms = jnp.stack(spread(by_step))
+    from_col, far_terms, row_terms = lax.optimization_barrier((from_col, far_terms, row_terms))
+    back = hold(swap(far_terms, groups))
+    joined = join(row_terms, from_col)
     out = exchange_near(joined.reshape(groups, subs, 3, cols, near_feats))
     return unpack(scal, out, back, tokens, feats)
 

time: 370 us -> 334 us (0.903)
  the two profiles are of different devices: /device:TPU:1 before, /device:TPU:58 now
where the time goes in v4:
time: 334 us; the launch traced here: 332 us
  waiting for transfers between devices  163 us (49%)
  starting transfers between devices  119 us (36%)
  Pallas kernels  38.7 us (12%)
  local copies, waits for them, and re-layouts  8.42 us (3%)
    all_to_all x3, waiting for transfers between devices, exchange_wide(): return lax.all_to_all(arr, 'wide', split_axis=0, concat_axis=0, tiled=True)  98 us
    ppermute x17, starting transfers between devices, swap(): return lax.ppermute(arr, 'narrow', pairs)  72.6 us
    ppermute x17, waiting for transfers between devices, swap(): return lax.ppermute(arr, 'narrow', pairs)  64.2 us
    all_to_all x3, starting transfers between devices, exchange_wide(): return lax.all_to_all(arr, 'wide', split_axis=0, concat_axis=0, tiled=True)  23.5 us
    ppermute x2, starting transfers between devices, shift(): return lax.ppermute(arr, 'narrow', pairs)  13.5 us
    all_to_all x2, starting transfers between devices, exchange_near(): lax.all_to_all(arr, 'narrow', split_axis=0, concat_axis=0, axis_index_gro...  9.4 us
    pallas_call x2, Pallas kernels, stats_call(): pl.pallas_call(lambda *refs: body(scale, *refs), grid=(heads,), in_specs=...  7.87 us
  transfers between devices with their start and end apart: 24, of which 10 were waited for; matrix products, arithmetic and copies ran while one was open for 1% of the time, Pallas kernels for 8%

profile of v4, /device:TPU:58, one launch (start us, length us, event | category | flops | bytes accessed | tf_op | source)
XLA Modules:
  0.0 332.0 jit_solution(5024432982079376171)
XLA Ops:
  6.7 14.8 %collective-permute-start = (bf16[8,4,16,256]{3,2,1,0:T(8,128)(2,1)S(1)}, bf16[8,4,16,256]{3,2,1,0:T(8,128)(2,1)S(1)}, u32[]{:S(2)}, u32[]{:S(2)}) collective-permute-start(bf16[8,4,16,256]{3,2,1,0:T(8,128)(2,1)S(1)} %get-tuple-element.22), channel_id=1, source_target_pairs={{0,8},{1,9},{2,10},{3,11},{4,12},{5,13},{6,14},{7,15},{8,0},{9,1},... | collective-permute-start | bytes 786440 | tf_op jit(solution)/shard_map/ppermute | solution.py:484
  21.6 4.7 %all-to-all-start = ((bf16[8,4,4,16,512]{4,3,2,1,0:T(8,128)(2,1)}), bf16[8,4,4,16,512]{4,3,2,1,0:T(8,128)(2,1)}, u32[]{:S(2)}, u32[]{:S(2)}) async-start(bf16[8,4,4,16,512]{4,3,2,1,0:T(8,128)(2,1)} %get-tuple-element.21), calls=%async_computation | async-start | bytes 4194304 | tf_op jit(solution)/shard_map/all_to_all | solution.py:471
  28.2 28.0 %collective-permute-done.in_ref = bf16[8,4,16,256]{3,2,1,0:T(8,128)(2,1)S(1)} collective-permute-done((bf16[8,4,16,256]{3,2,1,0:T(8,128)(2,1)S(1)}, bf16[8,4,16,256]{3,2,1,0:T(8,128)(2,1)S(1)}, u32[]{:S(2)}, u32[]{:S(2)}) %collective-permute-start) | collective-permute-done | bytes 262176 | tf_op jit(solution)/shard_map/ppermute | solution.py:484
  56.2 10.8 %all-to-all-start.1 = ((bf16[32,4,16,512]{3,2,1,0:T(8,128)(2,1)}), bf16[32,4,16,512]{3,2,1,0:T(8,128)(2,1)}, u32[]{:S(2)}, u32[]{:S(2)}) async-start(bf16[32,4,16,512]{3,2,1,0:T(8,128)(2,1)} %bitcast.6.refs_1_), calls=%async_computation.1 | async-start | bytes 4194304 | tf_op jit(solution)/shard_map/all_to_all | solution.py:476
  70.2 2.6 collective-permute-start.3
  74.1 3.1 collective-permute-start.4
  77.2 3.1 collective-permute-start.5
  80.3 3.9 %collective-permute-start.6 = (bf16[4,2,16,256]{3,2,1,0:T(8,128)(2,1)S(1)}, bf16[4,2,16,256]{3,2,1,0:T(8,128)(2,1)S(1)}, u32[]{:S(2)}, u32[]{:S(2)}) collective-permute-start(bf16[4,2,16,256]{3,2,1,0:T(8,128)(2,1)S(1)} %get-tuple-element.31), channel_id=1, source_target_pairs={{0,5},{1,4},{2,7},{3,6},{4,1},{5,0},{6,3},{7,2},{8,13},{9,12},{10,... | collective-permute-start | bytes 196616 | tf_op jit(solution)/shard_map/ppermute | solution.py:484
  86.4 4.8 %collective-permute-start.8 = (bf16[4,2,16,256]{3,2,1,0:T(8,128)(2,1)S(1)}, bf16[4,2,16,256]{3,2,1,0:T(8,128)(2,1)S(1)}, u32[]{:S(2)}, u32[]{:S(2)}) collective-permute-start(bf16[4,2,16,256]{3,2,1,0:T(8,128)(2,1)S(1)} %get-tuple-element.33), channel_id=1, source_target_pairs={{0,7},{1,6},{2,5},{3,4},{4,3},{5,2},{6,1},{7,0},{8,15},{9,14},{10,... | collective-permute-start | bytes 196616 | tf_op jit(solution)/shard_map/ppermute | solution.py:484
  93.4 3.0 off_stats.1
  96.4 12.2 %collective-permute-start.9 = (f32[2,2,512]{2,1,0:T(2,128)S(1)}, f32[2,2,512]{2,1,0:T(2,128)S(1)}, u32[]{:S(2)}, u32[]{:S(2)}) collective-permute-start(f32[2,2,512]{2,1,0:T(2,128)S(1)} %off_stats.1), channel_id=1, source_target_pairs={{0,8},{1,9},{2,10},{3,11},{4,12},{5,13},{6,14},{7,15},{16,24},{17,... | collective-permute-start | bytes 24584 | tf_op jit(solution)/shard_map/ppermute | solution.py:480
  108.7 3.9 %row_stats.1 = f32[4,2,512]{2,1,0:T(2,128)S(1)} custom-call(s32[4]{0:T(128)S(1)} %pad_add_fusion.refs_0_.scal_ref, bf16[32,4,16,512]{3,2,1,0:T(8,128)(2,1)} %bitcast.6.refs_1_), custom_call_target="tpu_custom_call" | custom-call | flops 1342177280 | bytes 4194304 | tf_op jit(solution)/shard_map/row_stats/pallas_call | solution.py:351
  112.8 50.7 %all-to-all-done.1.refs_1_ = bf16[32,4,16,512]{3,2,1,0:T(8,128)(2,1)} async-done(((bf16[32,4,16,512]{3,2,1,0:T(8,128)(2,1)}), bf16[32,4,16,512]{3,2,1,0:T(8,128)(2,1)}, u32[]{:S(2)}, u32[]{:S(2)}) %all-to-all-start.1) | async-done | bytes 2097184 | tf_op jit(solution)/shard_map/all_to_all | solution.py:476
  163.4 4.0 %col_stats.1 = f32[4,2,512]{2,1,0:T(2,128)S(1)} custom-call(s32[4]{0:T(128)S(1)} %pad_add_fusion.refs_0_.scal_ref, bf16[32,4,16,512]{3,2,1,0:T(8,128)(2,1)} %all-to-all-done.1.refs_1_), custom_call_target="tpu_custom_call" | custom-call | flops 1342177280 | bytes 4194304 | tf_op jit(solution)/shard_map/col_stats/pallas_call | solution.py:351
  168.4 6.2 %all-to-all-start.2 = ((f32[32,2,128]{2,1,0:T(2,128)}), f32[32,2,128]{2,1,0:T(2,128)S(1)}, u32[]{:S(2)}, u32[]{:S(2)}) async-start(f32[32,2,128]{2,1,0:T(2,128)} %copy.16), calls=%async_computation.2 | async-start | bytes 65536 | tf_op jit(solution)/shard_map/all_to_all | solution.py:476
  174.6 10.6 %all-to-all-done.2 = f32[32,2,128]{2,1,0:T(2,128)S(1)} async-done(((f32[32,2,128]{2,1,0:T(2,128)}), f32[32,2,128]{2,1,0:T(2,128)S(1)}, u32[]{:S(2)}, u32[]{:S(2)}) %all-to-all-start.2) | async-done | bytes 32800 | tf_op jit(solution)/shard_map/all_to_all | solution.py:476
  187.0 5.8 %col_grads.1 = bf16[32,3,16,512]{3,2,1,0:T(8,128)(2,1)} custom-call(s32[4]{0:T(128)S(1)} %pad_add_fusion.refs_0_.scal_ref, bf16[32,4,16,512]{3,2,1,0:T(8,128)(2,1)} %all-to-all-done.1.refs_1_, f32[4,2,512]{2,1,0:T(2,128)S(1)} %pad_maximum_fusion.2.refs_2_), custom_call_target="tpu_custom_call" | custom-call | flops 2684354560 | bytes 4194304 | tf_op jit(solution)/shard_map/col_grads/pallas_call | solution.py:428
  192.9 6.5 %all-to-all-start.3 = ((bf16[32,3,16,512]{3,2,1,0:T(8,128)(2,1)}), bf16[32,3,16,512]{3,2,1,0:T(8,128)(2,1)}, u32[]{:S(2)}, u32[]{:S(2)}) async-start(bf16[32,3,16,512]{3,2,1,0:T(8,128)(2,1)} %col_grads.1), calls=%async_computation.3 | async-start | bytes 3145728 | tf_op jit(solution)/shard_map/all_to_all | solution.py:476
  201.1 3.7 %off_grads.1 = (f32[2,512,256]{2,1,0:T(8,128)S(1)}, bf16[8,2,64,256]{3,2,1,0:T(8,128)(2,1)S(1)}) custom-call(s32[4]{0:T(128)S(1)} %copy-done.17, bf16[32,4,16,512]{3,2,1,0:T(8,128)(2,1)} %bitcast.6.refs_1_, f32[2,2,512]{2,1,0:T(2,128)S(1)} %fusion.2.refs_2_, bf16[4,2,16,256]{3,2,1,0:T(8,128)(2,1)S(1)} %copy-done.5, ...), custom_call_target="tpu_custom_call" | custom-call | flops 1677721600 | bytes 4194304 | tf_op jit(solution)/shard_map/off_grads/pallas_call | solution.py:283
  206.8 2.7 collective-permute-start.12
  209.5 3.0 collective-permute-start.13
  212.5 3.2 collective-permute-start.14
  215.6 3.8 %collective-permute-start.15 = (bf16[2,64,256]{2,1,0:T(8,128)(2,1)S(1)}, bf16[2,64,256]{2,1,0:T(8,128)(2,1)S(1)}, u32[]{:S(2)}, u32[]{:S(2)}) collective-permute-start(bf16[2,64,256]{2,1,0:T(8,128)(2,1)S(1)} %get-tuple-element.41), channel_id=1, source_target_pairs={{0,5},{1,4},{2,7},{3,6},{4,1},{5,0},{6,3},{7,2},{8,13},{9,12},{10,... | collective-permute-start | bytes 196616 | tf_op jit(solution)/shard_map/ppermute | solution.py:484
  219.5 5.6 %row_grads.1.row_ref = bf16[32,3,16,512]{3,2,1,0:T(8,128)(2,1)S(1)} custom-call(s32[4]{0:T(128)S(1)} %copy-done.17, bf16[32,4,16,512]{3,2,1,0:T(8,128)(2,1)} %bitcast.6.refs_1_, f32[4,2,512]{2,1,0:T(2,128)S(1)} %pad_maximum_fusion.1.refs_2_, f32[2,512,256]{2,1,0:T(8,128)S(1)} %get-tuple-element.35.refs_3_), custom_call_target="tpu_custom_call" | custom-call | flops 2684354560 | bytes 4194304 | tf_op jit(solution)/shard_map/row_grads/pallas_call | solution.py:407
  225.0 2.2 collective-permute-start.16
  227.3 4.7 %collective-permute-start.17 = (bf16[2,64,256]{2,1,0:T(8,128)(2,1)S(1)}, bf16[2,64,256]{2,1,0:T(8,128)(2,1)S(1)}, u32[]{:S(2)}, u32[]{:S(2)}) collective-permute-start(bf16[2,64,256]{2,1,0:T(8,128)(2,1)S(1)} %get-tuple-element.39), channel_id=1, source_target_pairs={{0,7},{1,6},{2,5},{3,4},{4,3},{5,2},{6,1},{7,0},{8,15},{9,14},{10,... | collective-permute-start | bytes 196616 | tf_op jit(solution)/shard_map/ppermute | solution.py:484
  234.4 36.8 %all-to-all-done.3.col_ref = bf16[32,3,16,512]{3,2,1,0:T(8,128)(2,1)} async-done(((bf16[32,3,16,512]{3,2,1,0:T(8,128)(2,1)}), bf16[32,3,16,512]{3,2,1,0:T(8,128)(2,1)}, u32[]{:S(2)}, u32[]{:S(2)}) %all-to-all-start.3) | async-done | bytes 1572896 | tf_op jit(solution)/shard_map/all_to_all | solution.py:476
  271.2 13.1 %collective-permute-start.18 = (bf16[8,2,64,256]{3,2,1,0:T(8,128)(2,1)S(1)}, bf16[8,2,64,256]{3,2,1,0:T(8,128)(2,1)S(1)}, u32[]{:S(2)}, u32[]{:S(2)}) collective-permute-start(bf16[8,2,64,256]{3,2,1,0:T(8,128)(2,1)S(1)} %bitcast_dynamic-update-slice_fusion), channel_id=1, source_target_pairs={{0,8},{1,9},{2,10},{3,11},{4,12},{5,13},{6,14},{7,15},{8,0},{9,1},... | collective-permute-start | bytes 1572872 | tf_op jit(solution)/shard_map/ppermute | solution.py:484
  284.3 3.7 %join.1 = bf16[32,3,16,512]{3,2,1,0:T(8,128)(2,1)} custom-call(bf16[32,3,16,512]{3,2,1,0:T(8,128)(2,1)S(1)} %row_grads.1.row_ref, bf16[32,3,16,512]{3,2,1,0:T(8,128)(2,1)} %all-to-all-done.3.col_ref), custom_call_target="tpu_custom_call" | custom-call | tf_op jit(solution)/shard_map/join/pallas_call | solution.py:448
  288.0 4.7 %all-to-all-start.4 = ((bf16[8,4,3,16,512]{4,3,2,1,0:T(8,128)(2,1)}), bf16[8,4,3,16,512]{4,3,2,1,0:T(8,128)(2,1)}, u32[]{:S(2)}, u32[]{:S(2)}) async-start(bf16[8,4,3,16,512]{4,3,2,1,0:T(8,128)(2,1)} %bitcast.31), calls=%async_computation.4 | async-start | bytes 3145728 | tf_op jit(solution)/shard_map/all_to_all | solution.py:471
  292.7 32.7 %collective-permute-done.18.in_ref = bf16[8,2,64,256]{3,2,1,0:T(8,128)(2,1)S(1)} collective-permute-done((bf16[8,2,64,256]{3,2,1,0:T(8,128)(2,1)S(1)}, bf16[8,2,64,256]{3,2,1,0:T(8,128)(2,1)S(1)}, u32[]{:S(2)}, u32[]{:S(2)}) %collective-permute-start.18) | collective-permute-done | bytes 524320 | tf_op jit(solution)/shard_map/ppermute | solution.py:484
  326.0 6.0 %unpack.1 = (bf16[64,4096]{1,0:T(8,128)(2,1)}, bf16[64,4096]{1,0:T(8,128)(2,1)}, bf16[64,4096]{1,0:T(8,128)(2,1)}) custom-call(s32[4]{0:T(128)S(1)} %copy-done.18, bf16[8,4,3,16,512]{4,3,2,1,0:T(8,128)(2,1)} %all-to-all-done.4.in_ref, bf16[8,2,64,256]{3,2,1,0:T(8,128)(2,1)S(1)} %hold.5.far_ref), custom_call_target="tpu_custom_call" | custom-call | tf_op jit(solution)/shard_map/unpack/pallas_call | solution.py:161
  (105 shorter events, 26.4 us)
Async XLA Ops:
  6.7 49.4 %collective-permute-start = (bf16[8,4,16,256]{3,2,1,0:T(8,128)(2,1)S(1)}, bf16[8,4,16,256]{3,2,1,0:T(8,128)(2,1)S(1)}, u32[]{:S(2)}, u32[]{:S(2)}) collective-permute-start(bf16[8,4,16,256]{3,2,1,0:T(8,128)(2,1)S(1)} %get-tuple-element.22), channel_id=1, source_target_pairs={{0,8},{1,9},{2,10},{3,11},{4,12},{5,13},{6,14},{7,15},{8,0},{9,1},... | collective-permute-start | bytes 786440 | tf_op jit(solution)/shard_map/ppermute | solution.py:484
  21.6 34.6 %all-to-all-start = ((bf16[8,4,4,16,512]{4,3,2,1,0:T(8,128)(2,1)}), bf16[8,4,4,16,512]{4,3,2,1,0:T(8,128)(2,1)}, u32[]{:S(2)}, u32[]{:S(2)}) async-start(bf16[8,4,4,16,512]{4,3,2,1,0:T(8,128)(2,1)} %get-tuple-element.21), calls=%async_computation | async-start | bytes 4194304 | tf_op jit(solution)/shard_map/all_to_all | solution.py:471
  26.3 41.0 %collective-permute-start.1 = (bf16[8,4,16,256]{3,2,1,0:T(8,128)(2,1)}, bf16[8,4,16,256]{3,2,1,0:T(8,128)(2,1)}, u32[]{:S(2)}, u32[]{:S(2)}) collective-permute-start(bf16[8,4,16,256]{3,2,1,0:T(8,128)(2,1)} %get-tuple-element.25), channel_id=1, source_target_pairs={{0,8},{1,9},{2,10},{3,11},{4,12},{5,13},{6,14},{7,15},{8,0},{9,1},... | collective-permute-start | bytes 786440 | tf_op jit(solution)/shard_map/ppermute | solution.py:484
  56.2 107.2 %all-to-all-start.1 = ((bf16[32,4,16,512]{3,2,1,0:T(8,128)(2,1)}), bf16[32,4,16,512]{3,2,1,0:T(8,128)(2,1)}, u32[]{:S(2)}, u32[]{:S(2)}) async-start(bf16[32,4,16,512]{3,2,1,0:T(8,128)(2,1)} %bitcast.6.refs_1_), calls=%async_computation.1 | async-start | bytes 4194304 | tf_op jit(solution)/shard_map/all_to_all | solution.py:476
  68.3 28.2 %copy-start.4 = (bf16[4,2,16,256]{3,2,1,0:T(8,128)(2,1)}, bf16[4,2,16,256]{3,2,1,0:T(8,128)(2,1)S(1)}, u32[]{:S(2)}) copy-start(bf16[4,2,16,256]{3,2,1,0:T(8,128)(2,1)S(1)} %get-tuple-element.26.refs_2_.refs_3_) | copy-start | bytes 196612
  68.3 15.9 %collective-permute-start.2 = (bf16[4,2,16,256]{3,2,1,0:T(8,128)(2,1)S(1)}, bf16[4,2,16,256]{3,2,1,0:T(8,128)(2,1)S(1)}, u32[]{:S(2)}, u32[]{:S(2)}) collective-permute-start(bf16[4,2,16,256]{3,2,1,0:T(8,128)(2,1)S(1)} %get-tuple-element.27), channel_id=1, source_target_pairs={{0,1},{1,0},{2,3},{3,2},{4,5},{5,4},{6,7},{7,6},{8,9},{9,8},{10,11... | collective-permute-start | bytes 196616 | tf_op jit(solution)/shard_map/ppermute | solution.py:484
  70.2 16.2 %collective-permute-start.3 = (bf16[4,2,16,256]{3,2,1,0:T(8,128)(2,1)S(1)}, bf16[4,2,16,256]{3,2,1,0:T(8,128)(2,1)S(1)}, u32[]{:S(2)}, u32[]{:S(2)}) collective-permute-start(bf16[4,2,16,256]{3,2,1,0:T(8,128)(2,1)S(1)} %get-tuple-element.28), channel_id=1, source_target_pairs={{0,2},{1,3},{2,0},{3,1},{4,6},{5,7},{6,4},{7,5},{8,10},{9,11},{10,... | collective-permute-start | bytes 196616 | tf_op jit(solution)/shard_map/ppermute | solution.py:484
  74.1 18.3 %collective-permute-start.4 = (bf16[4,2,16,256]{3,2,1,0:T(8,128)(2,1)S(1)}, bf16[4,2,16,256]{3,2,1,0:T(8,128)(2,1)S(1)}, u32[]{:S(2)}, u32[]{:S(2)}) collective-permute-start(bf16[4,2,16,256]{3,2,1,0:T(8,128)(2,1)S(1)} %get-tuple-element.29), channel_id=1, source_target_pairs={{0,3},{1,2},{2,1},{3,0},{4,7},{5,6},{6,5},{7,4},{8,11},{9,10},{10,... | collective-permute-start | bytes 196616 | tf_op jit(solution)/shard_map/ppermute | solution.py:484
  77.2 15.2 %collective-permute-start.5 = (bf16[4,2,16,256]{3,2,1,0:T(8,128)(2,1)S(1)}, bf16[4,2,16,256]{3,2,1,0:T(8,128)(2,1)S(1)}, u32[]{:S(2)}, u32[]{:S(2)}) collective-permute-start(bf16[4,2,16,256]{3,2,1,0:T(8,128)(2,1)S(1)} %get-tuple-element.30), channel_id=1, source_target_pairs={{0,4},{1,5},{2,6},{3,7},{4,0},{5,1},{6,2},{7,3},{8,12},{9,13},{10,... | collective-permute-start | bytes 196616 | tf_op jit(solution)/shard_map/ppermute | solution.py:484
  80.3 12.2 %collective-permute-start.6 = (bf16[4,2,16,256]{3,2,1,0:T(8,128)(2,1)S(1)}, bf16[4,2,16,256]{3,2,1,0:T(8,128)(2,1)S(1)}, u32[]{:S(2)}, u32[]{:S(2)}) collective-permute-start(bf16[4,2,16,256]{3,2,1,0:T(8,128)(2,1)S(1)} %get-tuple-element.31), channel_id=1, source_target_pairs={{0,5},{1,4},{2,7},{3,6},{4,1},{5,0},{6,3},{7,2},{8,13},{9,12},{10,... | collective-permute-start | bytes 196616 | tf_op jit(solution)/shard_map/ppermute | solution.py:484
  84.2 8.3 %collective-permute-start.7 = (bf16[4,2,16,256]{3,2,1,0:T(8,128)(2,1)S(1)}, bf16[4,2,16,256]{3,2,1,0:T(8,128)(2,1)S(1)}, u32[]{:S(2)}, u32[]{:S(2)}) collective-permute-start(bf16[4,2,16,256]{3,2,1,0:T(8,128)(2,1)S(1)} %get-tuple-element.32), channel_id=1, source_target_pairs={{0,6},{1,7},{2,4},{3,5},{4,2},{5,3},{6,0},{7,1},{8,14},{9,15},{10,... | collective-permute-start | bytes 196616 | tf_op jit(solution)/shard_map/ppermute | solution.py:484
  86.4 7.1 %collective-permute-start.8 = (bf16[4,2,16,256]{3,2,1,0:T(8,128)(2,1)S(1)}, bf16[4,2,16,256]{3,2,1,0:T(8,128)(2,1)S(1)}, u32[]{:S(2)}, u32[]{:S(2)}) collective-permute-start(bf16[4,2,16,256]{3,2,1,0:T(8,128)(2,1)S(1)} %get-tuple-element.33), channel_id=1, source_target_pairs={{0,7},{1,6},{2,5},{3,4},{4,3},{5,2},{6,1},{7,0},{8,15},{9,14},{10,... | collective-permute-start | bytes 196616 | tf_op jit(solution)/shard_map/ppermute | solution.py:484
  92.5 94.6 %copy-start.16 = (s32[4]{0:T(128)}, s32[4]{0:T(128)S(1)}, u32[]{:S(2)}) copy-start(s32[4]{0:T(128)S(1)} %pad_add_fusion.refs_0_.scal_ref) | copy-start | bytes 52
  92.5 20.1 %copy-start.6 = (bf16[4,2,16,256]{3,2,1,0:T(8,128)(2,1)}, bf16[4,2,16,256]{3,2,1,0:T(8,128)(2,1)S(1)}, u32[]{:S(2)}) copy-start(bf16[4,2,16,256]{3,2,1,0:T(8,128)(2,1)S(1)} %collective-permute-done.4.refs_5_.refs_6_) | copy-start | bytes 196612
  92.5 20.1 %copy-start.8 = (bf16[4,2,16,256]{3,2,1,0:T(8,128)(2,1)}, bf16[4,2,16,256]{3,2,1,0:T(8,128)(2,1)S(1)}, u32[]{:S(2)}) copy-start(bf16[4,2,16,256]{3,2,1,0:T(8,128)(2,1)S(1)} %collective-permute-done.5.refs_6_.refs_7_) | copy-start | bytes 196612
  92.5 20.1 %copy-start.10 = (bf16[4,2,16,256]{3,2,1,0:T(8,128)(2,1)}, bf16[4,2,16,256]{3,2,1,0:T(8,128)(2,1)S(1)}, u32[]{:S(2)}) copy-start(bf16[4,2,16,256]{3,2,1,0:T(8,128)(2,1)S(1)} %collective-permute-done.6.refs_7_.refs_8_) | copy-start | bytes 196612
  92.5 20.1 %copy-start.12 = (bf16[4,2,16,256]{3,2,1,0:T(8,128)(2,1)}, bf16[4,2,16,256]{3,2,1,0:T(8,128)(2,1)S(1)}, u32[]{:S(2)}) copy-start(bf16[4,2,16,256]{3,2,1,0:T(8,128)(2,1)S(1)} %collective-permute-done.7.refs_8_.refs_9_) | copy-start | bytes 196612
  93.4 19.2 %copy-start.14 = (bf16[4,2,16,256]{3,2,1,0:T(8,128)(2,1)}, bf16[4,2,16,256]{3,2,1,0:T(8,128)(2,1)S(1)}, u32[]{:S(2)}) copy-start(bf16[4,2,16,256]{3,2,1,0:T(8,128)(2,1)S(1)} %collective-permute-done.8.refs_9_.refs_10_) | copy-start | bytes 196612
  96.4 16.2 %collective-permute-start.9 = (f32[2,2,512]{2,1,0:T(2,128)S(1)}, f32[2,2,512]{2,1,0:T(2,128)S(1)}, u32[]{:S(2)}, u32[]{:S(2)}) collective-permute-start(f32[2,2,512]{2,1,0:T(2,128)S(1)} %off_stats.1), channel_id=1, source_target_pairs={{0,8},{1,9},{2,10},{3,11},{4,12},{5,13},{6,14},{7,15},{16,24},{17,... | collective-permute-start | bytes 24584 | tf_op jit(solution)/shard_map/ppermute | solution.py:480
  168.4 16.8 %all-to-all-start.2 = ((f32[32,2,128]{2,1,0:T(2,128)}), f32[32,2,128]{2,1,0:T(2,128)S(1)}, u32[]{:S(2)}, u32[]{:S(2)}) async-start(f32[32,2,128]{2,1,0:T(2,128)} %copy.16), calls=%async_computation.2 | async-start | bytes 65536 | tf_op jit(solution)/shard_map/all_to_all | solution.py:476
  185.7 7.2 %copy-start.19 = (f32[4,1,512]{2,1,0:T(1,128)}, f32[4,1,512]{2,1,0:T(1,128)S(1)}, u32[]{:S(2)}) copy-start(f32[4,1,512]{2,1,0:T(1,128)S(1)} %get-tuple-element.47) | copy-start | bytes 24580
  185.7 14.4 %collective-permute-start.10 = (f32[2,2,512]{2,1,0:T(2,128)S(1)}, f32[2,2,512]{2,1,0:T(2,128)S(1)}, u32[]{:S(2)}, u32[]{:S(2)}) collective-permute-start(f32[2,2,512]{2,1,0:T(2,128)S(1)} %fusion.3), channel_id=1, source_target_pairs={{8,0},{9,1},{10,2},{11,3},{12,4},{13,5},{14,6},{15,7},{24,16},{25,... | collective-permute-start | bytes 24584 | tf_op jit(solution)/shard_map/ppermute | solution.py:480
  192.9 78.3 %all-to-all-start.3 = ((bf16[32,3,16,512]{3,2,1,0:T(8,128)(2,1)}), bf16[32,3,16,512]{3,2,1,0:T(8,128)(2,1)}, u32[]{:S(2)}, u32[]{:S(2)}) async-start(bf16[32,3,16,512]{3,2,1,0:T(8,128)(2,1)} %col_grads.1), calls=%async_computation.3 | async-start | bytes 3145728 | tf_op jit(solution)/shard_map/all_to_all | solution.py:476
  204.9 20.2 %collective-permute-start.11 = (bf16[2,64,256]{2,1,0:T(8,128)(2,1)S(1)}, bf16[2,64,256]{2,1,0:T(8,128)(2,1)S(1)}, u32[]{:S(2)}, u32[]{:S(2)}) collective-permute-start(bf16[2,64,256]{2,1,0:T(8,128)(2,1)S(1)} %get-tuple-element.45), channel_id=1, source_target_pairs={{0,1},{1,0},{2,3},{3,2},{4,5},{5,4},{6,7},{7,6},{8,9},{9,8},{10,11... | collective-permute-start | bytes 196616 | tf_op jit(solution)/shard_map/ppermute | solution.py:484
  206.8 20.5 %collective-permute-start.12 = (bf16[2,64,256]{2,1,0:T(8,128)(2,1)S(1)}, bf16[2,64,256]{2,1,0:T(8,128)(2,1)S(1)}, u32[]{:S(2)}, u32[]{:S(2)}) collective-permute-start(bf16[2,64,256]{2,1,0:T(8,128)(2,1)S(1)} %get-tuple-element.44), channel_id=1, source_target_pairs={{0,2},{1,3},{2,0},{3,1},{4,6},{5,7},{6,4},{7,5},{8,10},{9,11},{10,... | collective-permute-start | bytes 196616 | tf_op jit(solution)/shard_map/ppermute | solution.py:484
  209.5 22.5 %collective-permute-start.13 = (bf16[2,64,256]{2,1,0:T(8,128)(2,1)S(1)}, bf16[2,64,256]{2,1,0:T(8,128)(2,1)S(1)}, u32[]{:S(2)}, u32[]{:S(2)}) collective-permute-start(bf16[2,64,256]{2,1,0:T(8,128)(2,1)S(1)} %get-tuple-element.43), channel_id=1, source_target_pairs={{0,3},{1,2},{2,1},{3,0},{4,7},{5,6},{6,5},{7,4},{8,11},{9,10},{10,... | collective-permute-start | bytes 196616 | tf_op jit(solution)/shard_map/ppermute | solution.py:484
  212.5 19.5 %collective-permute-start.14 = (bf16[2,64,256]{2,1,0:T(8,128)(2,1)S(1)}, bf16[2,64,256]{2,1,0:T(8,128)(2,1)S(1)}, u32[]{:S(2)}, u32[]{:S(2)}) collective-permute-start(bf16[2,64,256]{2,1,0:T(8,128)(2,1)S(1)} %get-tuple-element.42), channel_id=1, source_target_pairs={{0,4},{1,5},{2,6},{3,7},{4,0},{5,1},{6,2},{7,3},{8,12},{9,13},{10,... | collective-permute-start | bytes 196616 | tf_op jit(solution)/shard_map/ppermute | solution.py:484
  215.6 16.4 %collective-permute-start.15 = (bf16[2,64,256]{2,1,0:T(8,128)(2,1)S(1)}, bf16[2,64,256]{2,1,0:T(8,128)(2,1)S(1)}, u32[]{:S(2)}, u32[]{:S(2)}) collective-permute-start(bf16[2,64,256]{2,1,0:T(8,128)(2,1)S(1)} %get-tuple-element.41), channel_id=1, source_target_pairs={{0,5},{1,4},{2,7},{3,6},{4,1},{5,0},{6,3},{7,2},{8,13},{9,12},{10,... | collective-permute-start | bytes 196616 | tf_op jit(solution)/shard_map/ppermute | solution.py:484
  225.0 7.6 %collective-permute-start.16 = (bf16[2,64,256]{2,1,0:T(8,128)(2,1)S(1)}, bf16[2,64,256]{2,1,0:T(8,128)(2,1)S(1)}, u32[]{:S(2)}, u32[]{:S(2)}) collective-permute-start(bf16[2,64,256]{2,1,0:T(8,128)(2,1)S(1)} %get-tuple-element.40), channel_id=1, source_target_pairs={{0,6},{1,7},{2,4},{3,5},{4,2},{5,3},{6,0},{7,1},{8,14},{9,15},{10,... | collective-permute-start | bytes 196616 | tf_op jit(solution)/shard_map/ppermute | solution.py:484
  227.3 7.2 %collective-permute-start.17 = (bf16[2,64,256]{2,1,0:T(8,128)(2,1)S(1)}, bf16[2,64,256]{2,1,0:T(8,128)(2,1)S(1)}, u32[]{:S(2)}, u32[]{:S(2)}) collective-permute-start(bf16[2,64,256]{2,1,0:T(8,128)(2,1)S(1)} %get-tuple-element.39), channel_id=1, source_target_pairs={{0,7},{1,6},{2,5},{3,4},{4,3},{5,2},{6,1},{7,0},{8,15},{9,14},{10,... | collective-permute-start | bytes 196616 | tf_op jit(solution)/shard_map/ppermute | solution.py:484
  271.2 54.1 %collective-permute-start.18 = (bf16[8,2,64,256]{3,2,1,0:T(8,128)(2,1)S(1)}, bf16[8,2,64,256]{3,2,1,0:T(8,128)(2,1)S(1)}, u32[]{:S(2)}, u32[]{:S(2)}) collective-permute-start(bf16[8,2,64,256]{3,2,1,0:T(8,128)(2,1)S(1)} %bitcast_dynamic-update-slice_fusion), channel_id=1, source_target_pairs={{0,8},{1,9},{2,10},{3,11},{4,12},{5,13},{6,14},{7,15},{8,0},{9,1},... | collective-permute-start | bytes 1572872 | tf_op jit(solution)/shard_map/ppermute | solution.py:484
  288.0 37.4 %all-to-all-start.4 = ((bf16[8,4,3,16,512]{4,3,2,1,0:T(8,128)(2,1)}), bf16[8,4,3,16,512]{4,3,2,1,0:T(8,128)(2,1)}, u32[]{:S(2)}, u32[]{:S(2)}) async-start(bf16[8,4,3,16,512]{4,3,2,1,0:T(8,128)(2,1)} %bitcast.31), calls=%async_computation.4 | async-start | bytes 3145728 | tf_op jit(solution)/shard_map/all_to_all | solution.py:471
  (17 other events, 31.9 us)

commit v5 on v4

--- a/solution.py
+++ b/solution.py
@@ -11,8 +11,11 @@
 CB = 128
 HALVES = 2
 VMEM_BYTES = 16 * 1024 * 1024
+PACK_BYTES = 60 * 1024 * 1024
 
 masked_low = -1e30
+least_max = -1e29
+score_scale = 1.0 / math.sqrt(HEAD)
 f32 = jnp.float32
 bf16 = jnp.bfloat16
 QI, GI, KI, VI = 2, 3, 0, 1
@@ -87,7 +90,7 @@
         out_specs=[pl.BlockSpec(memory_space=pltpu.VMEM)] * 3,
         out_shape=[jax.ShapeDtypeStruct((groups, *shape), bf16) for shape in shapes],
         scratch_shapes=[pltpu.SemaphoreType.DMA, pltpu.SemaphoreType.DMA],
-        compiler_params=pltpu.CompilerParams(vmem_limit_bytes=VMEM_BYTES),
+        compiler_params=pltpu.CompilerParams(vmem_limit_bytes=PACK_BYTES),
         name="pack",
     )(*split)
 
@@ -96,22 +99,22 @@
 
 
 def hold_body(in_ref, out_ref):
-    out_ref[...] = in_ref[...]
+    out_ref[...] = jnp.zeros_like(out_ref)
 
 
 def hold(arr):
     return pl.pallas_call(
         hold_body,
-        in_specs=[pl.BlockSpec(memory_space=pltpu.VMEM)],
+        in_specs=[pl.BlockSpec(memory_space=pl.ANY)],
         out_specs=pl.BlockSpec(memory_space=pltpu.VMEM),
-        out_shape=jax.ShapeDtypeStruct(arr.shape, arr.dtype),
-        compiler_params=pltpu.CompilerParams(vmem_limit_bytes=VMEM_BYTES),
+        out_shape=jax.ShapeDtypeStruct((8, 128), f32),
+        compiler_params=pltpu.CompilerParams(vmem_limit_bytes=1024 * 1024),
         cost_estimate=LONG,
         name="hold",
     )(arr)
 
 
-def split_body(a_ref, b_ref, *out_refs):
+def split_body(a_ref, b_ref, token_ref, *out_refs):
     groups = len(out_refs)
     near = lax.rem(lax.axis_index("narrow"), groups)
     for step, ref in enumerate(out_refs):
@@ -119,60 +122,64 @@
             ref[:, i] = far_ref[near ^ step]
 
 
-def split(far_a, far_b):
+def split(far_a, far_b, token):
     groups, subs, cols, feats = far_a.shape
     whole = pl.BlockSpec(memory_space=pltpu.VMEM)
     return pl.pallas_call(
         split_body,
-        in_specs=[whole] * 2,
+        in_specs=[whole] * 2 + [pl.BlockSpec(memory_space=pl.ANY)],
         out_specs=[whole] * groups,
         out_shape=[jax.ShapeDtypeStruct((subs, 2, cols, feats), bf16)] * groups,
         compiler_params=pltpu.CompilerParams(vmem_limit_bytes=VMEM_BYTES),
         cost_estimate=LONG,
         name="split",
-    )(far_a, far_b)
-
-
-def unpack_body(scal_ref, in_ref, far_ref, q_ref, k_ref, v_ref):
-    _, subs, _, cols, _ = in_ref.shape
+    )(far_a, far_b, token)
+
+
+def unpack_body(scal_ref, in_ref, far_ref, token_ref, q_ref, k_ref, v_ref):
+    members, subs, _, cols, feats = in_ref.shape
     far_feats = far_ref.shape[-1]
-    for a, ref in enumerate((q_ref, k_ref, v_ref)):
-        for s in range(subs):
-            ref[s * cols : (s + 1) * cols, :] = in_ref[0, s, a]
-
-    def add(ref, terms, feats):
-        ref[:, feats] = (ref[:, feats].astype(f32) + terms.astype(f32)).astype(bf16)
+    for i in range(members):
+        for a, ref in enumerate((q_ref, k_ref, v_ref)):
+            for s in range(subs):
+                ref[s * cols : (s + 1) * cols, i * feats : (i + 1) * feats] = in_ref[i, s, a]
+
+    def add(ref, i, a, first):
+        place = (pl.program_id(0) * members + i) ^ scal_ref[3]
+        feat_cols = slice(i * feats + first, i * feats + first + far_feats)
+        total = ref[:, feat_cols].astype(f32) + far_ref[place, a].astype(f32)
+        ref[:, feat_cols] = total.astype(bf16)
 
     @pl.when(scal_ref[0] == 0)
     def _():
-        upper = slice(far_feats, 2 * far_feats)
-        add(k_ref, far_ref[0, 0], upper)
-        add(v_ref, far_ref[0, 1], upper)
+        for i in range(members):
+            add(k_ref, i, 0, far_feats)
+            add(v_ref, i, 1, far_feats)
 
     @pl.when(scal_ref[0] != 0)
     def _():
-        add(q_ref, far_ref[0, 0], slice(0, far_feats))
-
-
-def unpack(scal, arr, far, tokens, feats):
+        for i in range(members):
+            add(q_ref, i, 0, 0)
+
+
+def unpack(scal, arr, far, token, tokens, feats):
     groups, subs, _, cols, near_feats = arr.shape
+    members = 2
     out = jax.ShapeDtypeStruct((tokens, feats), bf16)
-    far_spec = pl.BlockSpec((1, *far.shape[1:]), lambda j, scal_ref: (j ^ scal_ref[3], 0, 0, 0))
     return pl.pallas_call(
         unpack_body,
-        grid_spec=pltpu.PrefetchScalarGridSpec(
-            num_scalar_prefetch=1,
-            grid=(groups,),
-            in_specs=[
-                pl.BlockSpec((1, subs, 3, cols, near_feats), lambda j, scal_ref: (j, 0, 0, 0, 0)),
-                far_spec,
-            ],
-            out_specs=[pl.BlockSpec((tokens, near_feats), lambda j, scal_ref: (0, j))] * 3,
-        ),
+        grid=(groups // members,),
+        in_specs=[
+            smem(),
+            pl.BlockSpec((members, subs, 3, cols, near_feats), lambda j: (j, 0, 0, 0, 0)),
+            pl.BlockSpec(far.shape, lambda j: (0, 0, 0, 0)),
+            pl.BlockSpec(memory_space=pl.ANY),
+        ],
+        out_specs=[pl.BlockSpec((tokens, members * near_feats), lambda j: (0, j))] * 3,
         out_shape=[out] * 3,
         compiler_params=params(),
         name="unpack",
-    )(scal, arr, far)
+    )(scal, arr, far, token)
 
 
 def flat(ref, index):
@@ -180,7 +187,7 @@
     return block.reshape(block.shape[0] * block.shape[1], block.shape[2])
 
 
-def row_masks(scal_ref, n):
+def row_mask(scal_ref, n):
     first = scal_ref[1] - scal_ref[0] * n
     u = lax.broadcasted_iota(jnp.int32, (n, n), 0)
     t = lax.broadcasted_iota(jnp.int32, (n, n), 1)
@@ -188,8 +195,7 @@
 
 
 def off_mask(scal_ref, n):
-    u = lax.broadcasted_iota(jnp.int32, (n, n), 0)
-    return u >= scal_ref[1]
+    return lax.broadcasted_iota(jnp.int32, (n, n), 0) >= scal_ref[1]
 
 
 def col_mask(scal_ref, n, cols):
@@ -199,28 +205,35 @@
     return same & (u < t) & (u >= scal_ref[2] * cols)
 
 
-def partial_stats(k, v, q, g, mask, scale):
-    s = jnp.where(mask, dot_nt(k, q) * scale, masked_low)
-    m = jnp.max(s, axis=0, keepdims=True)
-    e = jnp.where(mask, jnp.exp(s - m), 0.0)
+def fill_bias(bias_ref, mask):
+    @pl.when(pl.program_id(0) == 0)
+    def _():
+        bias_ref[...] = jnp.where(mask(bias_ref.shape[0]), 0.0, masked_low)
+
+
+def partial_stats(k, v, q, g, bias, scale):
+    s = dot_nt(k, q) * scale + bias
+    m = jnp.maximum(jnp.max(s, axis=0, keepdims=True), least_max)
+    e = jnp.exp2(s - m)
     total = jnp.sum(e, axis=0, keepdims=True)
     weighted = jnp.sum(e * dot_nt(v, g), axis=0, keepdims=True)
     some = total > 0.0
     total = jnp.where(some, total, 1.0)
-    return jnp.where(some, m + jnp.log(total), masked_low), weighted / total
+    return jnp.where(some, m + jnp.log2(total), masked_low), weighted / total
 
 
 def merge(lse_a, delta_a, lse_b, delta_b):
     top = jnp.maximum(lse_a, lse_b)
-    a = jnp.exp(lse_a - top)
-    b = jnp.exp(lse_b - top)
+    a = jnp.exp2(lse_a - top)
+    b = jnp.exp2(lse_b - top)
     total = a + b
-    return top + jnp.log(total), (a * delta_a + b * delta_b) / total
-
-
-def row_stats_body(scale, scal_ref, t_ref, out_ref):
+    return top + jnp.log2(total), (a * delta_a + b * delta_b) / total
+
+
+def row_stats_body(scale, scal_ref, t_ref, out_ref, bias_ref):
+    fill_bias(bias_ref, lambda n: row_mask(scal_ref, n))
     k, v, q, g = (flat(t_ref, i) for i in range(4))
-    lse, delta = partial_stats(k, v, q, g, row_masks(scal_ref, k.shape[0]), scale)
+    lse, delta = partial_stats(k, v, q, g, bias_ref[...], scale)
     out_ref[0, 0:1] = lse
     out_ref[0, 1:2] = delta
 
@@ -233,11 +246,12 @@
 
 
 def off_stats_body(scale, scal_ref, t_ref, *refs):
-    *piece_refs, out_ref, buf = refs
+    *piece_refs, out_ref, buf, bias_ref = refs
+    fill_bias(bias_ref, lambda n: off_mask(scal_ref, n))
     far_a, far_b = gather_far(scal_ref, piece_refs, buf)
 
     def run(k, v, q, g):
-        lse, delta = partial_stats(k, v, q, g, off_mask(scal_ref, k.shape[0]), scale)
+        lse, delta = partial_stats(k, v, q, g, bias_ref[...], scale)
         out_ref[0, 0:1] = lse
         out_ref[0, 1:2] = delta
 
@@ -250,12 +264,19 @@
         run(far_a, far_b, flat(t_ref, QI), flat(t_ref, GI))
 
 
-def col_stats_body(scale, scal_ref, t_ref, out_ref):
+def col_blocks(n):
+    step = n
+    return [slice(i, i + step) for i in range(0, n, step)]
+
+
+def col_stats_body(scale, scal_ref, t_ref, out_ref, bias_ref):
+    fill_bias(bias_ref, lambda n: col_mask(scal_ref, n, t_ref.shape[2]))
     k, v, q, g = (flat(t_ref, i) for i in range(4))
-    n = k.shape[0]
-    lse, delta = partial_stats(k, v, q, g, col_mask(scal_ref, n, t_ref.shape[2]), scale)
-    out_ref[0, 0:1] = lse
-    out_ref[0, 1:2] = delta
+    for part in col_blocks(k.shape[0]):
+        upto = slice(0, part.stop)
+        lse, delta = partial_stats(k[upto], v[upto], q[part], g[part], bias_ref[upto, part], scale)
+        out_ref[0, 0:1, part] = lse
+        out_ref[0, 1:2, part] = delta
 
 
 def smem():
@@ -272,7 +293,7 @@
     return pl.BlockSpec((a, b, c, HEAD), lambda h, scal_ref: (0, 0, 0, h + scal_ref[0] * heads))
 
 
-def off_call(body, scale, scal, t, extra, pieces, out_specs, out_shape, units, name):
+def off_call(body, scale, scal, t, extra, extra_specs, pieces, out_specs, out_shape, units, name):
     heads = pieces[0].shape[3] // HEAD
     tokens = pieces[0].shape[0] * pieces[0].shape[2]
     rows, _, cols, _ = t.shape
@@ -285,9 +306,12 @@
         grid_spec=pltpu.PrefetchScalarGridSpec(
             num_scalar_prefetch=1,
             grid=(heads,),
-            in_specs=[off_block(t, heads)] + [stat_spec] * len(extra) + piece_specs,
+            in_specs=[off_block(t, heads)] + [spec or stat_spec for spec in extra_specs] + piece_specs,
             out_specs=out_specs,
-            scratch_shapes=[pltpu.VMEM((2, len(pieces), tokens, HEAD), bf16)],
+            scratch_shapes=[
+                pltpu.VMEM((2, len(pieces), tokens, HEAD), bf16),
+                pltpu.VMEM((rows * cols, rows * cols), f32),
+            ],
         ),
         out_shape=out_shape,
         compiler_params=params(),
@@ -300,19 +324,20 @@
     heads = pieces[0].shape[3] // HEAD
     n = t.shape[0] * t.shape[2]
     return off_call(
-        off_stats_body, scale, scal, t, (), pieces,
+        off_stats_body, scale, scal, t, (), (), pieces,
         pl.BlockSpec((1, 2, n), lambda h, scal_ref: (h, 0, 0)),
         jax.ShapeDtypeStruct((heads, 2, n), f32), 2, "off_stats",
     )
 
 
-def off_grads_body(scale, scal_ref, t_ref, stat_ref, *refs):
-    *piece_refs, near_ref, far_ref, buf = refs
+def off_grads_body(scale, scal_ref, t_ref, stat_ref, token_ref, *refs):
+    *piece_refs, near_ref, far_ref, buf, bias_ref = refs
+    fill_bias(bias_ref, lambda n: off_mask(scal_ref, n))
     far_a, far_b = gather_far(scal_ref, piece_refs, buf)
     lse, delta = stat_ref[0, 0:1], stat_ref[0, 1:2]
 
     def run(k, v, q, g):
-        return block_grads(k, v, q, g, off_mask(scal_ref, k.shape[0]), lse, delta, scale)
+        return block_grads(k, v, q, g, bias_ref[...], lse, delta, scale)
 
     @pl.when(scal_ref[0] == 0)
     def _():
@@ -329,12 +354,13 @@
             far_ref[:, a] = d.astype(bf16).reshape(far_ref.shape[0], far_ref.shape[2], HEAD)
 
 
-def off_grads(scale, scal, t, stats, pieces):
+def off_grads(scale, scal, t, stats, token, pieces):
     n = t.shape[0] * t.shape[2]
     feats = pieces[0].shape[3]
     far_shape = (len(pieces), 2, n // len(pieces), feats)
     return off_call(
-        off_grads_body, scale, scal, t, (stats,), pieces,
+        off_grads_body, scale, scal, t, (stats, token),
+        (None, pl.BlockSpec(memory_space=pl.ANY)), pieces,
         [
             pl.BlockSpec((2, n, HEAD), lambda h, scal_ref: (0, 0, h)),
             pl.BlockSpec((*far_shape[:3], HEAD), lambda h, scal_ref: (0, 0, 0, h)),
@@ -354,25 +380,26 @@
         in_specs=[smem()] + [head_block(a) for a in arrays],
         out_specs=pl.BlockSpec((1, 2, n), lambda h: (h, 0, 0)),
         out_shape=jax.ShapeDtypeStruct((heads, 2, n), f32),
+        scratch_shapes=[pltpu.VMEM((n, n), f32)],
         compiler_params=params(),
         cost_estimate=cost(units),
         name=name,
     )(scal, *arrays)
 
 
-def block_grads(k, v, q, g, mask, lse, delta, scale):
-    p = jnp.where(mask, jnp.exp(dot_nt(k, q) * scale - lse), 0.0)
+def block_grads(k, v, q, g, bias, lse, delta, scale):
+    p = jnp.exp2(dot_nt(k, q) * scale + (bias - lse))
     ds = (p * (dot_nt(v, g) - delta)).astype(bf16)
     dv = dot_nn(p.astype(bf16), g)
-    dk = dot_nn(ds, q) * scale
-    dq = dot_tn(ds, k) * scale
+    dk = dot_nn(ds, q) * score_scale
+    dq = dot_tn(ds, k) * score_scale
     return dq, dk, dv
 
 
-def row_grads_body(scale, scal_ref, t_ref, stat_ref, off_ref, out_ref, sum_ref):
+def row_grads_body(scale, scal_ref, t_ref, stat_ref, off_ref, out_ref, sum_ref, bias_ref):
+    fill_bias(bias_ref, lambda n: row_mask(scal_ref, n))
     k, v, q, g = (flat(t_ref, i) for i in range(4))
-    mask = row_masks(scal_ref, k.shape[0])
-    grads = block_grads(k, v, q, g, mask, stat_ref[0, 0:1], stat_ref[0, 1:2], scale)
+    grads = block_grads(k, v, q, g, bias_ref[...], stat_ref[0, 0:1], stat_ref[0, 1:2], scale)
     upper = scal_ref[0] != 0
     has_off = (pl.program_id(0) >= pl.num_programs(0) // HALVES) == upper
     for a, d in enumerate(grads):
@@ -391,13 +418,23 @@
         out_ref[:, a] = sum_ref[a].astype(bf16).reshape(out_ref.shape[0], out_ref.shape[2], HEAD)
 
 
-def col_grads_body(scale, scal_ref, t_ref, stat_ref, out_ref):
+def col_grads_body(scale, scal_ref, t_ref, own_ref, got_ref, out_ref, sum_ref, bias_ref):
+    fill_bias(bias_ref, lambda n: col_mask(scal_ref, n, t_ref.shape[2]))
     k, v, q, g = (flat(t_ref, i) for i in range(4))
-    n = k.shape[0]
-    lse, delta = stat_ref[0, 0:1], stat_ref[0, 1:2]
-    grads = block_grads(k, v, q, g, col_mask(scal_ref, n, t_ref.shape[2]), lse, delta, scale)
-    for a, d in enumerate(grads):
-        out_ref[:, a] = d.astype(bf16).reshape(out_ref.shape[0], out_ref.shape[2], HEAD)
+    lse, delta = merge(own_ref[0, 0:1], own_ref[0, 1:2], got_ref[0, 0:1], got_ref[0, 1:2])
+    blocks = col_blocks(k.shape[0])
+    for i, part in enumerate(blocks):
+        upto = slice(0, part.stop)
+        dq, dk, dv = block_grads(
+            k[upto], v[upto], q[part], g[part], bias_ref[upto, part], lse[:, part], delta[:, part], scale
+        )
+        sum_ref[0, part] = dq
+        for a, d in ((1, dk), (2, dv)):
+            if i:
+                sum_ref[a, : part.start] += d[: part.start]
+            sum_ref[a, part] = d[part.start :]
+    for a in range(3):
+        out_ref[:, a] = sum_ref[a].astype(bf16).reshape(out_ref.shape[0], out_ref.shape[2], HEAD)
 
 
 def row_grads(scale, scal, t, stats, off):
@@ -415,26 +452,28 @@
         ],
         out_specs=pl.BlockSpec((rows, 3, cols, HEAD), lambda h: (0, 0, 0, h)),
         out_shape=jax.ShapeDtypeStruct((rows, 3, cols, feats), bf16),
-        scratch_shapes=[pltpu.VMEM((3, n, HEAD), f32)],
+        scratch_shapes=[pltpu.VMEM((3, n, HEAD), f32), pltpu.VMEM((n, n), f32)],
         compiler_params=params(),
         cost_estimate=cost(8),
         name="row_grads",
     )(scal, t, stats, off)
 
 
-def col_grads(scale, scal, t, stats):
+def col_grads(scale, scal, t, own, got):
     rows, _, cols, feats = t.shape
     n = rows * cols
+    stat_spec = pl.BlockSpec((1, 2, n), lambda h: (h, 0, 0))
     return pl.pallas_call(
         lambda *refs: col_grads_body(scale, *refs),
         grid=(feats // HEAD,),
-        in_specs=[smem(), head_block(t), pl.BlockSpec((1, 2, n), lambda h: (h, 0, 0))],
+        in_specs=[smem(), head_block(t), stat_spec, stat_spec],
         out_specs=pl.BlockSpec((rows, 3, cols, HEAD), lambda h: (0, 0, 0, h)),
         out_shape=jax.ShapeDtypeStruct((rows, 3, cols, feats), bf16),
+        scratch_shapes=[pltpu.VMEM((3, n, HEAD), f32), pltpu.VMEM((n, n), f32)],
         compiler_params=params(),
         cost_estimate=cost(8),
         name="col_grads",
-    )(scal, t, stats)
+    )(scal, t, own, got)
 
 
 def join_body(row_ref, col_ref, out_ref):
@@ -457,7 +496,7 @@
 
 
 def body(query_in, key_in, value_in, grad_out, row_start, col_start):
-    scale = 1.0 / math.sqrt(HEAD)
+    scale = score_scale * math.log2(math.e)
     tokens, feats = query_in.shape
     lanes = lax.axis_size("wide")
     narrow = lax.axis_size("narrow")
@@ -499,12 +538,13 @@
     near_feats = feats // groups
     heads = near_feats // HEAD
     near_heads = heads // HALVES
-    far_a = hold(swap(far_a, groups))
+    far_a = swap(far_a, groups)
+    token = hold(far_a)
     far_b = swap(far_b, groups)
     t = exchange_near(packed).reshape(lanes, 4, cols, near_feats)
-    t, far_a = lax.optimization_barrier((t, far_a))
+    t, token = lax.optimization_barrier((t, token))
     by_col = exchange_wide(t)
-    pieces = spread(split(far_a, far_b))
+    pieces = spread(split(far_a, far_b, token))
     diag_part = stats_call(row_stats_body, scale, scal, (t,), "row_stats", 4)
     own_off = off_stats(scale, scal, t, pieces)
     off_part = jnp.concatenate([shift(own_off, 0, 1), own_off])
@@ -517,14 +557,13 @@
     got = exchange_wide(sent).reshape(lanes, 4 * heads, cols).transpose(1, 0, 2)
     got = got.reshape(2, heads, 2, lanes * cols)
     row_lse, row_delta = merge(row_part[:, 0], row_part[:, 1], got[1, :, 0], got[1, :, 1])
-    col_lse, col_delta = merge(col_part[:, 0], col_part[:, 1], got[0, :, 0], got[0, :, 1])
     row_full = jnp.stack([row_lse, row_delta], axis=1)
-    col_full = jnp.stack([col_lse, col_delta], axis=1)
-
-    far_full = hold(shift(row_full[:near_heads], 1, 0))
-    from_col = exchange_wide(col_grads(scale, scal, by_col, col_full))
+
+    far_full = shift(row_full[:near_heads], 1, 0)
+    token = hold(far_full)
+    from_col = exchange_wide(col_grads(scale, scal, by_col, col_part, got[0]))
     off_full = jnp.where(half == 1, row_full[near_heads:], far_full)
-    off_terms, far_terms = off_grads(scale, scal, t, off_full, pieces)
+    off_terms, far_terms = off_grads(scale, scal, t, off_full, token, pieces)
     row_terms = row_grads(scale, scal, t, row_full, off_terms)
     by_step = [
         lax.dynamic_index_in_dim(far_terms, near_index ^ step, keepdims=False)
@@ -532,10 +571,11 @@
     ]
     far_terms = jnp.stack(spread(by_step))
     from_col, far_terms, row_terms = lax.optimization_barrier((from_col, far_terms, row_terms))
-    back = hold(swap(far_terms, groups))
+    back = swap(far_terms, groups)
+    token = hold(back)
     joined = join(row_terms, from_col)
     out = exchange_near(joined.reshape(groups, subs, 3, cols, near_feats))
-    return unpack(scal, out, back, tokens, feats)
+    return unpack(scal, out, back, token, tokens, feats)
 
 
 def solution(mesh):

time: 334 us -> 329 us (0.985)
    unnamed x56 -> x48, local copies, waits for them, and re-layouts: 5.77 us -> 2.36 us
where the time goes in v5:
time: 329 us; the launch traced here: 327 us
  waiting for transfers between devices  164 us (50%)
  starting transfers between devices  118 us (36%)
  Pallas kernels  37.1 us (11%)
  local copies, waits for them, and re-layouts  5.21 us (2%)
    all_to_all x3, waiting for transfers between devices, exchange_wide(): return lax.all_to_all(arr, 'wide', split_axis=0, concat_axis=0, tiled=True)  97.5 us
    ppermute x17, starting transfers between devices, swap(): return lax.ppermute(arr, 'narrow', pairs)  72.7 us
    ppermute x17, waiting for transfers between devices, swap(): return lax.ppermute(arr, 'narrow', pairs)  65.9 us
    all_to_all x3, starting transfers between devices, exchange_wide(): return lax.all_to_all(arr, 'wide', split_axis=0, concat_axis=0, tiled=True)  22.3 us
    ppermute x2, starting transfers between devices, shift(): return lax.ppermute(arr, 'narrow', pairs)  13.4 us
    all_to_all x2, starting transfers between devices, exchange_near(): lax.all_to_all(arr, 'narrow', split_axis=0, concat_axis=0, axis_index_gro...  9.38 us
    pallas_call x2, Pallas kernels, stats_call(): pl.pallas_call(lambda *refs: body(scale, *refs), grid=(heads,), in_specs=...  7.63 us
  transfers between devices with their start and end apart: 24, of which 10 were waited for; matrix products, arithmetic and copies ran while one was open for 1% of the time, Pallas kernels for 8%

profile of v5, /device:TPU:58, one launch (start us, length us, event | category | flops | bytes accessed | tf_op | source)
XLA Modules:
  0.0 327.1 jit_solution(12266243581842604725)
XLA Ops:
  0.6 3.3 %pack.1 = (bf16[8,4,16,256]{3,2,1,0:T(8,128)(2,1)}, bf16[8,4,16,256]{3,2,1,0:T(8,128)(2,1)}, bf16[8,4,4,16,512]{4,3,2,1,0:T(8,128)(2,1)}) custom-call(bf16[4,16,4096]{2,1,0:T(8,128)(2,1)} %bitcast.71, bf16[4,16,4096]{2,1,0:T(8,128)(2,1)} %bitcast.72, bf16[4,16,4096]{2,1,0:T(8,128)(2,1)} %bitcast.73, bf16[4,16,4096]{2,1,0:T(8,128)(2,1)} %bitcast.74), custom_call_target="tpu_custom_call" | custom-call | tf_op jit(solution)/shard_map/pack/pallas_call | solution.py:87
  4.0 14.8 %collective-permute-start = (bf16[8,4,16,256]{3,2,1,0:T(8,128)(2,1)}, bf16[8,4,16,256]{3,2,1,0:T(8,128)(2,1)S(1)}, u32[]{:S(2)}, u32[]{:S(2)}) collective-permute-start(bf16[8,4,16,256]{3,2,1,0:T(8,128)(2,1)} %get-tuple-element.22), channel_id=1, source_target_pairs={{0,8},{1,9},{2,10},{3,11},{4,12},{5,13},{6,14},{7,15},{8,0},{9,1},... | collective-permute-start | bytes 786440 | tf_op jit(solution)/shard_map/ppermute | solution.py:523
  18.8 4.7 %all-to-all-start = ((bf16[8,4,4,16,512]{4,3,2,1,0:T(8,128)(2,1)}), bf16[8,4,4,16,512]{4,3,2,1,0:T(8,128)(2,1)}, u32[]{:S(2)}, u32[]{:S(2)}) async-start(bf16[8,4,4,16,512]{4,3,2,1,0:T(8,128)(2,1)} %get-tuple-element.21), calls=%async_computation | async-start | bytes 4194304 | tf_op jit(solution)/shard_map/all_to_all | solution.py:510
  25.4 29.3 %collective-permute-done.in_ref.a_ref = bf16[8,4,16,256]{3,2,1,0:T(8,128)(2,1)S(1)} collective-permute-done((bf16[8,4,16,256]{3,2,1,0:T(8,128)(2,1)}, bf16[8,4,16,256]{3,2,1,0:T(8,128)(2,1)S(1)}, u32[]{:S(2)}, u32[]{:S(2)}) %collective-permute-start) | collective-permute-done | bytes 262176 | tf_op jit(solution)/shard_map/ppermute | solution.py:523
  54.7 9.6 %all-to-all-start.1 = ((bf16[32,4,16,512]{3,2,1,0:T(8,128)(2,1)}), bf16[32,4,16,512]{3,2,1,0:T(8,128)(2,1)}, u32[]{:S(2)}, u32[]{:S(2)}) async-start(bf16[32,4,16,512]{3,2,1,0:T(8,128)(2,1)} %bitcast.6.refs_1_), calls=%async_computation.1 | async-start | bytes 4194304 | tf_op jit(solution)/shard_map/all_to_all | solution.py:515
  67.9 2.6 collective-permute-start.3
  71.8 3.1 collective-permute-start.4
  74.9 2.9 collective-permute-start.5
  77.8 4.1 %collective-permute-start.6 = (bf16[4,2,16,256]{3,2,1,0:T(8,128)(2,1)S(1)}, bf16[4,2,16,256]{3,2,1,0:T(8,128)(2,1)S(1)}, u32[]{:S(2)}, u32[]{:S(2)}) collective-permute-start(bf16[4,2,16,256]{3,2,1,0:T(8,128)(2,1)S(1)} %get-tuple-element.31), channel_id=1, source_target_pairs={{0,5},{1,4},{2,7},{3,6},{4,1},{5,0},{6,3},{7,2},{8,13},{9,12},{10,... | collective-permute-start | bytes 196616 | tf_op jit(solution)/shard_map/ppermute | solution.py:523
  84.0 4.8 %collective-permute-start.8 = (bf16[4,2,16,256]{3,2,1,0:T(8,128)(2,1)S(1)}, bf16[4,2,16,256]{3,2,1,0:T(8,128)(2,1)S(1)}, u32[]{:S(2)}, u32[]{:S(2)}) collective-permute-start(bf16[4,2,16,256]{3,2,1,0:T(8,128)(2,1)S(1)} %get-tuple-element.33), channel_id=1, source_target_pairs={{0,7},{1,6},{2,5},{3,4},{4,3},{5,2},{6,1},{7,0},{8,15},{9,14},{10,... | collective-permute-start | bytes 196616 | tf_op jit(solution)/shard_map/ppermute | solution.py:523
  91.1 2.9 off_stats.1
  94.0 12.1 %collective-permute-start.9 = (f32[2,2,512]{2,1,0:T(2,128)S(1)}, f32[2,2,512]{2,1,0:T(2,128)S(1)}, u32[]{:S(2)}, u32[]{:S(2)}) collective-permute-start(f32[2,2,512]{2,1,0:T(2,128)S(1)} %off_stats.1), channel_id=1, source_target_pairs={{0,8},{1,9},{2,10},{3,11},{4,12},{5,13},{6,14},{7,15},{16,24},{17,... | collective-permute-start | bytes 24584 | tf_op jit(solution)/shard_map/ppermute | solution.py:519
  106.1 3.8 %row_stats.1 = f32[4,2,512]{2,1,0:T(2,128)S(1)} custom-call(s32[4]{0:T(128)S(1)} %pad_add_fusion.refs_0_.scal_ref, bf16[32,4,16,512]{3,2,1,0:T(8,128)(2,1)} %bitcast.6.refs_1_), custom_call_target="tpu_custom_call" | custom-call | flops 1342177280 | bytes 4194304 | tf_op jit(solution)/shard_map/row_stats/pallas_call | solution.py:377
  110.1 50.7 %all-to-all-done.1.refs_1_ = bf16[32,4,16,512]{3,2,1,0:T(8,128)(2,1)} async-done(((bf16[32,4,16,512]{3,2,1,0:T(8,128)(2,1)}), bf16[32,4,16,512]{3,2,1,0:T(8,128)(2,1)}, u32[]{:S(2)}, u32[]{:S(2)}) %all-to-all-start.1) | async-done | bytes 2097184 | tf_op jit(solution)/shard_map/all_to_all | solution.py:515
  160.8 3.8 %col_stats.1.refs_2_ = f32[4,2,512]{2,1,0:T(2,128)S(1)} custom-call(s32[4]{0:T(128)S(1)} %pad_add_fusion.refs_0_.scal_ref, bf16[32,4,16,512]{3,2,1,0:T(8,128)(2,1)} %all-to-all-done.1.refs_1_), custom_call_target="tpu_custom_call" | custom-call | flops 1342177280 | bytes 4194304 | tf_op jit(solution)/shard_map/col_stats/pallas_call | solution.py:377
  165.6 6.2 %all-to-all-start.2 = ((f32[32,2,128]{2,1,0:T(2,128)}), f32[32,2,128]{2,1,0:T(2,128)S(1)}, u32[]{:S(2)}, u32[]{:S(2)}) async-start(f32[32,2,128]{2,1,0:T(2,128)} %copy.18), calls=%async_computation.2 | async-start | bytes 65536 | tf_op jit(solution)/shard_map/all_to_all | solution.py:515
  171.8 10.6 %all-to-all-done.2 = f32[32,2,128]{2,1,0:T(2,128)S(1)} async-done(((f32[32,2,128]{2,1,0:T(2,128)}), f32[32,2,128]{2,1,0:T(2,128)S(1)}, u32[]{:S(2)}, u32[]{:S(2)}) %all-to-all-start.2) | async-done | bytes 32800 | tf_op jit(solution)/shard_map/all_to_all | solution.py:515
  184.4 5.9 %col_grads.1 = bf16[32,3,16,512]{3,2,1,0:T(8,128)(2,1)} custom-call(s32[4]{0:T(128)S(1)} %pad_add_fusion.refs_0_.scal_ref, bf16[32,4,16,512]{3,2,1,0:T(8,128)(2,1)} %all-to-all-done.1.refs_1_, f32[4,2,512]{2,1,0:T(2,128)S(1)} %col_stats.1.refs_2_, f32[4,2,512]{2,1,0:T(2,128)S(1)} %squeeze.42.refs_3_), custom_call_target="tpu_custom_call" | custom-call | flops 2684354560 | bytes 4194304 | tf_op jit(solution)/shard_map/col_grads/pallas_call | solution.py:466
  190.3 6.5 %all-to-all-start.3 = ((bf16[32,3,16,512]{3,2,1,0:T(8,128)(2,1)}), bf16[32,3,16,512]{3,2,1,0:T(8,128)(2,1)}, u32[]{:S(2)}, u32[]{:S(2)}) async-start(bf16[32,3,16,512]{3,2,1,0:T(8,128)(2,1)} %col_grads.1), calls=%async_computation.3 | async-start | bytes 3145728 | tf_op jit(solution)/shard_map/all_to_all | solution.py:515
  198.5 3.7 %off_grads.1 = (f32[2,512,256]{2,1,0:T(8,128)S(1)}, bf16[8,2,64,256]{3,2,1,0:T(8,128)(2,1)S(1)}) custom-call(s32[4]{0:T(128)S(1)} %pad_add_fusion.refs_0_.scal_ref, bf16[32,4,16,512]{3,2,1,0:T(8,128)(2,1)} %bitcast.6.refs_1_, f32[2,2,512]{2,1,0:T(2,128)S(1)} %fusion.2.refs_2_, f32[8,128]{1,0:T(8,128)S(1)} %hold.4.refs_3_, ...), custom_call_target="tpu_custom_call" | custom-call | flops 1677721600 | bytes 4194304 | tf_op jit(solution)/shard_map/off_grads/pallas_call | solution.py:304
  204.2 2.7 collective-permute-start.12
  206.9 3.0 collective-permute-start.13
  209.9 3.2 collective-permute-start.14
  213.1 3.8 %collective-permute-start.15 = (bf16[2,64,256]{2,1,0:T(8,128)(2,1)S(1)}, bf16[2,64,256]{2,1,0:T(8,128)(2,1)S(1)}, u32[]{:S(2)}, u32[]{:S(2)}) collective-permute-start(bf16[2,64,256]{2,1,0:T(8,128)(2,1)S(1)} %get-tuple-element.41), channel_id=1, source_target_pairs={{0,5},{1,4},{2,7},{3,6},{4,1},{5,0},{6,3},{7,2},{8,13},{9,12},{10,... | collective-permute-start | bytes 196616 | tf_op jit(solution)/shard_map/ppermute | solution.py:523
  217.5 5.3 %row_grads.1.row_ref = bf16[32,3,16,512]{3,2,1,0:T(8,128)(2,1)S(1)} custom-call(s32[4]{0:T(128)S(1)} %copy-done.13, bf16[32,4,16,512]{3,2,1,0:T(8,128)(2,1)} %bitcast.6.refs_1_, f32[4,2,512]{2,1,0:T(2,128)S(1)} %pad_maximum_fusion.1.refs_2_, f32[2,512,256]{2,1,0:T(8,128)S(1)} %get-tuple-element.35.refs_3_), custom_call_target="tpu_custom_call" | custom-call | flops 2684354560 | bytes 4194304 | tf_op jit(solution)/shard_map/row_grads/pallas_call | solution.py:444
  225.1 4.7 %collective-permute-start.17 = (bf16[2,64,256]{2,1,0:T(8,128)(2,1)S(1)}, bf16[2,64,256]{2,1,0:T(8,128)(2,1)S(1)}, u32[]{:S(2)}, u32[]{:S(2)}) collective-permute-start(bf16[2,64,256]{2,1,0:T(8,128)(2,1)S(1)} %get-tuple-element.39), channel_id=1, source_target_pairs={{0,7},{1,6},{2,5},{3,4},{4,3},{5,2},{6,1},{7,0},{8,15},{9,14},{10,... | collective-permute-start | bytes 196616 | tf_op jit(solution)/shard_map/ppermute | solution.py:523
  232.3 36.3 %all-to-all-done.3.col_ref = bf16[32,3,16,512]{3,2,1,0:T(8,128)(2,1)} async-done(((bf16[32,3,16,512]{3,2,1,0:T(8,128)(2,1)}), bf16[32,3,16,512]{3,2,1,0:T(8,128)(2,1)}, u32[]{:S(2)}, u32[]{:S(2)}) %all-to-all-start.3) | async-done | bytes 1572896 | tf_op jit(solution)/shard_map/all_to_all | solution.py:515
  268.6 13.1 %collective-permute-start.18 = (bf16[8,2,64,256]{3,2,1,0:T(8,128)(2,1)S(1)}, bf16[8,2,64,256]{3,2,1,0:T(8,128)(2,1)S(1)}, u32[]{:S(2)}, u32[]{:S(2)}) collective-permute-start(bf16[8,2,64,256]{3,2,1,0:T(8,128)(2,1)S(1)} %bitcast_dynamic-update-slice_fusion), channel_id=1, source_target_pairs={{0,8},{1,9},{2,10},{3,11},{4,12},{5,13},{6,14},{7,15},{8,0},{9,1},... | collective-permute-start | bytes 1572872 | tf_op jit(solution)/shard_map/ppermute | solution.py:523
  281.7 3.7 %join.1 = bf16[32,3,16,512]{3,2,1,0:T(8,128)(2,1)} custom-call(bf16[32,3,16,512]{3,2,1,0:T(8,128)(2,1)S(1)} %row_grads.1.row_ref, bf16[32,3,16,512]{3,2,1,0:T(8,128)(2,1)} %all-to-all-done.3.col_ref), custom_call_target="tpu_custom_call" | custom-call | tf_op jit(solution)/shard_map/join/pallas_call | solution.py:487
  285.4 4.7 %all-to-all-start.4 = ((bf16[8,4,3,16,512]{4,3,2,1,0:T(8,128)(2,1)}), bf16[8,4,3,16,512]{4,3,2,1,0:T(8,128)(2,1)}, u32[]{:S(2)}, u32[]{:S(2)}) async-start(bf16[8,4,3,16,512]{4,3,2,1,0:T(8,128)(2,1)} %bitcast.30), calls=%async_computation.4 | async-start | bytes 3145728 | tf_op jit(solution)/shard_map/all_to_all | solution.py:510
  290.1 32.7 %collective-permute-done.18.in_ref.far_ref = bf16[8,2,64,256]{3,2,1,0:T(8,128)(2,1)S(1)} collective-permute-done((bf16[8,2,64,256]{3,2,1,0:T(8,128)(2,1)S(1)}, bf16[8,2,64,256]{3,2,1,0:T(8,128)(2,1)S(1)}, u32[]{:S(2)}, u32[]{:S(2)}) %collective-permute-start.18) | collective-permute-done | bytes 524320 | tf_op jit(solution)/shard_map/ppermute | solution.py:523
  323.4 3.7 %unpack.1 = (bf16[64,4096]{1,0:T(8,128)(2,1)}, bf16[64,4096]{1,0:T(8,128)(2,1)}, bf16[64,4096]{1,0:T(8,128)(2,1)}) custom-call(s32[4]{0:T(128)S(1)} %copy-done.14, bf16[8,4,3,16,512]{4,3,2,1,0:T(8,128)(2,1)} %all-to-all-done.4.in_ref, bf16[8,2,64,256]{3,2,1,0:T(8,128)(2,1)S(1)} %collective-permute-done.18.in_ref.far_ref, f32[8,128]{1,0:T(8,128)S(1)} %hold.5.token_ref), custom_call_target="tpu_custom_call" | custom-call | tf_op jit(solution)/shard_map/unpack/pallas_call | solution.py:169
  (99 shorter events, 23.8 us)
Async XLA Ops:
  4.0 50.8 %collective-permute-start = (bf16[8,4,16,256]{3,2,1,0:T(8,128)(2,1)}, bf16[8,4,16,256]{3,2,1,0:T(8,128)(2,1)S(1)}, u32[]{:S(2)}, u32[]{:S(2)}) collective-permute-start(bf16[8,4,16,256]{3,2,1,0:T(8,128)(2,1)} %get-tuple-element.22), channel_id=1, source_target_pairs={{0,8},{1,9},{2,10},{3,11},{4,12},{5,13},{6,14},{7,15},{8,0},{9,1},... | collective-permute-start | bytes 786440 | tf_op jit(solution)/shard_map/ppermute | solution.py:523
  18.8 35.9 %all-to-all-start = ((bf16[8,4,4,16,512]{4,3,2,1,0:T(8,128)(2,1)}), bf16[8,4,4,16,512]{4,3,2,1,0:T(8,128)(2,1)}, u32[]{:S(2)}, u32[]{:S(2)}) async-start(bf16[8,4,4,16,512]{4,3,2,1,0:T(8,128)(2,1)} %get-tuple-element.21), calls=%async_computation | async-start | bytes 4194304 | tf_op jit(solution)/shard_map/all_to_all | solution.py:510
  23.5 41.4 %collective-permute-start.1 = (bf16[8,4,16,256]{3,2,1,0:T(8,128)(2,1)}, bf16[8,4,16,256]{3,2,1,0:T(8,128)(2,1)}, u32[]{:S(2)}, u32[]{:S(2)}) collective-permute-start(bf16[8,4,16,256]{3,2,1,0:T(8,128)(2,1)} %get-tuple-element.24), channel_id=1, source_target_pairs={{0,8},{1,9},{2,10},{3,11},{4,12},{5,13},{6,14},{7,15},{8,0},{9,1},... | collective-permute-start | bytes 786440 | tf_op jit(solution)/shard_map/ppermute | solution.py:523
  54.7 106.0 %all-to-all-start.1 = ((bf16[32,4,16,512]{3,2,1,0:T(8,128)(2,1)}), bf16[32,4,16,512]{3,2,1,0:T(8,128)(2,1)}, u32[]{:S(2)}, u32[]{:S(2)}) async-start(bf16[32,4,16,512]{3,2,1,0:T(8,128)(2,1)} %bitcast.6.refs_1_), calls=%async_computation.1 | async-start | bytes 4194304 | tf_op jit(solution)/shard_map/all_to_all | solution.py:515
  65.9 28.1 %copy-start = (bf16[4,2,16,256]{3,2,1,0:T(8,128)(2,1)}, bf16[4,2,16,256]{3,2,1,0:T(8,128)(2,1)S(1)}, u32[]{:S(2)}) copy-start(bf16[4,2,16,256]{3,2,1,0:T(8,128)(2,1)S(1)} %get-tuple-element.26.refs_2_.refs_4_) | copy-start | bytes 196612
  66.0 15.9 %collective-permute-start.2 = (bf16[4,2,16,256]{3,2,1,0:T(8,128)(2,1)S(1)}, bf16[4,2,16,256]{3,2,1,0:T(8,128)(2,1)S(1)}, u32[]{:S(2)}, u32[]{:S(2)}) collective-permute-start(bf16[4,2,16,256]{3,2,1,0:T(8,128)(2,1)S(1)} %get-tuple-element.27), channel_id=1, source_target_pairs={{0,1},{1,0},{2,3},{3,2},{4,5},{5,4},{6,7},{7,6},{8,9},{9,8},{10,11... | collective-permute-start | bytes 196616 | tf_op jit(solution)/shard_map/ppermute | solution.py:523
  67.9 16.2 %collective-permute-start.3 = (bf16[4,2,16,256]{3,2,1,0:T(8,128)(2,1)S(1)}, bf16[4,2,16,256]{3,2,1,0:T(8,128)(2,1)S(1)}, u32[]{:S(2)}, u32[]{:S(2)}) collective-permute-start(bf16[4,2,16,256]{3,2,1,0:T(8,128)(2,1)S(1)} %get-tuple-element.28), channel_id=1, source_target_pairs={{0,2},{1,3},{2,0},{3,1},{4,6},{5,7},{6,4},{7,5},{8,10},{9,11},{10,... | collective-permute-start | bytes 196616 | tf_op jit(solution)/shard_map/ppermute | solution.py:523
  71.8 18.3 %collective-permute-start.4 = (bf16[4,2,16,256]{3,2,1,0:T(8,128)(2,1)S(1)}, bf16[4,2,16,256]{3,2,1,0:T(8,128)(2,1)S(1)}, u32[]{:S(2)}, u32[]{:S(2)}) collective-permute-start(bf16[4,2,16,256]{3,2,1,0:T(8,128)(2,1)S(1)} %get-tuple-element.29), channel_id=1, source_target_pairs={{0,3},{1,2},{2,1},{3,0},{4,7},{5,6},{6,5},{7,4},{8,11},{9,10},{10,... | collective-permute-start | bytes 196616 | tf_op jit(solution)/shard_map/ppermute | solution.py:523
  74.9 15.2 %collective-permute-start.5 = (bf16[4,2,16,256]{3,2,1,0:T(8,128)(2,1)S(1)}, bf16[4,2,16,256]{3,2,1,0:T(8,128)(2,1)S(1)}, u32[]{:S(2)}, u32[]{:S(2)}) collective-permute-start(bf16[4,2,16,256]{3,2,1,0:T(8,128)(2,1)S(1)} %get-tuple-element.30), channel_id=1, source_target_pairs={{0,4},{1,5},{2,6},{3,7},{4,0},{5,1},{6,2},{7,3},{8,12},{9,13},{10,... | collective-permute-start | bytes 196616 | tf_op jit(solution)/shard_map/ppermute | solution.py:523
  77.8 12.4 %collective-permute-start.6 = (bf16[4,2,16,256]{3,2,1,0:T(8,128)(2,1)S(1)}, bf16[4,2,16,256]{3,2,1,0:T(8,128)(2,1)S(1)}, u32[]{:S(2)}, u32[]{:S(2)}) collective-permute-start(bf16[4,2,16,256]{3,2,1,0:T(8,128)(2,1)S(1)} %get-tuple-element.31), channel_id=1, source_target_pairs={{0,5},{1,4},{2,7},{3,6},{4,1},{5,0},{6,3},{7,2},{8,13},{9,12},{10,... | collective-permute-start | bytes 196616 | tf_op jit(solution)/shard_map/ppermute | solution.py:523
  81.9 8.3 %collective-permute-start.7 = (bf16[4,2,16,256]{3,2,1,0:T(8,128)(2,1)S(1)}, bf16[4,2,16,256]{3,2,1,0:T(8,128)(2,1)S(1)}, u32[]{:S(2)}, u32[]{:S(2)}) collective-permute-start(bf16[4,2,16,256]{3,2,1,0:T(8,128)(2,1)S(1)} %get-tuple-element.32), channel_id=1, source_target_pairs={{0,6},{1,7},{2,4},{3,5},{4,2},{5,3},{6,0},{7,1},{8,14},{9,15},{10,... | collective-permute-start | bytes 196616 | tf_op jit(solution)/shard_map/ppermute | solution.py:523
  84.0 7.1 %collective-permute-start.8 = (bf16[4,2,16,256]{3,2,1,0:T(8,128)(2,1)S(1)}, bf16[4,2,16,256]{3,2,1,0:T(8,128)(2,1)S(1)}, u32[]{:S(2)}, u32[]{:S(2)}) collective-permute-start(bf16[4,2,16,256]{3,2,1,0:T(8,128)(2,1)S(1)} %get-tuple-element.33), channel_id=1, source_target_pairs={{0,7},{1,6},{2,5},{3,4},{4,3},{5,2},{6,1},{7,0},{8,15},{9,14},{10,... | collective-permute-start | bytes 196616 | tf_op jit(solution)/shard_map/ppermute | solution.py:523
  90.1 108.1 %copy-start.12 = (s32[4]{0:T(128)}, s32[4]{0:T(128)S(1)}, u32[]{:S(2)}) copy-start(s32[4]{0:T(128)S(1)} %pad_add_fusion.refs_0_.scal_ref) | copy-start | bytes 52
  90.1 19.8 %copy-start.2 = (bf16[4,2,16,256]{3,2,1,0:T(8,128)(2,1)}, bf16[4,2,16,256]{3,2,1,0:T(8,128)(2,1)S(1)}, u32[]{:S(2)}) copy-start(bf16[4,2,16,256]{3,2,1,0:T(8,128)(2,1)S(1)} %collective-permute-done.4.refs_5_.refs_7_) | copy-start | bytes 196612
  90.2 19.8 %copy-start.4 = (bf16[4,2,16,256]{3,2,1,0:T(8,128)(2,1)}, bf16[4,2,16,256]{3,2,1,0:T(8,128)(2,1)S(1)}, u32[]{:S(2)}) copy-start(bf16[4,2,16,256]{3,2,1,0:T(8,128)(2,1)S(1)} %collective-permute-done.5.refs_6_.refs_8_) | copy-start | bytes 196612
  90.2 19.8 %copy-start.6 = (bf16[4,2,16,256]{3,2,1,0:T(8,128)(2,1)}, bf16[4,2,16,256]{3,2,1,0:T(8,128)(2,1)S(1)}, u32[]{:S(2)}) copy-start(bf16[4,2,16,256]{3,2,1,0:T(8,128)(2,1)S(1)} %collective-permute-done.6.refs_7_.refs_9_) | copy-start | bytes 196612
  90.2 19.8 %copy-start.8 = (bf16[4,2,16,256]{3,2,1,0:T(8,128)(2,1)}, bf16[4,2,16,256]{3,2,1,0:T(8,128)(2,1)S(1)}, u32[]{:S(2)}) copy-start(bf16[4,2,16,256]{3,2,1,0:T(8,128)(2,1)S(1)} %collective-permute-done.7.refs_8_.refs_10_) | copy-start | bytes 196612
  91.1 18.8 %copy-start.10 = (bf16[4,2,16,256]{3,2,1,0:T(8,128)(2,1)}, bf16[4,2,16,256]{3,2,1,0:T(8,128)(2,1)S(1)}, u32[]{:S(2)}) copy-start(bf16[4,2,16,256]{3,2,1,0:T(8,128)(2,1)S(1)} %collective-permute-done.8.refs_9_.refs_11_) | copy-start | bytes 196612
  94.0 16.0 %collective-permute-start.9 = (f32[2,2,512]{2,1,0:T(2,128)S(1)}, f32[2,2,512]{2,1,0:T(2,128)S(1)}, u32[]{:S(2)}, u32[]{:S(2)}) collective-permute-start(f32[2,2,512]{2,1,0:T(2,128)S(1)} %off_stats.1), channel_id=1, source_target_pairs={{0,8},{1,9},{2,10},{3,11},{4,12},{5,13},{6,14},{7,15},{16,24},{17,... | collective-permute-start | bytes 24584 | tf_op jit(solution)/shard_map/ppermute | solution.py:519
  165.6 16.8 %all-to-all-start.2 = ((f32[32,2,128]{2,1,0:T(2,128)}), f32[32,2,128]{2,1,0:T(2,128)S(1)}, u32[]{:S(2)}, u32[]{:S(2)}) async-start(f32[32,2,128]{2,1,0:T(2,128)} %copy.18), calls=%async_computation.2 | async-start | bytes 65536 | tf_op jit(solution)/shard_map/all_to_all | solution.py:515
  183.1 7.2 %copy-start.15 = (f32[4,1,512]{2,1,0:T(1,128)}, f32[4,1,512]{2,1,0:T(1,128)S(1)}, u32[]{:S(2)}) copy-start(f32[4,1,512]{2,1,0:T(1,128)S(1)} %get-tuple-element.47) | copy-start | bytes 24580
  183.1 14.4 %collective-permute-start.10 = (f32[2,2,512]{2,1,0:T(2,128)S(1)}, f32[2,2,512]{2,1,0:T(2,128)S(1)}, u32[]{:S(2)}, u32[]{:S(2)}) collective-permute-start(f32[2,2,512]{2,1,0:T(2,128)S(1)} %fusion.3), channel_id=1, source_target_pairs={{8,0},{9,1},{10,2},{11,3},{12,4},{13,5},{14,6},{15,7},{24,16},{25,... | collective-permute-start | bytes 24584 | tf_op jit(solution)/shard_map/ppermute | solution.py:519
  190.3 78.3 %all-to-all-start.3 = ((bf16[32,3,16,512]{3,2,1,0:T(8,128)(2,1)}), bf16[32,3,16,512]{3,2,1,0:T(8,128)(2,1)}, u32[]{:S(2)}, u32[]{:S(2)}) async-start(bf16[32,3,16,512]{3,2,1,0:T(8,128)(2,1)} %col_grads.1), calls=%async_computation.3 | async-start | bytes 3145728 | tf_op jit(solution)/shard_map/all_to_all | solution.py:515
  202.3 20.6 %collective-permute-start.11 = (bf16[2,64,256]{2,1,0:T(8,128)(2,1)S(1)}, bf16[2,64,256]{2,1,0:T(8,128)(2,1)S(1)}, u32[]{:S(2)}, u32[]{:S(2)}) collective-permute-start(bf16[2,64,256]{2,1,0:T(8,128)(2,1)S(1)} %get-tuple-element.45), channel_id=1, source_target_pairs={{0,1},{1,0},{2,3},{3,2},{4,5},{5,4},{6,7},{7,6},{8,9},{9,8},{10,11... | collective-permute-start | bytes 196616 | tf_op jit(solution)/shard_map/ppermute | solution.py:523
  204.2 20.9 %collective-permute-start.12 = (bf16[2,64,256]{2,1,0:T(8,128)(2,1)S(1)}, bf16[2,64,256]{2,1,0:T(8,128)(2,1)S(1)}, u32[]{:S(2)}, u32[]{:S(2)}) collective-permute-start(bf16[2,64,256]{2,1,0:T(8,128)(2,1)S(1)} %get-tuple-element.44), channel_id=1, source_target_pairs={{0,2},{1,3},{2,0},{3,1},{4,6},{5,7},{6,4},{7,5},{8,10},{9,11},{10,... | collective-permute-start | bytes 196616 | tf_op jit(solution)/shard_map/ppermute | solution.py:523
  206.9 22.9 %collective-permute-start.13 = (bf16[2,64,256]{2,1,0:T(8,128)(2,1)S(1)}, bf16[2,64,256]{2,1,0:T(8,128)(2,1)S(1)}, u32[]{:S(2)}, u32[]{:S(2)}) collective-permute-start(bf16[2,64,256]{2,1,0:T(8,128)(2,1)S(1)} %get-tuple-element.43), channel_id=1, source_target_pairs={{0,3},{1,2},{2,1},{3,0},{4,7},{5,6},{6,5},{7,4},{8,11},{9,10},{10,... | collective-permute-start | bytes 196616 | tf_op jit(solution)/shard_map/ppermute | solution.py:523
  209.9 20.0 %collective-permute-start.14 = (bf16[2,64,256]{2,1,0:T(8,128)(2,1)S(1)}, bf16[2,64,256]{2,1,0:T(8,128)(2,1)S(1)}, u32[]{:S(2)}, u32[]{:S(2)}) collective-permute-start(bf16[2,64,256]{2,1,0:T(8,128)(2,1)S(1)} %get-tuple-element.42), channel_id=1, source_target_pairs={{0,4},{1,5},{2,6},{3,7},{4,0},{5,1},{6,2},{7,3},{8,12},{9,13},{10,... | collective-permute-start | bytes 196616 | tf_op jit(solution)/shard_map/ppermute | solution.py:523
  213.1 16.8 %collective-permute-start.15 = (bf16[2,64,256]{2,1,0:T(8,128)(2,1)S(1)}, bf16[2,64,256]{2,1,0:T(8,128)(2,1)S(1)}, u32[]{:S(2)}, u32[]{:S(2)}) collective-permute-start(bf16[2,64,256]{2,1,0:T(8,128)(2,1)S(1)} %get-tuple-element.41), channel_id=1, source_target_pairs={{0,5},{1,4},{2,7},{3,6},{4,1},{5,0},{6,3},{7,2},{8,13},{9,12},{10,... | collective-permute-start | bytes 196616 | tf_op jit(solution)/shard_map/ppermute | solution.py:523
  222.9 7.6 %collective-permute-start.16 = (bf16[2,64,256]{2,1,0:T(8,128)(2,1)S(1)}, bf16[2,64,256]{2,1,0:T(8,128)(2,1)S(1)}, u32[]{:S(2)}, u32[]{:S(2)}) collective-permute-start(bf16[2,64,256]{2,1,0:T(8,128)(2,1)S(1)} %get-tuple-element.40), channel_id=1, source_target_pairs={{0,6},{1,7},{2,4},{3,5},{4,2},{5,3},{6,0},{7,1},{8,14},{9,15},{10,... | collective-permute-start | bytes 196616 | tf_op jit(solution)/shard_map/ppermute | solution.py:523
  225.1 7.2 %collective-permute-start.17 = (bf16[2,64,256]{2,1,0:T(8,128)(2,1)S(1)}, bf16[2,64,256]{2,1,0:T(8,128)(2,1)S(1)}, u32[]{:S(2)}, u32[]{:S(2)}) collective-permute-start(bf16[2,64,256]{2,1,0:T(8,128)(2,1)S(1)} %get-tuple-element.39), channel_id=1, source_target_pairs={{0,7},{1,6},{2,5},{3,4},{4,3},{5,2},{6,1},{7,0},{8,15},{9,14},{10,... | collective-permute-start | bytes 196616 | tf_op jit(solution)/shard_map/ppermute | solution.py:523
  268.6 54.1 %collective-permute-start.18 = (bf16[8,2,64,256]{3,2,1,0:T(8,128)(2,1)S(1)}, bf16[8,2,64,256]{3,2,1,0:T(8,128)(2,1)S(1)}, u32[]{:S(2)}, u32[]{:S(2)}) collective-permute-start(bf16[8,2,64,256]{3,2,1,0:T(8,128)(2,1)S(1)} %bitcast_dynamic-update-slice_fusion), channel_id=1, source_target_pairs={{0,8},{1,9},{2,10},{3,11},{4,12},{5,13},{6,14},{7,15},{8,0},{9,1},... | collective-permute-start | bytes 1572872 | tf_op jit(solution)/shard_map/ppermute | solution.py:523
  285.4 37.4 %all-to-all-start.4 = ((bf16[8,4,3,16,512]{4,3,2,1,0:T(8,128)(2,1)}), bf16[8,4,3,16,512]{4,3,2,1,0:T(8,128)(2,1)}, u32[]{:S(2)}, u32[]{:S(2)}) async-start(bf16[8,4,3,16,512]{4,3,2,1,0:T(8,128)(2,1)} %bitcast.30), calls=%async_computation.4 | async-start | bytes 3145728 | tf_op jit(solution)/shard_map/all_to_all | solution.py:510
  (13 other events, 27.4 us)

commit v6 on v5

--- a/solution.py
+++ b/solution.py
@@ -27,10 +27,6 @@
 
 def dot_nn(a, b):
     return lax.dot_general(a, b, (((1,), (0,)), ((), ())), preferred_element_type=f32)
-
-
-def dot_tn(a, b):
-    return lax.dot_general(a, b, (((0,), (0,)), ((), ())), preferred_element_type=f32)
 
 
 def params(n_axes=1):
@@ -95,6 +91,8 @@
     )(*split)
 
 
+STATS_STEP = 128
+GRADS_STEP = 256
 LONG = pl.CostEstimate(flops=200_000_000_000, bytes_accessed=400 << 20, transcendentals=0)
 
 
@@ -264,19 +262,36 @@
         run(far_a, far_b, flat(t_ref, QI), flat(t_ref, GI))
 
 
-def col_blocks(n):
-    step = n
-    return [slice(i, i + step) for i in range(0, n, step)]
-
-
-def col_stats_body(scale, scal_ref, t_ref, out_ref, bias_ref):
-    fill_bias(bias_ref, lambda n: col_mask(scal_ref, n, t_ref.shape[2]))
-    k, v, q, g = (flat(t_ref, i) for i in range(4))
-    for part in col_blocks(k.shape[0]):
-        upto = slice(0, part.stop)
-        lse, delta = partial_stats(k[upto], v[upto], q[part], g[part], bias_ref[upto, part], scale)
-        out_ref[0, 0:1, part] = lse
-        out_ref[0, 1:2, part] = delta
+def head_slices(ref, head):
+    feats = slice(head * HEAD, (head + 1) * HEAD)
+    blocks = (ref[:, i, :, feats] for i in range(ref.shape[1]))
+    return (b.reshape(b.shape[0] * b.shape[1], HEAD) for b in blocks)
+
+
+def col_stats_body(scale, scal_ref, t_ref, out_ref):
+    rows, _, cols, _ = t_ref.shape
+    bias = jnp.where(col_mask(scal_ref, rows * cols, cols), 0.0, masked_low)
+    for head in range(out_ref.shape[0]):
+        k, v, q, g = head_slices(t_ref, head)
+        for start in range(0, rows * cols, STATS_STEP):
+            part, upto = slice(start, start + STATS_STEP), slice(0, start + STATS_STEP)
+            lse, delta = partial_stats(k[upto], v[upto], q[part], g[part], bias[upto, part], scale)
+            out_ref[head, 0:1, part] = lse
+            out_ref[head, 1:2, part] = delta
+
+
+def col_stats(scale, scal, t):
+    rows, _, cols, feats = t.shape
+    whole = pl.BlockSpec(memory_space=pltpu.VMEM)
+    return pl.pallas_call(
+        lambda *refs: col_stats_body(scale, *refs),
+        in_specs=[smem(), whole],
+        out_specs=whole,
+        out_shape=jax.ShapeDtypeStruct((feats // HEAD, 2, rows * cols), f32),
+        compiler_params=pltpu.CompilerParams(vmem_limit_bytes=VMEM_BYTES),
+        cost_estimate=cost(4),
+        name="col_stats",
+    )(scal, t)
 
 
 def smem():
@@ -392,7 +407,7 @@
     ds = (p * (dot_nt(v, g) - delta)).astype(bf16)
     dv = dot_nn(p.astype(bf16), g)
     dk = dot_nn(ds, q) * score_scale
-    dq = dot_tn(ds, k) * score_scale
+    dq = dot_nn(k.T, ds).T * score_scale
     return dq, dk, dv
 
 
@@ -418,23 +433,32 @@
         out_ref[:, a] = sum_ref[a].astype(bf16).reshape(out_ref.shape[0], out_ref.shape[2], HEAD)
 
 
-def col_grads_body(scale, scal_ref, t_ref, own_ref, got_ref, out_ref, sum_ref, bias_ref):
-    fill_bias(bias_ref, lambda n: col_mask(scal_ref, n, t_ref.shape[2]))
-    k, v, q, g = (flat(t_ref, i) for i in range(4))
-    lse, delta = merge(own_ref[0, 0:1], own_ref[0, 1:2], got_ref[0, 0:1], got_ref[0, 1:2])
-    blocks = col_blocks(k.shape[0])
-    for i, part in enumerate(blocks):
-        upto = slice(0, part.stop)
-        dq, dk, dv = block_grads(
-            k[upto], v[upto], q[part], g[part], bias_ref[upto, part], lse[:, part], delta[:, part], scale
+def col_grads_body(scale, scal_ref, t_ref, own_ref, got_ref, out_ref):
+    rows, _, cols, _ = t_ref.shape
+    bias = jnp.where(col_mask(scal_ref, rows * cols, cols), 0.0, masked_low)
+    for head in range(own_ref.shape[0]):
+        k, v, q, g = head_slices(t_ref, head)
+        lse, delta = merge(
+            own_ref[head, 0:1], own_ref[head, 1:2], got_ref[head, 0:1], got_ref[head, 1:2]
         )
-        sum_ref[0, part] = dq
-        for a, d in ((1, dk), (2, dv)):
-            if i:
-                sum_ref[a, : part.start] += d[: part.start]
-            sum_ref[a, part] = d[part.start :]
-    for a in range(3):
-        out_ref[:, a] = sum_ref[a].astype(bf16).reshape(out_ref.shape[0], out_ref.shape[2], HEAD)
+        feats = slice(head * HEAD, (head + 1) * HEAD)
+
+        def put(a, part, d):
+            rows_here = slice(part.start // cols, part.stop // cols)
+            out_ref[rows_here, a, :, feats] = d.astype(bf16).reshape(-1, cols, HEAD)
+
+        n = rows * cols
+        dk_sum = dv_sum = None
+        for stop in range(n, 0, -GRADS_STEP):
+            part, upto = slice(stop - GRADS_STEP, stop), slice(0, stop)
+            dq, dk, dv = block_grads(
+                k[upto], v[upto], q[part], g[part], bias[upto, part], lse[:, part], delta[:, part], scale
+            )
+            dk_sum = dk if dk_sum is None else dk_sum[upto] + dk
+            dv_sum = dv if dv_sum is None else dv_sum[upto] + dv
+            put(0, part, dq)
+            put(1, part, dk_sum[part])
+            put(2, part, dv_sum[part])
 
 
 def row_grads(scale, scal, t, stats, off):
@@ -461,16 +485,13 @@
 
 def col_grads(scale, scal, t, own, got):
     rows, _, cols, feats = t.shape
-    n = rows * cols
-    stat_spec = pl.BlockSpec((1, 2, n), lambda h: (h, 0, 0))
+    whole = pl.BlockSpec(memory_space=pltpu.VMEM)
     return pl.pallas_call(
         lambda *refs: col_grads_body(scale, *refs),
-        grid=(feats // HEAD,),
-        in_specs=[smem(), head_block(t), stat_spec, stat_spec],
-        out_specs=pl.BlockSpec((rows, 3, cols, HEAD), lambda h: (0, 0, 0, h)),
+        in_specs=[smem(), whole, whole, whole],
+        out_specs=whole,
         out_shape=jax.ShapeDtypeStruct((rows, 3, cols, feats), bf16),
-        scratch_shapes=[pltpu.VMEM((3, n, HEAD), f32), pltpu.VMEM((n, n), f32)],
-        compiler_params=params(),
+        compiler_params=pltpu.CompilerParams(vmem_limit_bytes=VMEM_BYTES),
         cost_estimate=cost(8),
         name="col_grads",
     )(scal, t, own, got)
@@ -550,7 +571,7 @@
     off_part = jnp.concatenate([shift(own_off, 0, 1), own_off])
     lse, delta = merge(diag_part[:, 0], diag_part[:, 1], off_part[:, 0], off_part[:, 1])
     row_part = jnp.where(half == 1, jnp.stack([lse, delta], axis=1), diag_part)
-    col_part = stats_call(col_stats_body, scale, scal, (by_col,), "col_stats", 4)
+    col_part = col_stats(scale, scal, by_col)
 
     both = jnp.stack([row_part, col_part]).reshape(4 * heads, lanes, cols)
     sent = both.transpose(1, 0, 2).reshape(lanes, (4 * heads * cols) // HEAD, HEAD)

time: 329 us -> 327 us (level)
    pallas_call x2 -> x1, Pallas kernels: 7.63 us -> 3.82 us  [stats_call(): pl.pallas_call(lambda *refs: body(scale, *refs), grid=(heads,), in_specs=...]
    pallas_call x1 -> x2, Pallas kernels: 5.86 us -> 8.18 us  [the longest x1 5.36 us: col_grads(): pl.pallas_call(lambda *refs: col_grads_body(scale, *refs), in_specs=[smem...]
where the time goes in v6:
time: 327 us; the launch traced here: 326 us
  waiting for transfers between devices  164 us (50%)
  starting transfers between devices  118 us (36%)
  Pallas kernels  35.6 us (11%)
  local copies, waits for them, and re-layouts  5.21 us (2%)
    all_to_all x3, waiting for transfers between devices, exchange_wide(): return lax.all_to_all(arr, 'wide', split_axis=0, concat_axis=0, tiled=True)  96.8 us
    ppermute x17, starting transfers between devices, swap(): return lax.ppermute(arr, 'narrow', pairs)  72.7 us
    ppermute x17, waiting for transfers between devices, swap(): return lax.ppermute(arr, 'narrow', pairs)  65.9 us
    all_to_all x3, starting transfers between devices, exchange_wide(): return lax.all_to_all(arr, 'wide', split_axis=0, concat_axis=0, tiled=True)  22.3 us
    ppermute x2, starting transfers between devices, shift(): return lax.ppermute(arr, 'narrow', pairs)  13.4 us
    all_to_all x2, starting transfers between devices, exchange_near(): lax.all_to_all(arr, 'narrow', split_axis=0, concat_axis=0, axis_index_gro...  9.38 us
    pallas_call x2, Pallas kernels, off_call(): pl.pallas_call(lambda *refs: body(scale, *refs), grid_spec=pltpu.Prefetch...  6.61 us
  transfers between devices with their start and end apart: 24, of which 10 were waited for; matrix products, arithmetic and copies ran while one was open for 1% of the time, Pallas kernels for 8%

profile of v6, /device:TPU:58, one launch (start us, length us, event | category | flops | bytes accessed | tf_op | source)
XLA Modules:
  0.0 325.6 jit_solution(8962737415122421731)
XLA Ops:
  0.6 3.3 %pack.1 = (bf16[8,4,16,256]{3,2,1,0:T(8,128)(2,1)}, bf16[8,4,16,256]{3,2,1,0:T(8,128)(2,1)}, bf16[8,4,4,16,512]{4,3,2,1,0:T(8,128)(2,1)}) custom-call(bf16[4,16,4096]{2,1,0:T(8,128)(2,1)} %bitcast.71, bf16[4,16,4096]{2,1,0:T(8,128)(2,1)} %bitcast.72, bf16[4,16,4096]{2,1,0:T(8,128)(2,1)} %bitcast.73, bf16[4,16,4096]{2,1,0:T(8,128)(2,1)} %bitcast.74), custom_call_target="tpu_custom_call" | custom-call | tf_op jit(solution)/shard_map/pack/pallas_call | solution.py:83
  4.0 14.8 %collective-permute-start = (bf16[8,4,16,256]{3,2,1,0:T(8,128)(2,1)}, bf16[8,4,16,256]{3,2,1,0:T(8,128)(2,1)S(1)}, u32[]{:S(2)}, u32[]{:S(2)}) collective-permute-start(bf16[8,4,16,256]{3,2,1,0:T(8,128)(2,1)} %get-tuple-element.22), channel_id=1, source_target_pairs={{0,8},{1,9},{2,10},{3,11},{4,12},{5,13},{6,14},{7,15},{8,0},{9,1},... | collective-permute-start | bytes 786440 | tf_op jit(solution)/shard_map/ppermute | solution.py:544
  18.8 4.7 %all-to-all-start = ((bf16[8,4,4,16,512]{4,3,2,1,0:T(8,128)(2,1)}), bf16[8,4,4,16,512]{4,3,2,1,0:T(8,128)(2,1)}, u32[]{:S(2)}, u32[]{:S(2)}) async-start(bf16[8,4,4,16,512]{4,3,2,1,0:T(8,128)(2,1)} %get-tuple-element.21), calls=%async_computation | async-start | bytes 4194304 | tf_op jit(solution)/shard_map/all_to_all | solution.py:531
  25.4 29.3 %collective-permute-done.in_ref.a_ref = bf16[8,4,16,256]{3,2,1,0:T(8,128)(2,1)S(1)} collective-permute-done((bf16[8,4,16,256]{3,2,1,0:T(8,128)(2,1)}, bf16[8,4,16,256]{3,2,1,0:T(8,128)(2,1)S(1)}, u32[]{:S(2)}, u32[]{:S(2)}) %collective-permute-start) | collective-permute-done | bytes 262176 | tf_op jit(solution)/shard_map/ppermute | solution.py:544
  54.7 9.6 %all-to-all-start.1 = ((bf16[32,4,16,512]{3,2,1,0:T(8,128)(2,1)}), bf16[32,4,16,512]{3,2,1,0:T(8,128)(2,1)}, u32[]{:S(2)}, u32[]{:S(2)}) async-start(bf16[32,4,16,512]{3,2,1,0:T(8,128)(2,1)} %bitcast.6.refs_1_), calls=%async_computation.1 | async-start | bytes 4194304 | tf_op jit(solution)/shard_map/all_to_all | solution.py:536
  67.9 2.6 collective-permute-start.3
  71.8 3.1 collective-permute-start.4
  74.9 2.9 collective-permute-start.5
  77.8 4.1 %collective-permute-start.6 = (bf16[4,2,16,256]{3,2,1,0:T(8,128)(2,1)S(1)}, bf16[4,2,16,256]{3,2,1,0:T(8,128)(2,1)S(1)}, u32[]{:S(2)}, u32[]{:S(2)}) collective-permute-start(bf16[4,2,16,256]{3,2,1,0:T(8,128)(2,1)S(1)} %get-tuple-element.31), channel_id=1, source_target_pairs={{0,5},{1,4},{2,7},{3,6},{4,1},{5,0},{6,3},{7,2},{8,13},{9,12},{10,... | collective-permute-start | bytes 196616 | tf_op jit(solution)/shard_map/ppermute | solution.py:544
  84.0 4.8 %collective-permute-start.8 = (bf16[4,2,16,256]{3,2,1,0:T(8,128)(2,1)S(1)}, bf16[4,2,16,256]{3,2,1,0:T(8,128)(2,1)S(1)}, u32[]{:S(2)}, u32[]{:S(2)}) collective-permute-start(bf16[4,2,16,256]{3,2,1,0:T(8,128)(2,1)S(1)} %get-tuple-element.33), channel_id=1, source_target_pairs={{0,7},{1,6},{2,5},{3,4},{4,3},{5,2},{6,1},{7,0},{8,15},{9,14},{10,... | collective-permute-start | bytes 196616 | tf_op jit(solution)/shard_map/ppermute | solution.py:544
  91.1 2.9 off_stats.1
  94.0 12.1 %collective-permute-start.9 = (f32[2,2,512]{2,1,0:T(2,128)S(1)}, f32[2,2,512]{2,1,0:T(2,128)S(1)}, u32[]{:S(2)}, u32[]{:S(2)}) collective-permute-start(f32[2,2,512]{2,1,0:T(2,128)S(1)} %off_stats.1), channel_id=1, source_target_pairs={{0,8},{1,9},{2,10},{3,11},{4,12},{5,13},{6,14},{7,15},{16,24},{17,... | collective-permute-start | bytes 24584 | tf_op jit(solution)/shard_map/ppermute | solution.py:540
  106.1 3.8 %row_stats.1 = f32[4,2,512]{2,1,0:T(2,128)S(1)} custom-call(s32[4]{0:T(128)S(1)} %pad_add_fusion.refs_0_.scal_ref, bf16[32,4,16,512]{3,2,1,0:T(8,128)(2,1)} %bitcast.6.refs_1_), custom_call_target="tpu_custom_call" | custom-call | flops 1342177280 | bytes 4194304 | tf_op jit(solution)/shard_map/row_stats/pallas_call | solution.py:392
  110.1 50.7 %all-to-all-done.1.refs_1_ = bf16[32,4,16,512]{3,2,1,0:T(8,128)(2,1)} async-done(((bf16[32,4,16,512]{3,2,1,0:T(8,128)(2,1)}), bf16[32,4,16,512]{3,2,1,0:T(8,128)(2,1)}, u32[]{:S(2)}, u32[]{:S(2)}) %all-to-all-start.1) | async-done | bytes 2097184 | tf_op jit(solution)/shard_map/all_to_all | solution.py:536
  160.8 2.8 col_stats.1.refs_2_
  164.6 6.2 %all-to-all-start.2 = ((f32[32,2,128]{2,1,0:T(2,128)}), f32[32,2,128]{2,1,0:T(2,128)S(1)}, u32[]{:S(2)}, u32[]{:S(2)}) async-start(f32[32,2,128]{2,1,0:T(2,128)} %copy.18), calls=%async_computation.2 | async-start | bytes 65536 | tf_op jit(solution)/shard_map/all_to_all | solution.py:536
  170.8 10.6 %all-to-all-done.2 = f32[32,2,128]{2,1,0:T(2,128)S(1)} async-done(((f32[32,2,128]{2,1,0:T(2,128)}), f32[32,2,128]{2,1,0:T(2,128)S(1)}, u32[]{:S(2)}, u32[]{:S(2)}) %all-to-all-start.2) | async-done | bytes 32800 | tf_op jit(solution)/shard_map/all_to_all | solution.py:536
  183.4 5.4 %col_grads.1 = bf16[32,3,16,512]{3,2,1,0:T(8,128)(2,1)} custom-call(s32[4]{0:T(128)S(1)} %pad_add_fusion.refs_0_.scal_ref, bf16[32,4,16,512]{3,2,1,0:T(8,128)(2,1)} %all-to-all-done.1.refs_1_, f32[4,2,512]{2,1,0:T(2,128)S(1)} %col_stats.1.refs_2_, f32[4,2,512]{2,1,0:T(2,128)S(1)} %squeeze.42.refs_3_), custom_call_target="tpu_custom_call" | custom-call | flops 2684354560 | bytes 4194304 | tf_op jit(solution)/shard_map/col_grads/pallas_call | solution.py:489
  188.8 6.5 %all-to-all-start.3 = ((bf16[32,3,16,512]{3,2,1,0:T(8,128)(2,1)}), bf16[32,3,16,512]{3,2,1,0:T(8,128)(2,1)}, u32[]{:S(2)}, u32[]{:S(2)}) async-start(bf16[32,3,16,512]{3,2,1,0:T(8,128)(2,1)} %col_grads.1), calls=%async_computation.3 | async-start | bytes 3145728 | tf_op jit(solution)/shard_map/all_to_all | solution.py:536
  197.7 3.7 %off_grads.1 = (f32[2,512,256]{2,1,0:T(8,128)S(1)}, bf16[8,2,64,256]{3,2,1,0:T(8,128)(2,1)S(1)}) custom-call(s32[4]{0:T(128)S(1)} %pad_add_fusion.refs_0_.scal_ref, bf16[32,4,16,512]{3,2,1,0:T(8,128)(2,1)} %bitcast.6.refs_1_, f32[2,2,512]{2,1,0:T(2,128)S(1)} %fusion.2.refs_2_, f32[8,128]{1,0:T(8,128)S(1)} %hold.4.refs_3_, ...), custom_call_target="tpu_custom_call" | custom-call | flops 1677721600 | bytes 4194304 | tf_op jit(solution)/shard_map/off_grads/pallas_call | solution.py:319
  203.4 2.7 collective-permute-start.12
  206.1 3.0 collective-permute-start.13
  209.1 3.2 collective-permute-start.14
  212.3 3.8 %collective-permute-start.15 = (bf16[2,64,256]{2,1,0:T(8,128)(2,1)S(1)}, bf16[2,64,256]{2,1,0:T(8,128)(2,1)S(1)}, u32[]{:S(2)}, u32[]{:S(2)}) collective-permute-start(bf16[2,64,256]{2,1,0:T(8,128)(2,1)S(1)} %get-tuple-element.41), channel_id=1, source_target_pairs={{0,5},{1,4},{2,7},{3,6},{4,1},{5,0},{6,3},{7,2},{8,13},{9,12},{10,... | collective-permute-start | bytes 196616 | tf_op jit(solution)/shard_map/ppermute | solution.py:544
  216.7 5.3 %row_grads.1.row_ref = bf16[32,3,16,512]{3,2,1,0:T(8,128)(2,1)S(1)} custom-call(s32[4]{0:T(128)S(1)} %copy-done.13, bf16[32,4,16,512]{3,2,1,0:T(8,128)(2,1)} %bitcast.6.refs_1_, f32[4,2,512]{2,1,0:T(2,128)S(1)} %pad_maximum_fusion.1.refs_2_, f32[2,512,256]{2,1,0:T(8,128)S(1)} %get-tuple-element.35.refs_3_), custom_call_target="tpu_custom_call" | custom-call | flops 2684354560 | bytes 4194304 | tf_op jit(solution)/shard_map/row_grads/pallas_call | solution.py:468
  224.3 4.7 %collective-permute-start.17 = (bf16[2,64,256]{2,1,0:T(8,128)(2,1)S(1)}, bf16[2,64,256]{2,1,0:T(8,128)(2,1)S(1)}, u32[]{:S(2)}, u32[]{:S(2)}) collective-permute-start(bf16[2,64,256]{2,1,0:T(8,128)(2,1)S(1)} %get-tuple-element.39), channel_id=1, source_target_pairs={{0,7},{1,6},{2,5},{3,4},{4,3},{5,2},{6,1},{7,0},{8,15},{9,14},{10,... | collective-permute-start | bytes 196616 | tf_op jit(solution)/shard_map/ppermute | solution.py:544
  231.5 35.6 %all-to-all-done.3.col_ref = bf16[32,3,16,512]{3,2,1,0:T(8,128)(2,1)} async-done(((bf16[32,3,16,512]{3,2,1,0:T(8,128)(2,1)}), bf16[32,3,16,512]{3,2,1,0:T(8,128)(2,1)}, u32[]{:S(2)}, u32[]{:S(2)}) %all-to-all-start.3) | async-done | bytes 1572896 | tf_op jit(solution)/shard_map/all_to_all | solution.py:536
  267.1 13.1 %collective-permute-start.18 = (bf16[8,2,64,256]{3,2,1,0:T(8,128)(2,1)S(1)}, bf16[8,2,64,256]{3,2,1,0:T(8,128)(2,1)S(1)}, u32[]{:S(2)}, u32[]{:S(2)}) collective-permute-start(bf16[8,2,64,256]{3,2,1,0:T(8,128)(2,1)S(1)} %bitcast_dynamic-update-slice_fusion), channel_id=1, source_target_pairs={{0,8},{1,9},{2,10},{3,11},{4,12},{5,13},{6,14},{7,15},{8,0},{9,1},... | collective-permute-start | bytes 1572872 | tf_op jit(solution)/shard_map/ppermute | solution.py:544
  280.2 3.7 %join.1 = bf16[32,3,16,512]{3,2,1,0:T(8,128)(2,1)} custom-call(bf16[32,3,16,512]{3,2,1,0:T(8,128)(2,1)S(1)} %row_grads.1.row_ref, bf16[32,3,16,512]{3,2,1,0:T(8,128)(2,1)} %all-to-all-done.3.col_ref), custom_call_target="tpu_custom_call" | custom-call | tf_op jit(solution)/shard_map/join/pallas_call | solution.py:508
  283.9 4.7 %all-to-all-start.4 = ((bf16[8,4,3,16,512]{4,3,2,1,0:T(8,128)(2,1)}), bf16[8,4,3,16,512]{4,3,2,1,0:T(8,128)(2,1)}, u32[]{:S(2)}, u32[]{:S(2)}) async-start(bf16[8,4,3,16,512]{4,3,2,1,0:T(8,128)(2,1)} %bitcast.30), calls=%async_computation.4 | async-start | bytes 3145728 | tf_op jit(solution)/shard_map/all_to_all | solution.py:531
  288.6 32.7 %collective-permute-done.18.in_ref.far_ref = bf16[8,2,64,256]{3,2,1,0:T(8,128)(2,1)S(1)} collective-permute-done((bf16[8,2,64,256]{3,2,1,0:T(8,128)(2,1)S(1)}, bf16[8,2,64,256]{3,2,1,0:T(8,128)(2,1)S(1)}, u32[]{:S(2)}, u32[]{:S(2)}) %collective-permute-start.18) | collective-permute-done | bytes 524320 | tf_op jit(solution)/shard_map/ppermute | solution.py:544
  321.9 3.7 %unpack.1 = (bf16[64,4096]{1,0:T(8,128)(2,1)}, bf16[64,4096]{1,0:T(8,128)(2,1)}, bf16[64,4096]{1,0:T(8,128)(2,1)}) custom-call(s32[4]{0:T(128)S(1)} %copy-done.14, bf16[8,4,3,16,512]{4,3,2,1,0:T(8,128)(2,1)} %all-to-all-done.4.in_ref, bf16[8,2,64,256]{3,2,1,0:T(8,128)(2,1)S(1)} %collective-permute-done.18.in_ref.far_ref, f32[8,128]{1,0:T(8,128)S(1)} %hold.5.token_ref), custom_call_target="tpu_custom_call" | custom-call | tf_op jit(solution)/shard_map/unpack/pallas_call | solution.py:167
  (99 shorter events, 24.4 us)
Async XLA Ops:
  4.0 50.8 %collective-permute-start = (bf16[8,4,16,256]{3,2,1,0:T(8,128)(2,1)}, bf16[8,4,16,256]{3,2,1,0:T(8,128)(2,1)S(1)}, u32[]{:S(2)}, u32[]{:S(2)}) collective-permute-start(bf16[8,4,16,256]{3,2,1,0:T(8,128)(2,1)} %get-tuple-element.22), channel_id=1, source_target_pairs={{0,8},{1,9},{2,10},{3,11},{4,12},{5,13},{6,14},{7,15},{8,0},{9,1},... | collective-permute-start | bytes 786440 | tf_op jit(solution)/shard_map/ppermute | solution.py:544
  18.8 35.9 %all-to-all-start = ((bf16[8,4,4,16,512]{4,3,2,1,0:T(8,128)(2,1)}), bf16[8,4,4,16,512]{4,3,2,1,0:T(8,128)(2,1)}, u32[]{:S(2)}, u32[]{:S(2)}) async-start(bf16[8,4,4,16,512]{4,3,2,1,0:T(8,128)(2,1)} %get-tuple-element.21), calls=%async_computation | async-start | bytes 4194304 | tf_op jit(solution)/shard_map/all_to_all | solution.py:531
  23.5 41.4 %collective-permute-start.1 = (bf16[8,4,16,256]{3,2,1,0:T(8,128)(2,1)}, bf16[8,4,16,256]{3,2,1,0:T(8,128)(2,1)}, u32[]{:S(2)}, u32[]{:S(2)}) collective-permute-start(bf16[8,4,16,256]{3,2,1,0:T(8,128)(2,1)} %get-tuple-element.24), channel_id=1, source_target_pairs={{0,8},{1,9},{2,10},{3,11},{4,12},{5,13},{6,14},{7,15},{8,0},{9,1},... | collective-permute-start | bytes 786440 | tf_op jit(solution)/shard_map/ppermute | solution.py:544
  54.7 106.0 %all-to-all-start.1 = ((bf16[32,4,16,512]{3,2,1,0:T(8,128)(2,1)}), bf16[32,4,16,512]{3,2,1,0:T(8,128)(2,1)}, u32[]{:S(2)}, u32[]{:S(2)}) async-start(bf16[32,4,16,512]{3,2,1,0:T(8,128)(2,1)} %bitcast.6.refs_1_), calls=%async_computation.1 | async-start | bytes 4194304 | tf_op jit(solution)/shard_map/all_to_all | solution.py:536
  65.9 28.1 %copy-start = (bf16[4,2,16,256]{3,2,1,0:T(8,128)(2,1)}, bf16[4,2,16,256]{3,2,1,0:T(8,128)(2,1)S(1)}, u32[]{:S(2)}) copy-start(bf16[4,2,16,256]{3,2,1,0:T(8,128)(2,1)S(1)} %get-tuple-element.26.refs_2_.refs_4_) | copy-start | bytes 196612
  66.0 15.9 %collective-permute-start.2 = (bf16[4,2,16,256]{3,2,1,0:T(8,128)(2,1)S(1)}, bf16[4,2,16,256]{3,2,1,0:T(8,128)(2,1)S(1)}, u32[]{:S(2)}, u32[]{:S(2)}) collective-permute-start(bf16[4,2,16,256]{3,2,1,0:T(8,128)(2,1)S(1)} %get-tuple-element.27), channel_id=1, source_target_pairs={{0,1},{1,0},{2,3},{3,2},{4,5},{5,4},{6,7},{7,6},{8,9},{9,8},{10,11... | collective-permute-start | bytes 196616 | tf_op jit(solution)/shard_map/ppermute | solution.py:544
  67.9 16.2 %collective-permute-start.3 = (bf16[4,2,16,256]{3,2,1,0:T(8,128)(2,1)S(1)}, bf16[4,2,16,256]{3,2,1,0:T(8,128)(2,1)S(1)}, u32[]{:S(2)}, u32[]{:S(2)}) collective-permute-start(bf16[4,2,16,256]{3,2,1,0:T(8,128)(2,1)S(1)} %get-tuple-element.28), channel_id=1, source_target_pairs={{0,2},{1,3},{2,0},{3,1},{4,6},{5,7},{6,4},{7,5},{8,10},{9,11},{10,... | collective-permute-start | bytes 196616 | tf_op jit(solution)/shard_map/ppermute | solution.py:544
  71.8 18.3 %collective-permute-start.4 = (bf16[4,2,16,256]{3,2,1,0:T(8,128)(2,1)S(1)}, bf16[4,2,16,256]{3,2,1,0:T(8,128)(2,1)S(1)}, u32[]{:S(2)}, u32[]{:S(2)}) collective-permute-start(bf16[4,2,16,256]{3,2,1,0:T(8,128)(2,1)S(1)} %get-tuple-element.29), channel_id=1, source_target_pairs={{0,3},{1,2},{2,1},{3,0},{4,7},{5,6},{6,5},{7,4},{8,11},{9,10},{10,... | collective-permute-start | bytes 196616 | tf_op jit(solution)/shard_map/ppermute | solution.py:544
  74.9 15.2 %collective-permute-start.5 = (bf16[4,2,16,256]{3,2,1,0:T(8,128)(2,1)S(1)}, bf16[4,2,16,256]{3,2,1,0:T(8,128)(2,1)S(1)}, u32[]{:S(2)}, u32[]{:S(2)}) collective-permute-start(bf16[4,2,16,256]{3,2,1,0:T(8,128)(2,1)S(1)} %get-tuple-element.30), channel_id=1, source_target_pairs={{0,4},{1,5},{2,6},{3,7},{4,0},{5,1},{6,2},{7,3},{8,12},{9,13},{10,... | collective-permute-start | bytes 196616 | tf_op jit(solution)/shard_map/ppermute | solution.py:544
  77.8 12.4 %collective-permute-start.6 = (bf16[4,2,16,256]{3,2,1,0:T(8,128)(2,1)S(1)}, bf16[4,2,16,256]{3,2,1,0:T(8,128)(2,1)S(1)}, u32[]{:S(2)}, u32[]{:S(2)}) collective-permute-start(bf16[4,2,16,256]{3,2,1,0:T(8,128)(2,1)S(1)} %get-tuple-element.31), channel_id=1, source_target_pairs={{0,5},{1,4},{2,7},{3,6},{4,1},{5,0},{6,3},{7,2},{8,13},{9,12},{10,... | collective-permute-start | bytes 196616 | tf_op jit(solution)/shard_map/ppermute | solution.py:544
  81.9 8.3 %collective-permute-start.7 = (bf16[4,2,16,256]{3,2,1,0:T(8,128)(2,1)S(1)}, bf16[4,2,16,256]{3,2,1,0:T(8,128)(2,1)S(1)}, u32[]{:S(2)}, u32[]{:S(2)}) collective-permute-start(bf16[4,2,16,256]{3,2,1,0:T(8,128)(2,1)S(1)} %get-tuple-element.32), channel_id=1, source_target_pairs={{0,6},{1,7},{2,4},{3,5},{4,2},{5,3},{6,0},{7,1},{8,14},{9,15},{10,... | collective-permute-start | bytes 196616 | tf_op jit(solution)/shard_map/ppermute | solution.py:544
  84.0 7.1 %collective-permute-start.8 = (bf16[4,2,16,256]{3,2,1,0:T(8,128)(2,1)S(1)}, bf16[4,2,16,256]{3,2,1,0:T(8,128)(2,1)S(1)}, u32[]{:S(2)}, u32[]{:S(2)}) collective-permute-start(bf16[4,2,16,256]{3,2,1,0:T(8,128)(2,1)S(1)} %get-tuple-element.33), channel_id=1, source_target_pairs={{0,7},{1,6},{2,5},{3,4},{4,3},{5,2},{6,1},{7,0},{8,15},{9,14},{10,... | collective-permute-start | bytes 196616 | tf_op jit(solution)/shard_map/ppermute | solution.py:544
  90.1 107.2 %copy-start.12 = (s32[4]{0:T(128)}, s32[4]{0:T(128)S(1)}, u32[]{:S(2)}) copy-start(s32[4]{0:T(128)S(1)} %pad_add_fusion.refs_0_.scal_ref) | copy-start | bytes 52
  90.1 19.8 %copy-start.2 = (bf16[4,2,16,256]{3,2,1,0:T(8,128)(2,1)}, bf16[4,2,16,256]{3,2,1,0:T(8,128)(2,1)S(1)}, u32[]{:S(2)}) copy-start(bf16[4,2,16,256]{3,2,1,0:T(8,128)(2,1)S(1)} %collective-permute-done.4.refs_5_.refs_7_) | copy-start | bytes 196612
  90.2 19.8 %copy-start.4 = (bf16[4,2,16,256]{3,2,1,0:T(8,128)(2,1)}, bf16[4,2,16,256]{3,2,1,0:T(8,128)(2,1)S(1)}, u32[]{:S(2)}) copy-start(bf16[4,2,16,256]{3,2,1,0:T(8,128)(2,1)S(1)} %collective-permute-done.5.refs_6_.refs_8_) | copy-start | bytes 196612
  90.2 19.8 %copy-start.6 = (bf16[4,2,16,256]{3,2,1,0:T(8,128)(2,1)}, bf16[4,2,16,256]{3,2,1,0:T(8,128)(2,1)S(1)}, u32[]{:S(2)}) copy-start(bf16[4,2,16,256]{3,2,1,0:T(8,128)(2,1)S(1)} %collective-permute-done.6.refs_7_.refs_9_) | copy-start | bytes 196612
  90.2 19.8 %copy-start.8 = (bf16[4,2,16,256]{3,2,1,0:T(8,128)(2,1)}, bf16[4,2,16,256]{3,2,1,0:T(8,128)(2,1)S(1)}, u32[]{:S(2)}) copy-start(bf16[4,2,16,256]{3,2,1,0:T(8,128)(2,1)S(1)} %collective-permute-done.7.refs_8_.refs_10_) | copy-start | bytes 196612
  91.1 18.8 %copy-start.10 = (bf16[4,2,16,256]{3,2,1,0:T(8,128)(2,1)}, bf16[4,2,16,256]{3,2,1,0:T(8,128)(2,1)S(1)}, u32[]{:S(2)}) copy-start(bf16[4,2,16,256]{3,2,1,0:T(8,128)(2,1)S(1)} %collective-permute-done.8.refs_9_.refs_11_) | copy-start | bytes 196612
  94.0 16.0 %collective-permute-start.9 = (f32[2,2,512]{2,1,0:T(2,128)S(1)}, f32[2,2,512]{2,1,0:T(2,128)S(1)}, u32[]{:S(2)}, u32[]{:S(2)}) collective-permute-start(f32[2,2,512]{2,1,0:T(2,128)S(1)} %off_stats.1), channel_id=1, source_target_pairs={{0,8},{1,9},{2,10},{3,11},{4,12},{5,13},{6,14},{7,15},{16,24},{17,... | collective-permute-start | bytes 24584 | tf_op jit(solution)/shard_map/ppermute | solution.py:540
  164.6 16.8 %all-to-all-start.2 = ((f32[32,2,128]{2,1,0:T(2,128)}), f32[32,2,128]{2,1,0:T(2,128)S(1)}, u32[]{:S(2)}, u32[]{:S(2)}) async-start(f32[32,2,128]{2,1,0:T(2,128)} %copy.18), calls=%async_computation.2 | async-start | bytes 65536 | tf_op jit(solution)/shard_map/all_to_all | solution.py:536
  182.1 6.7 %copy-start.15 = (f32[4,1,512]{2,1,0:T(1,128)}, f32[4,1,512]{2,1,0:T(1,128)S(1)}, u32[]{:S(2)}) copy-start(f32[4,1,512]{2,1,0:T(1,128)S(1)} %get-tuple-element.47) | copy-start | bytes 24580
  182.1 14.5 %collective-permute-start.10 = (f32[2,2,512]{2,1,0:T(2,128)S(1)}, f32[2,2,512]{2,1,0:T(2,128)S(1)}, u32[]{:S(2)}, u32[]{:S(2)}) collective-permute-start(f32[2,2,512]{2,1,0:T(2,128)S(1)} %fusion.3), channel_id=1, source_target_pairs={{8,0},{9,1},{10,2},{11,3},{12,4},{13,5},{14,6},{15,7},{24,16},{25,... | collective-permute-start | bytes 24584 | tf_op jit(solution)/shard_map/ppermute | solution.py:540
  188.8 78.3 %all-to-all-start.3 = ((bf16[32,3,16,512]{3,2,1,0:T(8,128)(2,1)}), bf16[32,3,16,512]{3,2,1,0:T(8,128)(2,1)}, u32[]{:S(2)}, u32[]{:S(2)}) async-start(bf16[32,3,16,512]{3,2,1,0:T(8,128)(2,1)} %col_grads.1), calls=%async_computation.3 | async-start | bytes 3145728 | tf_op jit(solution)/shard_map/all_to_all | solution.py:536
  201.5 20.6 %collective-permute-start.11 = (bf16[2,64,256]{2,1,0:T(8,128)(2,1)S(1)}, bf16[2,64,256]{2,1,0:T(8,128)(2,1)S(1)}, u32[]{:S(2)}, u32[]{:S(2)}) collective-permute-start(bf16[2,64,256]{2,1,0:T(8,128)(2,1)S(1)} %get-tuple-element.45), channel_id=1, source_target_pairs={{0,1},{1,0},{2,3},{3,2},{4,5},{5,4},{6,7},{7,6},{8,9},{9,8},{10,11... | collective-permute-start | bytes 196616 | tf_op jit(solution)/shard_map/ppermute | solution.py:544
  203.4 20.9 %collective-permute-start.12 = (bf16[2,64,256]{2,1,0:T(8,128)(2,1)S(1)}, bf16[2,64,256]{2,1,0:T(8,128)(2,1)S(1)}, u32[]{:S(2)}, u32[]{:S(2)}) collective-permute-start(bf16[2,64,256]{2,1,0:T(8,128)(2,1)S(1)} %get-tuple-element.44), channel_id=1, source_target_pairs={{0,2},{1,3},{2,0},{3,1},{4,6},{5,7},{6,4},{7,5},{8,10},{9,11},{10,... | collective-permute-start | bytes 196616 | tf_op jit(solution)/shard_map/ppermute | solution.py:544
  206.1 22.9 %collective-permute-start.13 = (bf16[2,64,256]{2,1,0:T(8,128)(2,1)S(1)}, bf16[2,64,256]{2,1,0:T(8,128)(2,1)S(1)}, u32[]{:S(2)}, u32[]{:S(2)}) collective-permute-start(bf16[2,64,256]{2,1,0:T(8,128)(2,1)S(1)} %get-tuple-element.43), channel_id=1, source_target_pairs={{0,3},{1,2},{2,1},{3,0},{4,7},{5,6},{6,5},{7,4},{8,11},{9,10},{10,... | collective-permute-start | bytes 196616 | tf_op jit(solution)/shard_map/ppermute | solution.py:544
  209.1 19.9 %collective-permute-start.14 = (bf16[2,64,256]{2,1,0:T(8,128)(2,1)S(1)}, bf16[2,64,256]{2,1,0:T(8,128)(2,1)S(1)}, u32[]{:S(2)}, u32[]{:S(2)}) collective-permute-start(bf16[2,64,256]{2,1,0:T(8,128)(2,1)S(1)} %get-tuple-element.42), channel_id=1, source_target_pairs={{0,4},{1,5},{2,6},{3,7},{4,0},{5,1},{6,2},{7,3},{8,12},{9,13},{10,... | collective-permute-start | bytes 196616 | tf_op jit(solution)/shard_map/ppermute | solution.py:544
  212.3 16.8 %collective-permute-start.15 = (bf16[2,64,256]{2,1,0:T(8,128)(2,1)S(1)}, bf16[2,64,256]{2,1,0:T(8,128)(2,1)S(1)}, u32[]{:S(2)}, u32[]{:S(2)}) collective-permute-start(bf16[2,64,256]{2,1,0:T(8,128)(2,1)S(1)} %get-tuple-element.41), channel_id=1, source_target_pairs={{0,5},{1,4},{2,7},{3,6},{4,1},{5,0},{6,3},{7,2},{8,13},{9,12},{10,... | collective-permute-start | bytes 196616 | tf_op jit(solution)/shard_map/ppermute | solution.py:544
  222.0 7.6 %collective-permute-start.16 = (bf16[2,64,256]{2,1,0:T(8,128)(2,1)S(1)}, bf16[2,64,256]{2,1,0:T(8,128)(2,1)S(1)}, u32[]{:S(2)}, u32[]{:S(2)}) collective-permute-start(bf16[2,64,256]{2,1,0:T(8,128)(2,1)S(1)} %get-tuple-element.40), channel_id=1, source_target_pairs={{0,6},{1,7},{2,4},{3,5},{4,2},{5,3},{6,0},{7,1},{8,14},{9,15},{10,... | collective-permute-start | bytes 196616 | tf_op jit(solution)/shard_map/ppermute | solution.py:544
  224.3 7.2 %collective-permute-start.17 = (bf16[2,64,256]{2,1,0:T(8,128)(2,1)S(1)}, bf16[2,64,256]{2,1,0:T(8,128)(2,1)S(1)}, u32[]{:S(2)}, u32[]{:S(2)}) collective-permute-start(bf16[2,64,256]{2,1,0:T(8,128)(2,1)S(1)} %get-tuple-element.39), channel_id=1, source_target_pairs={{0,7},{1,6},{2,5},{3,4},{4,3},{5,2},{6,1},{7,0},{8,15},{9,14},{10,... | collective-permute-start | bytes 196616 | tf_op jit(solution)/shard_map/ppermute | solution.py:544
  267.1 54.1 %collective-permute-start.18 = (bf16[8,2,64,256]{3,2,1,0:T(8,128)(2,1)S(1)}, bf16[8,2,64,256]{3,2,1,0:T(8,128)(2,1)S(1)}, u32[]{:S(2)}, u32[]{:S(2)}) collective-permute-start(bf16[8,2,64,256]{3,2,1,0:T(8,128)(2,1)S(1)} %bitcast_dynamic-update-slice_fusion), channel_id=1, source_target_pairs={{0,8},{1,9},{2,10},{3,11},{4,12},{5,13},{6,14},{7,15},{8,0},{9,1},... | collective-permute-start | bytes 1572872 | tf_op jit(solution)/shard_map/ppermute | solution.py:544
  283.9 37.4 %all-to-all-start.4 = ((bf16[8,4,3,16,512]{4,3,2,1,0:T(8,128)(2,1)}), bf16[8,4,3,16,512]{4,3,2,1,0:T(8,128)(2,1)}, u32[]{:S(2)}, u32[]{:S(2)}) async-start(bf16[8,4,3,16,512]{4,3,2,1,0:T(8,128)(2,1)} %bitcast.30), calls=%async_computation.4 | async-start | bytes 3145728 | tf_op jit(solution)/shard_map/all_to_all | solution.py:531
  (13 other events, 26.9 us)

commit v7 on v6

--- a/solution.py
+++ b/solution.py
@@ -10,6 +10,8 @@
 HEAD = 128
 CB = 128
 HALVES = 2
+FIRST_SUBS = 1
+FIRST_UNITS, SPLIT_UNITS, FULL_UNITS, BACK_UNITS = 40, 100, 40, 40
 VMEM_BYTES = 16 * 1024 * 1024
 PACK_BYTES = 60 * 1024 * 1024
 
@@ -41,15 +43,19 @@
     )
 
 
-def pack_body(k_ref, v_ref, q_ref, g_ref, far_a_ref, far_b_ref, out_ref, near_sem, far_sem):
-    groups, feats, far_feats = out_ref.shape[0], out_ref.shape[-1], far_a_ref.shape[-1]
+def pack_body(k_ref, v_ref, q_ref, g_ref, first_ref, second_ref, out_ref, near_sem, far_sem):
+    groups, feats, far_feats = out_ref.shape[0], out_ref.shape[-1], first_ref.shape[-1]
+    cut = first_ref.shape[1]
     lower = lax.axis_index("narrow") < groups
 
     def far_copies(pair, first):
-        for ref, far_ref in zip(pair, (far_a_ref, far_b_ref)):
+        for a, ref in enumerate(pair):
             for j in range(groups):
-                src = ref.at[:, :, pl.ds(j * feats + first, far_feats)]
-                yield pltpu.make_async_copy(src, far_ref.at[j], far_sem)
+                lanes = pl.ds(j * feats + first, far_feats)
+                src = ref.at[:cut, :, lanes]
+                yield pltpu.make_async_copy(src, first_ref.at[j, :, a], far_sem)
+                src = ref.at[cut:, :, lanes]
+                yield pltpu.make_async_copy(src, second_ref.at[j, :, a], far_sem)
 
     def near_copies():
         for j in range(groups):
@@ -77,8 +83,12 @@
 
 def pack(k, v, q, g, groups, subs, cols):
     near_feats = k.shape[1] // groups
-    far = (subs, cols, near_feats // HALVES)
-    shapes = [far, far, (subs, 4, cols, near_feats)]
+    far_feats = near_feats // HALVES
+    shapes = [
+        (FIRST_SUBS, 2, cols, far_feats),
+        (subs - FIRST_SUBS, 2, cols, far_feats),
+        (subs, 4, cols, near_feats),
+    ]
     split = [a.reshape(subs, cols, a.shape[1]) for a in (k, v, q, g)]
     return pl.pallas_call(
         pack_body,
@@ -93,45 +103,48 @@
 
 STATS_STEP = 128
 GRADS_STEP = 256
-LONG = pl.CostEstimate(flops=200_000_000_000, bytes_accessed=400 << 20, transcendentals=0)
+def long(units):
+    return pl.CostEstimate(flops=units * 10**9, bytes_accessed=units << 21, transcendentals=0)
 
 
 def hold_body(in_ref, out_ref):
     out_ref[...] = jnp.zeros_like(out_ref)
 
 
-def hold(arr):
+def hold(arr, units):
     return pl.pallas_call(
         hold_body,
         in_specs=[pl.BlockSpec(memory_space=pl.ANY)],
         out_specs=pl.BlockSpec(memory_space=pltpu.VMEM),
         out_shape=jax.ShapeDtypeStruct((8, 128), f32),
         compiler_params=pltpu.CompilerParams(vmem_limit_bytes=1024 * 1024),
-        cost_estimate=LONG,
+        cost_estimate=long(units),
         name="hold",
     )(arr)
 
 
-def split_body(a_ref, b_ref, token_ref, *out_refs):
+def split_body(first_ref, second_ref, token_ref, *out_refs):
     groups = len(out_refs)
     near = lax.rem(lax.axis_index("narrow"), groups)
     for step, ref in enumerate(out_refs):
-        for i, far_ref in enumerate((a_ref, b_ref)):
-            ref[:, i] = far_ref[near ^ step]
-
-
-def split(far_a, far_b, token):
-    groups, subs, cols, feats = far_a.shape
+        cut = first_ref.shape[1]
+        ref[:cut] = first_ref[near ^ step]
+        ref[cut:] = second_ref[near ^ step]
+
+
+def split(first, second, token):
+    groups, _, arrays, cols, feats = first.shape
+    subs = first.shape[1] + second.shape[1]
     whole = pl.BlockSpec(memory_space=pltpu.VMEM)
     return pl.pallas_call(
         split_body,
-        in_specs=[whole] * 2 + [pl.BlockSpec(memory_space=pl.ANY)],
+        in_specs=[whole, whole, pl.BlockSpec(memory_space=pl.ANY)],
         out_specs=[whole] * groups,
-        out_shape=[jax.ShapeDtypeStruct((subs, 2, cols, feats), bf16)] * groups,
+        out_shape=[jax.ShapeDtypeStruct((subs, arrays, cols, feats), bf16)] * groups,
         compiler_params=pltpu.CompilerParams(vmem_limit_bytes=VMEM_BYTES),
-        cost_estimate=LONG,
+        cost_estimate=long(SPLIT_UNITS),
         name="split",
-    )(far_a, far_b, token)
+    )(first, second, token)
 
 
 def unpack_body(scal_ref, in_ref, far_ref, token_ref, q_ref, k_ref, v_ref):
@@ -555,17 +568,17 @@
     first_row = lax.dynamic_index_in_dim(col_start, block_id, keepdims=False)
     scal = jnp.stack([half, first_col, first_row, near_index]).astype(jnp.int32)
 
-    far_a, far_b, packed = pack(key_in, value_in, query_in, grad_out, groups, subs, cols)
+    far_first, far_second, packed = pack(key_in, value_in, query_in, grad_out, groups, subs, cols)
     near_feats = feats // groups
     heads = near_feats // HEAD
     near_heads = heads // HALVES
-    far_a = swap(far_a, groups)
-    token = hold(far_a)
-    far_b = swap(far_b, groups)
+    far_first = swap(far_first, groups)
+    token = hold(far_first, FIRST_UNITS)
+    far_second = swap(far_second, groups)
     t = exchange_near(packed).reshape(lanes, 4, cols, near_feats)
     t, token = lax.optimization_barrier((t, token))
     by_col = exchange_wide(t)
-    pieces = spread(split(far_a, far_b, token))
+    pieces = spread(split(far_first, far_second, token))
     diag_part = stats_call(row_stats_body, scale, scal, (t,), "row_stats", 4)
     own_off = off_stats(scale, scal, t, pieces)
     off_part = jnp.concatenate([shift(own_off, 0, 1), own_off])
@@ -581,7 +594,7 @@
     row_full = jnp.stack([row_lse, row_delta], axis=1)
 
     far_full = shift(row_full[:near_heads], 1, 0)
-    token = hold(far_full)
+    token = hold(far_full, FULL_UNITS)
     from_col = exchange_wide(col_grads(scale, scal, by_col, col_part, got[0]))
     off_full = jnp.where(half == 1, row_full[near_heads:], far_full)
     off_terms, far_terms = off_grads(scale, scal, t, off_full, token, pieces)
@@ -593,7 +606,7 @@
     far_terms = jnp.stack(spread(by_step))
     from_col, far_terms, row_terms = lax.optimization_barrier((from_col, far_terms, row_terms))
     back = swap(far_terms, groups)
-    token = hold(back)
+    token = hold(back, BACK_UNITS)
     joined = join(row_terms, from_col)
     out = exchange_near(joined.reshape(groups, subs, 3, cols, near_feats))
     return unpack(scal, out, back, token, tokens, feats)

time: 327 us -> 322 us (0.985)
  the two profiles are of different devices: /device:TPU:58 before, /device:TPU:56 now
where the time goes in v7:
time: 322 us; the launch traced here: 321 us
  waiting for transfers between devices  169 us (52%)
  starting transfers between devices  114 us (35%)
  Pallas kernels  28.1 us (9%)
  local copies, waits for them, and re-layouts  6.57 us (2%)
    all_to_all x3, waiting for transfers between devices, exchange_wide(): return lax.all_to_all(arr, 'wide', split_axis=0, concat_axis=0, tiled=True)  93.1 us
    ppermute x17, starting transfers between devices, swap(): return lax.ppermute(arr, 'narrow', pairs)  72.5 us
    ppermute x17, waiting for transfers between devices, swap(): return lax.ppermute(arr, 'narrow', pairs)  60.6 us
    all_to_all x3, starting transfers between devices, exchange_wide(): return lax.all_to_all(arr, 'wide', split_axis=0, concat_axis=0, tiled=True)  20.1 us
    ppermute x2, starting transfers between devices, shift(): return lax.ppermute(arr, 'narrow', pairs)  12.3 us
    all_to_all x2, waiting for transfers between devices, exchange_near(): lax.all_to_all(arr, 'narrow', split_axis=0, concat_axis=0, axis_index_gro...  11.3 us
    all_to_all x2, starting transfers between devices, exchange_near(): lax.all_to_all(arr, 'narrow', split_axis=0, concat_axis=0, axis_index_gro...  9.34 us
    pallas_call x2, Pallas kernels, off_call(): pl.pallas_call(lambda *refs: body(scale, *refs), grid_spec=pltpu.Prefetch...  6.61 us
  transfers between devices with their start and end apart: 24, of which 11 were waited for; matrix products, arithmetic and copies ran while one was open for 1% of the time, Pallas kernels for 6%

profile of v7, /device:TPU:56, one launch (start us, length us, event | category | flops | bytes accessed | tf_op | source)
XLA Modules:
  0.0 320.7 jit_solution(1543293438825345381)
XLA Ops:
  0.6 3.3 %pack.1 = (bf16[8,1,2,16,256]{4,3,2,1,0:T(8,128)(2,1)}, bf16[8,3,2,16,256]{4,3,2,1,0:T(8,128)(2,1)}, bf16[8,4,4,16,512]{4,3,2,1,0:T(8,128)(2,1)}) custom-call(bf16[4,16,4096]{2,1,0:T(8,128)(2,1)} %bitcast.71, bf16[4,16,4096]{2,1,0:T(8,128)(2,1)} %bitcast.72, bf16[4,16,4096]{2,1,0:T(8,128)(2,1)} %bitcast.73, bf16[4,16,4096]{2,1,0:T(8,128)(2,1)} %bitcast.74), custom_call_target="tpu_custom_call" | custom-call | tf_op jit(solution)/shard_map/pack/pallas_call | solution.py:93
  4.0 14.8 %collective-permute-start = (bf16[8,1,2,16,256]{4,3,2,1,0:T(8,128)(2,1)}, bf16[8,1,2,16,256]{4,3,2,1,0:T(8,128)(2,1)S(1)}, u32[]{:S(2)}, u32[]{:S(2)}) collective-permute-start(bf16[8,1,2,16,256]{4,3,2,1,0:T(8,128)(2,1)} %get-tuple-element.22), channel_id=1, source_target_pairs={{0,8},{1,9},{2,10},{3,11},{4,12},{5,13},{6,14},{7,15},{8,0},{9,1},... | collective-permute-start | bytes 393224 | tf_op jit(solution)/shard_map/ppermute | solution.py:557
  18.8 4.8 %all-to-all-start = ((bf16[8,4,4,16,512]{4,3,2,1,0:T(8,128)(2,1)}), bf16[8,4,4,16,512]{4,3,2,1,0:T(8,128)(2,1)}, u32[]{:S(2)}, u32[]{:S(2)}) async-start(bf16[8,4,4,16,512]{4,3,2,1,0:T(8,128)(2,1)} %get-tuple-element.21), calls=%async_computation | async-start | bytes 4194304 | tf_op jit(solution)/shard_map/all_to_all | solution.py:544
  25.6 12.0 %collective-permute-done.in_ref.first_ref = bf16[8,1,2,16,256]{4,3,2,1,0:T(8,128)(2,1)S(1)} collective-permute-done((bf16[8,1,2,16,256]{4,3,2,1,0:T(8,128)(2,1)}, bf16[8,1,2,16,256]{4,3,2,1,0:T(8,128)(2,1)S(1)}, u32[]{:S(2)}, u32[]{:S(2)}) %collective-permute-start) | collective-permute-done | bytes 131104 | tf_op jit(solution)/shard_map/ppermute | solution.py:557
  37.6 11.3 %all-to-all-done = bf16[8,4,4,16,512]{4,3,2,1,0:T(8,128)(2,1)} async-done(((bf16[8,4,4,16,512]{4,3,2,1,0:T(8,128)(2,1)}), bf16[8,4,4,16,512]{4,3,2,1,0:T(8,128)(2,1)}, u32[]{:S(2)}, u32[]{:S(2)}) %all-to-all-start) | async-done | bytes 2097184 | tf_op jit(solution)/shard_map/all_to_all | solution.py:544
  48.9 8.6 %all-to-all-start.1 = ((bf16[32,4,16,512]{3,2,1,0:T(8,128)(2,1)}), bf16[32,4,16,512]{3,2,1,0:T(8,128)(2,1)S(1)}, u32[]{:S(2)}, u32[]{:S(2)}) async-start(bf16[32,4,16,512]{3,2,1,0:T(8,128)(2,1)} %bitcast.6.refs_1_), calls=%async_computation.1 | async-start | bytes 4194304 | tf_op jit(solution)/shard_map/all_to_all | solution.py:549
  57.6 11.1 %collective-permute-done.1.second_ref = bf16[8,3,2,16,256]{4,3,2,1,0:T(8,128)(2,1)S(1)} collective-permute-done((bf16[8,3,2,16,256]{4,3,2,1,0:T(8,128)(2,1)S(1)}, bf16[8,3,2,16,256]{4,3,2,1,0:T(8,128)(2,1)S(1)}, u32[]{:S(2)}, u32[]{:S(2)}) %collective-permute-start.1) | collective-permute-done | bytes 393248 | tf_op jit(solution)/shard_map/ppermute | solution.py:557
  70.7 3.1 collective-permute-start.3
  75.1 2.5 collective-permute-start.4
  77.6 3.5 %collective-permute-start.5 = (bf16[4,2,16,256]{3,2,1,0:T(8,128)(2,1)S(1)}, bf16[4,2,16,256]{3,2,1,0:T(8,128)(2,1)S(1)}, u32[]{:S(2)}, u32[]{:S(2)}) collective-permute-start(bf16[4,2,16,256]{3,2,1,0:T(8,128)(2,1)S(1)} %get-tuple-element.30), channel_id=1, source_target_pairs={{0,4},{1,5},{2,6},{3,7},{4,0},{5,1},{6,2},{7,3},{8,12},{9,13},{10,... | collective-permute-start | bytes 196616 | tf_op jit(solution)/shard_map/ppermute | solution.py:557
  81.1 3.5 %collective-permute-start.6 = (bf16[4,2,16,256]{3,2,1,0:T(8,128)(2,1)S(1)}, bf16[4,2,16,256]{3,2,1,0:T(8,128)(2,1)S(1)}, u32[]{:S(2)}, u32[]{:S(2)}) collective-permute-start(bf16[4,2,16,256]{3,2,1,0:T(8,128)(2,1)S(1)} %get-tuple-element.31), channel_id=1, source_target_pairs={{0,5},{1,4},{2,7},{3,6},{4,1},{5,0},{6,3},{7,2},{8,13},{9,12},{10,... | collective-permute-start | bytes 196616 | tf_op jit(solution)/shard_map/ppermute | solution.py:557
  84.6 2.7 collective-permute-start.7
  87.3 4.2 %collective-permute-start.8 = (bf16[4,2,16,256]{3,2,1,0:T(8,128)(2,1)S(1)}, bf16[4,2,16,256]{3,2,1,0:T(8,128)(2,1)S(1)}, u32[]{:S(2)}, u32[]{:S(2)}) collective-permute-start(bf16[4,2,16,256]{3,2,1,0:T(8,128)(2,1)S(1)} %get-tuple-element.33), channel_id=1, source_target_pairs={{0,7},{1,6},{2,5},{3,4},{4,3},{5,2},{6,1},{7,0},{8,15},{9,14},{10,... | collective-permute-start | bytes 196616 | tf_op jit(solution)/shard_map/ppermute | solution.py:557
  94.7 2.9 off_stats.1
  97.6 11.0 %collective-permute-start.9 = (f32[2,2,512]{2,1,0:T(2,128)S(1)}, f32[2,2,512]{2,1,0:T(2,128)S(1)}, u32[]{:S(2)}, u32[]{:S(2)}) collective-permute-start(f32[2,2,512]{2,1,0:T(2,128)S(1)} %off_stats.1), channel_id=1, source_target_pairs={{0,8},{1,9},{2,10},{3,11},{4,12},{5,13},{6,14},{7,15},{16,24},{17,... | collective-permute-start | bytes 24584 | tf_op jit(solution)/shard_map/ppermute | solution.py:553
  108.6 3.8 %row_stats.1 = f32[4,2,512]{2,1,0:T(2,128)S(1)} custom-call(s32[4]{0:T(128)S(1)} %pad_add_fusion.refs_0_.scal_ref, bf16[32,4,16,512]{3,2,1,0:T(8,128)(2,1)} %bitcast.6.refs_1_), custom_call_target="tpu_custom_call" | custom-call | flops 1342177280 | bytes 4194304 | tf_op jit(solution)/shard_map/row_stats/pallas_call | solution.py:405
  112.5 46.9 %all-to-all-done.1.refs_1_ = bf16[32,4,16,512]{3,2,1,0:T(8,128)(2,1)S(1)} async-done(((bf16[32,4,16,512]{3,2,1,0:T(8,128)(2,1)}), bf16[32,4,16,512]{3,2,1,0:T(8,128)(2,1)S(1)}, u32[]{:S(2)}, u32[]{:S(2)}) %all-to-all-start.1) | async-done | bytes 2097184 | tf_op jit(solution)/shard_map/all_to_all | solution.py:549
  162.2 6.5 %all-to-all-start.2 = ((f32[32,2,128]{2,1,0:T(2,128)}), f32[32,2,128]{2,1,0:T(2,128)S(1)}, u32[]{:S(2)}, u32[]{:S(2)}) async-start(f32[32,2,128]{2,1,0:T(2,128)} %copy.18), calls=%async_computation.2 | async-start | bytes 65536 | tf_op jit(solution)/shard_map/all_to_all | solution.py:549
  168.7 11.4 %all-to-all-done.2 = f32[32,2,128]{2,1,0:T(2,128)S(1)} async-done(((f32[32,2,128]{2,1,0:T(2,128)}), f32[32,2,128]{2,1,0:T(2,128)S(1)}, u32[]{:S(2)}, u32[]{:S(2)}) %all-to-all-start.2) | async-done | bytes 32800 | tf_op jit(solution)/shard_map/all_to_all | solution.py:549
  182.2 3.1 col_grads.1
  186.5 5.0 %all-to-all-start.3 = ((bf16[32,3,16,512]{3,2,1,0:T(8,128)(2,1)}), bf16[32,3,16,512]{3,2,1,0:T(8,128)(2,1)S(1)}, u32[]{:S(2)}, u32[]{:S(2)}) async-start(bf16[32,3,16,512]{3,2,1,0:T(8,128)(2,1)} %copy-done), calls=%async_computation.3 | async-start | bytes 3145728 | tf_op jit(solution)/shard_map/all_to_all | solution.py:549
  191.4 3.8 %collective-permute-done.10.in_ref = f32[2,2,512]{2,1,0:T(2,128)S(1)} collective-permute-done((f32[2,2,512]{2,1,0:T(2,128)S(1)}, f32[2,2,512]{2,1,0:T(2,128)S(1)}, u32[]{:S(2)}, u32[]{:S(2)}) %collective-permute-start.10) | collective-permute-done | bytes 8224 | tf_op jit(solution)/shard_map/ppermute | solution.py:553
  195.3 3.8 %off_grads.1 = (f32[2,512,256]{2,1,0:T(8,128)S(1)}, bf16[8,2,64,256]{3,2,1,0:T(8,128)(2,1)S(1)}) custom-call(s32[4]{0:T(128)S(1)} %pad_add_fusion.refs_0_.scal_ref, bf16[32,4,16,512]{3,2,1,0:T(8,128)(2,1)} %bitcast.6.refs_1_, f32[2,2,512]{2,1,0:T(2,128)S(1)} %fusion.2.refs_2_, f32[8,128]{1,0:T(8,128)S(1)} %hold.4.refs_3_, ...), custom_call_target="tpu_custom_call" | custom-call | flops 1677721600 | bytes 4194304 | tf_op jit(solution)/shard_map/off_grads/pallas_call | solution.py:332
  203.4 3.4 %collective-permute-start.13 = (bf16[2,64,256]{2,1,0:T(8,128)(2,1)S(1)}, bf16[2,64,256]{2,1,0:T(8,128)(2,1)S(1)}, u32[]{:S(2)}, u32[]{:S(2)}) collective-permute-start(bf16[2,64,256]{2,1,0:T(8,128)(2,1)S(1)} %get-tuple-element.43), channel_id=1, source_target_pairs={{0,3},{1,2},{2,1},{3,0},{4,7},{5,6},{6,5},{7,4},{8,11},{9,10},{10,... | collective-permute-start | bytes 196616 | tf_op jit(solution)/shard_map/ppermute | solution.py:557
  206.7 3.0 collective-permute-start.14
  209.8 4.0 %collective-permute-start.15 = (bf16[2,64,256]{2,1,0:T(8,128)(2,1)S(1)}, bf16[2,64,256]{2,1,0:T(8,128)(2,1)S(1)}, u32[]{:S(2)}, u32[]{:S(2)}) collective-permute-start(bf16[2,64,256]{2,1,0:T(8,128)(2,1)S(1)} %get-tuple-element.41), channel_id=1, source_target_pairs={{0,5},{1,4},{2,7},{3,6},{4,1},{5,0},{6,3},{7,2},{8,13},{9,12},{10,... | collective-permute-start | bytes 196616 | tf_op jit(solution)/shard_map/ppermute | solution.py:557
  213.7 5.3 %row_grads.1.row_ref = bf16[32,3,16,512]{3,2,1,0:T(8,128)(2,1)S(1)} custom-call(s32[4]{0:T(128)S(1)} %pad_add_fusion.refs_0_.scal_ref, bf16[32,4,16,512]{3,2,1,0:T(8,128)(2,1)} %bitcast.6.refs_1_, f32[4,2,512]{2,1,0:T(2,128)S(1)} %pad_maximum_fusion.1.refs_2_, f32[2,512,256]{2,1,0:T(8,128)S(1)} %get-tuple-element.35.refs_3_), custom_call_target="tpu_custom_call" | custom-call | flops 2684354560 | bytes 4194304 | tf_op jit(solution)/shard_map/row_grads/pallas_call | solution.py:481
  222.4 4.8 %collective-permute-start.17 = (bf16[2,64,256]{2,1,0:T(8,128)(2,1)S(1)}, bf16[2,64,256]{2,1,0:T(8,128)(2,1)S(1)}, u32[]{:S(2)}, u32[]{:S(2)}) collective-permute-start(bf16[2,64,256]{2,1,0:T(8,128)(2,1)S(1)} %get-tuple-element.39), channel_id=1, source_target_pairs={{0,7},{1,6},{2,5},{3,4},{4,3},{5,2},{6,1},{7,0},{8,15},{9,14},{10,... | collective-permute-start | bytes 196616 | tf_op jit(solution)/shard_map/ppermute | solution.py:557
  229.5 34.8 %all-to-all-done.3.col_ref = bf16[32,3,16,512]{3,2,1,0:T(8,128)(2,1)S(1)} async-done(((bf16[32,3,16,512]{3,2,1,0:T(8,128)(2,1)}), bf16[32,3,16,512]{3,2,1,0:T(8,128)(2,1)S(1)}, u32[]{:S(2)}, u32[]{:S(2)}) %all-to-all-start.3) | async-done | bytes 1572896 | tf_op jit(solution)/shard_map/all_to_all | solution.py:549
  264.3 13.0 %collective-permute-start.18 = (bf16[8,2,64,256]{3,2,1,0:T(8,128)(2,1)S(1)}, bf16[8,2,64,256]{3,2,1,0:T(8,128)(2,1)S(1)}, u32[]{:S(2)}, u32[]{:S(2)}) collective-permute-start(bf16[8,2,64,256]{3,2,1,0:T(8,128)(2,1)S(1)} %bitcast_dynamic-update-slice_fusion), channel_id=1, source_target_pairs={{0,8},{1,9},{2,10},{3,11},{4,12},{5,13},{6,14},{7,15},{8,0},{9,1},... | collective-permute-start | bytes 1572872 | tf_op jit(solution)/shard_map/ppermute | solution.py:557
  280.5 4.5 %all-to-all-start.4 = ((bf16[8,4,3,16,512]{4,3,2,1,0:T(8,128)(2,1)}), bf16[8,4,3,16,512]{4,3,2,1,0:T(8,128)(2,1)S(1)}, u32[]{:S(2)}, u32[]{:S(2)}) async-start(bf16[8,4,3,16,512]{4,3,2,1,0:T(8,128)(2,1)} %bitcast.30), calls=%async_computation.4 | async-start | bytes 3145728 | tf_op jit(solution)/shard_map/all_to_all | solution.py:544
  285.0 33.3 %collective-permute-done.18.in_ref.far_ref = bf16[8,2,64,256]{3,2,1,0:T(8,128)(2,1)S(1)} collective-permute-done((bf16[8,2,64,256]{3,2,1,0:T(8,128)(2,1)S(1)}, bf16[8,2,64,256]{3,2,1,0:T(8,128)(2,1)S(1)}, u32[]{:S(2)}, u32[]{:S(2)}) %collective-permute-start.18) | collective-permute-done | bytes 524320 | tf_op jit(solution)/shard_map/ppermute | solution.py:557
  (69 shorter events, 29.7 us)
Async XLA Ops:
  4.0 33.6 %collective-permute-start = (bf16[8,1,2,16,256]{4,3,2,1,0:T(8,128)(2,1)}, bf16[8,1,2,16,256]{4,3,2,1,0:T(8,128)(2,1)S(1)}, u32[]{:S(2)}, u32[]{:S(2)}) collective-permute-start(bf16[8,1,2,16,256]{4,3,2,1,0:T(8,128)(2,1)} %get-tuple-element.22), channel_id=1, source_target_pairs={{0,8},{1,9},{2,10},{3,11},{4,12},{5,13},{6,14},{7,15},{8,0},{9,1},... | collective-permute-start | bytes 393224 | tf_op jit(solution)/shard_map/ppermute | solution.py:557
  18.8 4.8 %copy-start.3 = (bf16[8,3,2,16,256]{4,3,2,1,0:T(8,128)(2,1)S(1)}, bf16[8,3,2,16,256]{4,3,2,1,0:T(8,128)(2,1)}, u32[]{:S(2)}) copy-start(bf16[8,3,2,16,256]{4,3,2,1,0:T(8,128)(2,1)} %get-tuple-element.24) | copy-start | bytes 1179652
  18.8 30.1 %all-to-all-start = ((bf16[8,4,4,16,512]{4,3,2,1,0:T(8,128)(2,1)}), bf16[8,4,4,16,512]{4,3,2,1,0:T(8,128)(2,1)}, u32[]{:S(2)}, u32[]{:S(2)}) async-start(bf16[8,4,4,16,512]{4,3,2,1,0:T(8,128)(2,1)} %get-tuple-element.21), calls=%async_computation | async-start | bytes 4194304 | tf_op jit(solution)/shard_map/all_to_all | solution.py:544
  23.6 45.1 %collective-permute-start.1 = (bf16[8,3,2,16,256]{4,3,2,1,0:T(8,128)(2,1)S(1)}, bf16[8,3,2,16,256]{4,3,2,1,0:T(8,128)(2,1)S(1)}, u32[]{:S(2)}, u32[]{:S(2)}) collective-permute-start(bf16[8,3,2,16,256]{4,3,2,1,0:T(8,128)(2,1)S(1)} %copy-done.3), channel_id=1, source_target_pairs={{0,8},{1,9},{2,10},{3,11},{4,12},{5,13},{6,14},{7,15},{8,0},{9,1},... | collective-permute-start | bytes 1179656 | tf_op jit(solution)/shard_map/ppermute | solution.py:557
  48.9 110.6 %all-to-all-start.1 = ((bf16[32,4,16,512]{3,2,1,0:T(8,128)(2,1)}), bf16[32,4,16,512]{3,2,1,0:T(8,128)(2,1)S(1)}, u32[]{:S(2)}, u32[]{:S(2)}) async-start(bf16[32,4,16,512]{3,2,1,0:T(8,128)(2,1)} %bitcast.6.refs_1_), calls=%async_computation.1 | async-start | bytes 4194304 | tf_op jit(solution)/shard_map/all_to_all | solution.py:549
  57.5 16.4 %copy-start.4 = (s32[8]{0:T(128)S(1)}, s32[8]{0:T(128)}, u32[]{:S(2)}) copy-start(s32[8]{0:T(128)} %param.11) | copy-start | bytes 100
  57.5 16.9 %copy-start.5 = (s32[32]{0:T(128)S(1)}, s32[32]{0:T(128)}, u32[]{:S(2)}) copy-start(s32[32]{0:T(128)} %param.10) | copy-start | bytes 388
  68.7 15.9 %collective-permute-start.2 = (bf16[4,2,16,256]{3,2,1,0:T(8,128)(2,1)S(1)}, bf16[4,2,16,256]{3,2,1,0:T(8,128)(2,1)S(1)}, u32[]{:S(2)}, u32[]{:S(2)}) collective-permute-start(bf16[4,2,16,256]{3,2,1,0:T(8,128)(2,1)S(1)} %get-tuple-element.27), channel_id=1, source_target_pairs={{0,1},{1,0},{2,3},{3,2},{4,5},{5,4},{6,7},{7,6},{8,9},{9,8},{10,11... | collective-permute-start | bytes 196616 | tf_op jit(solution)/shard_map/ppermute | solution.py:557
  70.7 16.6 %collective-permute-start.3 = (bf16[4,2,16,256]{3,2,1,0:T(8,128)(2,1)S(1)}, bf16[4,2,16,256]{3,2,1,0:T(8,128)(2,1)S(1)}, u32[]{:S(2)}, u32[]{:S(2)}) collective-permute-start(bf16[4,2,16,256]{3,2,1,0:T(8,128)(2,1)S(1)} %get-tuple-element.28), channel_id=1, source_target_pairs={{0,2},{1,3},{2,0},{3,1},{4,6},{5,7},{6,4},{7,5},{8,10},{9,11},{10,... | collective-permute-start | bytes 196616 | tf_op jit(solution)/shard_map/ppermute | solution.py:557
  75.1 17.7 %collective-permute-start.4 = (bf16[4,2,16,256]{3,2,1,0:T(8,128)(2,1)S(1)}, bf16[4,2,16,256]{3,2,1,0:T(8,128)(2,1)S(1)}, u32[]{:S(2)}, u32[]{:S(2)}) collective-permute-start(bf16[4,2,16,256]{3,2,1,0:T(8,128)(2,1)S(1)} %get-tuple-element.29), channel_id=1, source_target_pairs={{0,3},{1,2},{2,1},{3,0},{4,7},{5,6},{6,5},{7,4},{8,11},{9,10},{10,... | collective-permute-start | bytes 196616 | tf_op jit(solution)/shard_map/ppermute | solution.py:557
  77.6 15.2 %collective-permute-start.5 = (bf16[4,2,16,256]{3,2,1,0:T(8,128)(2,1)S(1)}, bf16[4,2,16,256]{3,2,1,0:T(8,128)(2,1)S(1)}, u32[]{:S(2)}, u32[]{:S(2)}) collective-permute-start(bf16[4,2,16,256]{3,2,1,0:T(8,128)(2,1)S(1)} %get-tuple-element.30), channel_id=1, source_target_pairs={{0,4},{1,5},{2,6},{3,7},{4,0},{5,1},{6,2},{7,3},{8,12},{9,13},{10,... | collective-permute-start | bytes 196616 | tf_op jit(solution)/shard_map/ppermute | solution.py:557
  81.1 11.7 %collective-permute-start.6 = (bf16[4,2,16,256]{3,2,1,0:T(8,128)(2,1)S(1)}, bf16[4,2,16,256]{3,2,1,0:T(8,128)(2,1)S(1)}, u32[]{:S(2)}, u32[]{:S(2)}) collective-permute-start(bf16[4,2,16,256]{3,2,1,0:T(8,128)(2,1)S(1)} %get-tuple-element.31), channel_id=1, source_target_pairs={{0,5},{1,4},{2,7},{3,6},{4,1},{5,0},{6,3},{7,2},{8,13},{9,12},{10,... | collective-permute-start | bytes 196616 | tf_op jit(solution)/shard_map/ppermute | solution.py:557
  84.6 8.2 %collective-permute-start.7 = (bf16[4,2,16,256]{3,2,1,0:T(8,128)(2,1)S(1)}, bf16[4,2,16,256]{3,2,1,0:T(8,128)(2,1)S(1)}, u32[]{:S(2)}, u32[]{:S(2)}) collective-permute-start(bf16[4,2,16,256]{3,2,1,0:T(8,128)(2,1)S(1)} %get-tuple-element.32), channel_id=1, source_target_pairs={{0,6},{1,7},{2,4},{3,5},{4,2},{5,3},{6,0},{7,1},{8,14},{9,15},{10,... | collective-permute-start | bytes 196616 | tf_op jit(solution)/shard_map/ppermute | solution.py:557
  87.3 7.4 %collective-permute-start.8 = (bf16[4,2,16,256]{3,2,1,0:T(8,128)(2,1)S(1)}, bf16[4,2,16,256]{3,2,1,0:T(8,128)(2,1)S(1)}, u32[]{:S(2)}, u32[]{:S(2)}) collective-permute-start(bf16[4,2,16,256]{3,2,1,0:T(8,128)(2,1)S(1)} %get-tuple-element.33), channel_id=1, source_target_pairs={{0,7},{1,6},{2,5},{3,4},{4,3},{5,2},{6,1},{7,0},{8,15},{9,14},{10,... | collective-permute-start | bytes 196616 | tf_op jit(solution)/shard_map/ppermute | solution.py:557
  97.6 14.8 %collective-permute-start.9 = (f32[2,2,512]{2,1,0:T(2,128)S(1)}, f32[2,2,512]{2,1,0:T(2,128)S(1)}, u32[]{:S(2)}, u32[]{:S(2)}) collective-permute-start(f32[2,2,512]{2,1,0:T(2,128)S(1)} %off_stats.1), channel_id=1, source_target_pairs={{0,8},{1,9},{2,10},{3,11},{4,12},{5,13},{6,14},{7,15},{16,24},{17,... | collective-permute-start | bytes 24584 | tf_op jit(solution)/shard_map/ppermute | solution.py:553
  162.2 18.0 %all-to-all-start.2 = ((f32[32,2,128]{2,1,0:T(2,128)}), f32[32,2,128]{2,1,0:T(2,128)S(1)}, u32[]{:S(2)}, u32[]{:S(2)}) async-start(f32[32,2,128]{2,1,0:T(2,128)} %copy.18), calls=%async_computation.2 | async-start | bytes 65536 | tf_op jit(solution)/shard_map/all_to_all | solution.py:549
  180.9 14.4 %collective-permute-start.10 = (f32[2,2,512]{2,1,0:T(2,128)S(1)}, f32[2,2,512]{2,1,0:T(2,128)S(1)}, u32[]{:S(2)}, u32[]{:S(2)}) collective-permute-start(f32[2,2,512]{2,1,0:T(2,128)S(1)} %fusion.3), channel_id=1, source_target_pairs={{8,0},{9,1},{10,2},{11,3},{12,4},{13,5},{14,6},{15,7},{24,16},{25,... | collective-permute-start | bytes 24584 | tf_op jit(solution)/shard_map/ppermute | solution.py:553
  185.3 1.1 copy-start
  186.5 77.8 %all-to-all-start.3 = ((bf16[32,3,16,512]{3,2,1,0:T(8,128)(2,1)}), bf16[32,3,16,512]{3,2,1,0:T(8,128)(2,1)S(1)}, u32[]{:S(2)}, u32[]{:S(2)}) async-start(bf16[32,3,16,512]{3,2,1,0:T(8,128)(2,1)} %copy-done), calls=%async_computation.3 | async-start | bytes 3145728 | tf_op jit(solution)/shard_map/all_to_all | solution.py:549
  199.1 21.1 %collective-permute-start.11 = (bf16[2,64,256]{2,1,0:T(8,128)(2,1)S(1)}, bf16[2,64,256]{2,1,0:T(8,128)(2,1)S(1)}, u32[]{:S(2)}, u32[]{:S(2)}) collective-permute-start(bf16[2,64,256]{2,1,0:T(8,128)(2,1)S(1)} %get-tuple-element.45), channel_id=1, source_target_pairs={{0,1},{1,0},{2,3},{3,2},{4,5},{5,4},{6,7},{7,6},{8,9},{9,8},{10,11... | collective-permute-start | bytes 196616 | tf_op jit(solution)/shard_map/ppermute | solution.py:557
  201.1 21.3 %collective-permute-start.12 = (bf16[2,64,256]{2,1,0:T(8,128)(2,1)S(1)}, bf16[2,64,256]{2,1,0:T(8,128)(2,1)S(1)}, u32[]{:S(2)}, u32[]{:S(2)}) collective-permute-start(bf16[2,64,256]{2,1,0:T(8,128)(2,1)S(1)} %get-tuple-element.44), channel_id=1, source_target_pairs={{0,2},{1,3},{2,0},{3,1},{4,6},{5,7},{6,4},{7,5},{8,10},{9,11},{10,... | collective-permute-start | bytes 196616 | tf_op jit(solution)/shard_map/ppermute | solution.py:557
  203.4 23.8 %collective-permute-start.13 = (bf16[2,64,256]{2,1,0:T(8,128)(2,1)S(1)}, bf16[2,64,256]{2,1,0:T(8,128)(2,1)S(1)}, u32[]{:S(2)}, u32[]{:S(2)}) collective-permute-start(bf16[2,64,256]{2,1,0:T(8,128)(2,1)S(1)} %get-tuple-element.43), channel_id=1, source_target_pairs={{0,3},{1,2},{2,1},{3,0},{4,7},{5,6},{6,5},{7,4},{8,11},{9,10},{10,... | collective-permute-start | bytes 196616 | tf_op jit(solution)/shard_map/ppermute | solution.py:557
  206.7 20.5 %collective-permute-start.14 = (bf16[2,64,256]{2,1,0:T(8,128)(2,1)S(1)}, bf16[2,64,256]{2,1,0:T(8,128)(2,1)S(1)}, u32[]{:S(2)}, u32[]{:S(2)}) collective-permute-start(bf16[2,64,256]{2,1,0:T(8,128)(2,1)S(1)} %get-tuple-element.42), channel_id=1, source_target_pairs={{0,4},{1,5},{2,6},{3,7},{4,0},{5,1},{6,2},{7,3},{8,12},{9,13},{10,... | collective-permute-start | bytes 196616 | tf_op jit(solution)/shard_map/ppermute | solution.py:557
  209.8 17.5 %collective-permute-start.15 = (bf16[2,64,256]{2,1,0:T(8,128)(2,1)S(1)}, bf16[2,64,256]{2,1,0:T(8,128)(2,1)S(1)}, u32[]{:S(2)}, u32[]{:S(2)}) collective-permute-start(bf16[2,64,256]{2,1,0:T(8,128)(2,1)S(1)} %get-tuple-element.41), channel_id=1, source_target_pairs={{0,5},{1,4},{2,7},{3,6},{4,1},{5,0},{6,3},{7,2},{8,13},{9,12},{10,... | collective-permute-start | bytes 196616 | tf_op jit(solution)/shard_map/ppermute | solution.py:557
  219.1 1.2 copy-start.1
  220.2 7.6 %collective-permute-start.16 = (bf16[2,64,256]{2,1,0:T(8,128)(2,1)S(1)}, bf16[2,64,256]{2,1,0:T(8,128)(2,1)S(1)}, u32[]{:S(2)}, u32[]{:S(2)}) collective-permute-start(bf16[2,64,256]{2,1,0:T(8,128)(2,1)S(1)} %get-tuple-element.40), channel_id=1, source_target_pairs={{0,6},{1,7},{2,4},{3,5},{4,2},{5,3},{6,0},{7,1},{8,14},{9,15},{10,... | collective-permute-start | bytes 196616 | tf_op jit(solution)/shard_map/ppermute | solution.py:557
  222.4 7.1 %collective-permute-start.17 = (bf16[2,64,256]{2,1,0:T(8,128)(2,1)S(1)}, bf16[2,64,256]{2,1,0:T(8,128)(2,1)S(1)}, u32[]{:S(2)}, u32[]{:S(2)}) collective-permute-start(bf16[2,64,256]{2,1,0:T(8,128)(2,1)S(1)} %get-tuple-element.39), channel_id=1, source_target_pairs={{0,7},{1,6},{2,5},{3,4},{4,3},{5,2},{6,1},{7,0},{8,15},{9,14},{10,... | collective-permute-start | bytes 196616 | tf_op jit(solution)/shard_map/ppermute | solution.py:557
  264.3 54.0 %collective-permute-start.18 = (bf16[8,2,64,256]{3,2,1,0:T(8,128)(2,1)S(1)}, bf16[8,2,64,256]{3,2,1,0:T(8,128)(2,1)S(1)}, u32[]{:S(2)}, u32[]{:S(2)}) collective-permute-start(bf16[8,2,64,256]{3,2,1,0:T(8,128)(2,1)S(1)} %bitcast_dynamic-update-slice_fusion), channel_id=1, source_target_pairs={{0,8},{1,9},{2,10},{3,11},{4,12},{5,13},{6,14},{7,15},{8,0},{9,1},... | collective-permute-start | bytes 1572872 | tf_op jit(solution)/shard_map/ppermute | solution.py:557
  277.3 1.4 copy-start.2
  280.5 37.8 %all-to-all-start.4 = ((bf16[8,4,3,16,512]{4,3,2,1,0:T(8,128)(2,1)}), bf16[8,4,3,16,512]{4,3,2,1,0:T(8,128)(2,1)S(1)}, u32[]{:S(2)}, u32[]{:S(2)}) async-start(bf16[8,4,3,16,512]{4,3,2,1,0:T(8,128)(2,1)} %bitcast.30), calls=%async_computation.4 | async-start | bytes 3145728 | tf_op jit(solution)/shard_map/all_to_all | solution.py:544

commit v8 on v7

--- a/solution.py
+++ b/solution.py
@@ -107,20 +107,20 @@
     return pl.CostEstimate(flops=units * 10**9, bytes_accessed=units << 21, transcendentals=0)
 
 
-def hold_body(in_ref, out_ref):
-    out_ref[...] = jnp.zeros_like(out_ref)
-
-
-def hold(arr, units):
+def hold_body(*refs):
+    refs[-1][...] = jnp.zeros_like(refs[-1])
+
+
+def hold(arrays, units):
     return pl.pallas_call(
         hold_body,
-        in_specs=[pl.BlockSpec(memory_space=pl.ANY)],
+        in_specs=[pl.BlockSpec(memory_space=pl.ANY)] * len(arrays),
         out_specs=pl.BlockSpec(memory_space=pltpu.VMEM),
         out_shape=jax.ShapeDtypeStruct((8, 128), f32),
         compiler_params=pltpu.CompilerParams(vmem_limit_bytes=1024 * 1024),
         cost_estimate=long(units),
         name="hold",
-    )(arr)
+    )(*arrays)
 
 
 def split_body(first_ref, second_ref, token_ref, *out_refs):
@@ -147,7 +147,7 @@
     )(first, second, token)
 
 
-def unpack_body(scal_ref, in_ref, far_ref, token_ref, q_ref, k_ref, v_ref):
+def unpack_body(scal_ref, in_ref, far_ref, value_ref, token_ref, q_ref, k_ref, v_ref):
     members, subs, _, cols, feats = in_ref.shape
     far_feats = far_ref.shape[-1]
     for i in range(members):
@@ -155,25 +155,25 @@
             for s in range(subs):
                 ref[s * cols : (s + 1) * cols, i * feats : (i + 1) * feats] = in_ref[i, s, a]
 
-    def add(ref, i, a, first):
+    def add(ref, i, terms_ref, first):
         place = (pl.program_id(0) * members + i) ^ scal_ref[3]
         feat_cols = slice(i * feats + first, i * feats + first + far_feats)
-        total = ref[:, feat_cols].astype(f32) + far_ref[place, a].astype(f32)
+        total = ref[:, feat_cols].astype(f32) + terms_ref[place].astype(f32)
         ref[:, feat_cols] = total.astype(bf16)
 
     @pl.when(scal_ref[0] == 0)
     def _():
         for i in range(members):
-            add(k_ref, i, 0, far_feats)
-            add(v_ref, i, 1, far_feats)
+            add(k_ref, i, far_ref, far_feats)
+            add(v_ref, i, value_ref, far_feats)
 
     @pl.when(scal_ref[0] != 0)
     def _():
         for i in range(members):
-            add(q_ref, i, 0, 0)
-
-
-def unpack(scal, arr, far, token, tokens, feats):
+            add(q_ref, i, far_ref, 0)
+
+
+def unpack(scal, arr, far, value, token, tokens, feats):
     groups, subs, _, cols, near_feats = arr.shape
     members = 2
     out = jax.ShapeDtypeStruct((tokens, feats), bf16)
@@ -183,14 +183,15 @@
         in_specs=[
             smem(),
             pl.BlockSpec((members, subs, 3, cols, near_feats), lambda j: (j, 0, 0, 0, 0)),
-            pl.BlockSpec(far.shape, lambda j: (0, 0, 0, 0)),
+            pl.BlockSpec(far.shape, lambda j: (0, 0, 0)),
+            pl.BlockSpec(far.shape, lambda j: (0, 0, 0)),
             pl.BlockSpec(memory_space=pl.ANY),
         ],
         out_specs=[pl.BlockSpec((tokens, members * near_feats), lambda j: (0, j))] * 3,
         out_shape=[out] * 3,
         compiler_params=params(),
         name="unpack",
-    )(scal, arr, far, token)
+    )(scal, arr, far, value, token)
 
 
 def flat(ref, index):
@@ -573,7 +574,7 @@
     heads = near_feats // HEAD
     near_heads = heads // HALVES
     far_first = swap(far_first, groups)
-    token = hold(far_first, FIRST_UNITS)
+    token = hold([far_first], FIRST_UNITS)
     far_second = swap(far_second, groups)
     t = exchange_near(packed).reshape(lanes, 4, cols, near_feats)
     t, token = lax.optimization_barrier((t, token))
@@ -594,7 +595,7 @@
     row_full = jnp.stack([row_lse, row_delta], axis=1)
 
     far_full = shift(row_full[:near_heads], 1, 0)
-    token = hold(far_full, FULL_UNITS)
+    token = hold([far_full], FULL_UNITS)
     from_col = exchange_wide(col_grads(scale, scal, by_col, col_part, got[0]))
     off_full = jnp.where(half == 1, row_full[near_heads:], far_full)
     off_terms, far_terms = off_grads(scale, scal, t, off_full, token, pieces)
@@ -603,13 +604,17 @@
         lax.dynamic_index_in_dim(far_terms, near_index ^ step, keepdims=False)
         for step in range(groups)
     ]
-    far_terms = jnp.stack(spread(by_step))
-    from_col, far_terms, row_terms = lax.optimization_barrier((from_col, far_terms, row_terms))
-    back = swap(far_terms, groups)
-    token = hold(back, BACK_UNITS)
+    by_step = spread(by_step)
+    far_terms, far_value = (jnp.stack([piece[a] for piece in by_step]) for a in range(2))
+    from_col, far_terms, far_value, row_terms = lax.optimization_barrier(
+        (from_col, far_terms, far_value, row_terms)
+    )
+    far_value = shift(far_value, 1, 0)
+    far_terms = swap(far_terms, groups)
+    token = hold([far_terms, far_value], BACK_UNITS)
     joined = join(row_terms, from_col)
     out = exchange_near(joined.reshape(groups, subs, 3, cols, near_feats))
-    return unpack(scal, out, back, token, tokens, feats)
+    return unpack(scal, out, far_terms, far_value, token, tokens, feats)
 
 
 def solution(mesh):

time: 322 us -> 322 us (level)
  the two profiles are of different devices: /device:TPU:56 before, /device:TPU:61 now
where the time goes in v8:
time: 322 us; the launch traced here: 321 us
  waiting for transfers between devices  153 us (48%)
  starting transfers between devices  130 us (40%)
  Pallas kernels  28.2 us (9%)
  local copies, waits for them, and re-layouts  6.64 us (2%)
    all_to_all x3, waiting for transfers between devices, exchange_wide(): return lax.all_to_all(arr, 'wide', split_axis=0, concat_axis=0, tiled=True)  87 us
    ppermute x17, starting transfers between devices, swap(): return lax.ppermute(arr, 'narrow', pairs)  82.4 us
    ppermute x17, waiting for transfers between devices, swap(): return lax.ppermute(arr, 'narrow', pairs)  34.4 us
    all_to_all x3, starting transfers between devices, exchange_wide(): return lax.all_to_all(arr, 'wide', split_axis=0, concat_axis=0, tiled=True)  22.3 us
    all_to_all x2, waiting for transfers between devices, exchange_near(): lax.all_to_all(arr, 'narrow', split_axis=0, concat_axis=0, axis_index_gro...  18.3 us
    ppermute x3, starting transfers between devices, shift(): return lax.ppermute(arr, 'narrow', pairs)  13.5 us
    ppermute x3, waiting for transfers between devices, shift(): return lax.ppermute(arr, 'narrow', pairs)  13.4 us
    all_to_all x2, starting transfers between devices, exchange_near(): lax.all_to_all(arr, 'narrow', split_axis=0, concat_axis=0, axis_index_gro...  11.5 us
  transfers between devices with their start and end apart: 25, of which 11 were waited for; matrix products, arithmetic and copies ran while one was open for 1% of the time, Pallas kernels for 6%

profile of v8, /device:TPU:61, one launch (start us, length us, event | category | flops | bytes accessed | tf_op | source)
XLA Modules:
  0.0 320.6 jit_solution(11771105792269925970)
XLA Ops:
  0.6 3.3 %pack.1 = (bf16[8,1,2,16,256]{4,3,2,1,0:T(8,128)(2,1)}, bf16[8,3,2,16,256]{4,3,2,1,0:T(8,128)(2,1)}, bf16[8,4,4,16,512]{4,3,2,1,0:T(8,128)(2,1)}) custom-call(bf16[4,16,4096]{2,1,0:T(8,128)(2,1)} %bitcast.65, bf16[4,16,4096]{2,1,0:T(8,128)(2,1)} %bitcast.66, bf16[4,16,4096]{2,1,0:T(8,128)(2,1)} %bitcast.67, bf16[4,16,4096]{2,1,0:T(8,128)(2,1)} %bitcast.68), custom_call_target="tpu_custom_call" | custom-call | tf_op jit(solution)/shard_map/pack/pallas_call | solution.py:93
  4.0 14.5 %collective-permute-start = (bf16[8,1,2,16,256]{4,3,2,1,0:T(8,128)(2,1)}, bf16[8,1,2,16,256]{4,3,2,1,0:T(8,128)(2,1)S(1)}, u32[]{:S(2)}, u32[]{:S(2)}) collective-permute-start(bf16[8,1,2,16,256]{4,3,2,1,0:T(8,128)(2,1)} %get-tuple-element.23), channel_id=1, source_target_pairs={{0,8},{1,9},{2,10},{3,11},{4,12},{5,13},{6,14},{7,15},{8,0},{9,1},... | collective-permute-start | bytes 393224 | tf_op jit(solution)/shard_map/ppermute | solution.py:558
  18.5 5.4 %all-to-all-start = ((bf16[8,4,4,16,512]{4,3,2,1,0:T(8,128)(2,1)}), bf16[8,4,4,16,512]{4,3,2,1,0:T(8,128)(2,1)}, u32[]{:S(2)}, u32[]{:S(2)}) async-start(bf16[8,4,4,16,512]{4,3,2,1,0:T(8,128)(2,1)} %get-tuple-element.22), calls=%async_computation | async-start | bytes 4194304 | tf_op jit(solution)/shard_map/all_to_all | solution.py:545
  25.9 4.5 %collective-permute-done.refs_0_.first_ref = bf16[8,1,2,16,256]{4,3,2,1,0:T(8,128)(2,1)S(1)} collective-permute-done((bf16[8,1,2,16,256]{4,3,2,1,0:T(8,128)(2,1)}, bf16[8,1,2,16,256]{4,3,2,1,0:T(8,128)(2,1)S(1)}, u32[]{:S(2)}, u32[]{:S(2)}) %collective-permute-start) | collective-permute-done | bytes 131104 | tf_op jit(solution)/shard_map/ppermute | solution.py:558
  30.4 18.3 %all-to-all-done = bf16[8,4,4,16,512]{4,3,2,1,0:T(8,128)(2,1)} async-done(((bf16[8,4,4,16,512]{4,3,2,1,0:T(8,128)(2,1)}), bf16[8,4,4,16,512]{4,3,2,1,0:T(8,128)(2,1)}, u32[]{:S(2)}, u32[]{:S(2)}) %all-to-all-start) | async-done | bytes 2097184 | tf_op jit(solution)/shard_map/all_to_all | solution.py:545
  48.7 8.0 %all-to-all-start.1 = ((bf16[32,4,16,512]{3,2,1,0:T(8,128)(2,1)}), bf16[32,4,16,512]{3,2,1,0:T(8,128)(2,1)S(1)}, u32[]{:S(2)}, u32[]{:S(2)}) async-start(bf16[32,4,16,512]{3,2,1,0:T(8,128)(2,1)} %bitcast.6.refs_1_), calls=%async_computation.1 | async-start | bytes 4194304 | tf_op jit(solution)/shard_map/all_to_all | solution.py:550
  56.7 5.3 %collective-permute-done.1.second_ref = bf16[8,3,2,16,256]{4,3,2,1,0:T(8,128)(2,1)S(1)} collective-permute-done((bf16[8,3,2,16,256]{4,3,2,1,0:T(8,128)(2,1)S(1)}, bf16[8,3,2,16,256]{4,3,2,1,0:T(8,128)(2,1)S(1)}, u32[]{:S(2)}, u32[]{:S(2)}) %collective-permute-start.1) | collective-permute-done | bytes 393248 | tf_op jit(solution)/shard_map/ppermute | solution.py:558
  62.0 9.3 %collective-permute-start.2 = (bf16[4,2,16,256]{3,2,1,0:T(8,128)(2,1)S(1)}, bf16[4,2,16,256]{3,2,1,0:T(8,128)(2,1)S(1)}, u32[]{:S(2)}, u32[]{:S(2)}) collective-permute-start(bf16[4,2,16,256]{3,2,1,0:T(8,128)(2,1)S(1)} %get-tuple-element.28), channel_id=1, source_target_pairs={{0,1},{1,0},{2,3},{3,2},{4,5},{5,4},{6,7},{7,6},{8,9},{9,8},{10,11... | collective-permute-start | bytes 196616 | tf_op jit(solution)/shard_map/ppermute | solution.py:558
  71.4 2.8 collective-permute-start.3
  78.2 3.2 collective-permute-start.5
  81.3 4.0 %collective-permute-start.6 = (bf16[4,2,16,256]{3,2,1,0:T(8,128)(2,1)S(1)}, bf16[4,2,16,256]{3,2,1,0:T(8,128)(2,1)S(1)}, u32[]{:S(2)}, u32[]{:S(2)}) collective-permute-start(bf16[4,2,16,256]{3,2,1,0:T(8,128)(2,1)S(1)} %get-tuple-element.32), channel_id=1, source_target_pairs={{0,5},{1,4},{2,7},{3,6},{4,1},{5,0},{6,3},{7,2},{8,13},{9,12},{10,... | collective-permute-start | bytes 196616 | tf_op jit(solution)/shard_map/ppermute | solution.py:558
  87.4 4.7 %collective-permute-start.8 = (bf16[4,2,16,256]{3,2,1,0:T(8,128)(2,1)S(1)}, bf16[4,2,16,256]{3,2,1,0:T(8,128)(2,1)S(1)}, u32[]{:S(2)}, u32[]{:S(2)}) collective-permute-start(bf16[4,2,16,256]{3,2,1,0:T(8,128)(2,1)S(1)} %get-tuple-element.34), channel_id=1, source_target_pairs={{0,7},{1,6},{2,5},{3,4},{4,3},{5,2},{6,1},{7,0},{8,15},{9,14},{10,... | collective-permute-start | bytes 196616 | tf_op jit(solution)/shard_map/ppermute | solution.py:558
  95.1 2.9 off_stats.1
  98.0 10.9 %collective-permute-start.9 = (f32[2,2,512]{2,1,0:T(2,128)S(1)}, f32[2,2,512]{2,1,0:T(2,128)S(1)}, u32[]{:S(2)}, u32[]{:S(2)}) collective-permute-start(f32[2,2,512]{2,1,0:T(2,128)S(1)} %off_stats.1), channel_id=1, source_target_pairs={{0,8},{1,9},{2,10},{3,11},{4,12},{5,13},{6,14},{7,15},{16,24},{17,... | collective-permute-start | bytes 24584 | tf_op jit(solution)/shard_map/ppermute | solution.py:554
  108.9 3.8 %row_stats.1 = f32[4,2,512]{2,1,0:T(2,128)S(1)} custom-call(s32[4]{0:T(128)S(1)} %pad_add_fusion.refs_0_.scal_ref, bf16[32,4,16,512]{3,2,1,0:T(8,128)(2,1)} %bitcast.6.refs_1_), custom_call_target="tpu_custom_call" | custom-call | flops 1342177280 | bytes 4194304 | tf_op jit(solution)/shard_map/row_stats/pallas_call | solution.py:406
  112.9 44.6 %all-to-all-done.1.refs_1_ = bf16[32,4,16,512]{3,2,1,0:T(8,128)(2,1)S(1)} async-done(((bf16[32,4,16,512]{3,2,1,0:T(8,128)(2,1)}), bf16[32,4,16,512]{3,2,1,0:T(8,128)(2,1)S(1)}, u32[]{:S(2)}, u32[]{:S(2)}) %all-to-all-start.1) | async-done | bytes 2097184 | tf_op jit(solution)/shard_map/all_to_all | solution.py:550
  160.2 7.8 %all-to-all-start.2 = ((f32[32,2,128]{2,1,0:T(2,128)}), f32[32,2,128]{2,1,0:T(2,128)S(1)}, u32[]{:S(2)}, u32[]{:S(2)}) async-start(f32[32,2,128]{2,1,0:T(2,128)} %copy.18), calls=%async_computation.2 | async-start | bytes 65536 | tf_op jit(solution)/shard_map/all_to_all | solution.py:550
  168.0 8.8 %all-to-all-done.2 = f32[32,2,128]{2,1,0:T(2,128)S(1)} async-done(((f32[32,2,128]{2,1,0:T(2,128)}), f32[32,2,128]{2,1,0:T(2,128)S(1)}, u32[]{:S(2)}, u32[]{:S(2)}) %all-to-all-start.2) | async-done | bytes 32800 | tf_op jit(solution)/shard_map/all_to_all | solution.py:550
  178.9 3.1 col_grads.1
  183.2 6.5 %all-to-all-start.3 = ((bf16[32,3,16,512]{3,2,1,0:T(8,128)(2,1)}), bf16[32,3,16,512]{3,2,1,0:T(8,128)(2,1)S(1)}, u32[]{:S(2)}, u32[]{:S(2)}) async-start(bf16[32,3,16,512]{3,2,1,0:T(8,128)(2,1)} %copy-done), calls=%async_computation.3 | async-start | bytes 3145728 | tf_op jit(solution)/shard_map/all_to_all | solution.py:550
  190.7 3.8 %off_grads.1 = (f32[2,512,256]{2,1,0:T(8,128)S(1)}, bf16[8,2,64,256]{3,2,1,0:T(8,128)(2,1)S(1)}) custom-call(s32[4]{0:T(128)S(1)} %pad_add_fusion.refs_0_.scal_ref, bf16[32,4,16,512]{3,2,1,0:T(8,128)(2,1)} %bitcast.6.refs_1_, f32[2,2,512]{2,1,0:T(2,128)S(1)} %fusion.2.refs_2_, f32[8,128]{1,0:T(8,128)S(1)} %hold.4.refs_3_, ...), custom_call_target="tpu_custom_call" | custom-call | flops 1677721600 | bytes 4194304 | tf_op jit(solution)/shard_map/off_grads/pallas_call | solution.py:333
  194.5 5.6 %collective-permute-start.11 = (bf16[2,64,256]{2,1,0:T(8,128)(2,1)S(1)}, bf16[2,64,256]{2,1,0:T(8,128)(2,1)S(1)}, u32[]{:S(2)}, u32[]{:S(2)}) collective-permute-start(bf16[2,64,256]{2,1,0:T(8,128)(2,1)S(1)} %get-tuple-element.49), channel_id=1, source_target_pairs={{0,1},{1,0},{2,3},{3,2},{4,5},{5,4},{6,7},{7,6},{8,9},{9,8},{10,11... | collective-permute-start | bytes 196616 | tf_op jit(solution)/shard_map/ppermute | solution.py:558
  202.2 3.4 %collective-permute-start.13 = (bf16[2,64,256]{2,1,0:T(8,128)(2,1)S(1)}, bf16[2,64,256]{2,1,0:T(8,128)(2,1)S(1)}, u32[]{:S(2)}, u32[]{:S(2)}) collective-permute-start(bf16[2,64,256]{2,1,0:T(8,128)(2,1)S(1)} %get-tuple-element.47), channel_id=1, source_target_pairs={{0,3},{1,2},{2,1},{3,0},{4,7},{5,6},{6,5},{7,4},{8,11},{9,10},{10,... | collective-permute-start | bytes 196616 | tf_op jit(solution)/shard_map/ppermute | solution.py:558
  205.6 2.7 collective-permute-start.14
  208.3 4.4 %collective-permute-start.15 = (bf16[2,64,256]{2,1,0:T(8,128)(2,1)S(1)}, bf16[2,64,256]{2,1,0:T(8,128)(2,1)S(1)}, u32[]{:S(2)}, u32[]{:S(2)}) collective-permute-start(bf16[2,64,256]{2,1,0:T(8,128)(2,1)S(1)} %get-tuple-element.45), channel_id=1, source_target_pairs={{0,5},{1,4},{2,7},{3,6},{4,1},{5,0},{6,3},{7,2},{8,13},{9,12},{10,... | collective-permute-start | bytes 196616 | tf_op jit(solution)/shard_map/ppermute | solution.py:558
  212.8 5.3 %row_grads.1.row_ref = bf16[32,3,16,512]{3,2,1,0:T(8,128)(2,1)S(1)} custom-call(s32[4]{0:T(128)S(1)} %pad_add_fusion.refs_0_.scal_ref, bf16[32,4,16,512]{3,2,1,0:T(8,128)(2,1)} %bitcast.6.refs_1_, f32[4,2,512]{2,1,0:T(2,128)S(1)} %pad_maximum_fusion.1.refs_2_, f32[2,512,256]{2,1,0:T(8,128)S(1)} %get-tuple-element.36.refs_3_), custom_call_target="tpu_custom_call" | custom-call | flops 2684354560 | bytes 4194304 | tf_op jit(solution)/shard_map/row_grads/pallas_call | solution.py:482
  221.3 4.8 %collective-permute-start.17 = (bf16[2,64,256]{2,1,0:T(8,128)(2,1)S(1)}, bf16[2,64,256]{2,1,0:T(8,128)(2,1)S(1)}, u32[]{:S(2)}, u32[]{:S(2)}) collective-permute-start(bf16[2,64,256]{2,1,0:T(8,128)(2,1)S(1)} %get-tuple-element.43), channel_id=1, source_target_pairs={{0,7},{1,6},{2,5},{3,4},{4,3},{5,2},{6,1},{7,0},{8,15},{9,14},{10,... | collective-permute-start | bytes 196616 | tf_op jit(solution)/shard_map/ppermute | solution.py:558
  228.6 33.6 %all-to-all-done.3.col_ref = bf16[32,3,16,512]{3,2,1,0:T(8,128)(2,1)S(1)} async-done(((bf16[32,3,16,512]{3,2,1,0:T(8,128)(2,1)}), bf16[32,3,16,512]{3,2,1,0:T(8,128)(2,1)S(1)}, u32[]{:S(2)}, u32[]{:S(2)}) %all-to-all-start.3) | async-done | bytes 1572896 | tf_op jit(solution)/shard_map/all_to_all | solution.py:550
  262.2 12.5 %collective-permute-start.18 = (bf16[8,64,256]{2,1,0:T(8,128)(2,1)S(1)}, bf16[8,64,256]{2,1,0:T(8,128)(2,1)S(1)}, u32[]{:S(2)}, u32[]{:S(2)}) collective-permute-start(bf16[8,64,256]{2,1,0:T(8,128)(2,1)S(1)} %get-tuple-element.39), channel_id=1, source_target_pairs={{0,8},{1,9},{2,10},{3,11},{4,12},{5,13},{6,14},{7,15},{8,0},{9,1},... | collective-permute-start | bytes 786440 | tf_op jit(solution)/shard_map/ppermute | solution.py:558
  279.3 6.1 %all-to-all-start.4 = ((bf16[8,4,3,16,512]{4,3,2,1,0:T(8,128)(2,1)}), bf16[8,4,3,16,512]{4,3,2,1,0:T(8,128)(2,1)S(1)}, u32[]{:S(2)}, u32[]{:S(2)}) async-start(bf16[8,4,3,16,512]{4,3,2,1,0:T(8,128)(2,1)} %bitcast.25), calls=%async_computation.4 | async-start | bytes 3145728 | tf_op jit(solution)/shard_map/all_to_all | solution.py:545
  285.4 20.5 %collective-permute-done.18.refs_0_.far_ref = bf16[8,64,256]{2,1,0:T(8,128)(2,1)S(1)} collective-permute-done((bf16[8,64,256]{2,1,0:T(8,128)(2,1)S(1)}, bf16[8,64,256]{2,1,0:T(8,128)(2,1)S(1)}, u32[]{:S(2)}, u32[]{:S(2)}) %collective-permute-start.18) | collective-permute-done | bytes 262176 | tf_op jit(solution)/shard_map/ppermute | solution.py:558
  305.9 12.4 %collective-permute-done.19.refs_1_.value_ref = bf16[8,64,256]{2,1,0:T(8,128)(2,1)S(1)} collective-permute-done((bf16[8,64,256]{2,1,0:T(8,128)(2,1)S(1)}, bf16[8,64,256]{2,1,0:T(8,128)(2,1)S(1)}, u32[]{:S(2)}, u32[]{:S(2)}) %collective-permute-start.19) | collective-permute-done | bytes 262176 | tf_op jit(solution)/shard_map/ppermute | solution.py:554
  (72 shorter events, 32.5 us)
Async XLA Ops:
  4.0 26.4 %collective-permute-start = (bf16[8,1,2,16,256]{4,3,2,1,0:T(8,128)(2,1)}, bf16[8,1,2,16,256]{4,3,2,1,0:T(8,128)(2,1)S(1)}, u32[]{:S(2)}, u32[]{:S(2)}) collective-permute-start(bf16[8,1,2,16,256]{4,3,2,1,0:T(8,128)(2,1)} %get-tuple-element.23), channel_id=1, source_target_pairs={{0,8},{1,9},{2,10},{3,11},{4,12},{5,13},{6,14},{7,15},{8,0},{9,1},... | collective-permute-start | bytes 393224 | tf_op jit(solution)/shard_map/ppermute | solution.py:558
  18.5 5.4 %copy-start.3 = (bf16[8,3,2,16,256]{4,3,2,1,0:T(8,128)(2,1)S(1)}, bf16[8,3,2,16,256]{4,3,2,1,0:T(8,128)(2,1)}, u32[]{:S(2)}) copy-start(bf16[8,3,2,16,256]{4,3,2,1,0:T(8,128)(2,1)} %get-tuple-element.25) | copy-start | bytes 1179652
  18.5 30.2 %all-to-all-start = ((bf16[8,4,4,16,512]{4,3,2,1,0:T(8,128)(2,1)}), bf16[8,4,4,16,512]{4,3,2,1,0:T(8,128)(2,1)}, u32[]{:S(2)}, u32[]{:S(2)}) async-start(bf16[8,4,4,16,512]{4,3,2,1,0:T(8,128)(2,1)} %get-tuple-element.22), calls=%async_computation | async-start | bytes 4194304 | tf_op jit(solution)/shard_map/all_to_all | solution.py:545
  23.9 38.1 %collective-permute-start.1 = (bf16[8,3,2,16,256]{4,3,2,1,0:T(8,128)(2,1)S(1)}, bf16[8,3,2,16,256]{4,3,2,1,0:T(8,128)(2,1)S(1)}, u32[]{:S(2)}, u32[]{:S(2)}) collective-permute-start(bf16[8,3,2,16,256]{4,3,2,1,0:T(8,128)(2,1)S(1)} %copy-done.3), channel_id=1, source_target_pairs={{0,8},{1,9},{2,10},{3,11},{4,12},{5,13},{6,14},{7,15},{8,0},{9,1},... | collective-permute-start | bytes 1179656 | tf_op jit(solution)/shard_map/ppermute | solution.py:558
  48.7 108.8 %all-to-all-start.1 = ((bf16[32,4,16,512]{3,2,1,0:T(8,128)(2,1)}), bf16[32,4,16,512]{3,2,1,0:T(8,128)(2,1)S(1)}, u32[]{:S(2)}, u32[]{:S(2)}) async-start(bf16[32,4,16,512]{3,2,1,0:T(8,128)(2,1)} %bitcast.6.refs_1_), calls=%async_computation.1 | async-start | bytes 4194304 | tf_op jit(solution)/shard_map/all_to_all | solution.py:550
  56.7 17.6 %copy-start.4 = (s32[8]{0:T(128)S(1)}, s32[8]{0:T(128)}, u32[]{:S(2)}) copy-start(s32[8]{0:T(128)} %param.11) | copy-start | bytes 100
  56.7 18.1 %copy-start.5 = (s32[32]{0:T(128)S(1)}, s32[32]{0:T(128)}, u32[]{:S(2)}) copy-start(s32[32]{0:T(128)} %param.10) | copy-start | bytes 388
  62.0 23.3 %collective-permute-start.2 = (bf16[4,2,16,256]{3,2,1,0:T(8,128)(2,1)S(1)}, bf16[4,2,16,256]{3,2,1,0:T(8,128)(2,1)S(1)}, u32[]{:S(2)}, u32[]{:S(2)}) collective-permute-start(bf16[4,2,16,256]{3,2,1,0:T(8,128)(2,1)S(1)} %get-tuple-element.28), channel_id=1, source_target_pairs={{0,1},{1,0},{2,3},{3,2},{4,5},{5,4},{6,7},{7,6},{8,9},{9,8},{10,11... | collective-permute-start | bytes 196616 | tf_op jit(solution)/shard_map/ppermute | solution.py:558
  71.4 16.0 %collective-permute-start.3 = (bf16[4,2,16,256]{3,2,1,0:T(8,128)(2,1)S(1)}, bf16[4,2,16,256]{3,2,1,0:T(8,128)(2,1)S(1)}, u32[]{:S(2)}, u32[]{:S(2)}) collective-permute-start(bf16[4,2,16,256]{3,2,1,0:T(8,128)(2,1)S(1)} %get-tuple-element.29), channel_id=1, source_target_pairs={{0,2},{1,3},{2,0},{3,1},{4,6},{5,7},{6,4},{7,5},{8,10},{9,11},{10,... | collective-permute-start | bytes 196616 | tf_op jit(solution)/shard_map/ppermute | solution.py:558
  75.5 17.9 %collective-permute-start.4 = (bf16[4,2,16,256]{3,2,1,0:T(8,128)(2,1)S(1)}, bf16[4,2,16,256]{3,2,1,0:T(8,128)(2,1)S(1)}, u32[]{:S(2)}, u32[]{:S(2)}) collective-permute-start(bf16[4,2,16,256]{3,2,1,0:T(8,128)(2,1)S(1)} %get-tuple-element.30), channel_id=1, source_target_pairs={{0,3},{1,2},{2,1},{3,0},{4,7},{5,6},{6,5},{7,4},{8,11},{9,10},{10,... | collective-permute-start | bytes 196616 | tf_op jit(solution)/shard_map/ppermute | solution.py:558
  78.2 15.2 %collective-permute-start.5 = (bf16[4,2,16,256]{3,2,1,0:T(8,128)(2,1)S(1)}, bf16[4,2,16,256]{3,2,1,0:T(8,128)(2,1)S(1)}, u32[]{:S(2)}, u32[]{:S(2)}) collective-permute-start(bf16[4,2,16,256]{3,2,1,0:T(8,128)(2,1)S(1)} %get-tuple-element.31), channel_id=1, source_target_pairs={{0,4},{1,5},{2,6},{3,7},{4,0},{5,1},{6,2},{7,3},{8,12},{9,13},{10,... | collective-permute-start | bytes 196616 | tf_op jit(solution)/shard_map/ppermute | solution.py:558
  81.3 12.1 %collective-permute-start.6 = (bf16[4,2,16,256]{3,2,1,0:T(8,128)(2,1)S(1)}, bf16[4,2,16,256]{3,2,1,0:T(8,128)(2,1)S(1)}, u32[]{:S(2)}, u32[]{:S(2)}) collective-permute-start(bf16[4,2,16,256]{3,2,1,0:T(8,128)(2,1)S(1)} %get-tuple-element.32), channel_id=1, source_target_pairs={{0,5},{1,4},{2,7},{3,6},{4,1},{5,0},{6,3},{7,2},{8,13},{9,12},{10,... | collective-permute-start | bytes 196616 | tf_op jit(solution)/shard_map/ppermute | solution.py:558
  85.3 8.1 %collective-permute-start.7 = (bf16[4,2,16,256]{3,2,1,0:T(8,128)(2,1)S(1)}, bf16[4,2,16,256]{3,2,1,0:T(8,128)(2,1)S(1)}, u32[]{:S(2)}, u32[]{:S(2)}) collective-permute-start(bf16[4,2,16,256]{3,2,1,0:T(8,128)(2,1)S(1)} %get-tuple-element.33), channel_id=1, source_target_pairs={{0,6},{1,7},{2,4},{3,5},{4,2},{5,3},{6,0},{7,1},{8,14},{9,15},{10,... | collective-permute-start | bytes 196616 | tf_op jit(solution)/shard_map/ppermute | solution.py:558
  87.4 7.7 %collective-permute-start.8 = (bf16[4,2,16,256]{3,2,1,0:T(8,128)(2,1)S(1)}, bf16[4,2,16,256]{3,2,1,0:T(8,128)(2,1)S(1)}, u32[]{:S(2)}, u32[]{:S(2)}) collective-permute-start(bf16[4,2,16,256]{3,2,1,0:T(8,128)(2,1)S(1)} %get-tuple-element.34), channel_id=1, source_target_pairs={{0,7},{1,6},{2,5},{3,4},{4,3},{5,2},{6,1},{7,0},{8,15},{9,14},{10,... | collective-permute-start | bytes 196616 | tf_op jit(solution)/shard_map/ppermute | solution.py:558
  98.0 14.8 %collective-permute-start.9 = (f32[2,2,512]{2,1,0:T(2,128)S(1)}, f32[2,2,512]{2,1,0:T(2,128)S(1)}, u32[]{:S(2)}, u32[]{:S(2)}) collective-permute-start(f32[2,2,512]{2,1,0:T(2,128)S(1)} %off_stats.1), channel_id=1, source_target_pairs={{0,8},{1,9},{2,10},{3,11},{4,12},{5,13},{6,14},{7,15},{16,24},{17,... | collective-permute-start | bytes 24584 | tf_op jit(solution)/shard_map/ppermute | solution.py:554
  160.2 16.7 %all-to-all-start.2 = ((f32[32,2,128]{2,1,0:T(2,128)}), f32[32,2,128]{2,1,0:T(2,128)S(1)}, u32[]{:S(2)}, u32[]{:S(2)}) async-start(f32[32,2,128]{2,1,0:T(2,128)} %copy.18), calls=%async_computation.2 | async-start | bytes 65536 | tf_op jit(solution)/shard_map/all_to_all | solution.py:550
  177.6 13.1 %collective-permute-start.10 = (f32[2,2,512]{2,1,0:T(2,128)S(1)}, f32[2,2,512]{2,1,0:T(2,128)S(1)}, u32[]{:S(2)}, u32[]{:S(2)}) collective-permute-start(f32[2,2,512]{2,1,0:T(2,128)S(1)} %fusion.3), channel_id=1, source_target_pairs={{8,0},{9,1},{10,2},{11,3},{12,4},{13,5},{14,6},{15,7},{24,16},{25,... | collective-permute-start | bytes 24584 | tf_op jit(solution)/shard_map/ppermute | solution.py:554
  182.0 1.2 copy-start
  183.2 79.0 %all-to-all-start.3 = ((bf16[32,3,16,512]{3,2,1,0:T(8,128)(2,1)}), bf16[32,3,16,512]{3,2,1,0:T(8,128)(2,1)S(1)}, u32[]{:S(2)}, u32[]{:S(2)}) async-start(bf16[32,3,16,512]{3,2,1,0:T(8,128)(2,1)} %copy-done), calls=%async_computation.3 | async-start | bytes 3145728 | tf_op jit(solution)/shard_map/all_to_all | solution.py:550
  194.5 24.8 %collective-permute-start.11 = (bf16[2,64,256]{2,1,0:T(8,128)(2,1)S(1)}, bf16[2,64,256]{2,1,0:T(8,128)(2,1)S(1)}, u32[]{:S(2)}, u32[]{:S(2)}) collective-permute-start(bf16[2,64,256]{2,1,0:T(8,128)(2,1)S(1)} %get-tuple-element.49), channel_id=1, source_target_pairs={{0,1},{1,0},{2,3},{3,2},{4,5},{5,4},{6,7},{7,6},{8,9},{9,8},{10,11... | collective-permute-start | bytes 196616 | tf_op jit(solution)/shard_map/ppermute | solution.py:558
  200.1 21.1 %collective-permute-start.12 = (bf16[2,64,256]{2,1,0:T(8,128)(2,1)S(1)}, bf16[2,64,256]{2,1,0:T(8,128)(2,1)S(1)}, u32[]{:S(2)}, u32[]{:S(2)}) collective-permute-start(bf16[2,64,256]{2,1,0:T(8,128)(2,1)S(1)} %get-tuple-element.48), channel_id=1, source_target_pairs={{0,2},{1,3},{2,0},{3,1},{4,6},{5,7},{6,4},{7,5},{8,10},{9,11},{10,... | collective-permute-start | bytes 196616 | tf_op jit(solution)/shard_map/ppermute | solution.py:558
  202.2 23.9 %collective-permute-start.13 = (bf16[2,64,256]{2,1,0:T(8,128)(2,1)S(1)}, bf16[2,64,256]{2,1,0:T(8,128)(2,1)S(1)}, u32[]{:S(2)}, u32[]{:S(2)}) collective-permute-start(bf16[2,64,256]{2,1,0:T(8,128)(2,1)S(1)} %get-tuple-element.47), channel_id=1, source_target_pairs={{0,3},{1,2},{2,1},{3,0},{4,7},{5,6},{6,5},{7,4},{8,11},{9,10},{10,... | collective-permute-start | bytes 196616 | tf_op jit(solution)/shard_map/ppermute | solution.py:558
  205.6 20.5 %collective-permute-start.14 = (bf16[2,64,256]{2,1,0:T(8,128)(2,1)S(1)}, bf16[2,64,256]{2,1,0:T(8,128)(2,1)S(1)}, u32[]{:S(2)}, u32[]{:S(2)}) collective-permute-start(bf16[2,64,256]{2,1,0:T(8,128)(2,1)S(1)} %get-tuple-element.46), channel_id=1, source_target_pairs={{0,4},{1,5},{2,6},{3,7},{4,0},{5,1},{6,2},{7,3},{8,12},{9,13},{10,... | collective-permute-start | bytes 196616 | tf_op jit(solution)/shard_map/ppermute | solution.py:558
  208.3 17.8 %collective-permute-start.15 = (bf16[2,64,256]{2,1,0:T(8,128)(2,1)S(1)}, bf16[2,64,256]{2,1,0:T(8,128)(2,1)S(1)}, u32[]{:S(2)}, u32[]{:S(2)}) collective-permute-start(bf16[2,64,256]{2,1,0:T(8,128)(2,1)S(1)} %get-tuple-element.45), channel_id=1, source_target_pairs={{0,5},{1,4},{2,7},{3,6},{4,1},{5,0},{6,3},{7,2},{8,13},{9,12},{10,... | collective-permute-start | bytes 196616 | tf_op jit(solution)/shard_map/ppermute | solution.py:558
  218.1 1.2 copy-start.1
  219.3 6.8 %collective-permute-start.16 = (bf16[2,64,256]{2,1,0:T(8,128)(2,1)S(1)}, bf16[2,64,256]{2,1,0:T(8,128)(2,1)S(1)}, u32[]{:S(2)}, u32[]{:S(2)}) collective-permute-start(bf16[2,64,256]{2,1,0:T(8,128)(2,1)S(1)} %get-tuple-element.44), channel_id=1, source_target_pairs={{0,6},{1,7},{2,4},{3,5},{4,2},{5,3},{6,0},{7,1},{8,14},{9,15},{10,... | collective-permute-start | bytes 196616 | tf_op jit(solution)/shard_map/ppermute | solution.py:558
  221.3 7.3 %collective-permute-start.17 = (bf16[2,64,256]{2,1,0:T(8,128)(2,1)S(1)}, bf16[2,64,256]{2,1,0:T(8,128)(2,1)S(1)}, u32[]{:S(2)}, u32[]{:S(2)}) collective-permute-start(bf16[2,64,256]{2,1,0:T(8,128)(2,1)S(1)} %get-tuple-element.43), channel_id=1, source_target_pairs={{0,7},{1,6},{2,5},{3,4},{4,3},{5,2},{6,1},{7,0},{8,15},{9,14},{10,... | collective-permute-start | bytes 196616 | tf_op jit(solution)/shard_map/ppermute | solution.py:558
  262.2 43.7 %collective-permute-start.18 = (bf16[8,64,256]{2,1,0:T(8,128)(2,1)S(1)}, bf16[8,64,256]{2,1,0:T(8,128)(2,1)S(1)}, u32[]{:S(2)}, u32[]{:S(2)}) collective-permute-start(bf16[8,64,256]{2,1,0:T(8,128)(2,1)S(1)} %get-tuple-element.39), channel_id=1, source_target_pairs={{0,8},{1,9},{2,10},{3,11},{4,12},{5,13},{6,14},{7,15},{8,0},{9,1},... | collective-permute-start | bytes 786440 | tf_op jit(solution)/shard_map/ppermute | solution.py:558
  274.7 43.5 %collective-permute-start.19 = (bf16[8,64,256]{2,1,0:T(8,128)(2,1)S(1)}, bf16[8,64,256]{2,1,0:T(8,128)(2,1)S(1)}, u32[]{:S(2)}, u32[]{:S(2)}) collective-permute-start(bf16[8,64,256]{2,1,0:T(8,128)(2,1)S(1)} %get-tuple-element.40), channel_id=1, source_target_pairs={{8,0},{9,1},{10,2},{11,3},{12,4},{13,5},{14,6},{15,7},{24,16},{25,... | collective-permute-start | bytes 786440 | tf_op jit(solution)/shard_map/ppermute | solution.py:554
  276.0 1.4 copy-start.2
  279.3 39.0 %all-to-all-start.4 = ((bf16[8,4,3,16,512]{4,3,2,1,0:T(8,128)(2,1)}), bf16[8,4,3,16,512]{4,3,2,1,0:T(8,128)(2,1)S(1)}, u32[]{:S(2)}, u32[]{:S(2)}) async-start(bf16[8,4,3,16,512]{4,3,2,1,0:T(8,128)(2,1)} %bitcast.25), calls=%async_computation.4 | async-start | bytes 3145728 | tf_op jit(solution)/shard_map/all_to_all | solution.py:545

commit v9 on v8

--- a/solution.py
+++ b/solution.py
@@ -175,7 +175,7 @@
 
 def unpack(scal, arr, far, value, token, tokens, feats):
     groups, subs, _, cols, near_feats = arr.shape
-    members = 2
+    members = 4
     out = jax.ShapeDtypeStruct((tokens, feats), bf16)
     return pl.pallas_call(
         unpack_body,

time: 322 us -> 321 us (level)
  no operation moved by 1% of the time
where the time goes in v9:
time: 321 us; the launch traced here: 320 us
  waiting for transfers between devices  153 us (48%)
  starting transfers between devices  130 us (40%)
  Pallas kernels  27.7 us (9%)
  local copies, waits for them, and re-layouts  6.64 us (2%)
    all_to_all x3, waiting for transfers between devices, exchange_wide(): return lax.all_to_all(arr, 'wide', split_axis=0, concat_axis=0, tiled=True)  87 us
    ppermute x17, starting transfers between devices, swap(): return lax.ppermute(arr, 'narrow', pairs)  82.4 us
    ppermute x17, waiting for transfers between devices, swap(): return lax.ppermute(arr, 'narrow', pairs)  34.4 us
    all_to_all x3, starting transfers between devices, exchange_wide(): return lax.all_to_all(arr, 'wide', split_axis=0, concat_axis=0, tiled=True)  22.3 us
    all_to_all x2, waiting for transfers between devices, exchange_near(): lax.all_to_all(arr, 'narrow', split_axis=0, concat_axis=0, axis_index_gro...  18.3 us
    ppermute x3, starting transfers between devices, shift(): return lax.ppermute(arr, 'narrow', pairs)  13.5 us
    ppermute x3, waiting for transfers between devices, shift(): return lax.ppermute(arr, 'narrow', pairs)  13.4 us
    all_to_all x2, starting transfers between devices, exchange_near(): lax.all_to_all(arr, 'narrow', split_axis=0, concat_axis=0, axis_index_gro...  11.5 us
  transfers between devices with their start and end apart: 25, of which 11 were waited for; matrix products, arithmetic and copies ran while one was open for 1% of the time, Pallas kernels for 6%

profile of v9, /device:TPU:61, one launch (start us, length us, event | category | flops | bytes accessed | tf_op | source)
XLA Modules:
  0.0 320.1 jit_solution(16130546063559168371)
XLA Ops:
  0.6 3.3 %pack.1 = (bf16[8,1,2,16,256]{4,3,2,1,0:T(8,128)(2,1)}, bf16[8,3,2,16,256]{4,3,2,1,0:T(8,128)(2,1)}, bf16[8,4,4,16,512]{4,3,2,1,0:T(8,128)(2,1)}) custom-call(bf16[4,16,4096]{2,1,0:T(8,128)(2,1)} %bitcast.65, bf16[4,16,4096]{2,1,0:T(8,128)(2,1)} %bitcast.66, bf16[4,16,4096]{2,1,0:T(8,128)(2,1)} %bitcast.67, bf16[4,16,4096]{2,1,0:T(8,128)(2,1)} %bitcast.68), custom_call_target="tpu_custom_call" | custom-call | tf_op jit(solution)/shard_map/pack/pallas_call | solution.py:93
  4.0 14.5 %collective-permute-start = (bf16[8,1,2,16,256]{4,3,2,1,0:T(8,128)(2,1)}, bf16[8,1,2,16,256]{4,3,2,1,0:T(8,128)(2,1)S(1)}, u32[]{:S(2)}, u32[]{:S(2)}) collective-permute-start(bf16[8,1,2,16,256]{4,3,2,1,0:T(8,128)(2,1)} %get-tuple-element.23), channel_id=1, source_target_pairs={{0,8},{1,9},{2,10},{3,11},{4,12},{5,13},{6,14},{7,15},{8,0},{9,1},... | collective-permute-start | bytes 393224 | tf_op jit(solution)/shard_map/ppermute | solution.py:558
  18.5 5.4 %all-to-all-start = ((bf16[8,4,4,16,512]{4,3,2,1,0:T(8,128)(2,1)}), bf16[8,4,4,16,512]{4,3,2,1,0:T(8,128)(2,1)}, u32[]{:S(2)}, u32[]{:S(2)}) async-start(bf16[8,4,4,16,512]{4,3,2,1,0:T(8,128)(2,1)} %get-tuple-element.22), calls=%async_computation | async-start | bytes 4194304 | tf_op jit(solution)/shard_map/all_to_all | solution.py:545
  25.9 4.5 %collective-permute-done.refs_0_.first_ref = bf16[8,1,2,16,256]{4,3,2,1,0:T(8,128)(2,1)S(1)} collective-permute-done((bf16[8,1,2,16,256]{4,3,2,1,0:T(8,128)(2,1)}, bf16[8,1,2,16,256]{4,3,2,1,0:T(8,128)(2,1)S(1)}, u32[]{:S(2)}, u32[]{:S(2)}) %collective-permute-start) | collective-permute-done | bytes 131104 | tf_op jit(solution)/shard_map/ppermute | solution.py:558
  30.4 18.3 %all-to-all-done = bf16[8,4,4,16,512]{4,3,2,1,0:T(8,128)(2,1)} async-done(((bf16[8,4,4,16,512]{4,3,2,1,0:T(8,128)(2,1)}), bf16[8,4,4,16,512]{4,3,2,1,0:T(8,128)(2,1)}, u32[]{:S(2)}, u32[]{:S(2)}) %all-to-all-start) | async-done | bytes 2097184 | tf_op jit(solution)/shard_map/all_to_all | solution.py:545
  48.7 8.0 %all-to-all-start.1 = ((bf16[32,4,16,512]{3,2,1,0:T(8,128)(2,1)}), bf16[32,4,16,512]{3,2,1,0:T(8,128)(2,1)S(1)}, u32[]{:S(2)}, u32[]{:S(2)}) async-start(bf16[32,4,16,512]{3,2,1,0:T(8,128)(2,1)} %bitcast.6.refs_1_), calls=%async_computation.1 | async-start | bytes 4194304 | tf_op jit(solution)/shard_map/all_to_all | solution.py:550
  56.7 5.3 %collective-permute-done.1.second_ref = bf16[8,3,2,16,256]{4,3,2,1,0:T(8,128)(2,1)S(1)} collective-permute-done((bf16[8,3,2,16,256]{4,3,2,1,0:T(8,128)(2,1)S(1)}, bf16[8,3,2,16,256]{4,3,2,1,0:T(8,128)(2,1)S(1)}, u32[]{:S(2)}, u32[]{:S(2)}) %collective-permute-start.1) | collective-permute-done | bytes 393248 | tf_op jit(solution)/shard_map/ppermute | solution.py:558
  62.0 9.3 %collective-permute-start.2 = (bf16[4,2,16,256]{3,2,1,0:T(8,128)(2,1)S(1)}, bf16[4,2,16,256]{3,2,1,0:T(8,128)(2,1)S(1)}, u32[]{:S(2)}, u32[]{:S(2)}) collective-permute-start(bf16[4,2,16,256]{3,2,1,0:T(8,128)(2,1)S(1)} %get-tuple-element.28), channel_id=1, source_target_pairs={{0,1},{1,0},{2,3},{3,2},{4,5},{5,4},{6,7},{7,6},{8,9},{9,8},{10,11... | collective-permute-start | bytes 196616 | tf_op jit(solution)/shard_map/ppermute | solution.py:558
  71.4 2.8 collective-permute-start.3
  78.2 3.2 collective-permute-start.5
  81.3 4.0 %collective-permute-start.6 = (bf16[4,2,16,256]{3,2,1,0:T(8,128)(2,1)S(1)}, bf16[4,2,16,256]{3,2,1,0:T(8,128)(2,1)S(1)}, u32[]{:S(2)}, u32[]{:S(2)}) collective-permute-start(bf16[4,2,16,256]{3,2,1,0:T(8,128)(2,1)S(1)} %get-tuple-element.32), channel_id=1, source_target_pairs={{0,5},{1,4},{2,7},{3,6},{4,1},{5,0},{6,3},{7,2},{8,13},{9,12},{10,... | collective-permute-start | bytes 196616 | tf_op jit(solution)/shard_map/ppermute | solution.py:558
  87.4 4.7 %collective-permute-start.8 = (bf16[4,2,16,256]{3,2,1,0:T(8,128)(2,1)S(1)}, bf16[4,2,16,256]{3,2,1,0:T(8,128)(2,1)S(1)}, u32[]{:S(2)}, u32[]{:S(2)}) collective-permute-start(bf16[4,2,16,256]{3,2,1,0:T(8,128)(2,1)S(1)} %get-tuple-element.34), channel_id=1, source_target_pairs={{0,7},{1,6},{2,5},{3,4},{4,3},{5,2},{6,1},{7,0},{8,15},{9,14},{10,... | collective-permute-start | bytes 196616 | tf_op jit(solution)/shard_map/ppermute | solution.py:558
  95.1 2.9 off_stats.1
  98.0 10.9 %collective-permute-start.9 = (f32[2,2,512]{2,1,0:T(2,128)S(1)}, f32[2,2,512]{2,1,0:T(2,128)S(1)}, u32[]{:S(2)}, u32[]{:S(2)}) collective-permute-start(f32[2,2,512]{2,1,0:T(2,128)S(1)} %off_stats.1), channel_id=1, source_target_pairs={{0,8},{1,9},{2,10},{3,11},{4,12},{5,13},{6,14},{7,15},{16,24},{17,... | collective-permute-start | bytes 24584 | tf_op jit(solution)/shard_map/ppermute | solution.py:554
  108.9 3.8 %row_stats.1 = f32[4,2,512]{2,1,0:T(2,128)S(1)} custom-call(s32[4]{0:T(128)S(1)} %pad_add_fusion.refs_0_.scal_ref, bf16[32,4,16,512]{3,2,1,0:T(8,128)(2,1)} %bitcast.6.refs_1_), custom_call_target="tpu_custom_call" | custom-call | flops 1342177280 | bytes 4194304 | tf_op jit(solution)/shard_map/row_stats/pallas_call | solution.py:406
  112.9 44.6 %all-to-all-done.1.refs_1_ = bf16[32,4,16,512]{3,2,1,0:T(8,128)(2,1)S(1)} async-done(((bf16[32,4,16,512]{3,2,1,0:T(8,128)(2,1)}), bf16[32,4,16,512]{3,2,1,0:T(8,128)(2,1)S(1)}, u32[]{:S(2)}, u32[]{:S(2)}) %all-to-all-start.1) | async-done | bytes 2097184 | tf_op jit(solution)/shard_map/all_to_all | solution.py:550
  160.2 7.8 %all-to-all-start.2 = ((f32[32,2,128]{2,1,0:T(2,128)}), f32[32,2,128]{2,1,0:T(2,128)S(1)}, u32[]{:S(2)}, u32[]{:S(2)}) async-start(f32[32,2,128]{2,1,0:T(2,128)} %copy.18), calls=%async_computation.2 | async-start | bytes 65536 | tf_op jit(solution)/shard_map/all_to_all | solution.py:550
  168.0 8.8 %all-to-all-done.2 = f32[32,2,128]{2,1,0:T(2,128)S(1)} async-done(((f32[32,2,128]{2,1,0:T(2,128)}), f32[32,2,128]{2,1,0:T(2,128)S(1)}, u32[]{:S(2)}, u32[]{:S(2)}) %all-to-all-start.2) | async-done | bytes 32800 | tf_op jit(solution)/shard_map/all_to_all | solution.py:550
  178.9 3.1 col_grads.1
  183.2 6.5 %all-to-all-start.3 = ((bf16[32,3,16,512]{3,2,1,0:T(8,128)(2,1)}), bf16[32,3,16,512]{3,2,1,0:T(8,128)(2,1)S(1)}, u32[]{:S(2)}, u32[]{:S(2)}) async-start(bf16[32,3,16,512]{3,2,1,0:T(8,128)(2,1)} %copy-done), calls=%async_computation.3 | async-start | bytes 3145728 | tf_op jit(solution)/shard_map/all_to_all | solution.py:550
  190.7 3.8 %off_grads.1 = (f32[2,512,256]{2,1,0:T(8,128)S(1)}, bf16[8,2,64,256]{3,2,1,0:T(8,128)(2,1)S(1)}) custom-call(s32[4]{0:T(128)S(1)} %pad_add_fusion.refs_0_.scal_ref, bf16[32,4,16,512]{3,2,1,0:T(8,128)(2,1)} %bitcast.6.refs_1_, f32[2,2,512]{2,1,0:T(2,128)S(1)} %fusion.2.refs_2_, f32[8,128]{1,0:T(8,128)S(1)} %hold.4.refs_3_, ...), custom_call_target="tpu_custom_call" | custom-call | flops 1677721600 | bytes 4194304 | tf_op jit(solution)/shard_map/off_grads/pallas_call | solution.py:333
  194.5 5.6 %collective-permute-start.11 = (bf16[2,64,256]{2,1,0:T(8,128)(2,1)S(1)}, bf16[2,64,256]{2,1,0:T(8,128)(2,1)S(1)}, u32[]{:S(2)}, u32[]{:S(2)}) collective-permute-start(bf16[2,64,256]{2,1,0:T(8,128)(2,1)S(1)} %get-tuple-element.49), channel_id=1, source_target_pairs={{0,1},{1,0},{2,3},{3,2},{4,5},{5,4},{6,7},{7,6},{8,9},{9,8},{10,11... | collective-permute-start | bytes 196616 | tf_op jit(solution)/shard_map/ppermute | solution.py:558
  202.2 3.4 %collective-permute-start.13 = (bf16[2,64,256]{2,1,0:T(8,128)(2,1)S(1)}, bf16[2,64,256]{2,1,0:T(8,128)(2,1)S(1)}, u32[]{:S(2)}, u32[]{:S(2)}) collective-permute-start(bf16[2,64,256]{2,1,0:T(8,128)(2,1)S(1)} %get-tuple-element.47), channel_id=1, source_target_pairs={{0,3},{1,2},{2,1},{3,0},{4,7},{5,6},{6,5},{7,4},{8,11},{9,10},{10,... | collective-permute-start | bytes 196616 | tf_op jit(solution)/shard_map/ppermute | solution.py:558
  205.6 2.7 collective-permute-start.14
  208.3 4.4 %collective-permute-start.15 = (bf16[2,64,256]{2,1,0:T(8,128)(2,1)S(1)}, bf16[2,64,256]{2,1,0:T(8,128)(2,1)S(1)}, u32[]{:S(2)}, u32[]{:S(2)}) collective-permute-start(bf16[2,64,256]{2,1,0:T(8,128)(2,1)S(1)} %get-tuple-element.45), channel_id=1, source_target_pairs={{0,5},{1,4},{2,7},{3,6},{4,1},{5,0},{6,3},{7,2},{8,13},{9,12},{10,... | collective-permute-start | bytes 196616 | tf_op jit(solution)/shard_map/ppermute | solution.py:558
  212.8 5.3 %row_grads.1.row_ref = bf16[32,3,16,512]{3,2,1,0:T(8,128)(2,1)S(1)} custom-call(s32[4]{0:T(128)S(1)} %pad_add_fusion.refs_0_.scal_ref, bf16[32,4,16,512]{3,2,1,0:T(8,128)(2,1)} %bitcast.6.refs_1_, f32[4,2,512]{2,1,0:T(2,128)S(1)} %pad_maximum_fusion.1.refs_2_, f32[2,512,256]{2,1,0:T(8,128)S(1)} %get-tuple-element.36.refs_3_), custom_call_target="tpu_custom_call" | custom-call | flops 2684354560 | bytes 4194304 | tf_op jit(solution)/shard_map/row_grads/pallas_call | solution.py:482
  221.3 4.8 %collective-permute-start.17 = (bf16[2,64,256]{2,1,0:T(8,128)(2,1)S(1)}, bf16[2,64,256]{2,1,0:T(8,128)(2,1)S(1)}, u32[]{:S(2)}, u32[]{:S(2)}) collective-permute-start(bf16[2,64,256]{2,1,0:T(8,128)(2,1)S(1)} %get-tuple-element.43), channel_id=1, source_target_pairs={{0,7},{1,6},{2,5},{3,4},{4,3},{5,2},{6,1},{7,0},{8,15},{9,14},{10,... | collective-permute-start | bytes 196616 | tf_op jit(solution)/shard_map/ppermute | solution.py:558
  228.6 33.6 %all-to-all-done.3.col_ref = bf16[32,3,16,512]{3,2,1,0:T(8,128)(2,1)S(1)} async-done(((bf16[32,3,16,512]{3,2,1,0:T(8,128)(2,1)}), bf16[32,3,16,512]{3,2,1,0:T(8,128)(2,1)S(1)}, u32[]{:S(2)}, u32[]{:S(2)}) %all-to-all-start.3) | async-done | bytes 1572896 | tf_op jit(solution)/shard_map/all_to_all | solution.py:550
  262.2 12.5 %collective-permute-start.18 = (bf16[8,64,256]{2,1,0:T(8,128)(2,1)S(1)}, bf16[8,64,256]{2,1,0:T(8,128)(2,1)S(1)}, u32[]{:S(2)}, u32[]{:S(2)}) collective-permute-start(bf16[8,64,256]{2,1,0:T(8,128)(2,1)S(1)} %get-tuple-element.39), channel_id=1, source_target_pairs={{0,8},{1,9},{2,10},{3,11},{4,12},{5,13},{6,14},{7,15},{8,0},{9,1},... | collective-permute-start | bytes 786440 | tf_op jit(solution)/shard_map/ppermute | solution.py:558
  279.3 6.1 %all-to-all-start.4 = ((bf16[8,4,3,16,512]{4,3,2,1,0:T(8,128)(2,1)}), bf16[8,4,3,16,512]{4,3,2,1,0:T(8,128)(2,1)S(1)}, u32[]{:S(2)}, u32[]{:S(2)}) async-start(bf16[8,4,3,16,512]{4,3,2,1,0:T(8,128)(2,1)} %bitcast.25), calls=%async_computation.4 | async-start | bytes 3145728 | tf_op jit(solution)/shard_map/all_to_all | solution.py:545
  285.4 20.5 %collective-permute-done.18.refs_0_.far_ref = bf16[8,64,256]{2,1,0:T(8,128)(2,1)S(1)} collective-permute-done((bf16[8,64,256]{2,1,0:T(8,128)(2,1)S(1)}, bf16[8,64,256]{2,1,0:T(8,128)(2,1)S(1)}, u32[]{:S(2)}, u32[]{:S(2)}) %collective-permute-start.18) | collective-permute-done | bytes 262176 | tf_op jit(solution)/shard_map/ppermute | solution.py:558
  305.9 12.4 %collective-permute-done.19.refs_1_.value_ref = bf16[8,64,256]{2,1,0:T(8,128)(2,1)S(1)} collective-permute-done((bf16[8,64,256]{2,1,0:T(8,128)(2,1)S(1)}, bf16[8,64,256]{2,1,0:T(8,128)(2,1)S(1)}, u32[]{:S(2)}, u32[]{:S(2)}) %collective-permute-start.19) | collective-permute-done | bytes 262176 | tf_op jit(solution)/shard_map/ppermute | solution.py:554
  (72 shorter events, 32.0 us)
Async XLA Ops:
  4.0 26.4 %collective-permute-start = (bf16[8,1,2,16,256]{4,3,2,1,0:T(8,128)(2,1)}, bf16[8,1,2,16,256]{4,3,2,1,0:T(8,128)(2,1)S(1)}, u32[]{:S(2)}, u32[]{:S(2)}) collective-permute-start(bf16[8,1,2,16,256]{4,3,2,1,0:T(8,128)(2,1)} %get-tuple-element.23), channel_id=1, source_target_pairs={{0,8},{1,9},{2,10},{3,11},{4,12},{5,13},{6,14},{7,15},{8,0},{9,1},... | collective-permute-start | bytes 393224 | tf_op jit(solution)/shard_map/ppermute | solution.py:558
  18.5 5.4 %copy-start.3 = (bf16[8,3,2,16,256]{4,3,2,1,0:T(8,128)(2,1)S(1)}, bf16[8,3,2,16,256]{4,3,2,1,0:T(8,128)(2,1)}, u32[]{:S(2)}) copy-start(bf16[8,3,2,16,256]{4,3,2,1,0:T(8,128)(2,1)} %get-tuple-element.25) | copy-start | bytes 1179652
  18.5 30.2 %all-to-all-start = ((bf16[8,4,4,16,512]{4,3,2,1,0:T(8,128)(2,1)}), bf16[8,4,4,16,512]{4,3,2,1,0:T(8,128)(2,1)}, u32[]{:S(2)}, u32[]{:S(2)}) async-start(bf16[8,4,4,16,512]{4,3,2,1,0:T(8,128)(2,1)} %get-tuple-element.22), calls=%async_computation | async-start | bytes 4194304 | tf_op jit(solution)/shard_map/all_to_all | solution.py:545
  23.9 38.1 %collective-permute-start.1 = (bf16[8,3,2,16,256]{4,3,2,1,0:T(8,128)(2,1)S(1)}, bf16[8,3,2,16,256]{4,3,2,1,0:T(8,128)(2,1)S(1)}, u32[]{:S(2)}, u32[]{:S(2)}) collective-permute-start(bf16[8,3,2,16,256]{4,3,2,1,0:T(8,128)(2,1)S(1)} %copy-done.3), channel_id=1, source_target_pairs={{0,8},{1,9},{2,10},{3,11},{4,12},{5,13},{6,14},{7,15},{8,0},{9,1},... | collective-permute-start | bytes 1179656 | tf_op jit(solution)/shard_map/ppermute | solution.py:558
  48.7 108.8 %all-to-all-start.1 = ((bf16[32,4,16,512]{3,2,1,0:T(8,128)(2,1)}), bf16[32,4,16,512]{3,2,1,0:T(8,128)(2,1)S(1)}, u32[]{:S(2)}, u32[]{:S(2)}) async-start(bf16[32,4,16,512]{3,2,1,0:T(8,128)(2,1)} %bitcast.6.refs_1_), calls=%async_computation.1 | async-start | bytes 4194304 | tf_op jit(solution)/shard_map/all_to_all | solution.py:550
  56.7 17.6 %copy-start.4 = (s32[8]{0:T(128)S(1)}, s32[8]{0:T(128)}, u32[]{:S(2)}) copy-start(s32[8]{0:T(128)} %param.11) | copy-start | bytes 100
  56.7 18.1 %copy-start.5 = (s32[32]{0:T(128)S(1)}, s32[32]{0:T(128)}, u32[]{:S(2)}) copy-start(s32[32]{0:T(128)} %param.10) | copy-start | bytes 388
  62.0 23.3 %collective-permute-start.2 = (bf16[4,2,16,256]{3,2,1,0:T(8,128)(2,1)S(1)}, bf16[4,2,16,256]{3,2,1,0:T(8,128)(2,1)S(1)}, u32[]{:S(2)}, u32[]{:S(2)}) collective-permute-start(bf16[4,2,16,256]{3,2,1,0:T(8,128)(2,1)S(1)} %get-tuple-element.28), channel_id=1, source_target_pairs={{0,1},{1,0},{2,3},{3,2},{4,5},{5,4},{6,7},{7,6},{8,9},{9,8},{10,11... | collective-permute-start | bytes 196616 | tf_op jit(solution)/shard_map/ppermute | solution.py:558
  71.4 16.0 %collective-permute-start.3 = (bf16[4,2,16,256]{3,2,1,0:T(8,128)(2,1)S(1)}, bf16[4,2,16,256]{3,2,1,0:T(8,128)(2,1)S(1)}, u32[]{:S(2)}, u32[]{:S(2)}) collective-permute-start(bf16[4,2,16,256]{3,2,1,0:T(8,128)(2,1)S(1)} %get-tuple-element.29), channel_id=1, source_target_pairs={{0,2},{1,3},{2,0},{3,1},{4,6},{5,7},{6,4},{7,5},{8,10},{9,11},{10,... | collective-permute-start | bytes 196616 | tf_op jit(solution)/shard_map/ppermute | solution.py:558
  75.5 17.9 %collective-permute-start.4 = (bf16[4,2,16,256]{3,2,1,0:T(8,128)(2,1)S(1)}, bf16[4,2,16,256]{3,2,1,0:T(8,128)(2,1)S(1)}, u32[]{:S(2)}, u32[]{:S(2)}) collective-permute-start(bf16[4,2,16,256]{3,2,1,0:T(8,128)(2,1)S(1)} %get-tuple-element.30), channel_id=1, source_target_pairs={{0,3},{1,2},{2,1},{3,0},{4,7},{5,6},{6,5},{7,4},{8,11},{9,10},{10,... | collective-permute-start | bytes 196616 | tf_op jit(solution)/shard_map/ppermute | solution.py:558
  78.2 15.2 %collective-permute-start.5 = (bf16[4,2,16,256]{3,2,1,0:T(8,128)(2,1)S(1)}, bf16[4,2,16,256]{3,2,1,0:T(8,128)(2,1)S(1)}, u32[]{:S(2)}, u32[]{:S(2)}) collective-permute-start(bf16[4,2,16,256]{3,2,1,0:T(8,128)(2,1)S(1)} %get-tuple-element.31), channel_id=1, source_target_pairs={{0,4},{1,5},{2,6},{3,7},{4,0},{5,1},{6,2},{7,3},{8,12},{9,13},{10,... | collective-permute-start | bytes 196616 | tf_op jit(solution)/shard_map/ppermute | solution.py:558
  81.3 12.1 %collective-permute-start.6 = (bf16[4,2,16,256]{3,2,1,0:T(8,128)(2,1)S(1)}, bf16[4,2,16,256]{3,2,1,0:T(8,128)(2,1)S(1)}, u32[]{:S(2)}, u32[]{:S(2)}) collective-permute-start(bf16[4,2,16,256]{3,2,1,0:T(8,128)(2,1)S(1)} %get-tuple-element.32), channel_id=1, source_target_pairs={{0,5},{1,4},{2,7},{3,6},{4,1},{5,0},{6,3},{7,2},{8,13},{9,12},{10,... | collective-permute-start | bytes 196616 | tf_op jit(solution)/shard_map/ppermute | solution.py:558
  85.3 8.1 %collective-permute-start.7 = (bf16[4,2,16,256]{3,2,1,0:T(8,128)(2,1)S(1)}, bf16[4,2,16,256]{3,2,1,0:T(8,128)(2,1)S(1)}, u32[]{:S(2)}, u32[]{:S(2)}) collective-permute-start(bf16[4,2,16,256]{3,2,1,0:T(8,128)(2,1)S(1)} %get-tuple-element.33), channel_id=1, source_target_pairs={{0,6},{1,7},{2,4},{3,5},{4,2},{5,3},{6,0},{7,1},{8,14},{9,15},{10,... | collective-permute-start | bytes 196616 | tf_op jit(solution)/shard_map/ppermute | solution.py:558
  87.4 7.7 %collective-permute-start.8 = (bf16[4,2,16,256]{3,2,1,0:T(8,128)(2,1)S(1)}, bf16[4,2,16,256]{3,2,1,0:T(8,128)(2,1)S(1)}, u32[]{:S(2)}, u32[]{:S(2)}) collective-permute-start(bf16[4,2,16,256]{3,2,1,0:T(8,128)(2,1)S(1)} %get-tuple-element.34), channel_id=1, source_target_pairs={{0,7},{1,6},{2,5},{3,4},{4,3},{5,2},{6,1},{7,0},{8,15},{9,14},{10,... | collective-permute-start | bytes 196616 | tf_op jit(solution)/shard_map/ppermute | solution.py:558
  98.0 14.8 %collective-permute-start.9 = (f32[2,2,512]{2,1,0:T(2,128)S(1)}, f32[2,2,512]{2,1,0:T(2,128)S(1)}, u32[]{:S(2)}, u32[]{:S(2)}) collective-permute-start(f32[2,2,512]{2,1,0:T(2,128)S(1)} %off_stats.1), channel_id=1, source_target_pairs={{0,8},{1,9},{2,10},{3,11},{4,12},{5,13},{6,14},{7,15},{16,24},{17,... | collective-permute-start | bytes 24584 | tf_op jit(solution)/shard_map/ppermute | solution.py:554
  160.2 16.7 %all-to-all-start.2 = ((f32[32,2,128]{2,1,0:T(2,128)}), f32[32,2,128]{2,1,0:T(2,128)S(1)}, u32[]{:S(2)}, u32[]{:S(2)}) async-start(f32[32,2,128]{2,1,0:T(2,128)} %copy.18), calls=%async_computation.2 | async-start | bytes 65536 | tf_op jit(solution)/shard_map/all_to_all | solution.py:550
  177.6 13.1 %collective-permute-start.10 = (f32[2,2,512]{2,1,0:T(2,128)S(1)}, f32[2,2,512]{2,1,0:T(2,128)S(1)}, u32[]{:S(2)}, u32[]{:S(2)}) collective-permute-start(f32[2,2,512]{2,1,0:T(2,128)S(1)} %fusion.3), channel_id=1, source_target_pairs={{8,0},{9,1},{10,2},{11,3},{12,4},{13,5},{14,6},{15,7},{24,16},{25,... | collective-permute-start | bytes 24584 | tf_op jit(solution)/shard_map/ppermute | solution.py:554
  182.0 1.2 copy-start
  183.2 79.0 %all-to-all-start.3 = ((bf16[32,3,16,512]{3,2,1,0:T(8,128)(2,1)}), bf16[32,3,16,512]{3,2,1,0:T(8,128)(2,1)S(1)}, u32[]{:S(2)}, u32[]{:S(2)}) async-start(bf16[32,3,16,512]{3,2,1,0:T(8,128)(2,1)} %copy-done), calls=%async_computation.3 | async-start | bytes 3145728 | tf_op jit(solution)/shard_map/all_to_all | solution.py:550
  194.5 24.8 %collective-permute-start.11 = (bf16[2,64,256]{2,1,0:T(8,128)(2,1)S(1)}, bf16[2,64,256]{2,1,0:T(8,128)(2,1)S(1)}, u32[]{:S(2)}, u32[]{:S(2)}) collective-permute-start(bf16[2,64,256]{2,1,0:T(8,128)(2,1)S(1)} %get-tuple-element.49), channel_id=1, source_target_pairs={{0,1},{1,0},{2,3},{3,2},{4,5},{5,4},{6,7},{7,6},{8,9},{9,8},{10,11... | collective-permute-start | bytes 196616 | tf_op jit(solution)/shard_map/ppermute | solution.py:558
  200.1 21.1 %collective-permute-start.12 = (bf16[2,64,256]{2,1,0:T(8,128)(2,1)S(1)}, bf16[2,64,256]{2,1,0:T(8,128)(2,1)S(1)}, u32[]{:S(2)}, u32[]{:S(2)}) collective-permute-start(bf16[2,64,256]{2,1,0:T(8,128)(2,1)S(1)} %get-tuple-element.48), channel_id=1, source_target_pairs={{0,2},{1,3},{2,0},{3,1},{4,6},{5,7},{6,4},{7,5},{8,10},{9,11},{10,... | collective-permute-start | bytes 196616 | tf_op jit(solution)/shard_map/ppermute | solution.py:558
  202.2 23.9 %collective-permute-start.13 = (bf16[2,64,256]{2,1,0:T(8,128)(2,1)S(1)}, bf16[2,64,256]{2,1,0:T(8,128)(2,1)S(1)}, u32[]{:S(2)}, u32[]{:S(2)}) collective-permute-start(bf16[2,64,256]{2,1,0:T(8,128)(2,1)S(1)} %get-tuple-element.47), channel_id=1, source_target_pairs={{0,3},{1,2},{2,1},{3,0},{4,7},{5,6},{6,5},{7,4},{8,11},{9,10},{10,... | collective-permute-start | bytes 196616 | tf_op jit(solution)/shard_map/ppermute | solution.py:558
  205.6 20.5 %collective-permute-start.14 = (bf16[2,64,256]{2,1,0:T(8,128)(2,1)S(1)}, bf16[2,64,256]{2,1,0:T(8,128)(2,1)S(1)}, u32[]{:S(2)}, u32[]{:S(2)}) collective-permute-start(bf16[2,64,256]{2,1,0:T(8,128)(2,1)S(1)} %get-tuple-element.46), channel_id=1, source_target_pairs={{0,4},{1,5},{2,6},{3,7},{4,0},{5,1},{6,2},{7,3},{8,12},{9,13},{10,... | collective-permute-start | bytes 196616 | tf_op jit(solution)/shard_map/ppermute | solution.py:558
  208.3 17.8 %collective-permute-start.15 = (bf16[2,64,256]{2,1,0:T(8,128)(2,1)S(1)}, bf16[2,64,256]{2,1,0:T(8,128)(2,1)S(1)}, u32[]{:S(2)}, u32[]{:S(2)}) collective-permute-start(bf16[2,64,256]{2,1,0:T(8,128)(2,1)S(1)} %get-tuple-element.45), channel_id=1, source_target_pairs={{0,5},{1,4},{2,7},{3,6},{4,1},{5,0},{6,3},{7,2},{8,13},{9,12},{10,... | collective-permute-start | bytes 196616 | tf_op jit(solution)/shard_map/ppermute | solution.py:558
  218.1 1.2 copy-start.1
  219.3 6.8 %collective-permute-start.16 = (bf16[2,64,256]{2,1,0:T(8,128)(2,1)S(1)}, bf16[2,64,256]{2,1,0:T(8,128)(2,1)S(1)}, u32[]{:S(2)}, u32[]{:S(2)}) collective-permute-start(bf16[2,64,256]{2,1,0:T(8,128)(2,1)S(1)} %get-tuple-element.44), channel_id=1, source_target_pairs={{0,6},{1,7},{2,4},{3,5},{4,2},{5,3},{6,0},{7,1},{8,14},{9,15},{10,... | collective-permute-start | bytes 196616 | tf_op jit(solution)/shard_map/ppermute | solution.py:558
  221.3 7.3 %collective-permute-start.17 = (bf16[2,64,256]{2,1,0:T(8,128)(2,1)S(1)}, bf16[2,64,256]{2,1,0:T(8,128)(2,1)S(1)}, u32[]{:S(2)}, u32[]{:S(2)}) collective-permute-start(bf16[2,64,256]{2,1,0:T(8,128)(2,1)S(1)} %get-tuple-element.43), channel_id=1, source_target_pairs={{0,7},{1,6},{2,5},{3,4},{4,3},{5,2},{6,1},{7,0},{8,15},{9,14},{10,... | collective-permute-start | bytes 196616 | tf_op jit(solution)/shard_map/ppermute | solution.py:558
  262.2 43.7 %collective-permute-start.18 = (bf16[8,64,256]{2,1,0:T(8,128)(2,1)S(1)}, bf16[8,64,256]{2,1,0:T(8,128)(2,1)S(1)}, u32[]{:S(2)}, u32[]{:S(2)}) collective-permute-start(bf16[8,64,256]{2,1,0:T(8,128)(2,1)S(1)} %get-tuple-element.39), channel_id=1, source_target_pairs={{0,8},{1,9},{2,10},{3,11},{4,12},{5,13},{6,14},{7,15},{8,0},{9,1},... | collective-permute-start | bytes 786440 | tf_op jit(solution)/shard_map/ppermute | solution.py:558
  274.7 43.5 %collective-permute-start.19 = (bf16[8,64,256]{2,1,0:T(8,128)(2,1)S(1)}, bf16[8,64,256]{2,1,0:T(8,128)(2,1)S(1)}, u32[]{:S(2)}, u32[]{:S(2)}) collective-permute-start(bf16[8,64,256]{2,1,0:T(8,128)(2,1)S(1)} %get-tuple-element.40), channel_id=1, source_target_pairs={{8,0},{9,1},{10,2},{11,3},{12,4},{13,5},{14,6},{15,7},{24,16},{25,... | collective-permute-start | bytes 786440 | tf_op jit(solution)/shard_map/ppermute | solution.py:554
  276.0 1.4 copy-start.2
  279.3 39.0 %all-to-all-start.4 = ((bf16[8,4,3,16,512]{4,3,2,1,0:T(8,128)(2,1)}), bf16[8,4,3,16,512]{4,3,2,1,0:T(8,128)(2,1)S(1)}, u32[]{:S(2)}, u32[]{:S(2)}) async-start(bf16[8,4,3,16,512]{4,3,2,1,0:T(8,128)(2,1)} %bitcast.25), calls=%async_computation.4 | async-start | bytes 3145728 | tf_op jit(solution)/shard_map/all_to_all | solution.py:545
